TPU v7x, 256 devices: a whole 4x4x8 slice. The times are simulated.
256 devices in a mesh: dp: 16 (over z_hi, x), grp: 4 (over z_lo, core), rep: 4 (over y).
Axes of the slice: x: 4, y: 4, z: 8 (z_hi: 4, z_lo: 2; z = z_hi * 2 + z_lo), core: 2. Of those that a mesh axis runs over, the one named last changes fastest.
Arguments:
- activations: bfloat16 [32768, 4096], P(('dp', 'grp', 'rep')), may hold values from -60 to 60
- out_grads: bfloat16 [32768, 10240], P(('dp', 'grp', 'rep')), may hold values from -60 to 60
- a_running: float32 [16, 256, 256], replicated, may hold values from -40 to 60, as said below
- g_running: float32 [32, 320, 320], P('dp'), may hold values from -40 to 60, as said below
- grad_partial: bfloat16 [4, 4096, 10240], P('rep', 'grp', 'dp'), may hold values from -96 to 96
Outputs:
- preconditioned: bfloat16 [4096, 10240], P('grp', 'dp')
Inputs may be any that keep to these rules, and one draw needn't show every extreme that they name: `a_running`: each block is symmetric positive definite. `g_running`: each block is symmetric positive definite.
All inputs are finite; a program needn't handle non-finite values.
Results may differ from a plain program's by a relative error of at most 0.001.
Values may be sent and summed in bfloat16 or wider, within the bound.
No kernel may reach another device: no remote copies, remote signals or barrier semaphores. Data moves between devices by JAX's collectives and lax.ppermute only.
A program may use at most 128 MiB of HBM per device.

v0:
```python
import functools

import jax
import jax.numpy as jnp
from jax import lax
from jax.experimental import pallas as pl
from jax.experimental.pallas import tpu as pltpu
from jax.sharding import Mesh, PartitionSpec as P

BA = 256
BG = 320
BGP = 384
ITERS = 8
G_TILES = 112
A_TILES = 48

factor_decay = 0.9
damping = 0.1

ANY = pl.BlockSpec(memory_space=pl.ANY)
VMEM = pl.BlockSpec(memory_space=pltpu.VMEM)


def swap_cores(value):
    return lax.ppermute(value, "c", [(0, 1), (1, 0)])


def send_round(axis, chunks):
    size = lax.axis_size(axis)
    return [chunks[0]] + [
        lax.ppermute(chunks[s], axis, [(i, (i + s) % size) for i in range(size)])
        for s in range(1, size)
    ]


def pack_kernel(axis, width, src, *rest):
    outs, sem = rest[:4], rest[4]
    here = lax.axis_index(axis)
    copies = []
    for s in (1, 2, 3, 0):
        peer = lax.rem(here + s, 4)
        for q in range(4):
            start = pl.multiple_of((q * 4 + peer) * width, 128)
            copies.append(pltpu.make_async_copy(
                src.at[:, pl.ds(start, width)], outs[s].at[q], sem.at[s * 4 + q]
            ))
    for copy in copies:
        copy.start()
    for copy in copies:
        copy.wait()


def pack(samples, axis, width):
    piece = jax.ShapeDtypeStruct((4, samples.shape[0], width), samples.dtype)
    return pl.pallas_call(
        functools.partial(pack_kernel, axis, width),
        out_shape=[piece] * 4,
        in_specs=[ANY],
        out_specs=[ANY] * 4,
        scratch_shapes=[pltpu.SemaphoreType.DMA((16,))],
    )(samples)


def gram(v):
    return lax.dot_general(v, v, (((0,), (0,)), ((), ())), preferred_element_type=jnp.float32)


def grid_of(n):
    return (lax.broadcasted_iota(jnp.int32, (n, n), 0), lax.broadcasted_iota(jnp.int32, (n, n), 1))


def g_cov_kernel(i0, i1, i2, i3, own, other, rows, tiles):
    c = lax.axis_index("c")
    for s, ref in enumerate((i0, i1, i2, i3)):
        rows[s * 128:(s + 1) * 128, :] = ref[0]
    first = gram(rows[:, 0:BGP])[:BG, :BG]
    second = gram(rows[:, 2 * BG - BGP:2 * BG])[BGP - BG:, BGP - BG:]
    r, k = grid_of(BG)
    fold = jnp.where(r >= k, first, second)
    diag = jnp.sum(jnp.where(r == k, second, 0.0), axis=0, keepdims=True)
    half = BG // 2
    wide = jnp.concatenate([fold[:half], fold[half:]], axis=1)
    tail = jnp.concatenate([jnp.broadcast_to(diag, (8, BG)), jnp.zeros((8, BG), jnp.float32)], axis=1)
    for l in range(5):
        tiles[l * 21:l * 21 + 20] = wide[:, l * 128:(l + 1) * 128].reshape(20, 8, 128)
        tiles[l * 21 + 20] = tail[:, l * 128:(l + 1) * 128]
    tiles[105:] = jnp.zeros((7, 8, 128), jnp.float32)
    own[0] = tiles[pl.ds(c * 56, 56)]
    other[0] = tiles[pl.ds((1 - c) * 56, 56)]


def g_cov(chunks):
    spec = pl.BlockSpec((1, 128, 2 * BG), lambda q: (q, 0, 0))
    out = pl.BlockSpec((1, 56, 8, 128), lambda q: (q, 0, 0, 0))
    return pl.pallas_call(
        g_cov_kernel,
        grid=(4,),
        out_shape=[jax.ShapeDtypeStruct((4, 56, 8, 128), jnp.float32)] * 2,
        in_specs=[spec] * 4,
        out_specs=[out] * 2,
        scratch_shapes=[pltpu.VMEM((512, 2 * BG), jnp.bfloat16), pltpu.VMEM((G_TILES, 8, 128), jnp.float32)],
        compiler_params=pltpu.CompilerParams(vmem_limit_bytes=32 << 20),
    )(*chunks)


def a_cov_kernel(i0, i1, i2, i3, own, other, rows):
    c = lax.axis_index("c")
    r, k = grid_of(128)
    for zl in range(2):
        for which, out in ((c, own), (1 - c, other)):
            q = zl * 2 + which
            for s, ref in enumerate((i0, i1, i2, i3)):
                rows[s * 128:(s + 1) * 128, :] = ref[q]
            cov = gram(rows[...])
            corner = cov[128:, 128:]
            fold = jnp.where(r >= k, cov[:128, :128], corner)
            diag = jnp.sum(jnp.where(r == k, corner, 0.0), axis=0, keepdims=True)
            out[zl, 0:16] = cov[128:, :128].reshape(16, 8, 128)
            out[zl, 16:32] = fold.reshape(16, 8, 128)
            out[zl, 32] = jnp.broadcast_to(diag, (8, 128))
            out[zl, 33:] = jnp.zeros((A_TILES - 33, 8, 128), jnp.float32)


def a_cov(chunks):
    return pl.pallas_call(
        a_cov_kernel,
        out_shape=[jax.ShapeDtypeStruct((2, A_TILES, 8, 128), jnp.float32)] * 2,
        in_specs=[VMEM] * 4,
        out_specs=[VMEM] * 2,
        scratch_shapes=[pltpu.VMEM((512, BA), jnp.bfloat16)],
        compiler_params=pltpu.CompilerParams(vmem_limit_bytes=32 << 20),
    )(*chunks)


def reduce_pieces(value, axes):
    return jnp.sum(lax.all_to_all(value, axes, 0, 0, tiled=True), axis=0)


def gather_pieces(value, axes):
    size = lax.axis_size(axes)
    every = jnp.broadcast_to(value[None], (size, *value.shape))
    return lax.all_to_all(every, axes, 0, 0, tiled=True)


def split(value):
    high = value.astype(jnp.bfloat16)
    return high, (value - high.astype(jnp.float32)).astype(jnp.bfloat16)


def dot3(left, right):
    dot = functools.partial(jnp.dot, preferred_element_type=jnp.float32)
    return dot(left[0], right[0]) + (dot(left[0], right[1]) + dot(left[1], right[0]))


def newton(matrices, identity):
    n = identity.shape[0]
    state = []
    for matrix in matrices:
        trace = jnp.sum(matrix * identity)
        scaled = matrix / trace
        step = 2.0 * identity - scaled
        state.append((step / trace, dot3(split(scaled), split(step))))
    for _ in range(ITERS - 2):
        following = []
        for approx, product in state:
            both = dot3(split(jnp.concatenate([approx, product], axis=0)), split(2.0 * identity - product))
            following.append((both[:n], both[n:]))
        state = following
    return [dot3(split(approx), split(2.0 * identity - product)) for approx, product in state]


def a_side_kernel(tiles, running, g0, g1, g2, g3, left, *, token_total):
    r, k = grid_of(128)
    low = tiles[0:16].reshape(128, 128)
    fold = tiles[16:32].reshape(128, 128)
    diag = tiles[32][0:1]
    turned = fold.T
    top = jnp.where(r >= k, fold, turned)
    corner = jnp.where(r == k, jnp.broadcast_to(diag, (128, 128)), jnp.where(r < k, fold, turned))
    cov = jnp.concatenate([
        jnp.concatenate([top, low.T], axis=1), jnp.concatenate([low, corner], axis=1)
    ], axis=0)
    r, k = grid_of(BA)
    identity = jnp.where(r == k, 1.0, 0.0)
    mixed = factor_decay * running[0] + (1.0 - factor_decay) * cov / token_total
    inverse, = newton([mixed + damping * identity], identity)
    summed = (g0[...].astype(jnp.float32) + g1[...].astype(jnp.float32)) + (
        g2[...].astype(jnp.float32) + g3[...].astype(jnp.float32)
    )
    left[...] = dot3(split(inverse), split(summed))


def a_side(tiles, running, grads, token_total):
    return pl.pallas_call(
        functools.partial(a_side_kernel, token_total=token_total),
        out_shape=jax.ShapeDtypeStruct((BA, 2 * BG), jnp.float32),
        in_specs=[VMEM] * 6,
        out_specs=VMEM,
        compiler_params=pltpu.CompilerParams(vmem_limit_bytes=32 << 20),
        cost_estimate=pl.CostEstimate(flops=2_500_000_000, bytes_accessed=2_000_000, transcendentals=0),
    )(tiles, running, *grads)


def g_side_kernel(tiles, running, left, out, fold, wide, *, token_total):
    half = BG // 2
    for l in range(5):
        wide[:, l * 128:(l + 1) * 128] = tiles[l * 21:(l + 1) * 21].reshape(168, 128)
    fold[...] = jnp.zeros((BGP, BGP), jnp.float32)
    fold[0:half, 0:BG] = wide[0:half, 0:BG]
    fold[half:BG, 0:BG] = wide[0:half, BG:]
    diag = jnp.concatenate([wide[half:half + 1, 0:BG], jnp.zeros((1, BGP - BG), jnp.float32)], axis=1)
    r, k = grid_of(BGP)
    held = fold[...]
    turned = held.T
    first = jnp.where(r >= k, held, turned)
    second = jnp.where(r == k, jnp.broadcast_to(diag, (BGP, BGP)), jnp.where(r < k, held, turned))
    identity = jnp.where((r == k) & (r < BG), 1.0, 0.0)
    matrices = []
    for n, cov in enumerate((first, second)):
        fold[0:BG, 0:BG] = running[n]
        mixed = factor_decay * fold[...] + (1.0 - factor_decay) * cov / token_total
        matrices.append(mixed + damping * identity)
    inverse = newton(matrices, identity)
    for n in range(2):
        part = left[:, n * BG:(n + 1) * BG]
        done = dot3(split(part), split(inverse[n][:BG, :BG]))
        out[:, n * BG:(n + 1) * BG] = done.astype(jnp.bfloat16)


def g_side(tiles, running, left, token_total):
    return pl.pallas_call(
        functools.partial(g_side_kernel, token_total=token_total),
        out_shape=jax.ShapeDtypeStruct((BA, 2 * BG), jnp.bfloat16),
        in_specs=[VMEM] * 3,
        out_specs=VMEM,
        scratch_shapes=[pltpu.VMEM((BGP, BGP), jnp.float32), pltpu.VMEM((168, 2 * BG), jnp.float32)],
        compiler_params=pltpu.CompilerParams(vmem_limit_bytes=40 << 20),
        cost_estimate=pl.CostEstimate(flops=10_000_000_000, bytes_accessed=3_000_000, transcendentals=0),
    )(tiles, running, left)


def per_device(activations, out_grads, a_running, g_running, grad_partial):
    token_total = float(activations.shape[0] * 256)
    zl, c, y = lax.axis_index("zl"), lax.axis_index("c"), lax.axis_index("y")

    g_in = send_round("x", pack(out_grads, "x", 2 * BG))
    a_in = send_round("y", pack(activations, "y", BA))
    grads = send_round("y", [
        lax.dynamic_slice_in_dim(grad_partial[0], lax.rem(y + s, 4) * BA, BA, 0) for s in range(4)
    ])

    a_own, a_other = a_cov(a_in)
    a_part = a_own + swap_cores(a_other)
    a_piece = reduce_pieces(a_part.reshape(32, A_TILES // 2, 128), ("zl", "zh", "x"))
    a_tiles = gather_pieces(a_piece, ("zh", "x")).reshape(A_TILES, 8, 128)

    g_in, a_tiles, grads = lax.optimization_barrier((g_in, a_tiles, grads))
    g_own, g_other = g_cov(g_in)
    g_part = g_own + swap_cores(g_other)
    g_piece = reduce_pieces(g_part.reshape(32, 56, 128), ("zh", "zl", "y"))
    g_tiles = gather_pieces(g_piece, ("c", "zl", "y")).reshape(G_TILES, 8, 128)

    a_previous = lax.dynamic_slice_in_dim(a_running, (zl * 2 + c) * 4 + y, 1, 0)
    left = a_side(a_tiles, a_previous, grads, token_total)
    rows = g_side(g_tiles, g_running, left, token_total)

    out = jnp.zeros((4, BA, 2 * BG), jnp.bfloat16)
    for shift, got in enumerate(send_round("y", [rows] * 4)):
        out = lax.dynamic_update_slice_in_dim(out, got[None], lax.rem(y + 4 - shift, 4), 0)
    return out.reshape(4 * BA, 2 * BG)


def solution(mesh):
    fine = Mesh(mesh.devices.reshape(4, 4, 2, 2, 4), ("zh", "x", "zl", "c", "y"))
    tokens = P(("zh", "x", "zl", "c", "y"), None)
    placed = (tokens, tokens, P(), P(("zh", "x"), None, None), P("y", ("zl", "c"), ("zh", "x")))
    return jax.shard_map(
        per_device,
        mesh=fine,
        in_specs=placed,
        out_specs=P(("zl", "c"), ("zh", "x")),
        check_vma=False,
    )
```

profile of v0, /device:TPU:1, one launch (start us, length us, event | category | flops | bytes accessed | tf_op | source)
XLA Modules:
  0.0 276.3 jit_solution(13427249210928177289)
XLA Ops:
  0.0 33.0 %shard_map.56 = (bf16[4,128,256]{2,1,0:T(8,128)(2,1)}, bf16[4,128,256]{2,1,0:T(8,128)(2,1)}, bf16[4,128,256]{2,1,0:T(8,128)(2,1)}, bf16[4,128,256]{2,1,0:T(8,128)(2,1)}) custom-call(bf16[128,4096]{1,0:T(8,128)(2,1)} %src.3), custom_call_target="tpu_custom_call" | custom-call | tf_op jit(solution)/shard_map/pallas_call | solution.py:55
  33.0 2.2 collective-permute-start.3
  35.2 2.6 collective-permute-start.4
  37.8 1.1 collective-permute-start.5
  38.9 1.7 collective-permute-done.3.i1
  40.6 8.7 %collective-permute-done.4.i2 = bf16[4,128,256]{2,1,0:T(8,128)(2,1)S(1)} collective-permute-done((bf16[4,128,256]{2,1,0:T(8,128)(2,1)}, bf16[4,128,256]{2,1,0:T(8,128)(2,1)S(1)}, u32[]{:S(2)}, u32[]{:S(2)}) %collective-permute-start.4) | collective-permute-done | bytes 262176 | tf_op jit(solution)/shard_map/ppermute | solution.py:31
  49.4 0.9 copy-done.1
  50.3 0.5 shard_map.57
  50.8 1.6 collective-permute-start.6
  52.5 1.3 collective-permute-done.6
  53.8 0.8 add.63
  54.6 11.1 %all-to-all-start = ((f32[32,24,128]{2,1,0:T(8,128)}), f32[32,24,128]{2,1,0:T(8,128)}, u32[]{:S(2)}, u32[]{:S(2)}) async-start(f32[32,24,128]{2,1,0:T(8,128)} %bitcast), calls=%async_computation | async-start | bytes 786432 | tf_op jit(solution)/shard_map/all_to_all | solution.py:136
  65.8 1.0 dynamic-slice_bitcast_fusion
  66.8 1.0 collective-permute-start.7
  67.8 80.7 %shard_map.55 = (bf16[4,128,640]{2,1,0:T(8,128)(2,1)}, bf16[4,128,640]{2,1,0:T(8,128)(2,1)}, bf16[4,128,640]{2,1,0:T(8,128)(2,1)}, bf16[4,128,640]{2,1,0:T(8,128)(2,1)}) custom-call(bf16[128,10240]{1,0:T(8,128)(2,1)} %src.2), custom_call_target="tpu_custom_call" | custom-call | tf_op jit(solution)/shard_map/pallas_call | solution.py:55
  148.4 1.2 collective-permute-start
  149.7 2.4 collective-permute-start.1
  152.1 1.2 collective-permute-start.2
  153.3 1.0 reduce_sum.18
  154.3 0.7 broadcast_in_dim.28
  155.0 6.5 %all-to-all-start.1 = ((f32[16,24,128]{2,1,0:T(8,128)}), f32[16,24,128]{2,1,0:T(8,128)S(1)}, u32[]{:S(2)}, u32[]{:S(2)}) async-start(f32[16,24,128]{2,1,0:T(8,128)} %broadcast_in_dim.28), calls=%async_computation.1 | async-start | bytes 393216 | tf_op jit(solution)/shard_map/all_to_all | solution.py:142
  161.5 2.2 collective-permute-start.8
  163.7 1.3 collective-permute-start.9
  165.0 5.2 %collective-permute-done.8.g2 = bf16[256,640]{1,0:T(8,128)(2,1)S(1)} collective-permute-done((bf16[256,640]{1,0:T(8,128)(2,1)}, bf16[256,640]{1,0:T(8,128)(2,1)S(1)}, u32[]{:S(2)}, u32[]{:S(2)}) %collective-permute-start.8) | collective-permute-done | bytes 327712 | tf_op jit(solution)/shard_map/ppermute | solution.py:31
  170.1 0.7 copy-done.3
  170.9 7.4 %collective-permute-done.9.g3 = bf16[256,640]{1,0:T(8,128)(2,1)S(1)} collective-permute-done((bf16[256,640]{1,0:T(8,128)(2,1)}, bf16[256,640]{1,0:T(8,128)(2,1)S(1)}, u32[]{:S(2)}, u32[]{:S(2)}) %collective-permute-start.9) | collective-permute-done | bytes 327712 | tf_op jit(solution)/shard_map/ppermute | solution.py:31
  178.3 0.7 copy-done.5
  179.0 2.5 collective-permute-done.1.i2
  181.5 0.4 collective-permute-done.2.i3
  181.9 0.3 all-to-all-done.1
  182.2 3.2 %shard_map.58 = (f32[4,56,8,128]{3,2,1,0:T(8,128)S(1)}, f32[4,56,8,128]{3,2,1,0:T(8,128)S(1)}) custom-call(bf16[4,128,640]{2,1,0:T(8,128)(2,1)S(1)} %copy-done, bf16[4,128,640]{2,1,0:T(8,128)(2,1)S(1)} %collective-permute-done.i1, bf16[4,128,640]{2,1,0:T(8,128)(2,1)S(1)} %collective-permute-done.1.i2, bf16[4,128,640]{2,1,0:T(8,128)(2,1)S(1)} %collective-permute-done.2.i3), custom_call_target="tpu_custom_call" | custom-call | tf_op jit(solution)/shard_map/pallas_call | solution.py:95
  185.4 1.9 collective-permute-start.10
  187.3 2.1 collective-permute-done.10
  189.5 32.3 %all_to_all.20 = f32[32,56,128]{2,1,0:T(8,128)S(1)} all-to-all(f32[32,56,128]{2,1,0:T(8,128)S(1)} %bitcast.23), channel_id=1, replica_groups=mesh['zh'=4,'x'=4,'zl'=2,'c'=2,'y'=4] {'zh','zl','y'}, dimensions={0} | all-to-all | bytes 1835008 | tf_op jit(solution)/shard_map/all_to_all | solution.py:136
  221.9 0.8 broadcast_in_dim.29
  222.7 6.9 %all-to-all-start.3 = ((f32[16,56,128]{2,1,0:T(8,128)}), f32[16,56,128]{2,1,0:T(8,128)S(1)}, u32[]{:S(2)}, u32[]{:S(2)}) async-start(f32[16,56,128]{2,1,0:T(8,128)} %broadcast_in_dim.29), calls=%async_computation.3 | async-start | bytes 917504 | tf_op jit(solution)/shard_map/all_to_all | solution.py:142
  229.6 1.0 constant_dynamic-slice_fusion.running
  230.6 4.6 %shard_map.59.left = f32[256,640]{1,0:T(8,128)S(1)} custom-call(f32[48,8,128]{2,1,0:T(8,128)S(1)} %bitcast.22, f32[1,256,256]{2,1,0:T(8,128)S(1)} %constant_dynamic-slice_fusion.running, bf16[256,640]{1,0:T(8,128)(2,1)S(1)} %get-tuple-element.43.g0, bf16[256,640]{1,0:T(8,128)(2,1)S(1)} %collective-permute-done.7.g1, bf16[256,640]{1,0:T(8,128)(2,1)S(1)} %copy-done.4, ...), custom_call_target="tpu_custom_call" | custom-call | flops 2500000000 | bytes 2000000 | tf_op jit(solution)/shard_map/pallas_call | solution.py:194
  235.2 0.8 copy-done.7
  236.0 3.4 %all-to-all-done.3 = f32[16,56,128]{2,1,0:T(8,128)S(1)} async-done(((f32[16,56,128]{2,1,0:T(8,128)}), f32[16,56,128]{2,1,0:T(8,128)S(1)}, u32[]{:S(2)}, u32[]{:S(2)}) %all-to-all-start.3) | async-done | bytes 458784 | tf_op jit(solution)/shard_map/all_to_all | solution.py:142
  239.5 1.1 copy-done.8
  240.5 16.9 %shard_map.60 = bf16[256,640]{1,0:T(8,128)(2,1)S(1)} custom-call(f32[112,8,128]{2,1,0:T(8,128)S(1)} %bitcast.21, f32[2,320,320]{2,1,0:T(8,128)S(1)} %copy-done.2, f32[256,640]{1,0:T(8,128)S(1)} %copy-done.8), custom_call_target="tpu_custom_call" | custom-call | flops 10000000000 | bytes 3000000 | tf_op jit(solution)/shard_map/pallas_call | solution.py:231
  257.5 0.4 collective-permute-start.11
  257.9 0.7 collective-permute-start.12
  258.5 1.8 collective-permute-start.13
  260.5 14.4 %collective-permute-done.11 = bf16[256,640]{1,0:T(8,128)(2,1)S(1)} collective-permute-done((bf16[256,640]{1,0:T(8,128)(2,1)S(1)}, bf16[256,640]{1,0:T(8,128)(2,1)S(1)}, u32[]{:S(2)}, u32[]{:S(2)}) %collective-permute-start.11) | collective-permute-done | bytes 327712 | tf_op jit(solution)/shard_map/ppermute | solution.py:31
  275.0 0.2 collective-permute-done.13
  275.3 1.0 copy-done.9
  (28 shorter events, 0.5 us)
Async XLA Ops:
  33.0 7.6 %collective-permute-start.3 = (bf16[4,128,256]{2,1,0:T(8,128)(2,1)}, bf16[4,128,256]{2,1,0:T(8,128)(2,1)S(1)}, u32[]{:S(2)}, u32[]{:S(2)}) collective-permute-start(bf16[4,128,256]{2,1,0:T(8,128)(2,1)} %get-tuple-element.31), channel_id=1, source_target_pairs={{0,1},{1,2},{2,3},{3,0},{4,5},{5,6},{6,7},{7,4},{8,9},{9,10},{10,1... | collective-permute-start | bytes 786440 | tf_op jit(solution)/shard_map/ppermute | solution.py:31
  35.2 14.2 %collective-permute-start.4 = (bf16[4,128,256]{2,1,0:T(8,128)(2,1)}, bf16[4,128,256]{2,1,0:T(8,128)(2,1)S(1)}, u32[]{:S(2)}, u32[]{:S(2)}) collective-permute-start(bf16[4,128,256]{2,1,0:T(8,128)(2,1)} %get-tuple-element.32), channel_id=1, source_target_pairs={{0,2},{1,3},{2,0},{3,1},{4,6},{5,7},{6,4},{7,5},{8,10},{9,11},{10,... | collective-permute-start | bytes 786440 | tf_op jit(solution)/shard_map/ppermute | solution.py:31
  37.8 11.5 %collective-permute-start.5 = (bf16[4,128,256]{2,1,0:T(8,128)(2,1)}, bf16[4,128,256]{2,1,0:T(8,128)(2,1)S(1)}, u32[]{:S(2)}, u32[]{:S(2)}) collective-permute-start(bf16[4,128,256]{2,1,0:T(8,128)(2,1)} %get-tuple-element.33), channel_id=1, source_target_pairs={{0,3},{1,0},{2,1},{3,2},{4,7},{5,4},{6,5},{7,6},{8,11},{9,8},{10,9... | collective-permute-start | bytes 786440 | tf_op jit(solution)/shard_map/ppermute | solution.py:31
  49.4 1.0 copy-start.1
  50.3 15.5 %copy-start.10 = (bf16[1,1024,640]{2,1,0:T(8,128)(2,1)S(1)}, bf16[1,1024,640]{2,1,0:T(8,128)(2,1)}, u32[]{:S(2)}) copy-start(bf16[1,1024,640]{2,1,0:T(8,128)(2,1)} %param.9) | copy-start | bytes 3932164
  50.8 3.0 %collective-permute-start.6 = (f32[2,48,8,128]{3,2,1,0:T(8,128)S(1)}, f32[2,48,8,128]{3,2,1,0:T(8,128)S(1)}, u32[]{:S(2)}, u32[]{:S(2)}) collective-permute-start(f32[2,48,8,128]{3,2,1,0:T(8,128)S(1)} %get-tuple-element.35), channel_id=1, source_target_pairs={{0,4},{4,0},{1,5},{5,1},{2,6},{6,2},{3,7},{7,3},{8,12},{12,8},{9,1... | collective-permute-start | bytes 1179656 | tf_op jit(solution)/shard_map/ppermute | solution.py:25
  54.6 98.6 %all-to-all-start = ((f32[32,24,128]{2,1,0:T(8,128)}), f32[32,24,128]{2,1,0:T(8,128)}, u32[]{:S(2)}, u32[]{:S(2)}) async-start(f32[32,24,128]{2,1,0:T(8,128)} %bitcast), calls=%async_computation | async-start | bytes 786432 | tf_op jit(solution)/shard_map/all_to_all | solution.py:136
  66.8 96.9 %collective-permute-start.7 = (bf16[256,640]{1,0:T(8,128)(2,1)}, bf16[256,640]{1,0:T(8,128)(2,1)S(1)}, u32[]{:S(2)}, u32[]{:S(2)}) collective-permute-start(bf16[256,640]{1,0:T(8,128)(2,1)} %get-tuple-element.48), channel_id=1, source_target_pairs={{0,1},{1,2},{2,3},{3,0},{4,5},{5,6},{6,7},{7,4},{8,9},{9,10},{10,1... | collective-permute-start | bytes 983048 | tf_op jit(solution)/shard_map/ppermute | solution.py:31
  148.4 33.7 %copy-start = (bf16[4,128,640]{2,1,0:T(8,128)(2,1)S(1)}, bf16[4,128,640]{2,1,0:T(8,128)(2,1)}, u32[]{:S(2)}) copy-start(bf16[4,128,640]{2,1,0:T(8,128)(2,1)} %get-tuple-element.36.i0) | copy-start | bytes 1966084
  148.4 30.6 %collective-permute-start = (bf16[4,128,640]{2,1,0:T(8,128)(2,1)}, bf16[4,128,640]{2,1,0:T(8,128)(2,1)S(1)}, u32[]{:S(2)}, u32[]{:S(2)}) collective-permute-start(bf16[4,128,640]{2,1,0:T(8,128)(2,1)} %get-tuple-element.27), channel_id=1, source_target_pairs={{0,16},{16,32},{32,48},{48,0},{1,17},{17,33},{33,49},{49,1},{2,18}... | collective-permute-start | bytes 1966088 | tf_op jit(solution)/shard_map/ppermute | solution.py:31
  149.7 31.8 %collective-permute-start.1 = (bf16[4,128,640]{2,1,0:T(8,128)(2,1)}, bf16[4,128,640]{2,1,0:T(8,128)(2,1)S(1)}, u32[]{:S(2)}, u32[]{:S(2)}) collective-permute-start(bf16[4,128,640]{2,1,0:T(8,128)(2,1)} %get-tuple-element.28), channel_id=1, source_target_pairs={{0,32},{16,48},{32,0},{48,16},{1,33},{17,49},{33,1},{49,17},{2,34}... | collective-permute-start | bytes 1966088 | tf_op jit(solution)/shard_map/ppermute | solution.py:31
  152.1 29.8 %collective-permute-start.2 = (bf16[4,128,640]{2,1,0:T(8,128)(2,1)}, bf16[4,128,640]{2,1,0:T(8,128)(2,1)S(1)}, u32[]{:S(2)}, u32[]{:S(2)}) collective-permute-start(bf16[4,128,640]{2,1,0:T(8,128)(2,1)} %get-tuple-element.29), channel_id=1, source_target_pairs={{0,48},{16,0},{32,16},{48,32},{1,49},{17,1},{33,17},{49,33},{2,50}... | collective-permute-start | bytes 1966088 | tf_op jit(solution)/shard_map/ppermute | solution.py:31
  155.0 27.2 %all-to-all-start.1 = ((f32[16,24,128]{2,1,0:T(8,128)}), f32[16,24,128]{2,1,0:T(8,128)S(1)}, u32[]{:S(2)}, u32[]{:S(2)}) async-start(f32[16,24,128]{2,1,0:T(8,128)} %broadcast_in_dim.28), calls=%async_computation.1 | async-start | bytes 393216 | tf_op jit(solution)/shard_map/all_to_all | solution.py:142
  161.5 8.7 %collective-permute-start.8 = (bf16[256,640]{1,0:T(8,128)(2,1)}, bf16[256,640]{1,0:T(8,128)(2,1)S(1)}, u32[]{:S(2)}, u32[]{:S(2)}) collective-permute-start(bf16[256,640]{1,0:T(8,128)(2,1)} %get-tuple-element.50), channel_id=1, source_target_pairs={{0,2},{1,3},{2,0},{3,1},{4,6},{5,7},{6,4},{7,5},{8,10},{9,11},{10,... | collective-permute-start | bytes 983048 | tf_op jit(solution)/shard_map/ppermute | solution.py:31
  163.7 14.6 %collective-permute-start.9 = (bf16[256,640]{1,0:T(8,128)(2,1)}, bf16[256,640]{1,0:T(8,128)(2,1)S(1)}, u32[]{:S(2)}, u32[]{:S(2)}) collective-permute-start(bf16[256,640]{1,0:T(8,128)(2,1)} %get-tuple-element.47), channel_id=1, source_target_pairs={{0,3},{1,0},{2,1},{3,2},{4,7},{5,4},{6,5},{7,6},{8,11},{9,8},{10,9... | collective-permute-start | bytes 983048 | tf_op jit(solution)/shard_map/ppermute | solution.py:31
  170.1 0.7 copy-start.3
  178.3 0.7 copy-start.5
  185.4 4.0 %collective-permute-start.10 = (f32[4,56,8,128]{3,2,1,0:T(8,128)S(1)}, f32[4,56,8,128]{3,2,1,0:T(8,128)S(1)}, u32[]{:S(2)}, u32[]{:S(2)}) collective-permute-start(f32[4,56,8,128]{3,2,1,0:T(8,128)S(1)} %get-tuple-element.41), channel_id=1, source_target_pairs={{0,4},{4,0},{1,5},{5,1},{2,6},{6,2},{3,7},{7,3},{8,12},{12,8},{9,1... | collective-permute-start | bytes 2752520 | tf_op jit(solution)/shard_map/ppermute | solution.py:25
  221.8 8.7 %copy-start.4 = (bf16[256,640]{1,0:T(8,128)(2,1)S(1)}, bf16[256,640]{1,0:T(8,128)(2,1)}, u32[]{:S(2)}) copy-start(bf16[256,640]{1,0:T(8,128)(2,1)} %copy-done.3) | copy-start | bytes 983044
  221.8 8.7 %copy-start.6 = (bf16[256,640]{1,0:T(8,128)(2,1)S(1)}, bf16[256,640]{1,0:T(8,128)(2,1)}, u32[]{:S(2)}) copy-start(bf16[256,640]{1,0:T(8,128)(2,1)} %copy-done.5) | copy-start | bytes 983044
  222.7 16.7 %all-to-all-start.3 = ((f32[16,56,128]{2,1,0:T(8,128)}), f32[16,56,128]{2,1,0:T(8,128)S(1)}, u32[]{:S(2)}, u32[]{:S(2)}) async-start(f32[16,56,128]{2,1,0:T(8,128)} %broadcast_in_dim.29), calls=%async_computation.3 | async-start | bytes 917504 | tf_op jit(solution)/shard_map/all_to_all | solution.py:142
  230.6 8.9 %copy-start.2 = (f32[2,320,320]{2,1,0:T(8,128)S(1)}, f32[2,320,320]{2,1,0:T(8,128)}, u32[]{:S(2)}) copy-start(f32[2,320,320]{2,1,0:T(8,128)} %running.1) | copy-start | bytes 2457604
  235.2 0.8 copy-start.7
  239.4 1.1 copy-start.8
  257.5 17.4 %collective-permute-start.11 = (bf16[256,640]{1,0:T(8,128)(2,1)S(1)}, bf16[256,640]{1,0:T(8,128)(2,1)S(1)}, u32[]{:S(2)}, u32[]{:S(2)}) collective-permute-start(bf16[256,640]{1,0:T(8,128)(2,1)S(1)} %shard_map.60), channel_id=1, source_target_pairs={{0,1},{1,2},{2,3},{3,0},{4,5},{5,6},{6,7},{7,4},{8,9},{9,10},{10,1... | collective-permute-start | bytes 983048 | tf_op jit(solution)/shard_map/ppermute | solution.py:31
  257.9 17.1 %collective-permute-start.12 = (bf16[256,640]{1,0:T(8,128)(2,1)S(1)}, bf16[256,640]{1,0:T(8,128)(2,1)S(1)}, u32[]{:S(2)}, u32[]{:S(2)}) collective-permute-start(bf16[256,640]{1,0:T(8,128)(2,1)S(1)} %shard_map.60), channel_id=1, source_target_pairs={{0,2},{1,3},{2,0},{3,1},{4,6},{5,7},{6,4},{7,5},{8,10},{9,11},{10,... | collective-permute-start | bytes 983048 | tf_op jit(solution)/shard_map/ppermute | solution.py:31
  258.5 16.7 %collective-permute-start.13 = (bf16[256,640]{1,0:T(8,128)(2,1)S(1)}, bf16[256,640]{1,0:T(8,128)(2,1)S(1)}, u32[]{:S(2)}, u32[]{:S(2)}) collective-permute-start(bf16[256,640]{1,0:T(8,128)(2,1)S(1)} %shard_map.60), channel_id=1, source_target_pairs={{0,3},{1,0},{2,1},{3,2},{4,7},{5,4},{6,5},{7,6},{8,11},{9,8},{10,9... | collective-permute-start | bytes 983048 | tf_op jit(solution)/shard_map/ppermute | solution.py:31
  275.3 1.1 copy-start.9
where the time goes:
time: 277 us; the launch traced here: 276 us
  Pallas kernels  139 us (50%)
  waiting for transfers between devices  47.7 us (17%)
  starting transfers between devices  46.1 us (17%)
  blocking collectives  32.3 us (12%)
  local copies, waits for them, and re-layouts  9.13 us (3%)
    pallas_call x2, Pallas kernels, pack(): pl.pallas_call(functools.partial(pack_kernel, axis, width), out_shape=[pi...  114 us
    ppermute x12, waiting for transfers between devices, send_round(): lax.ppermute(chunks[s], axis, [(i, (i + s) % size) for i in range(size)])  40.5 us
    all_to_all x1, blocking collectives, reduce_pieces(): return jnp.sum(lax.all_to_all(value, axes, 0, 0, tiled=True), axis=0)  32.3 us
    ppermute x12, starting transfers between devices, send_round(): lax.ppermute(chunks[s], axis, [(i, (i + s) % size) for i in range(size)])  18 us
    pallas_call x1, Pallas kernels, g_side(): pl.pallas_call(functools.partial(g_side_kernel, token_total=token_total),...  16.9 us
    all_to_all x2, starting transfers between devices, gather_pieces(): return lax.all_to_all(every, axes, 0, 0, tiled=True)  13.4 us
    all_to_all x1, starting transfers between devices, reduce_pieces(): return jnp.sum(lax.all_to_all(value, axes, 0, 0, tiled=True), axis=0)  11.1 us
  transfers between devices with their start and end apart: 17, of which 12 were waited for; matrix products, arithmetic and copies ran while one was open for 1% of the time, Pallas kernels for 31%

commit v1 on v0

--- a/solution.py
+++ b/solution.py
@@ -17,7 +17,6 @@
 factor_decay = 0.9
 damping = 0.1
 
-ANY = pl.BlockSpec(memory_space=pl.ANY)
 VMEM = pl.BlockSpec(memory_space=pltpu.VMEM)
 
 
@@ -37,7 +36,7 @@
     outs, sem = rest[:4], rest[4]
     here = lax.axis_index(axis)
     copies = []
-    for s in (1, 2, 3, 0):
+    for s in (1, 3, 2, 0):
         peer = lax.rem(here + s, 4)
         for q in range(4):
             start = pl.multiple_of((q * 4 + peer) * width, 128)
@@ -55,8 +54,8 @@
     return pl.pallas_call(
         functools.partial(pack_kernel, axis, width),
         out_shape=[piece] * 4,
-        in_specs=[ANY],
-        out_specs=[ANY] * 4,
+        in_specs=[pl.BlockSpec(memory_space=pl.ANY)],
+        out_specs=[VMEM] * 4,
         scratch_shapes=[pltpu.SemaphoreType.DMA((16,))],
     )(samples)
 
@@ -241,24 +240,40 @@
 
 def per_device(activations, out_grads, a_running, g_running, grad_partial):
     token_total = float(activations.shape[0] * 256)
-    zl, c, y = lax.axis_index("zl"), lax.axis_index("c"), lax.axis_index("y")
-
-    g_in = send_round("x", pack(out_grads, "x", 2 * BG))
+    x, zl, c, y = (lax.axis_index(name) for name in ("x", "zl", "c", "y"))
+
+    g_chunks = pack(out_grads, "x", 2 * BG)
+    g_chunks, activations = lax.optimization_barrier((g_chunks, activations))
+    g_in = send_round("x", g_chunks)
     a_in = send_round("y", pack(activations, "y", BA))
     grads = send_round("y", [
         lax.dynamic_slice_in_dim(grad_partial[0], lax.rem(y + s, 4) * BA, BA, 0) for s in range(4)
     ])
-
+    g_in, a_in, grads = lax.optimization_barrier((g_in, a_in, grads))
+
+    g_own, g_other = g_cov(g_in)
     a_own, a_other = a_cov(a_in)
-    a_part = a_own + swap_cores(a_other)
-    a_piece = reduce_pieces(a_part.reshape(32, A_TILES // 2, 128), ("zl", "zh", "x"))
-    a_tiles = gather_pieces(a_piece, ("zh", "x")).reshape(A_TILES, 8, 128)
-
-    g_in, a_tiles, grads = lax.optimization_barrier((g_in, a_tiles, grads))
-    g_own, g_other = g_cov(g_in)
-    g_part = g_own + swap_cores(g_other)
-    g_piece = reduce_pieces(g_part.reshape(32, 56, 128), ("zh", "zl", "y"))
-    g_tiles = gather_pieces(g_piece, ("c", "zl", "y")).reshape(G_TILES, 8, 128)
+    g_part = (g_own + swap_cores(g_other)).reshape(4, 4, 14, 8, 128)
+    a_part = (a_own + swap_cores(a_other)).reshape(2, 4, 12, 8, 128)
+
+    g_lines = send_round("y", [
+        lax.dynamic_index_in_dim(g_part, lax.rem(y + s, 4), 1, keepdims=False) for s in range(4)
+    ])
+    a_lines = send_round("x", [
+        lax.dynamic_index_in_dim(a_part, lax.rem(x + s, 4), 1, keepdims=False) for s in range(4)
+    ])
+    g_lines, a_lines = lax.optimization_barrier((g_lines, a_lines))
+    g_line = (g_lines[0] + g_lines[1]) + (g_lines[2] + g_lines[3])
+    a_line = (a_lines[0] + a_lines[1]) + (a_lines[2] + a_lines[3])
+
+    both = jnp.concatenate([
+        g_line.reshape(8, 56, 128),
+        jnp.swapaxes(a_line.reshape(2, 4, 24, 128), 0, 1).reshape(8, 24, 128),
+    ], axis=1)
+    pieces = reduce_pieces(both, ("zh", "zl"))
+    a_tiles = gather_pieces(pieces[56:], ("x", "zh")).reshape(A_TILES, 8, 128)
+    g_piece, a_tiles = lax.optimization_barrier((pieces[:56], a_tiles))
+    g_tiles = gather_pieces(g_piece, ("c", "y", "zl")).reshape(G_TILES, 8, 128)
 
     a_previous = lax.dynamic_slice_in_dim(a_running, (zl * 2 + c) * 4 + y, 1, 0)
     left = a_side(a_tiles, a_previous, grads, token_total)

time: 277 us -> 158 us (0.57)
  Pallas kernels: 139 us -> 31.1 us
  blocking collectives: 32.3 us -> 18.1 us
  waiting for transfers between devices: 47.7 us -> 58.4 us
  starting transfers between devices: 46.1 us -> 40.2 us
    pallas_call x2, Pallas kernels: 114 us -> 5.89 us  [pack(): pl.pallas_call(functools.partial(pack_kernel, axis, width), out_shape=[pi...]
    all_to_all x1, blocking collectives: 32.3 us -> 18.1 us  [reduce_pieces(): return jnp.sum(lax.all_to_all(value, axes, 0, 0, tiled=True), axis=0)]
    all_to_all x1 -> x0, starting transfers between devices: 11.1 us -> none  [reduce_pieces(): return jnp.sum(lax.all_to_all(value, axes, 0, 0, tiled=True), axis=0)]
    all_to_all x2, waiting for transfers between devices: 3.74 us -> 12.3 us  [gather_pieces(): return lax.all_to_all(every, axes, 0, 0, tiled=True)]
    ppermute x12 -> x18, starting transfers between devices: 18 us -> 23.3 us  [send_round(): lax.ppermute(chunks[s], axis, [(i, (i + s) % size) for i in range(size)])]
    ppermute x12 -> x18, waiting for transfers between devices: 40.5 us -> 44.1 us  [send_round(): lax.ppermute(chunks[s], axis, [(i, (i + s) % size) for i in range(size)])]
  transfers between devices with their start and end apart: 17 -> 22, of which waited for: 12 -> 15; matrix products, arithmetic and copies ran while one was open for 1% -> 1% of each run, Pallas kernels for 31% -> 3%
where the time goes in v1:
time: 158 us; the launch traced here: 157 us
  waiting for transfers between devices  58.4 us (37%)
  starting transfers between devices  40.2 us (25%)
  Pallas kernels  31.1 us (20%)
  blocking collectives  18.1 us (11%)
  local copies, waits for them, and re-layouts  7.57 us (5%)
    ppermute x18, waiting for transfers between devices, send_round(): lax.ppermute(chunks[s], axis, [(i, (i + s) % size) for i in range(size)])  44.1 us
    ppermute x18, starting transfers between devices, send_round(): lax.ppermute(chunks[s], axis, [(i, (i + s) % size) for i in range(size)])  23.3 us
    all_to_all x1, blocking collectives, reduce_pieces(): return jnp.sum(lax.all_to_all(value, axes, 0, 0, tiled=True), axis=0)  18.1 us
    pallas_call x1, Pallas kernels, g_side(): pl.pallas_call(functools.partial(g_side_kernel, token_total=token_total),...  16.9 us
    all_to_all x2, starting transfers between devices, gather_pieces(): return lax.all_to_all(every, axes, 0, 0, tiled=True)  14.2 us
    all_to_all x2, waiting for transfers between devices, gather_pieces(): return lax.all_to_all(every, axes, 0, 0, tiled=True)  12.3 us
    pallas_call x2, Pallas kernels, pack(): pl.pallas_call(functools.partial(pack_kernel, axis, width), out_shape=[pi...  5.89 us
    unnamed x32, local copies, waits for them, and re-layouts  4.61 us
  transfers between devices with their start and end apart: 22, of which 15 were waited for; matrix products, arithmetic and copies ran while one was open for 1% of the time, Pallas kernels for 3%

profile of v1, /device:TPU:1, one launch (start us, length us, event | category | flops | bytes accessed | tf_op | source)
XLA Modules:
  0.0 157.2 jit_solution(10515264637206297338)
XLA Ops:
  0.0 3.5 %shard_map.55 = (bf16[4,128,640]{2,1,0:T(8,128)(2,1)}, bf16[4,128,640]{2,1,0:T(8,128)(2,1)}, bf16[4,128,640]{2,1,0:T(8,128)(2,1)}, bf16[4,128,640]{2,1,0:T(8,128)(2,1)}) custom-call(bf16[128,10240]{1,0:T(8,128)(2,1)} %src.1), custom_call_target="tpu_custom_call" | custom-call | tf_op jit(solution)/shard_map/pallas_call | solution.py:54
  3.5 2.4 %shard_map.56 = (bf16[4,128,256]{2,1,0:T(8,128)(2,1)}, bf16[4,128,256]{2,1,0:T(8,128)(2,1)}, bf16[4,128,256]{2,1,0:T(8,128)(2,1)}, bf16[4,128,256]{2,1,0:T(8,128)(2,1)}) custom-call(bf16[128,4096]{1,0:T(8,128)(2,1)} %src.2), custom_call_target="tpu_custom_call" | custom-call | tf_op jit(solution)/shard_map/pallas_call | solution.py:54
  5.9 2.2 %collective-permute-start.3 = (bf16[4,128,256]{2,1,0:T(8,128)(2,1)}, bf16[4,128,256]{2,1,0:T(8,128)(2,1)S(1)}, u32[]{:S(2)}, u32[]{:S(2)}) collective-permute-start(bf16[4,128,256]{2,1,0:T(8,128)(2,1)} %get-tuple-element.54), channel_id=1, source_target_pairs={{0,1},{1,2},{2,3},{3,0},{4,5},{5,6},{6,7},{7,4},{8,9},{9,10},{10,1... | collective-permute-start | bytes 786440 | tf_op jit(solution)/shard_map/ppermute | solution.py:30
  8.1 2.6 %collective-permute-start.4 = (bf16[4,128,256]{2,1,0:T(8,128)(2,1)}, bf16[4,128,256]{2,1,0:T(8,128)(2,1)S(1)}, u32[]{:S(2)}, u32[]{:S(2)}) collective-permute-start(bf16[4,128,256]{2,1,0:T(8,128)(2,1)} %get-tuple-element.55), channel_id=1, source_target_pairs={{0,2},{1,3},{2,0},{3,1},{4,6},{5,7},{6,4},{7,5},{8,10},{9,11},{10,... | collective-permute-start | bytes 786440 | tf_op jit(solution)/shard_map/ppermute | solution.py:30
  10.8 0.1 dynamic-slice_bitcast_fusion
  11.0 0.8 copy-done.15
  11.8 1.2 collective-permute-start
  13.0 2.5 %collective-permute-start.1 = (bf16[4,128,640]{2,1,0:T(8,128)(2,1)S(1)}, bf16[4,128,640]{2,1,0:T(8,128)(2,1)S(1)}, u32[]{:S(2)}, u32[]{:S(2)}) collective-permute-start(bf16[4,128,640]{2,1,0:T(8,128)(2,1)S(1)} %copy-done.14), channel_id=1, source_target_pairs={{0,32},{16,48},{32,0},{48,16},{1,33},{17,49},{33,1},{49,17},{2,34}... | collective-permute-start | bytes 1966088 | tf_op jit(solution)/shard_map/ppermute | solution.py:30
  15.5 2.5 %collective-permute-start.2 = (bf16[4,128,640]{2,1,0:T(8,128)(2,1)S(1)}, bf16[4,128,640]{2,1,0:T(8,128)(2,1)S(1)}, u32[]{:S(2)}, u32[]{:S(2)}) collective-permute-start(bf16[4,128,640]{2,1,0:T(8,128)(2,1)S(1)} %copy-done.13), channel_id=1, source_target_pairs={{0,48},{16,0},{32,16},{48,32},{1,49},{17,1},{33,17},{49,33},{2,50}... | collective-permute-start | bytes 1966088 | tf_op jit(solution)/shard_map/ppermute | solution.py:30
  18.0 4.3 %collective-permute-done.4.i2 = bf16[4,128,256]{2,1,0:T(8,128)(2,1)S(1)} collective-permute-done((bf16[4,128,256]{2,1,0:T(8,128)(2,1)}, bf16[4,128,256]{2,1,0:T(8,128)(2,1)S(1)}, u32[]{:S(2)}, u32[]{:S(2)}) %collective-permute-start.4) | collective-permute-done | bytes 262176 | tf_op jit(solution)/shard_map/ppermute | solution.py:30
  22.3 5.7 %collective-permute-done.5.i3 = bf16[4,128,256]{2,1,0:T(8,128)(2,1)S(1)} collective-permute-done((bf16[4,128,256]{2,1,0:T(8,128)(2,1)}, bf16[4,128,256]{2,1,0:T(8,128)(2,1)S(1)}, u32[]{:S(2)}, u32[]{:S(2)}) %collective-permute-start.5) | collective-permute-done | bytes 262176 | tf_op jit(solution)/shard_map/ppermute | solution.py:30
  28.0 0.2 collective-permute-start.7
  28.2 1.6 %collective-permute-start.8 = (bf16[256,640]{1,0:T(8,128)(2,1)S(1)}, bf16[256,640]{1,0:T(8,128)(2,1)S(1)}, u32[]{:S(2)}, u32[]{:S(2)}) collective-permute-start(bf16[256,640]{1,0:T(8,128)(2,1)S(1)} %get-tuple-element.83), channel_id=1, source_target_pairs={{0,3},{1,0},{2,1},{3,2},{4,7},{5,4},{6,5},{7,6},{8,11},{9,8},{10,9... | collective-permute-start | bytes 983048 | tf_op jit(solution)/shard_map/ppermute | solution.py:30
  29.8 6.0 %collective-permute-done.7.g2 = bf16[256,640]{1,0:T(8,128)(2,1)S(1)} collective-permute-done((bf16[256,640]{1,0:T(8,128)(2,1)S(1)}, bf16[256,640]{1,0:T(8,128)(2,1)S(1)}, u32[]{:S(2)}, u32[]{:S(2)}) %collective-permute-start.7) | collective-permute-done | bytes 327712 | tf_op jit(solution)/shard_map/ppermute | solution.py:30
  35.8 0.7 copy-done.5
  36.5 2.5 %collective-permute-done.8.g3 = bf16[256,640]{1,0:T(8,128)(2,1)S(1)} collective-permute-done((bf16[256,640]{1,0:T(8,128)(2,1)S(1)}, bf16[256,640]{1,0:T(8,128)(2,1)S(1)}, u32[]{:S(2)}, u32[]{:S(2)}) %collective-permute-start.8) | collective-permute-done | bytes 327712 | tf_op jit(solution)/shard_map/ppermute | solution.py:30
  39.0 4.0 %collective-permute-done.1.i2 = bf16[4,128,640]{2,1,0:T(8,128)(2,1)S(1)} collective-permute-done((bf16[4,128,640]{2,1,0:T(8,128)(2,1)S(1)}, bf16[4,128,640]{2,1,0:T(8,128)(2,1)S(1)}, u32[]{:S(2)}, u32[]{:S(2)}) %collective-permute-start.1) | collective-permute-done | bytes 655392 | tf_op jit(solution)/shard_map/ppermute | solution.py:30
  43.1 0.2 collective-permute-done.2.i3
  43.3 3.2 %shard_map.57 = (f32[4,56,8,128]{3,2,1,0:T(8,128)S(1)}, f32[4,56,8,128]{3,2,1,0:T(8,128)S(1)}) custom-call(bf16[4,128,640]{2,1,0:T(8,128)(2,1)S(1)} %copy-done, bf16[4,128,640]{2,1,0:T(8,128)(2,1)S(1)} %collective-permute-done.i1, bf16[4,128,640]{2,1,0:T(8,128)(2,1)S(1)} %collective-permute-done.1.i2, bf16[4,128,640]{2,1,0:T(8,128)(2,1)S(1)} %collective-permute-done.2.i3), custom_call_target="tpu_custom_call" | custom-call | tf_op jit(solution)/shard_map/pallas_call | solution.py:94
  46.6 2.6 %collective-permute-start.9 = (f32[4,56,8,128]{3,2,1,0:T(8,128)S(1)}, f32[4,56,8,128]{3,2,1,0:T(8,128)}, u32[]{:S(2)}, u32[]{:S(2)}) collective-permute-start(f32[4,56,8,128]{3,2,1,0:T(8,128)S(1)} %get-tuple-element.62), channel_id=1, source_target_pairs={{0,4},{4,0},{1,5},{5,1},{2,6},{6,2},{3,7},{7,3},{8,12},{12,8},{9,1... | collective-permute-start | bytes 2752520 | tf_op jit(solution)/shard_map/ppermute | solution.py:24
  49.1 0.5 shard_map.58
  49.8 2.0 %collective-permute-done.13 = f32[2,48,8,128]{3,2,1,0:T(8,128)S(1)} collective-permute-done((f32[2,48,8,128]{3,2,1,0:T(8,128)S(1)}, f32[2,48,8,128]{3,2,1,0:T(8,128)S(1)}, u32[]{:S(2)}, u32[]{:S(2)}) %collective-permute-start.13) | collective-permute-done | bytes 393248 | tf_op jit(solution)/shard_map/ppermute | solution.py:24
  51.9 1.3 add.120
  53.2 1.1 collective-permute-start.10
  54.3 2.5 %collective-permute-start.11 = (f32[4,14,8,128]{3,2,1,0:T(8,128)S(1)}, f32[4,14,8,128]{3,2,1,0:T(8,128)S(1)}, u32[]{:S(2)}, u32[]{:S(2)}) collective-permute-start(f32[4,14,8,128]{3,2,1,0:T(8,128)S(1)} %get-tuple-element.88), channel_id=1, source_target_pairs={{0,2},{1,3},{2,0},{3,1},{4,6},{5,7},{6,4},{7,5},{8,10},{9,11},{10,... | collective-permute-start | bytes 688136 | tf_op jit(solution)/shard_map/ppermute | solution.py:30
  56.8 1.7 %collective-permute-start.12 = (f32[4,14,8,128]{3,2,1,0:T(8,128)S(1)}, f32[4,14,8,128]{3,2,1,0:T(8,128)S(1)}, u32[]{:S(2)}, u32[]{:S(2)}) collective-permute-start(f32[4,14,8,128]{3,2,1,0:T(8,128)S(1)} %get-tuple-element.87), channel_id=1, source_target_pairs={{0,3},{1,0},{2,1},{3,2},{4,7},{5,4},{6,5},{7,6},{8,11},{9,8},{10,9... | collective-permute-start | bytes 688136 | tf_op jit(solution)/shard_map/ppermute | solution.py:30
  58.6 1.9 %collective-permute-start.15 = (f32[2,12,8,128]{3,2,1,0:T(8,128)S(1)}, f32[2,12,8,128]{3,2,1,0:T(8,128)S(1)}, u32[]{:S(2)}, u32[]{:S(2)}) collective-permute-start(f32[2,12,8,128]{3,2,1,0:T(8,128)S(1)} %get-tuple-element.92), channel_id=1, source_target_pairs={{0,32},{16,48},{32,0},{48,16},{1,33},{17,49},{33,1},{49,17},{2,34}... | collective-permute-start | bytes 294920 | tf_op jit(solution)/shard_map/ppermute | solution.py:30
  60.5 3.7 %collective-permute-done.14 = f32[2,12,8,128]{3,2,1,0:T(8,128)S(1)} collective-permute-done((f32[2,12,8,128]{3,2,1,0:T(8,128)S(1)}, f32[2,12,8,128]{3,2,1,0:T(8,128)S(1)}, u32[]{:S(2)}, u32[]{:S(2)}) %collective-permute-start.14) | collective-permute-done | bytes 98336 | tf_op jit(solution)/shard_map/ppermute | solution.py:30
  64.2 0.8 collective-permute-done.15
  65.1 2.8 %collective-permute-done.16 = f32[2,12,8,128]{3,2,1,0:T(8,128)S(1)} collective-permute-done((f32[2,12,8,128]{3,2,1,0:T(8,128)S(1)}, f32[2,12,8,128]{3,2,1,0:T(8,128)S(1)}, u32[]{:S(2)}, u32[]{:S(2)}) %collective-permute-start.16) | collective-permute-done | bytes 98336 | tf_op jit(solution)/shard_map/ppermute | solution.py:30
  68.0 18.1 %all_to_all.15 = f32[8,80,128]{2,1,0:T(8,128)S(1)} all-to-all(f32[8,80,128]{2,1,0:T(8,128)S(1)} %pad_maximum_fusion), channel_id=1, replica_groups=mesh['zh'=4,'x'=4,'zl'=2,'c'=2,'y'=4] {'zh','zl'}, dimensions={0} | all-to-all | bytes 655360 | tf_op jit(solution)/shard_map/all_to_all | solution.py:135
  86.2 0.7 broadcast_in_dim.28
  86.9 6.0 %all-to-all-start.1 = ((f32[16,24,128]{2,1,0:T(8,128)}), f32[16,24,128]{2,1,0:T(8,128)S(1)}, u32[]{:S(2)}, u32[]{:S(2)}) async-start(f32[16,24,128]{2,1,0:T(8,128)} %broadcast_in_dim.28), calls=%async_computation.1 | async-start | bytes 393216 | tf_op jit(solution)/shard_map/all_to_all | solution.py:141
  93.0 10.0 %all-to-all-done.1 = f32[16,24,128]{2,1,0:T(8,128)S(1)} async-done(((f32[16,24,128]{2,1,0:T(8,128)}), f32[16,24,128]{2,1,0:T(8,128)S(1)}, u32[]{:S(2)}, u32[]{:S(2)}) %all-to-all-start.1) | async-done | bytes 196640 | tf_op jit(solution)/shard_map/all_to_all | solution.py:141
  103.0 0.8 broadcast_in_dim.29
  103.8 8.1 %all-to-all-start.2 = ((f32[16,56,128]{2,1,0:T(8,128)}), f32[16,56,128]{2,1,0:T(8,128)S(1)}, u32[]{:S(2)}, u32[]{:S(2)}) async-start(f32[16,56,128]{2,1,0:T(8,128)} %broadcast_in_dim.29), calls=%async_computation.2 | async-start | bytes 917504 | tf_op jit(solution)/shard_map/all_to_all | solution.py:141
  111.9 1.0 constant_dynamic-slice_fusion.running
  112.9 4.6 %shard_map.59.left = f32[256,640]{1,0:T(8,128)S(1)} custom-call(f32[48,8,128]{2,1,0:T(8,128)S(1)} %bitcast.43, f32[1,256,256]{2,1,0:T(8,128)S(1)} %constant_dynamic-slice_fusion.running, bf16[256,640]{1,0:T(8,128)(2,1)S(1)} %get-tuple-element.79.g0, bf16[256,640]{1,0:T(8,128)(2,1)S(1)} %copy-done.4, bf16[256,640]{1,0:T(8,128)(2,1)S(1)} %copy-done.6, ...), custom_call_target="tpu_custom_call" | custom-call | flops 2500000000 | bytes 2000000 | tf_op jit(solution)/shard_map/pallas_call | solution.py:193
  117.5 0.8 copy-done.9
  118.3 2.2 %all-to-all-done.2 = f32[16,56,128]{2,1,0:T(8,128)S(1)} async-done(((f32[16,56,128]{2,1,0:T(8,128)}), f32[16,56,128]{2,1,0:T(8,128)S(1)}, u32[]{:S(2)}, u32[]{:S(2)}) %all-to-all-start.2) | async-done | bytes 458784 | tf_op jit(solution)/shard_map/all_to_all | solution.py:141
  120.6 1.1 copy-done.10
  121.7 16.9 %shard_map.60 = bf16[256,640]{1,0:T(8,128)(2,1)S(1)} custom-call(f32[112,8,128]{2,1,0:T(8,128)S(1)} %bitcast.42, f32[2,320,320]{2,1,0:T(8,128)S(1)} %copy-done.2, f32[256,640]{1,0:T(8,128)S(1)} %copy-done.10), custom_call_target="tpu_custom_call" | custom-call | flops 10000000000 | bytes 3000000 | tf_op jit(solution)/shard_map/pallas_call | solution.py:230
  138.7 2.5 %collective-permute-start.18 = (bf16[256,640]{1,0:T(8,128)(2,1)S(1)}, bf16[256,640]{1,0:T(8,128)(2,1)S(1)}, u32[]{:S(2)}, u32[]{:S(2)}) collective-permute-start(bf16[256,640]{1,0:T(8,128)(2,1)S(1)} %shard_map.60), channel_id=1, source_target_pairs={{0,2},{1,3},{2,0},{3,1},{4,6},{5,7},{6,4},{7,5},{8,10},{9,11},{10,... | collective-permute-start | bytes 983048 | tf_op jit(solution)/shard_map/ppermute | solution.py:30
  141.2 0.6 collective-permute-start.19
  141.9 6.0 %collective-permute-done.17 = bf16[256,640]{1,0:T(8,128)(2,1)S(1)} collective-permute-done((bf16[256,640]{1,0:T(8,128)(2,1)S(1)}, bf16[256,640]{1,0:T(8,128)(2,1)S(1)}, u32[]{:S(2)}, u32[]{:S(2)}) %collective-permute-start.17) | collective-permute-done | bytes 327712 | tf_op jit(solution)/shard_map/ppermute | solution.py:30
  148.0 7.6 %collective-permute-done.18 = bf16[256,640]{1,0:T(8,128)(2,1)S(1)} collective-permute-done((bf16[256,640]{1,0:T(8,128)(2,1)S(1)}, bf16[256,640]{1,0:T(8,128)(2,1)S(1)}, u32[]{:S(2)}, u32[]{:S(2)}) %collective-permute-start.18) | collective-permute-done | bytes 327712 | tf_op jit(solution)/shard_map/ppermute | solution.py:30
  155.6 0.5 collective-permute-done.19
  156.2 1.0 copy-done.11
  (55 shorter events, 1.0 us)
Async XLA Ops:
  0.0 10.7 %copy-start.12 = (bf16[1,1024,640]{2,1,0:T(8,128)(2,1)S(1)}, bf16[1,1024,640]{2,1,0:T(8,128)(2,1)}, u32[]{:S(2)}) copy-start(bf16[1,1024,640]{2,1,0:T(8,128)(2,1)} %param.9) | copy-start | bytes 3932164
  5.9 9.6 %collective-permute-start.3 = (bf16[4,128,256]{2,1,0:T(8,128)(2,1)}, bf16[4,128,256]{2,1,0:T(8,128)(2,1)S(1)}, u32[]{:S(2)}, u32[]{:S(2)}) collective-permute-start(bf16[4,128,256]{2,1,0:T(8,128)(2,1)} %get-tuple-element.54), channel_id=1, source_target_pairs={{0,1},{1,2},{2,3},{3,0},{4,5},{5,6},{6,7},{7,4},{8,9},{9,10},{10,1... | collective-permute-start | bytes 786440 | tf_op jit(solution)/shard_map/ppermute | solution.py:30
  8.1 14.2 %collective-permute-start.4 = (bf16[4,128,256]{2,1,0:T(8,128)(2,1)}, bf16[4,128,256]{2,1,0:T(8,128)(2,1)S(1)}, u32[]{:S(2)}, u32[]{:S(2)}) collective-permute-start(bf16[4,128,256]{2,1,0:T(8,128)(2,1)} %get-tuple-element.55), channel_id=1, source_target_pairs={{0,2},{1,3},{2,0},{3,1},{4,6},{5,7},{6,4},{7,5},{8,10},{9,11},{10,... | collective-permute-start | bytes 786440 | tf_op jit(solution)/shard_map/ppermute | solution.py:30
  10.7 1.1 copy-start.15
  10.7 2.3 %copy-start.14 = (bf16[4,128,640]{2,1,0:T(8,128)(2,1)S(1)}, bf16[4,128,640]{2,1,0:T(8,128)(2,1)}, u32[]{:S(2)}) copy-start(bf16[4,128,640]{2,1,0:T(8,128)(2,1)} %get-tuple-element.50) | copy-start | bytes 1966084
  10.7 4.8 %copy-start.13 = (bf16[4,128,640]{2,1,0:T(8,128)(2,1)S(1)}, bf16[4,128,640]{2,1,0:T(8,128)(2,1)}, u32[]{:S(2)}) copy-start(bf16[4,128,640]{2,1,0:T(8,128)(2,1)} %get-tuple-element.51) | copy-start | bytes 1966084
  10.7 32.6 %copy-start = (bf16[4,128,640]{2,1,0:T(8,128)(2,1)S(1)}, bf16[4,128,640]{2,1,0:T(8,128)(2,1)}, u32[]{:S(2)}) copy-start(bf16[4,128,640]{2,1,0:T(8,128)(2,1)} %get-tuple-element.57.i0) | copy-start | bytes 1966084
  10.9 17.3 %collective-permute-start.6 = (bf16[256,640]{1,0:T(8,128)(2,1)S(1)}, bf16[256,640]{1,0:T(8,128)(2,1)S(1)}, u32[]{:S(2)}, u32[]{:S(2)}) collective-permute-start(bf16[256,640]{1,0:T(8,128)(2,1)S(1)} %get-tuple-element.84), channel_id=1, source_target_pairs={{0,1},{1,2},{2,3},{3,0},{4,5},{5,6},{6,7},{7,4},{8,9},{9,10},{10,1... | collective-permute-start | bytes 983048 | tf_op jit(solution)/shard_map/ppermute | solution.py:30
  11.8 27.2 %collective-permute-start = (bf16[4,128,640]{2,1,0:T(8,128)(2,1)S(1)}, bf16[4,128,640]{2,1,0:T(8,128)(2,1)S(1)}, u32[]{:S(2)}, u32[]{:S(2)}) collective-permute-start(bf16[4,128,640]{2,1,0:T(8,128)(2,1)S(1)} %copy-done.15), channel_id=1, source_target_pairs={{0,16},{16,32},{32,48},{48,0},{1,17},{17,33},{33,49},{49,1},{2,18}... | collective-permute-start | bytes 1966088 | tf_op jit(solution)/shard_map/ppermute | solution.py:30
  13.0 30.0 %collective-permute-start.1 = (bf16[4,128,640]{2,1,0:T(8,128)(2,1)S(1)}, bf16[4,128,640]{2,1,0:T(8,128)(2,1)S(1)}, u32[]{:S(2)}, u32[]{:S(2)}) collective-permute-start(bf16[4,128,640]{2,1,0:T(8,128)(2,1)S(1)} %copy-done.14), channel_id=1, source_target_pairs={{0,32},{16,48},{32,0},{48,16},{1,33},{17,49},{33,1},{49,17},{2,34}... | collective-permute-start | bytes 1966088 | tf_op jit(solution)/shard_map/ppermute | solution.py:30
  15.5 27.8 %collective-permute-start.2 = (bf16[4,128,640]{2,1,0:T(8,128)(2,1)S(1)}, bf16[4,128,640]{2,1,0:T(8,128)(2,1)S(1)}, u32[]{:S(2)}, u32[]{:S(2)}) collective-permute-start(bf16[4,128,640]{2,1,0:T(8,128)(2,1)S(1)} %copy-done.13), channel_id=1, source_target_pairs={{0,48},{16,0},{32,16},{48,32},{1,49},{17,1},{33,17},{49,33},{2,50}... | collective-permute-start | bytes 1966088 | tf_op jit(solution)/shard_map/ppermute | solution.py:30
  22.3 5.7 %collective-permute-start.5 = (bf16[4,128,256]{2,1,0:T(8,128)(2,1)}, bf16[4,128,256]{2,1,0:T(8,128)(2,1)S(1)}, u32[]{:S(2)}, u32[]{:S(2)}) collective-permute-start(bf16[4,128,256]{2,1,0:T(8,128)(2,1)} %get-tuple-element.56), channel_id=1, source_target_pairs={{0,3},{1,0},{2,1},{3,2},{4,7},{5,4},{6,5},{7,6},{8,11},{9,8},{10,9... | collective-permute-start | bytes 786440 | tf_op jit(solution)/shard_map/ppermute | solution.py:30
  28.0 7.7 %collective-permute-start.7 = (bf16[256,640]{1,0:T(8,128)(2,1)S(1)}, bf16[256,640]{1,0:T(8,128)(2,1)S(1)}, u32[]{:S(2)}, u32[]{:S(2)}) collective-permute-start(bf16[256,640]{1,0:T(8,128)(2,1)S(1)} %get-tuple-element.86), channel_id=1, source_target_pairs={{0,2},{1,3},{2,0},{3,1},{4,6},{5,7},{6,4},{7,5},{8,10},{9,11},{10,... | collective-permute-start | bytes 983048 | tf_op jit(solution)/shard_map/ppermute | solution.py:30
  28.2 18.3 %copy-start.3 = (bf16[256,640]{1,0:T(8,128)(2,1)}, bf16[256,640]{1,0:T(8,128)(2,1)S(1)}, u32[]{:S(2)}) copy-start(bf16[256,640]{1,0:T(8,128)(2,1)S(1)} %collective-permute-done.6.g1) | copy-start | bytes 983044
  28.2 10.8 %collective-permute-start.8 = (bf16[256,640]{1,0:T(8,128)(2,1)S(1)}, bf16[256,640]{1,0:T(8,128)(2,1)S(1)}, u32[]{:S(2)}, u32[]{:S(2)}) collective-permute-start(bf16[256,640]{1,0:T(8,128)(2,1)S(1)} %get-tuple-element.83), channel_id=1, source_target_pairs={{0,3},{1,0},{2,1},{3,2},{4,7},{5,4},{6,5},{7,6},{8,11},{9,8},{10,9... | collective-permute-start | bytes 983048 | tf_op jit(solution)/shard_map/ppermute | solution.py:30
  35.8 0.7 copy-start.5
  39.0 7.5 %copy-start.7 = (bf16[256,640]{1,0:T(8,128)(2,1)}, bf16[256,640]{1,0:T(8,128)(2,1)S(1)}, u32[]{:S(2)}) copy-start(bf16[256,640]{1,0:T(8,128)(2,1)S(1)} %collective-permute-done.8.g3) | copy-start | bytes 983044
  43.3 5.8 %copy-start.1 = (bf16[4,128,256]{2,1,0:T(8,128)(2,1)S(1)}, bf16[4,128,256]{2,1,0:T(8,128)(2,1)}, u32[]{:S(2)}) copy-start(bf16[4,128,256]{2,1,0:T(8,128)(2,1)} %get-tuple-element.63.i0) | copy-start | bytes 786436
  46.6 5.3 %collective-permute-start.9 = (f32[4,56,8,128]{3,2,1,0:T(8,128)S(1)}, f32[4,56,8,128]{3,2,1,0:T(8,128)}, u32[]{:S(2)}, u32[]{:S(2)}) collective-permute-start(f32[4,56,8,128]{3,2,1,0:T(8,128)S(1)} %get-tuple-element.62), channel_id=1, source_target_pairs={{0,4},{4,0},{1,5},{5,1},{2,6},{6,2},{3,7},{7,3},{8,12},{12,8},{9,1... | collective-permute-start | bytes 2752520 | tf_op jit(solution)/shard_map/ppermute | solution.py:24
  49.6 2.2 %collective-permute-start.13 = (f32[2,48,8,128]{3,2,1,0:T(8,128)S(1)}, f32[2,48,8,128]{3,2,1,0:T(8,128)S(1)}, u32[]{:S(2)}, u32[]{:S(2)}) collective-permute-start(f32[2,48,8,128]{3,2,1,0:T(8,128)S(1)} %get-tuple-element.68), channel_id=1, source_target_pairs={{0,4},{4,0},{1,5},{5,1},{2,6},{6,2},{3,7},{7,3},{8,12},{12,8},{9,1... | collective-permute-start | bytes 1179656 | tf_op jit(solution)/shard_map/ppermute | solution.py:24
  53.2 14.7 %collective-permute-start.10 = (f32[4,14,8,128]{3,2,1,0:T(8,128)S(1)}, f32[4,14,8,128]{3,2,1,0:T(8,128)S(1)}, u32[]{:S(2)}, u32[]{:S(2)}) collective-permute-start(f32[4,14,8,128]{3,2,1,0:T(8,128)S(1)} %get-tuple-element.89), channel_id=1, source_target_pairs={{0,1},{1,2},{2,3},{3,0},{4,5},{5,6},{6,7},{7,4},{8,9},{9,10},{10,1... | collective-permute-start | bytes 688136 | tf_op jit(solution)/shard_map/ppermute | solution.py:30
  54.3 13.5 %collective-permute-start.11 = (f32[4,14,8,128]{3,2,1,0:T(8,128)S(1)}, f32[4,14,8,128]{3,2,1,0:T(8,128)S(1)}, u32[]{:S(2)}, u32[]{:S(2)}) collective-permute-start(f32[4,14,8,128]{3,2,1,0:T(8,128)S(1)} %get-tuple-element.88), channel_id=1, source_target_pairs={{0,2},{1,3},{2,0},{3,1},{4,6},{5,7},{6,4},{7,5},{8,10},{9,11},{10,... | collective-permute-start | bytes 688136 | tf_op jit(solution)/shard_map/ppermute | solution.py:30
  56.8 11.1 %collective-permute-start.12 = (f32[4,14,8,128]{3,2,1,0:T(8,128)S(1)}, f32[4,14,8,128]{3,2,1,0:T(8,128)S(1)}, u32[]{:S(2)}, u32[]{:S(2)}) collective-permute-start(f32[4,14,8,128]{3,2,1,0:T(8,128)S(1)} %get-tuple-element.87), channel_id=1, source_target_pairs={{0,3},{1,0},{2,1},{3,2},{4,7},{5,4},{6,5},{7,6},{8,11},{9,8},{10,9... | collective-permute-start | bytes 688136 | tf_op jit(solution)/shard_map/ppermute | solution.py:30
  58.5 5.7 %collective-permute-start.14 = (f32[2,12,8,128]{3,2,1,0:T(8,128)S(1)}, f32[2,12,8,128]{3,2,1,0:T(8,128)S(1)}, u32[]{:S(2)}, u32[]{:S(2)}) collective-permute-start(f32[2,12,8,128]{3,2,1,0:T(8,128)S(1)} %get-tuple-element.93), channel_id=1, source_target_pairs={{0,16},{16,32},{32,48},{48,0},{1,17},{17,33},{33,49},{49,1},{2,18}... | collective-permute-start | bytes 294920 | tf_op jit(solution)/shard_map/ppermute | solution.py:30
  58.6 6.4 %collective-permute-start.15 = (f32[2,12,8,128]{3,2,1,0:T(8,128)S(1)}, f32[2,12,8,128]{3,2,1,0:T(8,128)S(1)}, u32[]{:S(2)}, u32[]{:S(2)}) collective-permute-start(f32[2,12,8,128]{3,2,1,0:T(8,128)S(1)} %get-tuple-element.92), channel_id=1, source_target_pairs={{0,32},{16,48},{32,0},{48,16},{1,33},{17,49},{33,1},{49,17},{2,34}... | collective-permute-start | bytes 294920 | tf_op jit(solution)/shard_map/ppermute | solution.py:30
  64.2 3.7 %collective-permute-start.16 = (f32[2,12,8,128]{3,2,1,0:T(8,128)S(1)}, f32[2,12,8,128]{3,2,1,0:T(8,128)S(1)}, u32[]{:S(2)}, u32[]{:S(2)}) collective-permute-start(f32[2,12,8,128]{3,2,1,0:T(8,128)S(1)} %get-tuple-element.91), channel_id=1, source_target_pairs={{0,48},{16,0},{32,16},{48,32},{1,49},{17,1},{33,17},{49,33},{2,50}... | collective-permute-start | bytes 294920 | tf_op jit(solution)/shard_map/ppermute | solution.py:30
  86.2 26.7 %copy-start.4 = (bf16[256,640]{1,0:T(8,128)(2,1)S(1)}, bf16[256,640]{1,0:T(8,128)(2,1)}, u32[]{:S(2)}) copy-start(bf16[256,640]{1,0:T(8,128)(2,1)} %copy-done.3) | copy-start | bytes 983044
  86.2 26.7 %copy-start.6 = (bf16[256,640]{1,0:T(8,128)(2,1)S(1)}, bf16[256,640]{1,0:T(8,128)(2,1)}, u32[]{:S(2)}) copy-start(bf16[256,640]{1,0:T(8,128)(2,1)} %copy-done.5) | copy-start | bytes 983044
  86.2 26.7 %copy-start.8 = (bf16[256,640]{1,0:T(8,128)(2,1)S(1)}, bf16[256,640]{1,0:T(8,128)(2,1)}, u32[]{:S(2)}) copy-start(bf16[256,640]{1,0:T(8,128)(2,1)} %copy-done.7) | copy-start | bytes 983044
  86.9 16.1 %all-to-all-start.1 = ((f32[16,24,128]{2,1,0:T(8,128)}), f32[16,24,128]{2,1,0:T(8,128)S(1)}, u32[]{:S(2)}, u32[]{:S(2)}) async-start(f32[16,24,128]{2,1,0:T(8,128)} %broadcast_in_dim.28), calls=%async_computation.1 | async-start | bytes 393216 | tf_op jit(solution)/shard_map/all_to_all | solution.py:141
  103.8 16.8 %all-to-all-start.2 = ((f32[16,56,128]{2,1,0:T(8,128)}), f32[16,56,128]{2,1,0:T(8,128)S(1)}, u32[]{:S(2)}, u32[]{:S(2)}) async-start(f32[16,56,128]{2,1,0:T(8,128)} %broadcast_in_dim.29), calls=%async_computation.2 | async-start | bytes 917504 | tf_op jit(solution)/shard_map/all_to_all | solution.py:141
  112.9 7.6 %copy-start.2 = (f32[2,320,320]{2,1,0:T(8,128)S(1)}, f32[2,320,320]{2,1,0:T(8,128)}, u32[]{:S(2)}) copy-start(f32[2,320,320]{2,1,0:T(8,128)} %running.1) | copy-start | bytes 2457604
  117.5 0.8 copy-start.9
  120.6 1.1 copy-start.10
  138.6 9.3 %collective-permute-start.17 = (bf16[256,640]{1,0:T(8,128)(2,1)S(1)}, bf16[256,640]{1,0:T(8,128)(2,1)S(1)}, u32[]{:S(2)}, u32[]{:S(2)}) collective-permute-start(bf16[256,640]{1,0:T(8,128)(2,1)S(1)} %shard_map.60), channel_id=1, source_target_pairs={{0,1},{1,2},{2,3},{3,0},{4,5},{5,6},{6,7},{7,4},{8,9},{9,10},{10,1... | collective-permute-start | bytes 983048 | tf_op jit(solution)/shard_map/ppermute | solution.py:30
  138.7 16.8 %collective-permute-start.18 = (bf16[256,640]{1,0:T(8,128)(2,1)S(1)}, bf16[256,640]{1,0:T(8,128)(2,1)S(1)}, u32[]{:S(2)}, u32[]{:S(2)}) collective-permute-start(bf16[256,640]{1,0:T(8,128)(2,1)S(1)} %shard_map.60), channel_id=1, source_target_pairs={{0,2},{1,3},{2,0},{3,1},{4,6},{5,7},{6,4},{7,5},{8,10},{9,11},{10,... | collective-permute-start | bytes 983048 | tf_op jit(solution)/shard_map/ppermute | solution.py:30
  141.2 14.9 %collective-permute-start.19 = (bf16[256,640]{1,0:T(8,128)(2,1)S(1)}, bf16[256,640]{1,0:T(8,128)(2,1)S(1)}, u32[]{:S(2)}, u32[]{:S(2)}) collective-permute-start(bf16[256,640]{1,0:T(8,128)(2,1)S(1)} %shard_map.60), channel_id=1, source_target_pairs={{0,3},{1,0},{2,1},{3,2},{4,7},{5,4},{6,5},{7,6},{8,11},{9,8},{10,9... | collective-permute-start | bytes 983048 | tf_op jit(solution)/shard_map/ppermute | solution.py:30
  156.2 1.1 copy-start.11

commit v2 on v1

v2 whole, which is shorter than its diff:
```python
import functools

import jax
import jax.numpy as jnp
from jax import lax
from jax.experimental import pallas as pl
from jax.experimental.pallas import tpu as pltpu
from jax.sharding import Mesh, PartitionSpec as P

BA = 256
BG = 320
BGP = 384
ITERS = 8
G_TILES = 56
A_TILES = 48

factor_decay = 0.9
damping = 0.1

VMEM = pl.BlockSpec(memory_space=pltpu.VMEM)


def swap_cores(value):
    return lax.ppermute(value, "c", [(0, 1), (1, 0)])


def send_round(axis, chunks):
    size = lax.axis_size(axis)
    return [chunks[0]] + [
        lax.ppermute(chunks[s], axis, [(i, (i + s) % size) for i in range(size)])
        for s in range(1, size)
    ]


def pack_kernel(axis, width, src, *rest):
    outs, sem = rest[:4], rest[4]
    here = lax.axis_index(axis)
    copies = []
    for s in (1, 3, 2, 0):
        peer = lax.rem(here + s, 4)
        for q in range(4):
            start = pl.multiple_of((q * 4 + peer) * width, 128)
            copies.append(pltpu.make_async_copy(
                src.at[:, pl.ds(start, width)], outs[s].at[q], sem.at[s * 4 + q]
            ))
    for copy in copies:
        copy.start()
    for copy in copies:
        copy.wait()


def pack(samples, axis, width):
    piece = jax.ShapeDtypeStruct((4, samples.shape[0], width), samples.dtype)
    return pl.pallas_call(
        functools.partial(pack_kernel, axis, width),
        out_shape=[piece] * 4,
        in_specs=[pl.BlockSpec(memory_space=pl.ANY)],
        out_specs=[VMEM] * 4,
        scratch_shapes=[pltpu.SemaphoreType.DMA((16,))],
    )(samples)


def gram(v):
    return lax.dot_general(v, v, (((0,), (0,)), ((), ())), preferred_element_type=jnp.float32)


def grid_of(n):
    return (lax.broadcasted_iota(jnp.int32, (n, n), 0), lax.broadcasted_iota(jnp.int32, (n, n), 1))


def fold_block(cov, tiles, n):
    r, k = grid_of(128)
    corner = cov[128:256, 128:256]
    fold = jnp.where(r >= k, cov[0:128, 0:128], corner)
    diag = jnp.sum(jnp.where(r == k, corner, 0.0), axis=0, keepdims=True)
    tiles[n, 0:16] = fold.reshape(16, 8, 128)
    tiles[n, 16:32] = cov[128:256, 0:128].reshape(16, 8, 128)
    tiles[n, 32:40] = cov[256:BG, 0:128].reshape(8, 8, 128)
    tiles[n, 40:48] = cov[256:BG, 128:256].reshape(8, 8, 128)
    beside = jnp.concatenate([
        jnp.broadcast_to(diag[:, 0:64], (8, 64)),
        jnp.broadcast_to(diag[:, 64:128], (8, 64)),
        jnp.zeros((48, 64), jnp.float32),
    ], axis=0)
    tiles[n, 48:56] = jnp.concatenate([cov[256:BG, 256:BG], beside], axis=1).reshape(8, 8, 128)


def g_cov_kernel(i0, i1, i2, i3, own, other, rows, tiles):
    c = lax.axis_index("c")
    for s, ref in enumerate((i0, i1, i2, i3)):
        rows[s * 128:(s + 1) * 128, :] = ref[0]
    fold_block(gram(rows[:, 0:BGP]), tiles, 0)
    fold_block(gram(rows[:, 2 * BG - BGP:2 * BG])[BGP - BG:, BGP - BG:], tiles, 1)
    own[0] = tiles[c]
    other[0] = tiles[1 - c]


def g_cov(chunks):
    spec = pl.BlockSpec((1, 128, 2 * BG), lambda q: (q, 0, 0))
    out = pl.BlockSpec((1, 56, 8, 128), lambda q: (q, 0, 0, 0))
    return pl.pallas_call(
        g_cov_kernel,
        grid=(4,),
        out_shape=[jax.ShapeDtypeStruct((4, 56, 8, 128), jnp.float32)] * 2,
        in_specs=[spec] * 4,
        out_specs=[out] * 2,
        scratch_shapes=[pltpu.VMEM((512, 2 * BG), jnp.bfloat16), pltpu.VMEM((2, G_TILES, 8, 128), jnp.float32)],
        compiler_params=pltpu.CompilerParams(vmem_limit_bytes=32 << 20),
    )(*chunks)


def a_cov_kernel(i0, i1, i2, i3, own, other, rows):
    c = lax.axis_index("c")
    r, k = grid_of(128)
    for zl in range(2):
        for which, out in ((c, own), (1 - c, other)):
            q = zl * 2 + which
            for s, ref in enumerate((i0, i1, i2, i3)):
                rows[s * 128:(s + 1) * 128, :] = ref[q]
            cov = gram(rows[...])
            corner = cov[128:, 128:]
            fold = jnp.where(r >= k, cov[:128, :128], corner)
            diag = jnp.sum(jnp.where(r == k, corner, 0.0), axis=0, keepdims=True)
            out[zl, 0:16] = cov[128:, :128].reshape(16, 8, 128)
            out[zl, 16:32] = fold.reshape(16, 8, 128)
            out[zl, 32] = jnp.broadcast_to(diag, (8, 128))
            out[zl, 33:] = jnp.zeros((A_TILES - 33, 8, 128), jnp.float32)


def a_cov(chunks):
    return pl.pallas_call(
        a_cov_kernel,
        out_shape=[jax.ShapeDtypeStruct((2, A_TILES, 8, 128), jnp.float32)] * 2,
        in_specs=[VMEM] * 4,
        out_specs=[VMEM] * 2,
        scratch_shapes=[pltpu.VMEM((512, BA), jnp.bfloat16)],
        compiler_params=pltpu.CompilerParams(vmem_limit_bytes=32 << 20),
    )(*chunks)


def reduce_pieces(value, axes):
    return jnp.sum(lax.all_to_all(value, axes, 0, 0, tiled=True), axis=0)


def split(value):
    high = value.astype(jnp.bfloat16)
    return high, (value - high.astype(jnp.float32)).astype(jnp.bfloat16)


def dot3(left, right):
    dot = functools.partial(jnp.dot, preferred_element_type=jnp.float32)
    return dot(left[0], right[0]) + (dot(left[0], right[1]) + dot(left[1], right[0]))


def three(value):
    high, low = split(value)
    return high, high, low


def newton_even(matrix, identity, lhs, rhs):
    n = identity.shape[0]

    def put(approx, product):
        for i, part in enumerate(three(approx)):
            lhs[0:n, i * n:(i + 1) * n] = part
        for i, part in enumerate(three(product)):
            lhs[n:2 * n, i * n:(i + 1) * n] = part
        high, low = split(2.0 * identity - product)
        rhs[0:n], rhs[n:2 * n], rhs[2 * n:3 * n] = high, low, high

    trace = jnp.sum(matrix * identity)
    put(identity / trace, matrix / trace)

    def step(_, carry):
        both = jnp.dot(lhs[...], rhs[...], preferred_element_type=jnp.float32)
        put(both[:n], both[n:])
        return carry

    lax.fori_loop(0, ITERS - 1, step, 0)
    return jnp.dot(lhs[0:n], rhs[...], preferred_element_type=jnp.float32)


def a_side_kernel(got, running, g0, g1, g2, g3, keep, send, tiles, lhs, rhs, *, token_total):
    c, x = lax.axis_index("c"), lax.axis_index("x")
    for s in range(4):
        tiles[pl.ds(lax.rem(x + 4 - s, 4) * 12, 12)] = got[s]
    r, k = grid_of(128)
    low = tiles[0:16].reshape(128, 128)
    fold = tiles[16:32].reshape(128, 128)
    diag = tiles[32][0:1]
    turned = fold.T
    top = jnp.where(r >= k, fold, turned)
    corner = jnp.where(r == k, jnp.broadcast_to(diag, (128, 128)), jnp.where(r < k, fold, turned))
    cov = jnp.concatenate([
        jnp.concatenate([top, low.T], axis=1), jnp.concatenate([low, corner], axis=1)
    ], axis=0)
    r, k = grid_of(BA)
    identity = jnp.where(r == k, 1.0, 0.0)
    mixed = factor_decay * running[0] + (1.0 - factor_decay) * cov / token_total
    inverse = newton_even(mixed + damping * identity, identity, lhs, rhs)
    summed = (g0[...].astype(jnp.float32) + g1[...].astype(jnp.float32)) + (
        g2[...].astype(jnp.float32) + g3[...].astype(jnp.float32)
    )
    left = dot3(split(inverse), split(summed))
    keep[...] = jnp.where(c == 0, left[:, 0:BG], left[:, BG:])
    send[...] = jnp.where(c == 0, left[:, BG:], left[:, 0:BG])


def a_side(tiles, running, grads, token_total):
    return pl.pallas_call(
        functools.partial(a_side_kernel, token_total=token_total),
        out_shape=[jax.ShapeDtypeStruct((BA, BG), jnp.float32)] * 2,
        in_specs=[VMEM] * 6,
        out_specs=[VMEM] * 2,
        scratch_shapes=[
            pltpu.VMEM((A_TILES, 8, 128), jnp.float32),
            pltpu.VMEM((2 * BA, 3 * BA), jnp.bfloat16), pltpu.VMEM((3 * BA, BA), jnp.bfloat16)
        ],
        compiler_params=pltpu.CompilerParams(vmem_limit_bytes=32 << 20),
        cost_estimate=pl.CostEstimate(flops=2_500_000_000, bytes_accessed=2_000_000, transcendentals=0),
    )(tiles, running, *grads)


def turned_tail(main):
    tail = main[256:BG]
    return jnp.concatenate([tail, jnp.zeros_like(tail)], axis=0).T


def unfold_block(tiles):
    r, k = grid_of(128)
    fold = tiles[0:16].reshape(128, 128)
    low = tiles[16:32].reshape(128, 128)
    last = tiles[48:56].reshape(64, 128)
    diag = jnp.concatenate([last[0:1, 64:128], last[8:9, 64:128]], axis=1)
    turned = fold.T
    first = jnp.where(r >= k, fold, turned)
    second = jnp.where(r == k, jnp.broadcast_to(diag, (128, 128)), jnp.where(r < k, fold, turned))
    bottom = [tiles[32:40].reshape(64, 128), tiles[40:48].reshape(64, 128)]
    main = jnp.concatenate([
        jnp.concatenate([first, low.T], axis=1),
        jnp.concatenate([low, second], axis=1),
        jnp.concatenate(bottom, axis=1),
    ], axis=0)
    empty = jnp.zeros((64, 128), jnp.float32)
    r, k = lax.broadcasted_iota(jnp.int32, (64, 128), 0), lax.broadcasted_iota(jnp.int32, (64, 128), 1)
    tail = jnp.concatenate([jnp.concatenate([part, empty], axis=0).T for part in bottom]
                           + [jnp.where(k < 64, last, 0.0)], axis=0)
    return main, tail


def g_put(lhs, rhs_main, rhs_tail, ident, approx, product):
    for row, (main, tail) in ((0, approx), (BG, product)):
        for i, (part, edge) in enumerate(zip(three(main), three(tail))):
            lhs[row:row + BG, i * BGP:i * BGP + 256] = part
            lhs[row:row + BG, i * BGP + 256:(i + 1) * BGP] = edge
    for rhs, same, value in ((rhs_main, ident[0], product[0]), (rhs_tail, ident[1], product[1])):
        high, low = split(2.0 * same - value)
        rhs[0:BG] = high
        rhs[BGP:BGP + BG] = low
        rhs[2 * BGP:2 * BGP + BG] = high


def g_side_kernel(
    got, running, left_own, left_sibling, own, sibling, tiles, lhs, rhs_main, rhs_tail, *, token_total
):
    c, y, zl = (lax.axis_index(name) for name in ("c", "y", "zl"))
    for z, near in enumerate((zl, 1 - zl)):
        for s in range(4):
            tiles[pl.ds(lax.rem(y + 4 - s, 4) * 14 + near * 7, 7)] = got[z, s]
    new_sum = unfold_block(tiles)
    previous = running[c, :, 0:256], jnp.concatenate(
        [running[c, :, 256:BG], jnp.zeros((BG, 64), jnp.float32)], axis=1
    )
    r, k = lax.broadcasted_iota(jnp.int32, (BG, 256), 0), lax.broadcasted_iota(jnp.int32, (BG, 256), 1)
    ident = [jnp.where(r == k, 1.0, 0.0)]
    r, k = lax.broadcasted_iota(jnp.int32, (BG, 128), 0), lax.broadcasted_iota(jnp.int32, (BG, 128), 1)
    ident.append(jnp.where(r == k + 256, 1.0, 0.0))
    matrix = [
        (factor_decay * before + (1.0 - factor_decay) * cov / token_total) + damping * same
        for before, cov, same in zip(previous, new_sum, ident)
    ]
    trace = sum(jnp.sum(part * same) for part, same in zip(matrix, ident))
    rhs_main[...] = jnp.zeros(rhs_main.shape, jnp.bfloat16)
    rhs_tail[...] = jnp.zeros(rhs_tail.shape, jnp.bfloat16)
    put = functools.partial(g_put, lhs, rhs_main, rhs_tail, ident)
    put([same / trace for same in ident], [part / trace for part in matrix])

    def product(rows):
        main = jnp.dot(lhs[0:rows], rhs_main[...], preferred_element_type=jnp.float32)
        corners = [
            jnp.dot(lhs[row + 256:row + BG], rhs_tail[...], preferred_element_type=jnp.float32)
            for row in range(0, rows, BG)
        ]
        return [
            (main[row:row + BG], jnp.concatenate([turned_tail(main[row:row + BG]), corner], axis=0))
            for row, corner in zip(range(0, rows, BG), corners)
        ]

    def step(_, carry):
        put(*product(2 * BG))
        return carry

    lax.fori_loop(0, ITERS - 1, step, 0)
    (main, tail), = product(BG)
    inverse = split(jnp.concatenate([main, tail], axis=1))
    for left, out in ((left_sibling, sibling), (left_own, own)):
        out[...] = dot3(split(left[...]), inverse)[:, 0:BG].astype(jnp.bfloat16)


def g_side(got, running, left_own, left_sibling, token_total):
    return pl.pallas_call(
        functools.partial(g_side_kernel, token_total=token_total),
        out_shape=[jax.ShapeDtypeStruct((BA, BG), jnp.bfloat16)] * 2,
        in_specs=[VMEM] * 4,
        out_specs=[VMEM] * 2,
        scratch_shapes=[
            pltpu.VMEM((G_TILES, 8, 128), jnp.float32),
            pltpu.VMEM((2 * BG, 3 * BGP), jnp.bfloat16),
            pltpu.VMEM((3 * BGP, 256), jnp.bfloat16),
            pltpu.VMEM((3 * BGP, 128), jnp.bfloat16),
        ],
        compiler_params=pltpu.CompilerParams(vmem_limit_bytes=40 << 20),
        cost_estimate=pl.CostEstimate(flops=6_000_000_000, bytes_accessed=3_000_000, transcendentals=0),
    )(got, running, left_own, left_sibling)


def per_device(activations, out_grads, a_running, g_running, grad_partial):
    token_total = float(activations.shape[0] * 256)
    x, zl, c, y = (lax.axis_index(name) for name in ("x", "zl", "c", "y"))

    g_chunks = pack(out_grads, "x", 2 * BG)
    g_chunks, activations = lax.optimization_barrier((g_chunks, activations))
    g_in = send_round("x", g_chunks)
    a_in = send_round("y", pack(activations, "y", BA))
    g_in, a_in = lax.optimization_barrier((g_in, a_in))

    g_own, g_other = g_cov(g_in)
    a_own, a_other = a_cov(a_in)
    g_part = (g_own + swap_cores(g_other)).reshape(4, 4, 14, 8, 128)
    a_part = (a_own + swap_cores(a_other)).reshape(2, 4, 12, 8, 128)

    g_lines = send_round("y", [
        lax.dynamic_index_in_dim(g_part, lax.rem(y + s, 4), 1, keepdims=False) for s in range(4)
    ])
    a_lines = send_round("x", [
        lax.dynamic_index_in_dim(a_part, lax.rem(x + s, 4), 1, keepdims=False) for s in range(4)
    ])
    g_lines, a_lines, grad_partial = lax.optimization_barrier((g_lines, a_lines, grad_partial))
    grads = send_round("y", [
        lax.dynamic_slice_in_dim(grad_partial[0], lax.rem(y + s, 4) * BA, BA, 0) for s in range(4)
    ])
    g_line = (g_lines[0] + g_lines[1]) + (g_lines[2] + g_lines[3])
    a_line = (a_lines[0] + a_lines[1]) + (a_lines[2] + a_lines[3])

    both = jnp.concatenate([
        g_line.reshape(8, 56, 128),
        jnp.broadcast_to(a_line.reshape(1, 2, 96, 128), (4, 2, 96, 128)).reshape(8, 96, 128),
    ], axis=1)
    pieces = reduce_pieces(both, ("zh", "zl"))
    pieces, grads = lax.optimization_barrier((pieces, grads))

    g_rows = jnp.stack(send_round("y", [pieces[:56]] * 4))
    a_tiles = jnp.stack(send_round("x", [pieces[56:]] * 4)).reshape(4, 12, 8, 128)
    g_tiles = jnp.stack([g_rows, lax.ppermute(g_rows, "zl", [(0, 1), (1, 0)])]).reshape(2, 4, 7, 8, 128)

    a_previous = lax.dynamic_slice_in_dim(a_running, (zl * 2 + c) * 4 + y, 1, 0)
    left, left_send = a_side(a_tiles, a_previous, grads, token_total)
    own, sibling = g_side(g_tiles, g_running, left, swap_cores(left_send), token_total)
    got = swap_cores(sibling)
    rows = jnp.concatenate([jnp.where(c == 0, own, got), jnp.where(c == 0, got, own)], axis=1)

    out = jnp.zeros((4, BA, 2 * BG), jnp.bfloat16)
    for shift, got in enumerate(send_round("y", [rows] * 4)):
        out = lax.dynamic_update_slice_in_dim(out, got[None], lax.rem(y + 4 - shift, 4), 0)
    return out.reshape(4 * BA, 2 * BG)


def solution(mesh):
    fine = Mesh(mesh.devices.reshape(4, 4, 2, 2, 4), ("zh", "x", "zl", "c", "y"))
    tokens = P(("zh", "x", "zl", "c", "y"), None)
    placed = (tokens, tokens, P(), P(("zh", "x"), None, None), P("y", ("zl", "c"), ("zh", "x")))
    return jax.shard_map(
        per_device,
        mesh=fine,
        in_specs=placed,
        out_specs=P(("zl", "c"), ("zh", "x")),
        check_vma=False,
    )
```

time: 158 us -> 138 us (0.87)
  blocking collectives: 18.1 us -> 0 us
  starting transfers between devices: 40.2 us -> 52.3 us
  Pallas kernels: 31.1 us -> 22.4 us
  local copies, waits for them, and re-layouts: 7.57 us -> 3.41 us
    all_to_all x1 -> x0, blocking collectives: 18.1 us -> none  [reduce_pieces(): return jnp.sum(lax.all_to_all(value, axes, 0, 0, tiled=True), axis=0)]
    ppermute x18 -> x24, starting transfers between devices: 23.3 us -> 37.9 us  [send_round(): lax.ppermute(chunks[s], axis, [(i, (i + s) % size) for i in range(size)])]
    pallas_call x1, Pallas kernels: 16.9 us -> 7.67 us  [g_side(): pl.pallas_call(functools.partial(g_side_kernel, token_total=token_total),...]
    all_to_all x2 -> x1, starting transfers between devices: 14.2 us -> 8.2 us  [reduce_pieces(): return jnp.sum(lax.all_to_all(value, axes, 0, 0, tiled=True), axis=0)]
    ppermute x18 -> x24, waiting for transfers between devices: 44.1 us -> 39.7 us  [send_round(): lax.ppermute(chunks[s], axis, [(i, (i + s) % size) for i in range(size)])]
    ppermute x0 -> x1, waiting for transfers between devices: none -> 3.74 us  [per_device(): lax.ppermute(g_rows, 'zl', [(0, 1), (1, 0)])]
    unnamed x32 -> x10, local copies, waits for them, and re-layouts: 4.61 us -> 1.07 us
    ppermute x2 -> x4, starting transfers between devices: 2.7 us -> 5.08 us  [swap_cores(): return lax.ppermute(value, 'c', [(0, 1), (1, 0)])]
  transfers between devices with their start and end apart: 22 -> 30, of which waited for: 15 -> 14; matrix products, arithmetic and copies ran while one was open for 1% -> 2% of each run, Pallas kernels for 3% -> 5%
where the time goes in v2:
time: 138 us; the launch traced here: 137 us
  waiting for transfers between devices  57.5 us (42%)
  starting transfers between devices  52.3 us (38%)
  Pallas kernels  22.4 us (16%)
  local copies, waits for them, and re-layouts  3.41 us (2%)
    ppermute x24, waiting for transfers between devices, send_round(): lax.ppermute(chunks[s], axis, [(i, (i + s) % size) for i in range(size)])  39.7 us
    ppermute x24, starting transfers between devices, send_round(): lax.ppermute(chunks[s], axis, [(i, (i + s) % size) for i in range(size)])  37.9 us
    all_to_all x1, waiting for transfers between devices, reduce_pieces(): return jnp.sum(lax.all_to_all(value, axes, 0, 0, tiled=True), axis=0)  11 us
    all_to_all x1, starting transfers between devices, reduce_pieces(): return jnp.sum(lax.all_to_all(value, axes, 0, 0, tiled=True), axis=0)  8.2 us
    pallas_call x1, Pallas kernels, g_side(): pl.pallas_call(functools.partial(g_side_kernel, token_total=token_total),...  7.67 us
    pallas_call x2, Pallas kernels, pack(): pl.pallas_call(functools.partial(pack_kernel, axis, width), out_shape=[pi...  5.8 us
    ppermute x4, starting transfers between devices, swap_cores(): return lax.ppermute(value, 'c', [(0, 1), (1, 0)])  5.08 us
    pallas_call x1, Pallas kernels, a_side(): pl.pallas_call(functools.partial(a_side_kernel, token_total=token_total),...  4.28 us
  transfers between devices with their start and end apart: 30, of which 14 were waited for; matrix products, arithmetic and copies ran while one was open for 2% of the time, Pallas kernels for 5%

profile of v2, /device:TPU:1, one launch (start us, length us, event | category | flops | bytes accessed | tf_op | source)
XLA Modules:
  0.0 137.3 jit_solution(15045417440507968880)
XLA Ops:
  0.0 3.4 %shard_map.55 = (bf16[4,128,640]{2,1,0:T(8,128)(2,1)}, bf16[4,128,640]{2,1,0:T(8,128)(2,1)}, bf16[4,128,640]{2,1,0:T(8,128)(2,1)}, bf16[4,128,640]{2,1,0:T(8,128)(2,1)}) custom-call(bf16[128,10240]{1,0:T(8,128)(2,1)} %src.1), custom_call_target="tpu_custom_call" | custom-call | tf_op jit(solution)/shard_map/pallas_call | solution.py:54
  3.4 2.1 %collective-permute-start = (bf16[4,128,640]{2,1,0:T(8,128)(2,1)}, bf16[4,128,640]{2,1,0:T(8,128)(2,1)S(1)}, u32[]{:S(2)}, u32[]{:S(2)}) collective-permute-start(bf16[4,128,640]{2,1,0:T(8,128)(2,1)} %get-tuple-element.53), channel_id=1, source_target_pairs={{0,16},{16,32},{32,48},{48,0},{1,17},{17,33},{33,49},{49,1},{2,18}... | collective-permute-start | bytes 1966088 | tf_op jit(solution)/shard_map/ppermute | solution.py:30
  5.6 2.5 %collective-permute-start.1 = (bf16[4,128,640]{2,1,0:T(8,128)(2,1)}, bf16[4,128,640]{2,1,0:T(8,128)(2,1)S(1)}, u32[]{:S(2)}, u32[]{:S(2)}) collective-permute-start(bf16[4,128,640]{2,1,0:T(8,128)(2,1)} %get-tuple-element.54), channel_id=1, source_target_pairs={{0,32},{16,48},{32,0},{48,16},{1,33},{17,49},{33,1},{49,17},{2,34}... | collective-permute-start | bytes 1966088 | tf_op jit(solution)/shard_map/ppermute | solution.py:30
  8.0 1.2 collective-permute-start.2
  9.2 2.4 %shard_map.56 = (bf16[4,128,256]{2,1,0:T(8,128)(2,1)}, bf16[4,128,256]{2,1,0:T(8,128)(2,1)}, bf16[4,128,256]{2,1,0:T(8,128)(2,1)}, bf16[4,128,256]{2,1,0:T(8,128)(2,1)}) custom-call(bf16[128,4096]{1,0:T(8,128)(2,1)} %src.2), custom_call_target="tpu_custom_call" | custom-call | tf_op jit(solution)/shard_map/pallas_call | solution.py:54
  11.6 1.4 %collective-permute-start.3 = (bf16[4,128,256]{2,1,0:T(8,128)(2,1)}, bf16[4,128,256]{2,1,0:T(8,128)(2,1)S(1)}, u32[]{:S(2)}, u32[]{:S(2)}) collective-permute-start(bf16[4,128,256]{2,1,0:T(8,128)(2,1)} %get-tuple-element.58), channel_id=1, source_target_pairs={{0,1},{1,2},{2,3},{3,0},{4,5},{5,6},{6,7},{7,4},{8,9},{9,10},{10,1... | collective-permute-start | bytes 786440 | tf_op jit(solution)/shard_map/ppermute | solution.py:30
  12.9 2.6 %collective-permute-start.4 = (bf16[4,128,256]{2,1,0:T(8,128)(2,1)}, bf16[4,128,256]{2,1,0:T(8,128)(2,1)S(1)}, u32[]{:S(2)}, u32[]{:S(2)}) collective-permute-start(bf16[4,128,256]{2,1,0:T(8,128)(2,1)} %get-tuple-element.59), channel_id=1, source_target_pairs={{0,2},{1,3},{2,0},{3,1},{4,6},{5,7},{6,4},{7,5},{8,10},{9,11},{10,... | collective-permute-start | bytes 786440 | tf_op jit(solution)/shard_map/ppermute | solution.py:30
  15.5 3.9 %collective-permute-done.3.i1 = bf16[4,128,256]{2,1,0:T(8,128)(2,1)S(1)} collective-permute-done((bf16[4,128,256]{2,1,0:T(8,128)(2,1)}, bf16[4,128,256]{2,1,0:T(8,128)(2,1)S(1)}, u32[]{:S(2)}, u32[]{:S(2)}) %collective-permute-start.3) | collective-permute-done | bytes 262176 | tf_op jit(solution)/shard_map/ppermute | solution.py:30
  19.5 1.4 %collective-permute-start.5 = (bf16[4,128,256]{2,1,0:T(8,128)(2,1)}, bf16[4,128,256]{2,1,0:T(8,128)(2,1)S(1)}, u32[]{:S(2)}, u32[]{:S(2)}) collective-permute-start(bf16[4,128,256]{2,1,0:T(8,128)(2,1)} %get-tuple-element.60), channel_id=1, source_target_pairs={{0,3},{1,0},{2,1},{3,2},{4,7},{5,4},{6,5},{7,6},{8,11},{9,8},{10,9... | collective-permute-start | bytes 786440 | tf_op jit(solution)/shard_map/ppermute | solution.py:30
  20.9 5.3 %collective-permute-done.4.i2 = bf16[4,128,256]{2,1,0:T(8,128)(2,1)S(1)} collective-permute-done((bf16[4,128,256]{2,1,0:T(8,128)(2,1)}, bf16[4,128,256]{2,1,0:T(8,128)(2,1)S(1)}, u32[]{:S(2)}, u32[]{:S(2)}) %collective-permute-start.4) | collective-permute-done | bytes 262176 | tf_op jit(solution)/shard_map/ppermute | solution.py:30
  26.2 10.2 %collective-permute-done.1.i2 = bf16[4,128,640]{2,1,0:T(8,128)(2,1)S(1)} collective-permute-done((bf16[4,128,640]{2,1,0:T(8,128)(2,1)}, bf16[4,128,640]{2,1,0:T(8,128)(2,1)S(1)}, u32[]{:S(2)}, u32[]{:S(2)}) %collective-permute-start.1) | collective-permute-done | bytes 655392 | tf_op jit(solution)/shard_map/ppermute | solution.py:30
  36.4 4.2 %shard_map.57 = (f32[4,56,8,128]{3,2,1,0:T(8,128)S(1)}, f32[4,56,8,128]{3,2,1,0:T(8,128)}) custom-call(bf16[4,128,640]{2,1,0:T(8,128)(2,1)S(1)} %copy-done, bf16[4,128,640]{2,1,0:T(8,128)(2,1)S(1)} %collective-permute-done.i1, bf16[4,128,640]{2,1,0:T(8,128)(2,1)S(1)} %collective-permute-done.1.i2, bf16[4,128,640]{2,1,0:T(8,128)(2,1)S(1)} %collective-permute-done.2.i3), custom_call_target="tpu_custom_call" | custom-call | tf_op jit(solution)/shard_map/pallas_call | solution.py:101
  40.6 1.5 %collective-permute-start.6 = (f32[4,56,8,128]{3,2,1,0:T(8,128)}, f32[4,56,8,128]{3,2,1,0:T(8,128)S(1)}, u32[]{:S(2)}, u32[]{:S(2)}) collective-permute-start(f32[4,56,8,128]{3,2,1,0:T(8,128)} %get-tuple-element.66), channel_id=1, source_target_pairs={{0,4},{4,0},{1,5},{5,1},{2,6},{6,2},{3,7},{7,3},{8,12},{12,8},{9,1... | collective-permute-start | bytes 2752520 | tf_op jit(solution)/shard_map/ppermute | solution.py:24
  42.8 2.0 %collective-permute-done.10 = f32[2,48,8,128]{3,2,1,0:T(8,128)S(1)} collective-permute-done((f32[2,48,8,128]{3,2,1,0:T(8,128)S(1)}, f32[2,48,8,128]{3,2,1,0:T(8,128)S(1)}, u32[]{:S(2)}, u32[]{:S(2)}) %collective-permute-start.10) | collective-permute-done | bytes 393248 | tf_op jit(solution)/shard_map/ppermute | solution.py:24
  45.0 1.4 collective-permute-start.7
  46.4 2.6 %collective-permute-start.8 = (f32[4,14,8,128]{3,2,1,0:T(8,128)S(1)}, f32[4,14,8,128]{3,2,1,0:T(8,128)S(1)}, u32[]{:S(2)}, u32[]{:S(2)}) collective-permute-start(f32[4,14,8,128]{3,2,1,0:T(8,128)S(1)} %get-tuple-element.98), channel_id=1, source_target_pairs={{0,2},{1,3},{2,0},{3,1},{4,6},{5,7},{6,4},{7,5},{8,10},{9,11},{10,... | collective-permute-start | bytes 688136 | tf_op jit(solution)/shard_map/ppermute | solution.py:30
  49.0 1.1 collective-permute-start.9
  50.1 1.1 collective-permute-start.11
  51.2 2.1 %collective-permute-start.12 = (f32[2,12,8,128]{3,2,1,0:T(8,128)S(1)}, f32[2,12,8,128]{3,2,1,0:T(8,128)S(1)}, u32[]{:S(2)}, u32[]{:S(2)}) collective-permute-start(f32[2,12,8,128]{3,2,1,0:T(8,128)S(1)} %get-tuple-element.104), channel_id=1, source_target_pairs={{0,32},{16,48},{32,0},{48,16},{1,33},{17,49},{33,1},{49,17},{2,34}... | collective-permute-start | bytes 294920 | tf_op jit(solution)/shard_map/ppermute | solution.py:30
  53.3 1.5 %collective-permute-done.11 = f32[2,12,8,128]{3,2,1,0:T(8,128)S(1)} collective-permute-done((f32[2,12,8,128]{3,2,1,0:T(8,128)S(1)}, f32[2,12,8,128]{3,2,1,0:T(8,128)S(1)}, u32[]{:S(2)}, u32[]{:S(2)}) %collective-permute-start.11) | collective-permute-done | bytes 98336 | tf_op jit(solution)/shard_map/ppermute | solution.py:30
  54.9 1.0 collective-permute-start.13
  55.9 1.1 collective-permute-done.12
  57.1 1.7 %collective-permute-done.13 = f32[2,12,8,128]{3,2,1,0:T(8,128)S(1)} collective-permute-done((f32[2,12,8,128]{3,2,1,0:T(8,128)S(1)}, f32[2,12,8,128]{3,2,1,0:T(8,128)S(1)}, u32[]{:S(2)}, u32[]{:S(2)}) %collective-permute-start.13) | collective-permute-done | bytes 98336 | tf_op jit(solution)/shard_map/ppermute | solution.py:30
  58.8 0.5 collective-permute-done.8
  59.4 0.9 pad_maximum_fusion
  60.3 8.2 %all-to-all-start = ((f32[8,152,128]{2,1,0:T(8,128)}), f32[8,152,128]{2,1,0:T(8,128)S(1)}, u32[]{:S(2)}, u32[]{:S(2)}) async-start(f32[8,152,128]{2,1,0:T(8,128)} %pad_maximum_fusion), calls=%async_computation | async-start | bytes 1245184 | tf_op jit(solution)/shard_map/all_to_all | solution.py:142
  68.5 1.0 dynamic-slice_bitcast_fusion
  69.5 1.0 collective-permute-start.14
  70.5 2.8 %collective-permute-start.15 = (bf16[256,640]{1,0:T(8,128)(2,1)}, bf16[256,640]{1,0:T(8,128)(2,1)S(1)}, u32[]{:S(2)}, u32[]{:S(2)}) collective-permute-start(bf16[256,640]{1,0:T(8,128)(2,1)} %get-tuple-element.94), channel_id=1, source_target_pairs={{0,2},{1,3},{2,0},{3,1},{4,6},{5,7},{6,4},{7,5},{8,10},{9,11},{10,... | collective-permute-start | bytes 983048 | tf_op jit(solution)/shard_map/ppermute | solution.py:30
  73.6 1.0 constant_dynamic-slice_fusion.running
  74.6 11.0 %all-to-all-done = f32[8,152,128]{2,1,0:T(8,128)S(1)} async-done(((f32[8,152,128]{2,1,0:T(8,128)}), f32[8,152,128]{2,1,0:T(8,128)S(1)}, u32[]{:S(2)}, u32[]{:S(2)}) %all-to-all-start) | async-done | bytes 622624 | tf_op jit(solution)/shard_map/all_to_all | solution.py:142
  85.6 1.6 %collective-permute-done.15.g2 = bf16[256,640]{1,0:T(8,128)(2,1)S(1)} collective-permute-done((bf16[256,640]{1,0:T(8,128)(2,1)}, bf16[256,640]{1,0:T(8,128)(2,1)S(1)}, u32[]{:S(2)}, u32[]{:S(2)}) %collective-permute-start.15) | collective-permute-done | bytes 327712 | tf_op jit(solution)/shard_map/ppermute | solution.py:30
  87.2 1.4 %collective-permute-start.21 = (f32[96,128]{1,0:T(8,128)S(1)}, f32[96,128]{1,0:T(8,128)S(1)}, u32[]{:S(2)}, u32[]{:S(2)}) collective-permute-start(f32[96,128]{1,0:T(8,128)S(1)} %get-tuple-element.108), channel_id=1, source_target_pairs={{0,16},{16,32},{32,48},{48,0},{1,17},{17,33},{33,49},{49,1},{2,18}... | collective-permute-start | bytes 147464 | tf_op jit(solution)/shard_map/ppermute | solution.py:30
  88.6 2.1 %collective-permute-start.22 = (f32[96,128]{1,0:T(8,128)S(1)}, f32[96,128]{1,0:T(8,128)S(1)}, u32[]{:S(2)}, u32[]{:S(2)}) collective-permute-start(f32[96,128]{1,0:T(8,128)S(1)} %get-tuple-element.108), channel_id=1, source_target_pairs={{0,32},{16,48},{32,0},{48,16},{1,33},{17,49},{33,1},{49,17},{2,34}... | collective-permute-start | bytes 147464 | tf_op jit(solution)/shard_map/ppermute | solution.py:30
  90.7 1.3 collective-permute-start.23
  92.0 2.1 %collective-permute-start.17 = (f32[56,128]{1,0:T(8,128)S(1)}, f32[56,128]{1,0:T(8,128)S(1)}, u32[]{:S(2)}, u32[]{:S(2)}) collective-permute-start(f32[56,128]{1,0:T(8,128)S(1)} %get-tuple-element.111), channel_id=1, source_target_pairs={{0,1},{1,2},{2,3},{3,0},{4,5},{5,6},{6,7},{7,4},{8,9},{9,10},{10,1... | collective-permute-start | bytes 86024 | tf_op jit(solution)/shard_map/ppermute | solution.py:30
  94.1 2.8 %collective-permute-start.18 = (f32[56,128]{1,0:T(8,128)S(1)}, f32[56,128]{1,0:T(8,128)S(1)}, u32[]{:S(2)}, u32[]{:S(2)}) collective-permute-start(f32[56,128]{1,0:T(8,128)S(1)} %get-tuple-element.111), channel_id=1, source_target_pairs={{0,2},{1,3},{2,0},{3,1},{4,6},{5,7},{6,4},{7,5},{8,10},{9,11},{10,... | collective-permute-start | bytes 86024 | tf_op jit(solution)/shard_map/ppermute | solution.py:30
  97.0 4.3 %shard_map.59 = (f32[256,320]{1,0:T(8,128)S(1)}, f32[256,320]{1,0:T(8,128)S(1)}) custom-call(f32[4,12,8,128]{3,2,1,0:T(8,128)S(1)} %pad_maximum_fusion.3.got, f32[1,256,256]{2,1,0:T(8,128)S(1)} %constant_dynamic-slice_fusion.running, bf16[256,640]{1,0:T(8,128)(2,1)S(1)} %get-tuple-element.83.g0, bf16[256,640]{1,0:T(8,128)(2,1)S(1)} %collective-permute-done.14.g1, ...), custom_call_target="tpu_custom_call" | custom-call | flops 2500000000 | bytes 2000000 | tf_op jit(solution)/shard_map/pallas_call | solution.py:210
  101.3 2.5 %collective-permute-start.24 = (f32[256,320]{1,0:T(8,128)S(1)}, f32[256,320]{1,0:T(8,128)S(1)}, u32[]{:S(2)}, u32[]{:S(2)}) collective-permute-start(f32[256,320]{1,0:T(8,128)S(1)} %get-tuple-element.88), channel_id=1, source_target_pairs={{0,4},{4,0},{1,5},{5,1},{2,6},{6,2},{3,7},{7,3},{8,12},{12,8},{9,1... | collective-permute-start | bytes 983048 | tf_op jit(solution)/shard_map/ppermute | solution.py:24
  103.9 1.1 collective-permute-start.20
  104.9 3.7 %collective-permute-done.20 = f32[4,56,128]{2,1,0:T(8,128)S(1)} collective-permute-done((f32[4,56,128]{2,1,0:T(8,128)S(1)}, f32[4,56,128]{2,1,0:T(8,128)S(1)}, u32[]{:S(2)}, u32[]{:S(2)}) %collective-permute-start.20) | collective-permute-done | bytes 114720 | tf_op jit(solution)/shard_map/ppermute | solution.py:364
  108.7 7.7 %shard_map.60 = (bf16[256,320]{1,0:T(8,128)(2,1)S(1)}, bf16[256,320]{1,0:T(8,128)(2,1)S(1)}) custom-call(f32[2,4,7,8,128]{4,3,2,1,0:T(8,128)S(1)} %pad_maximum_fusion.2.got, f32[2,320,320]{2,1,0:T(8,128)S(1)} %copy-done.2, f32[256,320]{1,0:T(8,128)S(1)} %get-tuple-element.87.left_own, f32[256,320]{1,0:T(8,128)S(1)} %collective-permute-done.24.left_sibling), custom_call_target="tpu_custom_call" | custom-call | flops 6000000000 | bytes 3000000 | tf_op jit(solution)/shard_map/pallas_call | solution.py:311
  116.4 0.9 collective-permute-start.25
  117.3 1.1 collective-permute-done.25
  118.7 1.2 collective-permute-start.26
  120.1 2.3 %collective-permute-start.28 = (bf16[256,640]{1,0:T(8,128)(2,1)S(1)}, bf16[256,640]{1,0:T(8,128)(2,1)S(1)}, u32[]{:S(2)}, u32[]{:S(2)}) collective-permute-start(bf16[256,640]{1,0:T(8,128)(2,1)S(1)} %get-tuple-element.92), channel_id=1, source_target_pairs={{0,3},{1,0},{2,1},{3,2},{4,7},{5,4},{6,5},{7,6},{8,11},{9,8},{10,9... | collective-permute-start | bytes 983048 | tf_op jit(solution)/shard_map/ppermute | solution.py:30
  122.4 13.5 %collective-permute-done.26 = bf16[256,640]{1,0:T(8,128)(2,1)S(1)} collective-permute-done((bf16[256,640]{1,0:T(8,128)(2,1)S(1)}, bf16[256,640]{1,0:T(8,128)(2,1)S(1)}, u32[]{:S(2)}, u32[]{:S(2)}) %collective-permute-start.26) | collective-permute-done | bytes 327712 | tf_op jit(solution)/shard_map/ppermute | solution.py:30
  136.3 1.0 copy-done.3
  (50 shorter events, 2.2 us)
Async XLA Ops:
  3.4 33.0 %copy-start = (bf16[4,128,640]{2,1,0:T(8,128)(2,1)S(1)}, bf16[4,128,640]{2,1,0:T(8,128)(2,1)}, u32[]{:S(2)}) copy-start(bf16[4,128,640]{2,1,0:T(8,128)(2,1)} %get-tuple-element.61.i0) | copy-start | bytes 1966084
  3.4 22.7 %collective-permute-start = (bf16[4,128,640]{2,1,0:T(8,128)(2,1)}, bf16[4,128,640]{2,1,0:T(8,128)(2,1)S(1)}, u32[]{:S(2)}, u32[]{:S(2)}) collective-permute-start(bf16[4,128,640]{2,1,0:T(8,128)(2,1)} %get-tuple-element.53), channel_id=1, source_target_pairs={{0,16},{16,32},{32,48},{48,0},{1,17},{17,33},{33,49},{49,1},{2,18}... | collective-permute-start | bytes 1966088 | tf_op jit(solution)/shard_map/ppermute | solution.py:30
  5.6 30.8 %collective-permute-start.1 = (bf16[4,128,640]{2,1,0:T(8,128)(2,1)}, bf16[4,128,640]{2,1,0:T(8,128)(2,1)S(1)}, u32[]{:S(2)}, u32[]{:S(2)}) collective-permute-start(bf16[4,128,640]{2,1,0:T(8,128)(2,1)} %get-tuple-element.54), channel_id=1, source_target_pairs={{0,32},{16,48},{32,0},{48,16},{1,33},{17,49},{33,1},{49,17},{2,34}... | collective-permute-start | bytes 1966088 | tf_op jit(solution)/shard_map/ppermute | solution.py:30
  8.0 28.4 %collective-permute-start.2 = (bf16[4,128,640]{2,1,0:T(8,128)(2,1)}, bf16[4,128,640]{2,1,0:T(8,128)(2,1)S(1)}, u32[]{:S(2)}, u32[]{:S(2)}) collective-permute-start(bf16[4,128,640]{2,1,0:T(8,128)(2,1)} %get-tuple-element.55), channel_id=1, source_target_pairs={{0,48},{16,0},{32,16},{48,32},{1,49},{17,1},{33,17},{49,33},{2,50}... | collective-permute-start | bytes 1966088 | tf_op jit(solution)/shard_map/ppermute | solution.py:30
  11.6 7.9 %collective-permute-start.3 = (bf16[4,128,256]{2,1,0:T(8,128)(2,1)}, bf16[4,128,256]{2,1,0:T(8,128)(2,1)S(1)}, u32[]{:S(2)}, u32[]{:S(2)}) collective-permute-start(bf16[4,128,256]{2,1,0:T(8,128)(2,1)} %get-tuple-element.58), channel_id=1, source_target_pairs={{0,1},{1,2},{2,3},{3,0},{4,5},{5,6},{6,7},{7,4},{8,9},{9,10},{10,1... | collective-permute-start | bytes 786440 | tf_op jit(solution)/shard_map/ppermute | solution.py:30
  12.9 13.3 %collective-permute-start.4 = (bf16[4,128,256]{2,1,0:T(8,128)(2,1)}, bf16[4,128,256]{2,1,0:T(8,128)(2,1)S(1)}, u32[]{:S(2)}, u32[]{:S(2)}) collective-permute-start(bf16[4,128,256]{2,1,0:T(8,128)(2,1)} %get-tuple-element.59), channel_id=1, source_target_pairs={{0,2},{1,3},{2,0},{3,1},{4,6},{5,7},{6,4},{7,5},{8,10},{9,11},{10,... | collective-permute-start | bytes 786440 | tf_op jit(solution)/shard_map/ppermute | solution.py:30
  19.5 6.7 %collective-permute-start.5 = (bf16[4,128,256]{2,1,0:T(8,128)(2,1)}, bf16[4,128,256]{2,1,0:T(8,128)(2,1)S(1)}, u32[]{:S(2)}, u32[]{:S(2)}) collective-permute-start(bf16[4,128,256]{2,1,0:T(8,128)(2,1)} %get-tuple-element.60), channel_id=1, source_target_pairs={{0,3},{1,0},{2,1},{3,2},{4,7},{5,4},{6,5},{7,6},{8,11},{9,8},{10,9... | collective-permute-start | bytes 786440 | tf_op jit(solution)/shard_map/ppermute | solution.py:30
  36.4 5.7 %copy-start.1 = (bf16[4,128,256]{2,1,0:T(8,128)(2,1)S(1)}, bf16[4,128,256]{2,1,0:T(8,128)(2,1)}, u32[]{:S(2)}) copy-start(bf16[4,128,256]{2,1,0:T(8,128)(2,1)} %get-tuple-element.67.i0) | copy-start | bytes 786436
  40.6 4.2 %collective-permute-start.6 = (f32[4,56,8,128]{3,2,1,0:T(8,128)}, f32[4,56,8,128]{3,2,1,0:T(8,128)S(1)}, u32[]{:S(2)}, u32[]{:S(2)}) collective-permute-start(f32[4,56,8,128]{3,2,1,0:T(8,128)} %get-tuple-element.66), channel_id=1, source_target_pairs={{0,4},{4,0},{1,5},{5,1},{2,6},{6,2},{3,7},{7,3},{8,12},{12,8},{9,1... | collective-permute-start | bytes 2752520 | tf_op jit(solution)/shard_map/ppermute | solution.py:24
  42.6 2.2 %collective-permute-start.10 = (f32[2,48,8,128]{3,2,1,0:T(8,128)S(1)}, f32[2,48,8,128]{3,2,1,0:T(8,128)S(1)}, u32[]{:S(2)}, u32[]{:S(2)}) collective-permute-start(f32[2,48,8,128]{3,2,1,0:T(8,128)S(1)} %get-tuple-element.72), channel_id=1, source_target_pairs={{0,4},{4,0},{1,5},{5,1},{2,6},{6,2},{3,7},{7,3},{8,12},{12,8},{9,1... | collective-permute-start | bytes 1179656 | tf_op jit(solution)/shard_map/ppermute | solution.py:24
  45.0 13.7 %collective-permute-start.7 = (f32[4,14,8,128]{3,2,1,0:T(8,128)S(1)}, f32[4,14,8,128]{3,2,1,0:T(8,128)S(1)}, u32[]{:S(2)}, u32[]{:S(2)}) collective-permute-start(f32[4,14,8,128]{3,2,1,0:T(8,128)S(1)} %get-tuple-element.99), channel_id=1, source_target_pairs={{0,1},{1,2},{2,3},{3,0},{4,5},{5,6},{6,7},{7,4},{8,9},{9,10},{10,1... | collective-permute-start | bytes 688136 | tf_op jit(solution)/shard_map/ppermute | solution.py:30
  46.4 12.9 %collective-permute-start.8 = (f32[4,14,8,128]{3,2,1,0:T(8,128)S(1)}, f32[4,14,8,128]{3,2,1,0:T(8,128)S(1)}, u32[]{:S(2)}, u32[]{:S(2)}) collective-permute-start(f32[4,14,8,128]{3,2,1,0:T(8,128)S(1)} %get-tuple-element.98), channel_id=1, source_target_pairs={{0,2},{1,3},{2,0},{3,1},{4,6},{5,7},{6,4},{7,5},{8,10},{9,11},{10,... | collective-permute-start | bytes 688136 | tf_op jit(solution)/shard_map/ppermute | solution.py:30
  49.0 10.3 %collective-permute-start.9 = (f32[4,14,8,128]{3,2,1,0:T(8,128)S(1)}, f32[4,14,8,128]{3,2,1,0:T(8,128)S(1)}, u32[]{:S(2)}, u32[]{:S(2)}) collective-permute-start(f32[4,14,8,128]{3,2,1,0:T(8,128)S(1)} %get-tuple-element.97), channel_id=1, source_target_pairs={{0,3},{1,0},{2,1},{3,2},{4,7},{5,4},{6,5},{7,6},{8,11},{9,8},{10,9... | collective-permute-start | bytes 688136 | tf_op jit(solution)/shard_map/ppermute | solution.py:30
  50.1 4.8 %collective-permute-start.11 = (f32[2,12,8,128]{3,2,1,0:T(8,128)S(1)}, f32[2,12,8,128]{3,2,1,0:T(8,128)S(1)}, u32[]{:S(2)}, u32[]{:S(2)}) collective-permute-start(f32[2,12,8,128]{3,2,1,0:T(8,128)S(1)} %get-tuple-element.105), channel_id=1, source_target_pairs={{0,16},{16,32},{32,48},{48,0},{1,17},{17,33},{33,49},{49,1},{2,18}... | collective-permute-start | bytes 294920 | tf_op jit(solution)/shard_map/ppermute | solution.py:30
  51.2 5.8 %collective-permute-start.12 = (f32[2,12,8,128]{3,2,1,0:T(8,128)S(1)}, f32[2,12,8,128]{3,2,1,0:T(8,128)S(1)}, u32[]{:S(2)}, u32[]{:S(2)}) collective-permute-start(f32[2,12,8,128]{3,2,1,0:T(8,128)S(1)} %get-tuple-element.104), channel_id=1, source_target_pairs={{0,32},{16,48},{32,0},{48,16},{1,33},{17,49},{33,1},{49,17},{2,34}... | collective-permute-start | bytes 294920 | tf_op jit(solution)/shard_map/ppermute | solution.py:30
  54.9 3.9 %collective-permute-start.13 = (f32[2,12,8,128]{3,2,1,0:T(8,128)S(1)}, f32[2,12,8,128]{3,2,1,0:T(8,128)S(1)}, u32[]{:S(2)}, u32[]{:S(2)}) collective-permute-start(f32[2,12,8,128]{3,2,1,0:T(8,128)S(1)} %get-tuple-element.103), channel_id=1, source_target_pairs={{0,48},{16,0},{32,16},{48,32},{1,49},{17,1},{33,17},{49,33},{2,50}... | collective-permute-start | bytes 294920 | tf_op jit(solution)/shard_map/ppermute | solution.py:30
  59.4 9.1 %copy-start.4 = (bf16[1,1024,640]{2,1,0:T(8,128)(2,1)S(1)}, bf16[1,1024,640]{2,1,0:T(8,128)(2,1)}, u32[]{:S(2)}) copy-start(bf16[1,1024,640]{2,1,0:T(8,128)(2,1)} %param.9) | copy-start | bytes 3932164
  60.3 25.3 %all-to-all-start = ((f32[8,152,128]{2,1,0:T(8,128)}), f32[8,152,128]{2,1,0:T(8,128)S(1)}, u32[]{:S(2)}, u32[]{:S(2)}) async-start(f32[8,152,128]{2,1,0:T(8,128)} %pad_maximum_fusion), calls=%async_computation | async-start | bytes 1245184 | tf_op jit(solution)/shard_map/all_to_all | solution.py:142
  69.5 16.1 %collective-permute-start.14 = (bf16[256,640]{1,0:T(8,128)(2,1)}, bf16[256,640]{1,0:T(8,128)(2,1)S(1)}, u32[]{:S(2)}, u32[]{:S(2)}) collective-permute-start(bf16[256,640]{1,0:T(8,128)(2,1)} %get-tuple-element.95), channel_id=1, source_target_pairs={{0,1},{1,2},{2,3},{3,0},{4,5},{5,6},{6,7},{7,4},{8,9},{9,10},{10,1... | collective-permute-start | bytes 983048 | tf_op jit(solution)/shard_map/ppermute | solution.py:30
  70.5 16.8 %collective-permute-start.15 = (bf16[256,640]{1,0:T(8,128)(2,1)}, bf16[256,640]{1,0:T(8,128)(2,1)S(1)}, u32[]{:S(2)}, u32[]{:S(2)}) collective-permute-start(bf16[256,640]{1,0:T(8,128)(2,1)} %get-tuple-element.94), channel_id=1, source_target_pairs={{0,2},{1,3},{2,0},{3,1},{4,6},{5,7},{6,4},{7,5},{8,10},{9,11},{10,... | collective-permute-start | bytes 983048 | tf_op jit(solution)/shard_map/ppermute | solution.py:30
  73.3 13.9 %collective-permute-start.16 = (bf16[256,640]{1,0:T(8,128)(2,1)}, bf16[256,640]{1,0:T(8,128)(2,1)S(1)}, u32[]{:S(2)}, u32[]{:S(2)}) collective-permute-start(bf16[256,640]{1,0:T(8,128)(2,1)} %get-tuple-element.93), channel_id=1, source_target_pairs={{0,3},{1,0},{2,1},{3,2},{4,7},{5,4},{6,5},{7,6},{8,11},{9,8},{10,9... | collective-permute-start | bytes 983048 | tf_op jit(solution)/shard_map/ppermute | solution.py:30
  87.2 9.7 %collective-permute-start.21 = (f32[96,128]{1,0:T(8,128)S(1)}, f32[96,128]{1,0:T(8,128)S(1)}, u32[]{:S(2)}, u32[]{:S(2)}) collective-permute-start(f32[96,128]{1,0:T(8,128)S(1)} %get-tuple-element.108), channel_id=1, source_target_pairs={{0,16},{16,32},{32,48},{48,0},{1,17},{17,33},{33,49},{49,1},{2,18}... | collective-permute-start | bytes 147464 | tf_op jit(solution)/shard_map/ppermute | solution.py:30
  88.6 8.3 %collective-permute-start.22 = (f32[96,128]{1,0:T(8,128)S(1)}, f32[96,128]{1,0:T(8,128)S(1)}, u32[]{:S(2)}, u32[]{:S(2)}) collective-permute-start(f32[96,128]{1,0:T(8,128)S(1)} %get-tuple-element.108), channel_id=1, source_target_pairs={{0,32},{16,48},{32,0},{48,16},{1,33},{17,49},{33,1},{49,17},{2,34}... | collective-permute-start | bytes 147464 | tf_op jit(solution)/shard_map/ppermute | solution.py:30
  90.7 6.2 %collective-permute-start.23 = (f32[96,128]{1,0:T(8,128)S(1)}, f32[96,128]{1,0:T(8,128)S(1)}, u32[]{:S(2)}, u32[]{:S(2)}) collective-permute-start(f32[96,128]{1,0:T(8,128)S(1)} %get-tuple-element.108), channel_id=1, source_target_pairs={{0,48},{16,0},{32,16},{48,32},{1,49},{17,1},{33,17},{49,33},{2,50}... | collective-permute-start | bytes 147464 | tf_op jit(solution)/shard_map/ppermute | solution.py:30
  92.0 11.8 %collective-permute-start.17 = (f32[56,128]{1,0:T(8,128)S(1)}, f32[56,128]{1,0:T(8,128)S(1)}, u32[]{:S(2)}, u32[]{:S(2)}) collective-permute-start(f32[56,128]{1,0:T(8,128)S(1)} %get-tuple-element.111), channel_id=1, source_target_pairs={{0,1},{1,2},{2,3},{3,0},{4,5},{5,6},{6,7},{7,4},{8,9},{9,10},{10,1... | collective-permute-start | bytes 86024 | tf_op jit(solution)/shard_map/ppermute | solution.py:30
  94.1 9.7 %collective-permute-start.18 = (f32[56,128]{1,0:T(8,128)S(1)}, f32[56,128]{1,0:T(8,128)S(1)}, u32[]{:S(2)}, u32[]{:S(2)}) collective-permute-start(f32[56,128]{1,0:T(8,128)S(1)} %get-tuple-element.111), channel_id=1, source_target_pairs={{0,2},{1,3},{2,0},{3,1},{4,6},{5,7},{6,4},{7,5},{8,10},{9,11},{10,... | collective-permute-start | bytes 86024 | tf_op jit(solution)/shard_map/ppermute | solution.py:30
  96.9 6.9 %collective-permute-start.19 = (f32[56,128]{1,0:T(8,128)S(1)}, f32[56,128]{1,0:T(8,128)S(1)}, u32[]{:S(2)}, u32[]{:S(2)}) collective-permute-start(f32[56,128]{1,0:T(8,128)S(1)} %get-tuple-element.111), channel_id=1, source_target_pairs={{0,3},{1,0},{2,1},{3,2},{4,7},{5,4},{6,5},{7,6},{8,11},{9,8},{10,9... | collective-permute-start | bytes 86024 | tf_op jit(solution)/shard_map/ppermute | solution.py:30
  97.0 11.7 %copy-start.2 = (f32[2,320,320]{2,1,0:T(8,128)S(1)}, f32[2,320,320]{2,1,0:T(8,128)}, u32[]{:S(2)}) copy-start(f32[2,320,320]{2,1,0:T(8,128)} %running.1) | copy-start | bytes 2457604
  101.3 7.4 %collective-permute-start.24 = (f32[256,320]{1,0:T(8,128)S(1)}, f32[256,320]{1,0:T(8,128)S(1)}, u32[]{:S(2)}, u32[]{:S(2)}) collective-permute-start(f32[256,320]{1,0:T(8,128)S(1)} %get-tuple-element.88), channel_id=1, source_target_pairs={{0,4},{4,0},{1,5},{5,1},{2,6},{6,2},{3,7},{7,3},{8,12},{12,8},{9,1... | collective-permute-start | bytes 983048 | tf_op jit(solution)/shard_map/ppermute | solution.py:24
  103.9 4.8 %collective-permute-start.20 = (f32[4,56,128]{2,1,0:T(8,128)S(1)}, f32[4,56,128]{2,1,0:T(8,128)S(1)}, u32[]{:S(2)}, u32[]{:S(2)}) collective-permute-start(f32[4,56,128]{2,1,0:T(8,128)S(1)} %pad_maximum_fusion.4), channel_id=1, source_target_pairs={{0,8},{8,0},{1,9},{9,1},{2,10},{10,2},{3,11},{11,3},{4,12},{12,4},... | collective-permute-start | bytes 344072 | tf_op jit(solution)/shard_map/ppermute | solution.py:364
  116.4 2.0 %collective-permute-start.25 = (bf16[256,320]{1,0:T(8,128)(2,1)S(1)}, bf16[256,320]{1,0:T(8,128)(2,1)S(1)}, u32[]{:S(2)}, u32[]{:S(2)}) collective-permute-start(bf16[256,320]{1,0:T(8,128)(2,1)S(1)} %get-tuple-element.90), channel_id=1, source_target_pairs={{0,4},{4,0},{1,5},{5,1},{2,6},{6,2},{3,7},{7,3},{8,12},{12,8},{9,1... | collective-permute-start | bytes 491528 | tf_op jit(solution)/shard_map/ppermute | solution.py:24
  118.7 17.2 %collective-permute-start.26 = (bf16[256,640]{1,0:T(8,128)(2,1)S(1)}, bf16[256,640]{1,0:T(8,128)(2,1)S(1)}, u32[]{:S(2)}, u32[]{:S(2)}) collective-permute-start(bf16[256,640]{1,0:T(8,128)(2,1)S(1)} %get-tuple-element.92), channel_id=1, source_target_pairs={{0,1},{1,2},{2,3},{3,0},{4,5},{5,6},{6,7},{7,4},{8,9},{9,10},{10,1... | collective-permute-start | bytes 983048 | tf_op jit(solution)/shard_map/ppermute | solution.py:30
  119.9 16.1 %collective-permute-start.27 = (bf16[256,640]{1,0:T(8,128)(2,1)S(1)}, bf16[256,640]{1,0:T(8,128)(2,1)S(1)}, u32[]{:S(2)}, u32[]{:S(2)}) collective-permute-start(bf16[256,640]{1,0:T(8,128)(2,1)S(1)} %get-tuple-element.92), channel_id=1, source_target_pairs={{0,2},{1,3},{2,0},{3,1},{4,6},{5,7},{6,4},{7,5},{8,10},{9,11},{10,... | collective-permute-start | bytes 983048 | tf_op jit(solution)/shard_map/ppermute | solution.py:30
  120.1 16.1 %collective-permute-start.28 = (bf16[256,640]{1,0:T(8,128)(2,1)S(1)}, bf16[256,640]{1,0:T(8,128)(2,1)S(1)}, u32[]{:S(2)}, u32[]{:S(2)}) collective-permute-start(bf16[256,640]{1,0:T(8,128)(2,1)S(1)} %get-tuple-element.92), channel_id=1, source_target_pairs={{0,3},{1,0},{2,1},{3,2},{4,7},{5,4},{6,5},{7,6},{8,11},{9,8},{10,9... | collective-permute-start | bytes 983048 | tf_op jit(solution)/shard_map/ppermute | solution.py:30
  136.3 1.1 copy-start.3

commit v3 on v2

--- a/solution.py
+++ b/solution.py
@@ -12,7 +12,7 @@
 BGP = 384
 ITERS = 8
 G_TILES = 56
-A_TILES = 48
+A_TILES = 36
 
 factor_decay = 0.9
 damping = 0.1
@@ -24,40 +24,73 @@
     return lax.ppermute(value, "c", [(0, 1), (1, 0)])
 
 
+def send(value, axis, s):
+    return lax.ppermute(value, axis, [(i, (i + s) % 4) for i in range(4)])
+
+
+def swap_pair(value):
+    return lax.ppermute(value, "zl", [(0, 1), (1, 0)])
+
+
 def send_round(axis, chunks):
-    size = lax.axis_size(axis)
-    return [chunks[0]] + [
-        lax.ppermute(chunks[s], axis, [(i, (i + s) % size) for i in range(size)])
-        for s in range(1, size)
-    ]
-
-
-def pack_kernel(axis, width, src, *rest):
-    outs, sem = rest[:4], rest[4]
-    here = lax.axis_index(axis)
-    copies = []
-    for s in (1, 3, 2, 0):
-        peer = lax.rem(here + s, 4)
-        for q in range(4):
-            start = pl.multiple_of((q * 4 + peer) * width, 128)
-            copies.append(pltpu.make_async_copy(
-                src.at[:, pl.ds(start, width)], outs[s].at[q], sem.at[s * 4 + q]
-            ))
+    return [chunks[0]] + [send(chunks[s], axis, s) for s in range(1, 4)]
+
+
+def run_copies(pairs, sem):
+    copies = [pltpu.make_async_copy(src, dst, sem.at[i]) for i, (src, dst) in enumerate(pairs)]
     for copy in copies:
         copy.start()
     for copy in copies:
         copy.wait()
 
 
-def pack(samples, axis, width):
-    piece = jax.ShapeDtypeStruct((4, samples.shape[0], width), samples.dtype)
-    return pl.pallas_call(
-        functools.partial(pack_kernel, axis, width),
-        out_shape=[piece] * 4,
-        in_specs=[pl.BlockSpec(memory_space=pl.ANY)],
-        out_specs=[VMEM] * 4,
-        scratch_shapes=[pltpu.SemaphoreType.DMA((16,))],
-    )(samples)
+def x_chunk(src, s, out):
+    peer = lax.rem(lax.axis_index("x") + s, 4)
+    for q in range(4):
+        start = pl.multiple_of((q * 4 + peer) * 2 * BG, 128)
+        yield src.at[:, pl.ds(start, 2 * BG)], out.at[q]
+
+
+def y_chunk(samples, grads, s, out):
+    peer = lax.rem(lax.axis_index("y") + s, 4)
+    for q in range(4):
+        start = pl.multiple_of((q * 4 + peer) * BA, 128)
+        yield samples.at[:, pl.ds(start, BA)], out.at[:, pl.ds(q * BA, BA)]
+    for h in range(2):
+        start = pl.multiple_of(peer * BA + h * 128, 128)
+        yield grads.at[0, pl.ds(start, 128), :], out.at[:, pl.ds(4 * BA + h * 2 * BG, 2 * BG)]
+
+
+def near_x_kernel(src, out1, out3, sem):
+    run_copies([pair for s, out in ((1, out1), (3, out3)) for pair in x_chunk(src, s, out)], sem)
+
+
+def near_y_kernel(samples, grads, out1, out3, sem):
+    run_copies([pair for s, out in ((1, out1), (3, out3)) for pair in y_chunk(samples, grads, s, out)], sem)
+
+
+def rest_kernel(src, samples, grads, running, far_x, far_y, own_x, own_y, previous, sem):
+    zl, c, y = (lax.axis_index(name) for name in ("zl", "c", "y"))
+    run_copies([
+        *x_chunk(src, 2, far_x), *y_chunk(samples, grads, 2, far_y),
+        *x_chunk(src, 0, own_x), *y_chunk(samples, grads, 0, own_y),
+        (running.at[(zl * 2 + c) * 4 + y], previous),
+    ], sem)
+
+
+X_CHUNK = jax.ShapeDtypeStruct((4, 128, 2 * BG), jnp.bfloat16)
+Y_CHUNK = jax.ShapeDtypeStruct((128, 4 * BA + 4 * BG), jnp.bfloat16)
+PREVIOUS = jax.ShapeDtypeStruct((BA, BA), jnp.float32)
+
+
+def pack(kernel, count, out_shape, *args):
+    return pl.pallas_call(
+        kernel,
+        out_shape=out_shape,
+        in_specs=[pl.BlockSpec(memory_space=pl.ANY)] * len(args),
+        out_specs=[VMEM] * len(out_shape),
+        scratch_shapes=[pltpu.SemaphoreType.DMA((count,))],
+    )(*args)
 
 
 def gram(v):
@@ -105,26 +138,28 @@
         in_specs=[spec] * 4,
         out_specs=[out] * 2,
         scratch_shapes=[pltpu.VMEM((512, 2 * BG), jnp.bfloat16), pltpu.VMEM((2, G_TILES, 8, 128), jnp.float32)],
-        compiler_params=pltpu.CompilerParams(vmem_limit_bytes=32 << 20),
+        compiler_params=pltpu.CompilerParams(vmem_limit_bytes=16 << 20),
     )(*chunks)
 
 
-def a_cov_kernel(i0, i1, i2, i3, own, other, rows):
+def a_cov_kernel(i0, i1, i2, i3, own, other, rows, tiles):
     c = lax.axis_index("c")
     r, k = grid_of(128)
     for zl in range(2):
-        for which, out in ((c, own), (1 - c, other)):
-            q = zl * 2 + which
+        for core in range(2):
+            q = zl * 2 + core
             for s, ref in enumerate((i0, i1, i2, i3)):
-                rows[s * 128:(s + 1) * 128, :] = ref[q]
+                rows[s * 128:(s + 1) * 128, :] = ref[:, q * BA:(q + 1) * BA]
             cov = gram(rows[...])
             corner = cov[128:, 128:]
             fold = jnp.where(r >= k, cov[:128, :128], corner)
             diag = jnp.sum(jnp.where(r == k, corner, 0.0), axis=0, keepdims=True)
-            out[zl, 0:16] = cov[128:, :128].reshape(16, 8, 128)
-            out[zl, 16:32] = fold.reshape(16, 8, 128)
-            out[zl, 32] = jnp.broadcast_to(diag, (8, 128))
-            out[zl, 33:] = jnp.zeros((A_TILES - 33, 8, 128), jnp.float32)
+            tiles[core, 0:16] = cov[128:, :128].reshape(16, 8, 128)
+            tiles[core, 16:32] = fold.reshape(16, 8, 128)
+            tiles[core, 32] = jnp.broadcast_to(diag, (8, 128))
+            tiles[core, 33:] = jnp.zeros((A_TILES - 33, 8, 128), jnp.float32)
+        own[zl] = tiles[c]
+        other[zl] = tiles[1 - c]
 
 
 def a_cov(chunks):
@@ -133,13 +168,61 @@
         out_shape=[jax.ShapeDtypeStruct((2, A_TILES, 8, 128), jnp.float32)] * 2,
         in_specs=[VMEM] * 4,
         out_specs=[VMEM] * 2,
-        scratch_shapes=[pltpu.VMEM((512, BA), jnp.bfloat16)],
-        compiler_params=pltpu.CompilerParams(vmem_limit_bytes=32 << 20),
+        scratch_shapes=[pltpu.VMEM((512, BA), jnp.bfloat16), pltpu.VMEM((2, A_TILES, 8, 128), jnp.float32)],
+        compiler_params=pltpu.CompilerParams(vmem_limit_bytes=16 << 20),
     )(*chunks)
 
 
-def reduce_pieces(value, axes):
-    return jnp.sum(lax.all_to_all(value, axes, 0, 0, tiled=True), axis=0)
+def tile_shape(*dims):
+    return jax.ShapeDtypeStruct((*dims, 8, 128), jnp.float32)
+
+
+def local(kernel, out_shape, *args):
+    return pl.pallas_call(
+        kernel,
+        out_shape=out_shape,
+        in_specs=[VMEM] * len(args),
+        out_specs=jax.tree.map(lambda _: VMEM, out_shape),
+        compiler_params=pltpu.CompilerParams(vmem_limit_bytes=16 << 20),
+    )(*args)
+
+
+def cores_kernel(g_own, g_got, a_own, a_got, *outs):
+    x, y = lax.axis_index("x"), lax.axis_index("y")
+    for s in range(4):
+        place = pl.ds(lax.rem(y + s, 4) * 14, 14)
+        outs[s][...] = g_own[:, place] + g_got[:, place]
+        place = pl.ds(lax.rem(x + s, 4) * 9, 9)
+        outs[4 + s][...] = a_own[:, place] + a_got[:, place]
+
+
+def lines_kernel(g0, g1, g2, g3, a0, a1, a2, a3, keep, turn):
+    zl = lax.axis_index("zl")
+    for out, side in ((keep, zl), (turn, 1 - zl)):
+        for q in range(4):
+            place = pl.ds(side * 7, 7)
+            out[q * 7:q * 7 + 7] = (g0[q, place] + g1[q, place]) + (g2[q, place] + g3[q, place])
+        out[28:] = (a0[side] + a1[side]) + (a2[side] + a3[side])
+
+
+def pairs_kernel(keep, got, *outs):
+    zh = lax.axis_index("zh")
+    a_sum = keep[28:] + got[28:]
+    for s in range(4):
+        place = pl.ds(lax.rem(zh + s, 4) * 7, 7)
+        outs[s][0:7] = keep[place] + got[place]
+        outs[s][7:] = a_sum
+
+
+def pieces_kernel(p0, p1, p2, p3, g_piece, a_piece):
+    g_piece[...] = (p0[0:7] + p1[0:7]) + (p2[0:7] + p3[0:7])
+    a_piece[...] = (p0[7:] + p1[7:]) + (p2[7:] + p3[7:])
+
+
+def join_kernel(own, got, out):
+    zl = lax.axis_index("zl")
+    out[pl.ds(zl * 7, 7)] = own[...]
+    out[pl.ds((1 - zl) * 7, 7)] = got[...]
 
 
 def split(value):
@@ -180,10 +263,10 @@
     return jnp.dot(lhs[0:n], rhs[...], preferred_element_type=jnp.float32)
 
 
-def a_side_kernel(got, running, g0, g1, g2, g3, keep, send, tiles, lhs, rhs, *, token_total):
-    c, x = lax.axis_index("c"), lax.axis_index("x")
-    for s in range(4):
-        tiles[pl.ds(lax.rem(x + 4 - s, 4) * 12, 12)] = got[s]
+def a_side_kernel(p0, p1, p2, p3, running, g0, g1, g2, g3, left, tiles, lhs, rhs, *, token_total):
+    x = lax.axis_index("x")
+    for s, got in enumerate((p0, p1, p2, p3)):
+        tiles[pl.ds(lax.rem(x + 4 - s, 4) * 9, 9)] = got[...]
     r, k = grid_of(128)
     low = tiles[0:16].reshape(128, 128)
     fold = tiles[16:32].reshape(128, 128)
@@ -196,34 +279,40 @@
     ], axis=0)
     r, k = grid_of(BA)
     identity = jnp.where(r == k, 1.0, 0.0)
-    mixed = factor_decay * running[0] + (1.0 - factor_decay) * cov / token_total
+    mixed = factor_decay * running[...] + (1.0 - factor_decay) * cov / token_total
     inverse = newton_even(mixed + damping * identity, identity, lhs, rhs)
-    summed = (g0[...].astype(jnp.float32) + g1[...].astype(jnp.float32)) + (
-        g2[...].astype(jnp.float32) + g3[...].astype(jnp.float32)
-    )
-    left = dot3(split(inverse), split(summed))
-    keep[...] = jnp.where(c == 0, left[:, 0:BG], left[:, BG:])
-    send[...] = jnp.where(c == 0, left[:, BG:], left[:, 0:BG])
-
-
-def a_side(tiles, running, grads, token_total):
+    summed = []
+    for h in range(2):
+        begin = 4 * BA + h * 2 * BG
+        g = [ref[:, begin:begin + 2 * BG].astype(jnp.float32) for ref in (g0, g1, g2, g3)]
+        summed.append((g[0] + g[1]) + (g[2] + g[3]))
+    summed = jnp.concatenate(summed, axis=0)
+    done = dot3(split(inverse), split(summed))
+    for n in range(2):
+        left[n] = done[:, n * BG:(n + 1) * BG]
+
+
+def a_side(pieces, running, grads, token_total):
     return pl.pallas_call(
         functools.partial(a_side_kernel, token_total=token_total),
-        out_shape=[jax.ShapeDtypeStruct((BA, BG), jnp.float32)] * 2,
-        in_specs=[VMEM] * 6,
-        out_specs=[VMEM] * 2,
+        out_shape=jax.ShapeDtypeStruct((2, BA, BG), jnp.float32),
+        in_specs=[VMEM] * 9,
+        out_specs=VMEM,
         scratch_shapes=[
             pltpu.VMEM((A_TILES, 8, 128), jnp.float32),
             pltpu.VMEM((2 * BA, 3 * BA), jnp.bfloat16), pltpu.VMEM((3 * BA, BA), jnp.bfloat16)
         ],
-        compiler_params=pltpu.CompilerParams(vmem_limit_bytes=32 << 20),
+        compiler_params=pltpu.CompilerParams(vmem_limit_bytes=16 << 20),
         cost_estimate=pl.CostEstimate(flops=2_500_000_000, bytes_accessed=2_000_000, transcendentals=0),
-    )(tiles, running, *grads)
+    )(*pieces, running, *grads)
 
 
 def turned_tail(main):
     tail = main[256:BG]
     return jnp.concatenate([tail, jnp.zeros_like(tail)], axis=0).T
+
+
+HALF = jax.ShapeDtypeStruct((128, 2 * BG), jnp.bfloat16)
 
 
 def unfold_block(tiles):
@@ -260,13 +349,15 @@
         rhs[2 * BGP:2 * BGP + BG] = high
 
 
-def g_side_kernel(
-    got, running, left_own, left_sibling, own, sibling, tiles, lhs, rhs_main, rhs_tail, *, token_total
-):
-    c, y, zl = (lax.axis_index(name) for name in ("c", "y", "zl"))
-    for z, near in enumerate((zl, 1 - zl)):
-        for s in range(4):
-            tiles[pl.ds(lax.rem(y + 4 - s, 4) * 14 + near * 7, 7)] = got[z, s]
+def half_rows(left, inverse):
+    done = dot3(split(left), (inverse[0], inverse[1]))[:, 0:BG].astype(jnp.bfloat16)
+    return jnp.concatenate([done[0:128], done[128:BA]], axis=1)
+
+
+def g_side_kernel(p0, p1, p2, p3, running, left, out, rows, tiles, lhs, rhs_main, rhs_tail, *, token_total):
+    c, y = lax.axis_index("c"), lax.axis_index("y")
+    for s, got in enumerate((p0, p1, p2, p3)):
+        tiles[pl.ds(lax.rem(y + 4 - s, 4) * 14, 14)] = got[...]
     new_sum = unfold_block(tiles)
     previous = running[c, :, 0:256], jnp.concatenate(
         [running[c, :, 256:BG], jnp.zeros((BG, 64), jnp.float32)], axis=1
@@ -302,16 +393,15 @@
 
     lax.fori_loop(0, ITERS - 1, step, 0)
     (main, tail), = product(BG)
-    inverse = split(jnp.concatenate([main, tail], axis=1))
-    for left, out in ((left_sibling, sibling), (left_own, own)):
-        out[...] = dot3(split(left[...]), inverse)[:, 0:BG].astype(jnp.bfloat16)
-
-
-def g_side(got, running, left_own, left_sibling, token_total):
+    out[0], out[1] = split(jnp.concatenate([main, tail], axis=1))
+    rows[...] = half_rows(left[c], out)
+
+
+def g_side(pieces, running, left, token_total):
     return pl.pallas_call(
         functools.partial(g_side_kernel, token_total=token_total),
-        out_shape=[jax.ShapeDtypeStruct((BA, BG), jnp.bfloat16)] * 2,
-        in_specs=[VMEM] * 4,
+        out_shape=[jax.ShapeDtypeStruct((2, BG, BGP), jnp.bfloat16), HALF],
+        in_specs=[VMEM] * 6,
         out_specs=[VMEM] * 2,
         scratch_shapes=[
             pltpu.VMEM((G_TILES, 8, 128), jnp.float32),
@@ -319,60 +409,67 @@
             pltpu.VMEM((3 * BGP, 256), jnp.bfloat16),
             pltpu.VMEM((3 * BGP, 128), jnp.bfloat16),
         ],
-        compiler_params=pltpu.CompilerParams(vmem_limit_bytes=40 << 20),
+        compiler_params=pltpu.CompilerParams(vmem_limit_bytes=16 << 20),
         cost_estimate=pl.CostEstimate(flops=6_000_000_000, bytes_accessed=3_000_000, transcendentals=0),
-    )(got, running, left_own, left_sibling)
+    )(*pieces, running, left)
+
+
+def apply_kernel(left, theirs, rows):
+    rows[...] = half_rows(left[1 - lax.axis_index("c")], theirs)
+
+
+def assemble_kernel(*refs):
+    first, second, out = refs[:4], refs[4:8], refs[8]
+    c, y = lax.axis_index("c"), lax.axis_index("y")
+    for s in range(4):
+        mine, theirs = first[s][...], second[s][...]
+        halves = jnp.where(c == 0, mine, theirs), jnp.where(c == 0, theirs, mine)
+        start = pl.multiple_of(lax.rem(y + 4 - s, 4) * BA, BA)
+        for h in range(2):
+            out[pl.ds(start + h * 128, 128), :] = jnp.concatenate(
+                [half[:, h * BG:(h + 1) * BG] for half in halves], axis=1
+            )
 
 
 def per_device(activations, out_grads, a_running, g_running, grad_partial):
     token_total = float(activations.shape[0] * 256)
-    x, zl, c, y = (lax.axis_index(name) for name in ("x", "zl", "c", "y"))
-
-    g_chunks = pack(out_grads, "x", 2 * BG)
-    g_chunks, activations = lax.optimization_barrier((g_chunks, activations))
-    g_in = send_round("x", g_chunks)
-    a_in = send_round("y", pack(activations, "y", BA))
-    g_in, a_in = lax.optimization_barrier((g_in, a_in))
+    y = lax.axis_index("y")
+
+    near_x = pack(near_x_kernel, 8, [X_CHUNK] * 2, out_grads)
+    near_x, activations = lax.optimization_barrier((near_x, activations))
+    near_y = pack(near_y_kernel, 12, [Y_CHUNK] * 2, activations, grad_partial)
+    near_y, out_grads = lax.optimization_barrier((near_y, out_grads))
+    far_x, far_y, own_x, own_y, a_previous = pack(
+        rest_kernel, 21, [X_CHUNK, Y_CHUNK, X_CHUNK, Y_CHUNK, PREVIOUS],
+        out_grads, activations, grad_partial, a_running,
+    )
+    g_in = [send(near_x[0], "x", 1), send(near_x[1], "x", 3)]
+    y_in = [send(near_y[0], "y", 1), send(near_y[1], "y", 3)]
+    g_in, y_in, far_x, far_y = lax.optimization_barrier((g_in, y_in, far_x, far_y))
+    g_in = [own_x, *g_in, send(far_x, "x", 2)]
+    y_in = [own_y, *y_in, send(far_y, "y", 2)]
+    g_in, y_in = lax.optimization_barrier((g_in, y_in))
 
     g_own, g_other = g_cov(g_in)
-    a_own, a_other = a_cov(a_in)
-    g_part = (g_own + swap_cores(g_other)).reshape(4, 4, 14, 8, 128)
-    a_part = (a_own + swap_cores(a_other)).reshape(2, 4, 12, 8, 128)
-
-    g_lines = send_round("y", [
-        lax.dynamic_index_in_dim(g_part, lax.rem(y + s, 4), 1, keepdims=False) for s in range(4)
-    ])
-    a_lines = send_round("x", [
-        lax.dynamic_index_in_dim(a_part, lax.rem(x + s, 4), 1, keepdims=False) for s in range(4)
-    ])
-    g_lines, a_lines, grad_partial = lax.optimization_barrier((g_lines, a_lines, grad_partial))
-    grads = send_round("y", [
-        lax.dynamic_slice_in_dim(grad_partial[0], lax.rem(y + s, 4) * BA, BA, 0) for s in range(4)
-    ])
-    g_line = (g_lines[0] + g_lines[1]) + (g_lines[2] + g_lines[3])
-    a_line = (a_lines[0] + a_lines[1]) + (a_lines[2] + a_lines[3])
-
-    both = jnp.concatenate([
-        g_line.reshape(8, 56, 128),
-        jnp.broadcast_to(a_line.reshape(1, 2, 96, 128), (4, 2, 96, 128)).reshape(8, 96, 128),
-    ], axis=1)
-    pieces = reduce_pieces(both, ("zh", "zl"))
-    pieces, grads = lax.optimization_barrier((pieces, grads))
-
-    g_rows = jnp.stack(send_round("y", [pieces[:56]] * 4))
-    a_tiles = jnp.stack(send_round("x", [pieces[56:]] * 4)).reshape(4, 12, 8, 128)
-    g_tiles = jnp.stack([g_rows, lax.ppermute(g_rows, "zl", [(0, 1), (1, 0)])]).reshape(2, 4, 7, 8, 128)
-
-    a_previous = lax.dynamic_slice_in_dim(a_running, (zl * 2 + c) * 4 + y, 1, 0)
-    left, left_send = a_side(a_tiles, a_previous, grads, token_total)
-    own, sibling = g_side(g_tiles, g_running, left, swap_cores(left_send), token_total)
-    got = swap_cores(sibling)
-    rows = jnp.concatenate([jnp.where(c == 0, own, got), jnp.where(c == 0, got, own)], axis=1)
-
-    out = jnp.zeros((4, BA, 2 * BG), jnp.bfloat16)
-    for shift, got in enumerate(send_round("y", [rows] * 4)):
-        out = lax.dynamic_update_slice_in_dim(out, got[None], lax.rem(y + 4 - shift, 4), 0)
-    return out.reshape(4 * BA, 2 * BG)
+    a_own, a_other = a_cov(y_in)
+    cut = local(
+        cores_kernel, [tile_shape(4, 14)] * 4 + [tile_shape(2, 9)] * 4,
+        g_own, swap_cores(g_other), a_own, swap_cores(a_other),
+    )
+    lines = lax.optimization_barrier(send_round("y", cut[:4]) + send_round("x", cut[4:]))
+    keep, turn = local(lines_kernel, [tile_shape(37)] * 2, *lines)
+    cut = local(pairs_kernel, [tile_shape(16)] * 4, keep, swap_pair(turn))
+    g_piece, a_piece = local(pieces_kernel, [tile_shape(7), tile_shape(9)], *send_round("zh", cut))
+
+    a_pieces = send_round("x", [a_piece] * 4)
+    g_pair = local(join_kernel, tile_shape(14), g_piece, swap_pair(g_piece))
+    g_pieces = send_round("y", [g_pair] * 4)
+    left = a_side(a_pieces, a_previous, y_in, token_total)
+    g_pieces, left = lax.optimization_barrier((g_pieces, left))
+    inverse, first = g_side(g_pieces, g_running, left, token_total)
+    second = local(apply_kernel, HALF, left, swap_cores(inverse))
+    parts = send_round("y", [first] * 4) + send_round("y", [second] * 4)
+    return local(assemble_kernel, jax.ShapeDtypeStruct((4 * BA, 2 * BG), jnp.bfloat16), *parts)
 
 
 def solution(mesh):

time: 138 us -> 132 us (0.957)
  waiting for transfers between devices: 57.5 us -> 49.3 us
  Pallas kernels: 22.4 us -> 26.6 us
  local copies, waits for them, and re-layouts: 3.41 us -> 1.1 us
  starting transfers between devices: 52.3 us -> 54.4 us
    all_to_all x1 -> x0, waiting for transfers between devices: 11 us -> none  [reduce_pieces(): return jnp.sum(lax.all_to_all(value, axes, 0, 0, tiled=True), axis=0)]
    all_to_all x1 -> x0, starting transfers between devices: 8.2 us -> none  [reduce_pieces(): return jnp.sum(lax.all_to_all(value, axes, 0, 0, tiled=True), axis=0)]
    ppermute x25 -> x29, starting transfers between devices: 39 us -> 44.6 us  [the longest x27 42.2 us: send(): return lax.ppermute(value, axis, [(i, (i + s) % 4) for i in range(4)])]
    pallas_call x2 -> x10, Pallas kernels: 5.8 us -> 10.8 us  [the longest x3 8.61 us: pack(): pl.pallas_call(kernel, out_shape=out_shape, in_specs=[pl.BlockSpec(memory...]
    ppermute x4 -> x3, starting transfers between devices: 5.08 us -> 9.73 us  [swap_cores(): return lax.ppermute(value, 'c', [(0, 1), (1, 0)])]
    ppermute x25 -> x29, waiting for transfers between devices: 43.4 us -> 47.5 us  [the longest x27 43 us: send(): return lax.ppermute(value, axis, [(i, (i + s) % 4) for i in range(4)])]
    dynamic_slice x2 -> x0, local copies, waits for them, and re-layouts: 1.96 us -> none  [the longest x1 0.99 us: per_device(): lax.dynamic_slice_in_dim(grad_partial[0], lax.rem(y + s, 4) * BA, BA, 0)]
    ppermute x4 -> x3, waiting for transfers between devices: 3.09 us -> 1.8 us  [swap_cores(): return lax.ppermute(value, 'c', [(0, 1), (1, 0)])]
  transfers between devices with their start and end apart: 30 -> 32, of which waited for: 14 -> 16; matrix products, arithmetic and copies ran while one was open for 2% -> 0% of each run, Pallas kernels for 5% -> 9%
where the time goes in v3:
time: 132 us
  starting transfers between devices  54.4 us (41%)
  waiting for transfers between devices  49.3 us (37%)
  Pallas kernels  26.6 us (20%)
    ppermute x27, waiting for transfers between devices, send(): return lax.ppermute(value, axis, [(i, (i + s) % 4) for i in range(4)])  43 us
    ppermute x27, starting transfers between devices, send(): return lax.ppermute(value, axis, [(i, (i + s) % 4) for i in range(4)])  42.2 us
    ppermute x3, starting transfers between devices, swap_cores(): return lax.ppermute(value, 'c', [(0, 1), (1, 0)])  9.73 us
    pallas_call x3, Pallas kernels, pack(): pl.pallas_call(kernel, out_shape=out_shape, in_specs=[pl.BlockSpec(memory...  8.61 us
    pallas_call x1, Pallas kernels, g_side(): pl.pallas_call(functools.partial(g_side_kernel, token_total=token_total),...  7.62 us
    ppermute x2, waiting for transfers between devices, swap_pair(): return lax.ppermute(value, 'zl', [(0, 1), (1, 0)])  4.56 us
    pallas_call x1, Pallas kernels, a_side(): pl.pallas_call(functools.partial(a_side_kernel, token_total=token_total),...  4.14 us
    pallas_call x1, Pallas kernels, g_cov(): pl.pallas_call(g_cov_kernel, grid=(4,), out_shape=[jax.ShapeDtypeStruct((...  3.44 us
  transfers between devices with their start and end apart: 32, of which 16 were waited for; matrix products, arithmetic and copies ran while one was open for 0% of the time, Pallas kernels for 9%

profile of v3, /device:TPU:1, one launch (start us, length us, event | category | flops | bytes accessed | tf_op | source)
XLA Modules:
  0.0 131.5 jit_solution(12024607522587612785)
XLA Ops:
  0.0 2.6 %shard_map.55 = (bf16[4,128,640]{2,1,0:T(8,128)(2,1)}, bf16[4,128,640]{2,1,0:T(8,128)(2,1)}) custom-call(bf16[128,10240]{1,0:T(8,128)(2,1)} %src.2), custom_call_target="tpu_custom_call" | custom-call | tf_op jit(solution)/shard_map/pallas_call | solution.py:87
  2.6 2.1 %collective-permute-start = (bf16[4,128,640]{2,1,0:T(8,128)(2,1)}, bf16[4,128,640]{2,1,0:T(8,128)(2,1)S(1)}, u32[]{:S(2)}, u32[]{:S(2)}) collective-permute-start(bf16[4,128,640]{2,1,0:T(8,128)(2,1)} %get-tuple-element.76), channel_id=1, source_target_pairs={{0,16},{16,32},{32,48},{48,0},{1,17},{17,33},{33,49},{49,1},{2,18}... | collective-permute-start | bytes 1966088 | tf_op jit(solution)/shard_map/ppermute | solution.py:28
  4.7 1.4 %collective-permute-start.1 = (bf16[4,128,640]{2,1,0:T(8,128)(2,1)}, bf16[4,128,640]{2,1,0:T(8,128)(2,1)S(1)}, u32[]{:S(2)}, u32[]{:S(2)}) collective-permute-start(bf16[4,128,640]{2,1,0:T(8,128)(2,1)} %get-tuple-element.77), channel_id=1, source_target_pairs={{0,48},{16,0},{32,16},{48,32},{1,49},{17,1},{33,17},{49,33},{2,50}... | collective-permute-start | bytes 1966088 | tf_op jit(solution)/shard_map/ppermute | solution.py:28
  6.1 2.5 %shard_map.56 = (bf16[128,2304]{1,0:T(8,128)(2,1)}, bf16[128,2304]{1,0:T(8,128)(2,1)}) custom-call(bf16[128,4096]{1,0:T(8,128)(2,1)} %samples.1, bf16[1,1024,640]{2,1,0:T(8,128)(2,1)} %grads.3), custom_call_target="tpu_custom_call" | custom-call | tf_op jit(solution)/shard_map/pallas_call | solution.py:87
  8.5 1.5 %collective-permute-start.2 = (bf16[128,2304]{1,0:T(8,128)(2,1)}, bf16[128,2304]{1,0:T(8,128)(2,1)S(1)}, u32[]{:S(2)}, u32[]{:S(2)}) collective-permute-start(bf16[128,2304]{1,0:T(8,128)(2,1)} %get-tuple-element.78), channel_id=1, source_target_pairs={{0,1},{1,2},{2,3},{3,0},{4,5},{5,6},{6,7},{7,4},{8,9},{9,10},{10,1... | collective-permute-start | bytes 1769480 | tf_op jit(solution)/shard_map/ppermute | solution.py:28
  10.0 1.5 %collective-permute-start.3 = (bf16[128,2304]{1,0:T(8,128)(2,1)}, bf16[128,2304]{1,0:T(8,128)(2,1)S(1)}, u32[]{:S(2)}, u32[]{:S(2)}) collective-permute-start(bf16[128,2304]{1,0:T(8,128)(2,1)} %get-tuple-element.79), channel_id=1, source_target_pairs={{0,3},{1,0},{2,1},{3,2},{4,7},{5,4},{6,5},{7,6},{8,11},{9,8},{10,9... | collective-permute-start | bytes 1769480 | tf_op jit(solution)/shard_map/ppermute | solution.py:28
  11.6 3.6 %shard_map.57 = (bf16[4,128,640]{2,1,0:T(8,128)(2,1)}, bf16[128,2304]{1,0:T(8,128)(2,1)}, bf16[4,128,640]{2,1,0:T(8,128)(2,1)}, bf16[128,2304]{1,0:T(8,128)(2,1)}, f32[256,256]{1,0:T(8,128)}) custom-call(bf16[128,10240]{1,0:T(8,128)(2,1)} %src.2, bf16[128,4096]{1,0:T(8,128)(2,1)} %samples.1, bf16[1,1024,640]{2,1,0:T(8,128)(2,1)} %grads.3, ...), custom_call_target="tpu_custom_call" | custom-call | tf_op jit(solution)/shard_map/pallas_call | solution.py:87
  15.1 7.0 %collective-permute-done.2.i1.g1 = bf16[128,2304]{1,0:T(8,128)(2,1)S(1)} collective-permute-done((bf16[128,2304]{1,0:T(8,128)(2,1)}, bf16[128,2304]{1,0:T(8,128)(2,1)S(1)}, u32[]{:S(2)}, u32[]{:S(2)}) %collective-permute-start.2) | collective-permute-done | bytes 589856 | tf_op jit(solution)/shard_map/ppermute | solution.py:28
  22.1 1.2 collective-permute-done.3.i2.g2
  23.3 2.2 %collective-permute-start.4 = (bf16[4,128,640]{2,1,0:T(8,128)(2,1)}, bf16[4,128,640]{2,1,0:T(8,128)(2,1)S(1)}, u32[]{:S(2)}, u32[]{:S(2)}) collective-permute-start(bf16[4,128,640]{2,1,0:T(8,128)(2,1)} %get-tuple-element.84), channel_id=1, source_target_pairs={{0,32},{16,48},{32,0},{48,16},{1,33},{17,49},{33,1},{49,17},{2,34}... | collective-permute-start | bytes 1966088 | tf_op jit(solution)/shard_map/ppermute | solution.py:28
  25.5 2.2 %collective-permute-start.5 = (bf16[128,2304]{1,0:T(8,128)(2,1)}, bf16[128,2304]{1,0:T(8,128)(2,1)S(1)}, u32[]{:S(2)}, u32[]{:S(2)}) collective-permute-start(bf16[128,2304]{1,0:T(8,128)(2,1)} %get-tuple-element.88), channel_id=1, source_target_pairs={{0,2},{1,3},{2,0},{3,1},{4,6},{5,7},{6,4},{7,5},{8,10},{9,11},{10,... | collective-permute-start | bytes 1769480 | tf_op jit(solution)/shard_map/ppermute | solution.py:28
  27.7 11.9 %collective-permute-done.5.i3.g3 = bf16[128,2304]{1,0:T(8,128)(2,1)S(1)} collective-permute-done((bf16[128,2304]{1,0:T(8,128)(2,1)}, bf16[128,2304]{1,0:T(8,128)(2,1)S(1)}, u32[]{:S(2)}, u32[]{:S(2)}) %collective-permute-start.5) | collective-permute-done | bytes 589856 | tf_op jit(solution)/shard_map/ppermute | solution.py:28
  39.7 1.1 copy-done
  40.7 3.4 %shard_map.58 = (f32[4,56,8,128]{3,2,1,0:T(8,128)S(1)}, f32[4,56,8,128]{3,2,1,0:T(8,128)S(1)}) custom-call(bf16[4,128,640]{2,1,0:T(8,128)(2,1)S(1)} %copy-done, bf16[4,128,640]{2,1,0:T(8,128)(2,1)S(1)} %collective-permute-done.i1, bf16[4,128,640]{2,1,0:T(8,128)(2,1)S(1)} %collective-permute-done.1.i2, bf16[4,128,640]{2,1,0:T(8,128)(2,1)S(1)} %collective-permute-done.4.i3), custom_call_target="tpu_custom_call" | custom-call | tf_op jit(solution)/shard_map/pallas_call | solution.py:134
  44.2 3.4 %collective-permute-start.6 = (f32[4,56,8,128]{3,2,1,0:T(8,128)S(1)}, f32[4,56,8,128]{3,2,1,0:T(8,128)S(1)}, u32[]{:S(2)}, u32[]{:S(2)}) collective-permute-start(f32[4,56,8,128]{3,2,1,0:T(8,128)S(1)} %get-tuple-element.94), channel_id=1, source_target_pairs={{0,4},{4,0},{1,5},{5,1},{2,6},{6,2},{3,7},{7,3},{8,12},{12,8},{9,1... | collective-permute-start | bytes 2752520 | tf_op jit(solution)/shard_map/ppermute | solution.py:24
  47.6 0.6 shard_map.59
  48.3 1.8 %collective-permute-done.7.a_got = f32[2,36,8,128]{3,2,1,0:T(8,128)S(1)} collective-permute-done((f32[2,36,8,128]{3,2,1,0:T(8,128)S(1)}, f32[2,36,8,128]{3,2,1,0:T(8,128)S(1)}, u32[]{:S(2)}, u32[]{:S(2)}) %collective-permute-start.7) | collective-permute-done | bytes 294944 | tf_op jit(solution)/shard_map/ppermute | solution.py:24
  50.2 1.0 collective-permute-start.8
  51.2 2.8 %collective-permute-start.9 = (f32[4,14,8,128]{3,2,1,0:T(8,128)S(1)}, f32[4,14,8,128]{3,2,1,0:T(8,128)S(1)}, u32[]{:S(2)}, u32[]{:S(2)}) collective-permute-start(f32[4,14,8,128]{3,2,1,0:T(8,128)S(1)} %get-tuple-element.103), channel_id=1, source_target_pairs={{0,2},{1,3},{2,0},{3,1},{4,6},{5,7},{6,4},{7,5},{8,10},{9,11},{10,... | collective-permute-start | bytes 688136 | tf_op jit(solution)/shard_map/ppermute | solution.py:28
  54.0 0.6 collective-permute-start.10
  54.9 2.0 %collective-permute-start.12 = (f32[2,9,8,128]{3,2,1,0:T(8,128)S(1)}, f32[2,9,8,128]{3,2,1,0:T(8,128)S(1)}, u32[]{:S(2)}, u32[]{:S(2)}) collective-permute-start(f32[2,9,8,128]{3,2,1,0:T(8,128)S(1)} %get-tuple-element.107), channel_id=1, source_target_pairs={{0,32},{16,48},{32,0},{48,16},{1,33},{17,49},{33,1},{49,17},{2,34}... | collective-permute-start | bytes 221192 | tf_op jit(solution)/shard_map/ppermute | solution.py:28
  56.9 2.9 %collective-permute-done.11.a1 = f32[2,9,8,128]{3,2,1,0:T(8,128)S(1)} collective-permute-done((f32[2,9,8,128]{3,2,1,0:T(8,128)S(1)}, f32[2,9,8,128]{3,2,1,0:T(8,128)S(1)}, u32[]{:S(2)}, u32[]{:S(2)}) %collective-permute-start.11) | collective-permute-done | bytes 73760 | tf_op jit(solution)/shard_map/ppermute | solution.py:28
  59.8 3.5 %collective-permute-done.13.a3 = f32[2,9,8,128]{3,2,1,0:T(8,128)S(1)} collective-permute-done((f32[2,9,8,128]{3,2,1,0:T(8,128)S(1)}, f32[2,9,8,128]{3,2,1,0:T(8,128)S(1)}, u32[]{:S(2)}, u32[]{:S(2)}) %collective-permute-start.13) | collective-permute-done | bytes 73760 | tf_op jit(solution)/shard_map/ppermute | solution.py:28
  63.3 0.9 collective-permute-done.9.g2
  64.3 1.7 %collective-permute-start.14 = (f32[37,8,128]{2,1,0:T(8,128)S(1)}, f32[37,8,128]{2,1,0:T(8,128)S(1)}, u32[]{:S(2)}, u32[]{:S(2)}) collective-permute-start(f32[37,8,128]{2,1,0:T(8,128)S(1)} %get-tuple-element.118), channel_id=1, source_target_pairs={{0,8},{8,0},{1,9},{9,1},{2,10},{10,2},{3,11},{11,3},{4,12},{12,4},... | collective-permute-start | bytes 454664 | tf_op jit(solution)/shard_map/ppermute | solution.py:32
  66.0 2.6 %collective-permute-done.14.got = f32[37,8,128]{2,1,0:T(8,128)S(1)} collective-permute-done((f32[37,8,128]{2,1,0:T(8,128)S(1)}, f32[37,8,128]{2,1,0:T(8,128)S(1)}, u32[]{:S(2)}, u32[]{:S(2)}) %collective-permute-start.14) | collective-permute-done | bytes 151584 | tf_op jit(solution)/shard_map/ppermute | solution.py:32
  68.6 3.3 %collective-permute-start.15 = (f32[16,8,128]{2,1,0:T(8,128)S(1)}, f32[16,8,128]{2,1,0:T(8,128)S(1)}, u32[]{:S(2)}, u32[]{:S(2)}) collective-permute-start(f32[16,8,128]{2,1,0:T(8,128)S(1)} %get-tuple-element.120), channel_id=1, source_target_pairs={{0,64},{64,128},{128,192},{192,0},{1,65},{65,129},{129,193},{193,1... | collective-permute-start | bytes 196616 | tf_op jit(solution)/shard_map/ppermute | solution.py:28
  71.9 4.9 %collective-permute-start.16 = (f32[16,8,128]{2,1,0:T(8,128)S(1)}, f32[16,8,128]{2,1,0:T(8,128)S(1)}, u32[]{:S(2)}, u32[]{:S(2)}) collective-permute-start(f32[16,8,128]{2,1,0:T(8,128)S(1)} %get-tuple-element.121), channel_id=1, source_target_pairs={{0,128},{64,192},{128,0},{192,64},{1,129},{65,193},{129,1},{193,65... | collective-permute-start | bytes 196616 | tf_op jit(solution)/shard_map/ppermute | solution.py:28
  76.8 2.4 %collective-permute-start.17 = (f32[16,8,128]{2,1,0:T(8,128)S(1)}, f32[16,8,128]{2,1,0:T(8,128)S(1)}, u32[]{:S(2)}, u32[]{:S(2)}) collective-permute-start(f32[16,8,128]{2,1,0:T(8,128)S(1)} %get-tuple-element.122), channel_id=1, source_target_pairs={{0,192},{64,0},{128,64},{192,128},{1,193},{65,1},{129,65},{193,129... | collective-permute-start | bytes 196616 | tf_op jit(solution)/shard_map/ppermute | solution.py:28
  79.5 2.1 %collective-permute-done.17.p3 = f32[16,8,128]{2,1,0:T(8,128)S(1)} collective-permute-done((f32[16,8,128]{2,1,0:T(8,128)S(1)}, f32[16,8,128]{2,1,0:T(8,128)S(1)}, u32[]{:S(2)}, u32[]{:S(2)}) %collective-permute-start.17) | collective-permute-done | bytes 65568 | tf_op jit(solution)/shard_map/ppermute | solution.py:28
  81.6 1.2 collective-permute-start.24
  82.9 0.9 collective-permute-start.23
  84.0 0.7 collective-permute-start.18
  84.7 2.0 %collective-permute-done.18.got = f32[7,8,128]{2,1,0:T(8,128)S(1)} collective-permute-done((f32[7,8,128]{2,1,0:T(8,128)S(1)}, f32[7,8,128]{2,1,0:T(8,128)S(1)}, u32[]{:S(2)}, u32[]{:S(2)}) %collective-permute-start.18) | collective-permute-done | bytes 28704 | tf_op jit(solution)/shard_map/ppermute | solution.py:32
  86.7 4.7 %collective-permute-start.21 = (f32[14,8,128]{2,1,0:T(8,128)S(1)}, f32[14,8,128]{2,1,0:T(8,128)S(1)}, u32[]{:S(2)}, u32[]{:S(2)}) collective-permute-start(f32[14,8,128]{2,1,0:T(8,128)S(1)} %shard_map.64.p0), channel_id=1, source_target_pairs={{0,3},{1,0},{2,1},{3,2},{4,7},{5,4},{6,5},{7,6},{8,11},{9,8},{10,9... | collective-permute-start | bytes 172040 | tf_op jit(solution)/shard_map/ppermute | solution.py:28
  92.1 4.1 %shard_map.65.left = f32[2,256,320]{2,1,0:T(8,128)S(1)} custom-call(f32[9,8,128]{2,1,0:T(8,128)S(1)} %get-tuple-element.124.p0, f32[9,8,128]{2,1,0:T(8,128)S(1)} %collective-permute-done.22.p1, f32[9,8,128]{2,1,0:T(8,128)S(1)} %collective-permute-done.23.p2, f32[9,8,128]{2,1,0:T(8,128)S(1)} %collective-permute-done.24.p3, f32[256,256]{1,0:T(8,128)S(1)} %copy-done.3, ...), custom_call_target="tpu_custom_call" | custom-call | flops 2500000000 | bytes 2000000 | tf_op jit(solution)/shard_map/pallas_call | solution.py:296
  96.5 7.6 %shard_map.66 = (bf16[2,320,384]{2,1,0:T(8,128)(2,1)S(1)}, bf16[128,640]{1,0:T(8,128)(2,1)S(1)}) custom-call(f32[14,8,128]{2,1,0:T(8,128)S(1)} %shard_map.64.p0, f32[14,8,128]{2,1,0:T(8,128)S(1)} %collective-permute-done.19.p1, f32[14,8,128]{2,1,0:T(8,128)S(1)} %collective-permute-done.20.p2, f32[14,8,128]{2,1,0:T(8,128)S(1)} %collective-permute-done.21.p3, ...), custom_call_target="tpu_custom_call" | custom-call | flops 6000000000 | bytes 3000000 | tf_op jit(solution)/shard_map/pallas_call | solution.py:401
  104.1 6.2 %collective-permute-start.28 = (bf16[2,320,384]{2,1,0:T(8,128)(2,1)S(1)}, bf16[2,320,384]{2,1,0:T(8,128)(2,1)S(1)}, u32[]{:S(2)}, u32[]{:S(2)}) collective-permute-start(bf16[2,320,384]{2,1,0:T(8,128)(2,1)S(1)} %get-tuple-element.132), channel_id=1, source_target_pairs={{0,4},{4,0},{1,5},{5,1},{2,6},{6,2},{3,7},{7,3},{8,12},{12,8},{9,1... | collective-permute-start | bytes 1474568 | tf_op jit(solution)/shard_map/ppermute | solution.py:24
  110.3 1.8 %collective-permute-start.27 = (bf16[128,640]{1,0:T(8,128)(2,1)S(1)}, bf16[128,640]{1,0:T(8,128)(2,1)S(1)}, u32[]{:S(2)}, u32[]{:S(2)}) collective-permute-start(bf16[128,640]{1,0:T(8,128)(2,1)S(1)} %get-tuple-element.131.refs_0_), channel_id=1, source_target_pairs={{0,3},{1,0},{2,1},{3,2},{4,7},{5,4},{6,5},{7,6},{8,11},{9,8},{10,9... | collective-permute-start | bytes 491528 | tf_op jit(solution)/shard_map/ppermute | solution.py:28
  112.1 1.0 collective-permute-start.26
  113.1 0.6 shard_map.67.refs_4_
  113.7 2.8 %collective-permute-start.31 = (bf16[128,640]{1,0:T(8,128)(2,1)S(1)}, bf16[128,640]{1,0:T(8,128)(2,1)S(1)}, u32[]{:S(2)}, u32[]{:S(2)}) collective-permute-start(bf16[128,640]{1,0:T(8,128)(2,1)S(1)} %shard_map.67.refs_4_), channel_id=1, source_target_pairs={{0,3},{1,0},{2,1},{3,2},{4,7},{5,4},{6,5},{7,6},{8,11},{9,8},{10,9... | collective-permute-start | bytes 491528 | tf_op jit(solution)/shard_map/ppermute | solution.py:28
  116.5 0.8 collective-permute-start.30
  117.2 1.9 %collective-permute-done.26.refs_2_ = bf16[128,640]{1,0:T(8,128)(2,1)S(1)} collective-permute-done((bf16[128,640]{1,0:T(8,128)(2,1)S(1)}, bf16[128,640]{1,0:T(8,128)(2,1)S(1)}, u32[]{:S(2)}, u32[]{:S(2)}) %collective-permute-start.26) | collective-permute-done | bytes 163872 | tf_op jit(solution)/shard_map/ppermute | solution.py:28
  119.1 4.8 %collective-permute-done.25.refs_1_ = bf16[128,640]{1,0:T(8,128)(2,1)S(1)} collective-permute-done((bf16[128,640]{1,0:T(8,128)(2,1)S(1)}, bf16[128,640]{1,0:T(8,128)(2,1)S(1)}, u32[]{:S(2)}, u32[]{:S(2)}) %collective-permute-start.25) | collective-permute-done | bytes 163872 | tf_op jit(solution)/shard_map/ppermute | solution.py:28
  123.9 2.3 %collective-permute-done.30.refs_6_ = bf16[128,640]{1,0:T(8,128)(2,1)S(1)} collective-permute-done((bf16[128,640]{1,0:T(8,128)(2,1)S(1)}, bf16[128,640]{1,0:T(8,128)(2,1)S(1)}, u32[]{:S(2)}, u32[]{:S(2)}) %collective-permute-start.30) | collective-permute-done | bytes 163872 | tf_op jit(solution)/shard_map/ppermute | solution.py:28
  126.2 4.0 %collective-permute-done.29.refs_5_ = bf16[128,640]{1,0:T(8,128)(2,1)S(1)} collective-permute-done((bf16[128,640]{1,0:T(8,128)(2,1)S(1)}, bf16[128,640]{1,0:T(8,128)(2,1)S(1)}, u32[]{:S(2)}, u32[]{:S(2)}) %collective-permute-start.29) | collective-permute-done | bytes 163872 | tf_op jit(solution)/shard_map/ppermute | solution.py:28
  130.2 1.3 %shard_map.68 = bf16[1024,640]{1,0:T(8,128)(2,1)} custom-call(bf16[128,640]{1,0:T(8,128)(2,1)S(1)} %get-tuple-element.131.refs_0_, bf16[128,640]{1,0:T(8,128)(2,1)S(1)} %collective-permute-done.25.refs_1_, bf16[128,640]{1,0:T(8,128)(2,1)S(1)} %collective-permute-done.26.refs_2_, bf16[128,640]{1,0:T(8,128)(2,1)S(1)} %collective-permute-done.27.refs_3_, ...), custom_call_target="tpu_custom_call" | custom-call | tf_op jit(solution)/shard_map/pallas_call | solution.py:181
  (38 shorter events, 2.1 us)
Async XLA Ops:
  2.6 20.7 %collective-permute-start = (bf16[4,128,640]{2,1,0:T(8,128)(2,1)}, bf16[4,128,640]{2,1,0:T(8,128)(2,1)S(1)}, u32[]{:S(2)}, u32[]{:S(2)}) collective-permute-start(bf16[4,128,640]{2,1,0:T(8,128)(2,1)} %get-tuple-element.76), channel_id=1, source_target_pairs={{0,16},{16,32},{32,48},{48,0},{1,17},{17,33},{33,49},{49,1},{2,18}... | collective-permute-start | bytes 1966088 | tf_op jit(solution)/shard_map/ppermute | solution.py:28
  4.7 18.6 %collective-permute-start.1 = (bf16[4,128,640]{2,1,0:T(8,128)(2,1)}, bf16[4,128,640]{2,1,0:T(8,128)(2,1)S(1)}, u32[]{:S(2)}, u32[]{:S(2)}) collective-permute-start(bf16[4,128,640]{2,1,0:T(8,128)(2,1)} %get-tuple-element.77), channel_id=1, source_target_pairs={{0,48},{16,0},{32,16},{48,32},{1,49},{17,1},{33,17},{49,33},{2,50}... | collective-permute-start | bytes 1966088 | tf_op jit(solution)/shard_map/ppermute | solution.py:28
  8.5 13.6 %collective-permute-start.2 = (bf16[128,2304]{1,0:T(8,128)(2,1)}, bf16[128,2304]{1,0:T(8,128)(2,1)S(1)}, u32[]{:S(2)}, u32[]{:S(2)}) collective-permute-start(bf16[128,2304]{1,0:T(8,128)(2,1)} %get-tuple-element.78), channel_id=1, source_target_pairs={{0,1},{1,2},{2,3},{3,0},{4,5},{5,6},{6,7},{7,4},{8,9},{9,10},{10,1... | collective-permute-start | bytes 1769480 | tf_op jit(solution)/shard_map/ppermute | solution.py:28
  10.0 13.3 %collective-permute-start.3 = (bf16[128,2304]{1,0:T(8,128)(2,1)}, bf16[128,2304]{1,0:T(8,128)(2,1)S(1)}, u32[]{:S(2)}, u32[]{:S(2)}) collective-permute-start(bf16[128,2304]{1,0:T(8,128)(2,1)} %get-tuple-element.79), channel_id=1, source_target_pairs={{0,3},{1,0},{2,1},{3,2},{4,7},{5,4},{6,5},{7,6},{8,11},{9,8},{10,9... | collective-permute-start | bytes 1769480 | tf_op jit(solution)/shard_map/ppermute | solution.py:28
  23.3 16.4 %collective-permute-start.4 = (bf16[4,128,640]{2,1,0:T(8,128)(2,1)}, bf16[4,128,640]{2,1,0:T(8,128)(2,1)S(1)}, u32[]{:S(2)}, u32[]{:S(2)}) collective-permute-start(bf16[4,128,640]{2,1,0:T(8,128)(2,1)} %get-tuple-element.84), channel_id=1, source_target_pairs={{0,32},{16,48},{32,0},{48,16},{1,33},{17,49},{33,1},{49,17},{2,34}... | collective-permute-start | bytes 1966088 | tf_op jit(solution)/shard_map/ppermute | solution.py:28
  25.5 14.2 %collective-permute-start.5 = (bf16[128,2304]{1,0:T(8,128)(2,1)}, bf16[128,2304]{1,0:T(8,128)(2,1)S(1)}, u32[]{:S(2)}, u32[]{:S(2)}) collective-permute-start(bf16[128,2304]{1,0:T(8,128)(2,1)} %get-tuple-element.88), channel_id=1, source_target_pairs={{0,2},{1,3},{2,0},{3,1},{4,6},{5,7},{6,4},{7,5},{8,10},{9,11},{10,... | collective-permute-start | bytes 1769480 | tf_op jit(solution)/shard_map/ppermute | solution.py:28
  39.7 1.1 copy-start
  40.7 6.8 %copy-start.1 = (bf16[128,2304]{1,0:T(8,128)(2,1)S(1)}, bf16[128,2304]{1,0:T(8,128)(2,1)}, u32[]{:S(2)}) copy-start(bf16[128,2304]{1,0:T(8,128)(2,1)} %get-tuple-element.95.i0.g0) | copy-start | bytes 1769476
  44.2 5.9 %collective-permute-start.6 = (f32[4,56,8,128]{3,2,1,0:T(8,128)S(1)}, f32[4,56,8,128]{3,2,1,0:T(8,128)S(1)}, u32[]{:S(2)}, u32[]{:S(2)}) collective-permute-start(f32[4,56,8,128]{3,2,1,0:T(8,128)S(1)} %get-tuple-element.94), channel_id=1, source_target_pairs={{0,4},{4,0},{1,5},{5,1},{2,6},{6,2},{3,7},{7,3},{8,12},{12,8},{9,1... | collective-permute-start | bytes 2752520 | tf_op jit(solution)/shard_map/ppermute | solution.py:24
  48.2 43.9 %copy-start.3 = (f32[256,256]{1,0:T(8,128)S(1)}, f32[256,256]{1,0:T(8,128)}, u32[]{:S(2)}) copy-start(f32[256,256]{1,0:T(8,128)} %get-tuple-element.125.running) | copy-start | bytes 786436
  48.2 1.9 %collective-permute-start.7 = (f32[2,36,8,128]{3,2,1,0:T(8,128)S(1)}, f32[2,36,8,128]{3,2,1,0:T(8,128)S(1)}, u32[]{:S(2)}, u32[]{:S(2)}) collective-permute-start(f32[2,36,8,128]{3,2,1,0:T(8,128)S(1)} %get-tuple-element.100), channel_id=1, source_target_pairs={{0,4},{4,0},{1,5},{5,1},{2,6},{6,2},{3,7},{7,3},{8,12},{12,8},{9,1... | collective-permute-start | bytes 884744 | tf_op jit(solution)/shard_map/ppermute | solution.py:24
  50.2 13.1 %collective-permute-start.8 = (f32[4,14,8,128]{3,2,1,0:T(8,128)S(1)}, f32[4,14,8,128]{3,2,1,0:T(8,128)S(1)}, u32[]{:S(2)}, u32[]{:S(2)}) collective-permute-start(f32[4,14,8,128]{3,2,1,0:T(8,128)S(1)} %get-tuple-element.102), channel_id=1, source_target_pairs={{0,1},{1,2},{2,3},{3,0},{4,5},{5,6},{6,7},{7,4},{8,9},{9,10},{10,1... | collective-permute-start | bytes 688136 | tf_op jit(solution)/shard_map/ppermute | solution.py:28
  51.2 13.0 %collective-permute-start.9 = (f32[4,14,8,128]{3,2,1,0:T(8,128)S(1)}, f32[4,14,8,128]{3,2,1,0:T(8,128)S(1)}, u32[]{:S(2)}, u32[]{:S(2)}) collective-permute-start(f32[4,14,8,128]{3,2,1,0:T(8,128)S(1)} %get-tuple-element.103), channel_id=1, source_target_pairs={{0,2},{1,3},{2,0},{3,1},{4,6},{5,7},{6,4},{7,5},{8,10},{9,11},{10,... | collective-permute-start | bytes 688136 | tf_op jit(solution)/shard_map/ppermute | solution.py:28
  54.0 10.3 %collective-permute-start.10 = (f32[4,14,8,128]{3,2,1,0:T(8,128)S(1)}, f32[4,14,8,128]{3,2,1,0:T(8,128)S(1)}, u32[]{:S(2)}, u32[]{:S(2)}) collective-permute-start(f32[4,14,8,128]{3,2,1,0:T(8,128)S(1)} %get-tuple-element.104), channel_id=1, source_target_pairs={{0,3},{1,0},{2,1},{3,2},{4,7},{5,4},{6,5},{7,6},{8,11},{9,8},{10,9... | collective-permute-start | bytes 688136 | tf_op jit(solution)/shard_map/ppermute | solution.py:28
  54.6 5.2 %collective-permute-start.11 = (f32[2,9,8,128]{3,2,1,0:T(8,128)S(1)}, f32[2,9,8,128]{3,2,1,0:T(8,128)S(1)}, u32[]{:S(2)}, u32[]{:S(2)}) collective-permute-start(f32[2,9,8,128]{3,2,1,0:T(8,128)S(1)} %get-tuple-element.106), channel_id=1, source_target_pairs={{0,16},{16,32},{32,48},{48,0},{1,17},{17,33},{33,49},{49,1},{2,18}... | collective-permute-start | bytes 221192 | tf_op jit(solution)/shard_map/ppermute | solution.py:28
  54.9 4.9 %collective-permute-start.12 = (f32[2,9,8,128]{3,2,1,0:T(8,128)S(1)}, f32[2,9,8,128]{3,2,1,0:T(8,128)S(1)}, u32[]{:S(2)}, u32[]{:S(2)}) collective-permute-start(f32[2,9,8,128]{3,2,1,0:T(8,128)S(1)} %get-tuple-element.107), channel_id=1, source_target_pairs={{0,32},{16,48},{32,0},{48,16},{1,33},{17,49},{33,1},{49,17},{2,34}... | collective-permute-start | bytes 221192 | tf_op jit(solution)/shard_map/ppermute | solution.py:28
  59.8 3.5 %collective-permute-start.13 = (f32[2,9,8,128]{3,2,1,0:T(8,128)S(1)}, f32[2,9,8,128]{3,2,1,0:T(8,128)S(1)}, u32[]{:S(2)}, u32[]{:S(2)}) collective-permute-start(f32[2,9,8,128]{3,2,1,0:T(8,128)S(1)} %get-tuple-element.108), channel_id=1, source_target_pairs={{0,48},{16,0},{32,16},{48,32},{1,49},{17,1},{33,17},{49,33},{2,50}... | collective-permute-start | bytes 221192 | tf_op jit(solution)/shard_map/ppermute | solution.py:28
  64.3 4.3 %collective-permute-start.14 = (f32[37,8,128]{2,1,0:T(8,128)S(1)}, f32[37,8,128]{2,1,0:T(8,128)S(1)}, u32[]{:S(2)}, u32[]{:S(2)}) collective-permute-start(f32[37,8,128]{2,1,0:T(8,128)S(1)} %get-tuple-element.118), channel_id=1, source_target_pairs={{0,8},{8,0},{1,9},{9,1},{2,10},{10,2},{3,11},{11,3},{4,12},{12,4},... | collective-permute-start | bytes 454664 | tf_op jit(solution)/shard_map/ppermute | solution.py:32
  68.6 10.6 %collective-permute-start.15 = (f32[16,8,128]{2,1,0:T(8,128)S(1)}, f32[16,8,128]{2,1,0:T(8,128)S(1)}, u32[]{:S(2)}, u32[]{:S(2)}) collective-permute-start(f32[16,8,128]{2,1,0:T(8,128)S(1)} %get-tuple-element.120), channel_id=1, source_target_pairs={{0,64},{64,128},{128,192},{192,0},{1,65},{65,129},{129,193},{193,1... | collective-permute-start | bytes 196616 | tf_op jit(solution)/shard_map/ppermute | solution.py:28
  71.9 7.6 %collective-permute-start.16 = (f32[16,8,128]{2,1,0:T(8,128)S(1)}, f32[16,8,128]{2,1,0:T(8,128)S(1)}, u32[]{:S(2)}, u32[]{:S(2)}) collective-permute-start(f32[16,8,128]{2,1,0:T(8,128)S(1)} %get-tuple-element.121), channel_id=1, source_target_pairs={{0,128},{64,192},{128,0},{192,64},{1,129},{65,193},{129,1},{193,65... | collective-permute-start | bytes 196616 | tf_op jit(solution)/shard_map/ppermute | solution.py:28
  76.8 4.8 %collective-permute-start.17 = (f32[16,8,128]{2,1,0:T(8,128)S(1)}, f32[16,8,128]{2,1,0:T(8,128)S(1)}, u32[]{:S(2)}, u32[]{:S(2)}) collective-permute-start(f32[16,8,128]{2,1,0:T(8,128)S(1)} %get-tuple-element.122), channel_id=1, source_target_pairs={{0,192},{64,0},{128,64},{192,128},{1,193},{65,1},{129,65},{193,129... | collective-permute-start | bytes 196616 | tf_op jit(solution)/shard_map/ppermute | solution.py:28
  81.6 10.0 %collective-permute-start.24 = (f32[9,8,128]{2,1,0:T(8,128)S(1)}, f32[9,8,128]{2,1,0:T(8,128)S(1)}, u32[]{:S(2)}, u32[]{:S(2)}) collective-permute-start(f32[9,8,128]{2,1,0:T(8,128)S(1)} %get-tuple-element.124.p0), channel_id=1, source_target_pairs={{0,48},{16,0},{32,16},{48,32},{1,49},{17,1},{33,17},{49,33},{2,50}... | collective-permute-start | bytes 110600 | tf_op jit(solution)/shard_map/ppermute | solution.py:28
  82.9 9.2 %collective-permute-start.23 = (f32[9,8,128]{2,1,0:T(8,128)S(1)}, f32[9,8,128]{2,1,0:T(8,128)S(1)}, u32[]{:S(2)}, u32[]{:S(2)}) collective-permute-start(f32[9,8,128]{2,1,0:T(8,128)S(1)} %get-tuple-element.124.p0), channel_id=1, source_target_pairs={{0,32},{16,48},{32,0},{48,16},{1,33},{17,49},{33,1},{49,17},{2,34}... | collective-permute-start | bytes 110600 | tf_op jit(solution)/shard_map/ppermute | solution.py:28
  83.8 8.3 %collective-permute-start.22 = (f32[9,8,128]{2,1,0:T(8,128)S(1)}, f32[9,8,128]{2,1,0:T(8,128)S(1)}, u32[]{:S(2)}, u32[]{:S(2)}) collective-permute-start(f32[9,8,128]{2,1,0:T(8,128)S(1)} %get-tuple-element.124.p0), channel_id=1, source_target_pairs={{0,16},{16,32},{32,48},{48,0},{1,17},{17,33},{33,49},{49,1},{2,18}... | collective-permute-start | bytes 110600 | tf_op jit(solution)/shard_map/ppermute | solution.py:28
  84.0 2.7 %collective-permute-start.18 = (f32[7,8,128]{2,1,0:T(8,128)S(1)}, f32[7,8,128]{2,1,0:T(8,128)S(1)}, u32[]{:S(2)}, u32[]{:S(2)}) collective-permute-start(f32[7,8,128]{2,1,0:T(8,128)S(1)} %get-tuple-element.123.own), channel_id=1, source_target_pairs={{0,8},{8,0},{1,9},{9,1},{2,10},{10,2},{3,11},{11,3},{4,12},{12,4},... | collective-permute-start | bytes 86024 | tf_op jit(solution)/shard_map/ppermute | solution.py:32
  86.7 9.5 %collective-permute-start.21 = (f32[14,8,128]{2,1,0:T(8,128)S(1)}, f32[14,8,128]{2,1,0:T(8,128)S(1)}, u32[]{:S(2)}, u32[]{:S(2)}) collective-permute-start(f32[14,8,128]{2,1,0:T(8,128)S(1)} %shard_map.64.p0), channel_id=1, source_target_pairs={{0,3},{1,0},{2,1},{3,2},{4,7},{5,4},{6,5},{7,6},{8,11},{9,8},{10,9... | collective-permute-start | bytes 172040 | tf_op jit(solution)/shard_map/ppermute | solution.py:28
  91.4 4.9 %collective-permute-start.20 = (f32[14,8,128]{2,1,0:T(8,128)S(1)}, f32[14,8,128]{2,1,0:T(8,128)S(1)}, u32[]{:S(2)}, u32[]{:S(2)}) collective-permute-start(f32[14,8,128]{2,1,0:T(8,128)S(1)} %shard_map.64.p0), channel_id=1, source_target_pairs={{0,2},{1,3},{2,0},{3,1},{4,6},{5,7},{6,4},{7,5},{8,10},{9,11},{10,... | collective-permute-start | bytes 172040 | tf_op jit(solution)/shard_map/ppermute | solution.py:28
  91.6 4.9 %collective-permute-start.19 = (f32[14,8,128]{2,1,0:T(8,128)S(1)}, f32[14,8,128]{2,1,0:T(8,128)S(1)}, u32[]{:S(2)}, u32[]{:S(2)}) collective-permute-start(f32[14,8,128]{2,1,0:T(8,128)S(1)} %shard_map.64.p0), channel_id=1, source_target_pairs={{0,1},{1,2},{2,3},{3,0},{4,5},{5,6},{6,7},{7,4},{8,9},{9,10},{10,1... | collective-permute-start | bytes 172040 | tf_op jit(solution)/shard_map/ppermute | solution.py:28
  92.1 4.4 %copy-start.2 = (f32[2,320,320]{2,1,0:T(8,128)S(1)}, f32[2,320,320]{2,1,0:T(8,128)}, u32[]{:S(2)}) copy-start(f32[2,320,320]{2,1,0:T(8,128)} %running.3) | copy-start | bytes 2457604
  104.1 9.0 %collective-permute-start.28 = (bf16[2,320,384]{2,1,0:T(8,128)(2,1)S(1)}, bf16[2,320,384]{2,1,0:T(8,128)(2,1)S(1)}, u32[]{:S(2)}, u32[]{:S(2)}) collective-permute-start(bf16[2,320,384]{2,1,0:T(8,128)(2,1)S(1)} %get-tuple-element.132), channel_id=1, source_target_pairs={{0,4},{4,0},{1,5},{5,1},{2,6},{6,2},{3,7},{7,3},{8,12},{12,8},{9,1... | collective-permute-start | bytes 1474568 | tf_op jit(solution)/shard_map/ppermute | solution.py:24
  110.3 6.9 %collective-permute-start.27 = (bf16[128,640]{1,0:T(8,128)(2,1)S(1)}, bf16[128,640]{1,0:T(8,128)(2,1)S(1)}, u32[]{:S(2)}, u32[]{:S(2)}) collective-permute-start(bf16[128,640]{1,0:T(8,128)(2,1)S(1)} %get-tuple-element.131.refs_0_), channel_id=1, source_target_pairs={{0,3},{1,0},{2,1},{3,2},{4,7},{5,4},{6,5},{7,6},{8,11},{9,8},{10,9... | collective-permute-start | bytes 491528 | tf_op jit(solution)/shard_map/ppermute | solution.py:28
  112.1 7.0 %collective-permute-start.26 = (bf16[128,640]{1,0:T(8,128)(2,1)S(1)}, bf16[128,640]{1,0:T(8,128)(2,1)S(1)}, u32[]{:S(2)}, u32[]{:S(2)}) collective-permute-start(bf16[128,640]{1,0:T(8,128)(2,1)S(1)} %get-tuple-element.131.refs_0_), channel_id=1, source_target_pairs={{0,2},{1,3},{2,0},{3,1},{4,6},{5,7},{6,4},{7,5},{8,10},{9,11},{10,... | collective-permute-start | bytes 491528 | tf_op jit(solution)/shard_map/ppermute | solution.py:28
  113.1 10.8 %collective-permute-start.25 = (bf16[128,640]{1,0:T(8,128)(2,1)S(1)}, bf16[128,640]{1,0:T(8,128)(2,1)S(1)}, u32[]{:S(2)}, u32[]{:S(2)}) collective-permute-start(bf16[128,640]{1,0:T(8,128)(2,1)S(1)} %get-tuple-element.131.refs_0_), channel_id=1, source_target_pairs={{0,1},{1,2},{2,3},{3,0},{4,5},{5,6},{6,7},{7,4},{8,9},{9,10},{10,1... | collective-permute-start | bytes 491528 | tf_op jit(solution)/shard_map/ppermute | solution.py:28
  113.7 10.2 %collective-permute-start.31 = (bf16[128,640]{1,0:T(8,128)(2,1)S(1)}, bf16[128,640]{1,0:T(8,128)(2,1)S(1)}, u32[]{:S(2)}, u32[]{:S(2)}) collective-permute-start(bf16[128,640]{1,0:T(8,128)(2,1)S(1)} %shard_map.67.refs_4_), channel_id=1, source_target_pairs={{0,3},{1,0},{2,1},{3,2},{4,7},{5,4},{6,5},{7,6},{8,11},{9,8},{10,9... | collective-permute-start | bytes 491528 | tf_op jit(solution)/shard_map/ppermute | solution.py:28
  116.5 9.7 %collective-permute-start.30 = (bf16[128,640]{1,0:T(8,128)(2,1)S(1)}, bf16[128,640]{1,0:T(8,128)(2,1)S(1)}, u32[]{:S(2)}, u32[]{:S(2)}) collective-permute-start(bf16[128,640]{1,0:T(8,128)(2,1)S(1)} %shard_map.67.refs_4_), channel_id=1, source_target_pairs={{0,2},{1,3},{2,0},{3,1},{4,6},{5,7},{6,4},{7,5},{8,10},{9,11},{10,... | collective-permute-start | bytes 491528 | tf_op jit(solution)/shard_map/ppermute | solution.py:28
  117.2 12.9 %collective-permute-start.29 = (bf16[128,640]{1,0:T(8,128)(2,1)S(1)}, bf16[128,640]{1,0:T(8,128)(2,1)S(1)}, u32[]{:S(2)}, u32[]{:S(2)}) collective-permute-start(bf16[128,640]{1,0:T(8,128)(2,1)S(1)} %shard_map.67.refs_4_), channel_id=1, source_target_pairs={{0,1},{1,2},{2,3},{3,0},{4,5},{5,6},{6,7},{7,4},{8,9},{9,10},{10,1... | collective-permute-start | bytes 491528 | tf_op jit(solution)/shard_map/ppermute | solution.py:28

commit v4 on v3

--- a/solution.py
+++ b/solution.py
@@ -244,23 +244,23 @@
     n = identity.shape[0]
 
     def put(approx, product):
-        for i, part in enumerate(three(approx)):
-            lhs[0:n, i * n:(i + 1) * n] = part
-        for i, part in enumerate(three(product)):
-            lhs[n:2 * n, i * n:(i + 1) * n] = part
         high, low = split(2.0 * identity - product)
         rhs[0:n], rhs[n:2 * n], rhs[2 * n:3 * n] = high, low, high
+        for i, part in enumerate(three(product)):
+            lhs[0:n, i * n:(i + 1) * n] = part
+        for i, part in enumerate(three(approx)):
+            lhs[n:2 * n, i * n:(i + 1) * n] = part
 
     trace = jnp.sum(matrix * identity)
     put(identity / trace, matrix / trace)
 
     def step(_, carry):
         both = jnp.dot(lhs[...], rhs[...], preferred_element_type=jnp.float32)
-        put(both[:n], both[n:])
+        put(both[n:], both[:n])
         return carry
 
     lax.fori_loop(0, ITERS - 1, step, 0)
-    return jnp.dot(lhs[0:n], rhs[...], preferred_element_type=jnp.float32)
+    return jnp.dot(lhs[n:2 * n], rhs[...], preferred_element_type=jnp.float32)
 
 
 def a_side_kernel(p0, p1, p2, p3, running, g0, g1, g2, g3, left, tiles, lhs, rhs, *, token_total):
@@ -337,16 +337,16 @@
     return main, tail
 
 
-def g_put(lhs, rhs_main, rhs_tail, ident, approx, product):
-    for row, (main, tail) in ((0, approx), (BG, product)):
-        for i, (part, edge) in enumerate(zip(three(main), three(tail))):
-            lhs[row:row + BG, i * BGP:i * BGP + 256] = part
-            lhs[row:row + BG, i * BGP + 256:(i + 1) * BGP] = edge
+def g_put(lhs, rhs_main, rhs_tail, ident, product, approx):
     for rhs, same, value in ((rhs_main, ident[0], product[0]), (rhs_tail, ident[1], product[1])):
         high, low = split(2.0 * same - value)
         rhs[0:BG] = high
         rhs[BGP:BGP + BG] = low
         rhs[2 * BGP:2 * BGP + BG] = high
+    for row, (main, tail) in ((0, product), (BG, approx)):
+        for i, (part, edge) in enumerate(zip(three(main), three(tail))):
+            lhs[row:row + BG, i * BGP:i * BGP + 256] = part
+            lhs[row:row + BG, i * BGP + 256:(i + 1) * BGP] = edge
 
 
 def half_rows(left, inverse):
@@ -374,25 +374,20 @@
     rhs_main[...] = jnp.zeros(rhs_main.shape, jnp.bfloat16)
     rhs_tail[...] = jnp.zeros(rhs_tail.shape, jnp.bfloat16)
     put = functools.partial(g_put, lhs, rhs_main, rhs_tail, ident)
-    put([same / trace for same in ident], [part / trace for part in matrix])
-
-    def product(rows):
-        main = jnp.dot(lhs[0:rows], rhs_main[...], preferred_element_type=jnp.float32)
-        corners = [
-            jnp.dot(lhs[row + 256:row + BG], rhs_tail[...], preferred_element_type=jnp.float32)
-            for row in range(0, rows, BG)
-        ]
-        return [
-            (main[row:row + BG], jnp.concatenate([turned_tail(main[row:row + BG]), corner], axis=0))
-            for row, corner in zip(range(0, rows, BG), corners)
-        ]
+    put([part / trace for part in matrix], [same / trace for same in ident])
+
+    def times(row):
+        main = jnp.dot(lhs[row:row + BG], rhs_main[...], preferred_element_type=jnp.float32)
+        corner = jnp.dot(lhs[row + 256:row + BG], rhs_tail[...], preferred_element_type=jnp.float32)
+        return main, jnp.concatenate([turned_tail(main), corner], axis=0)
 
     def step(_, carry):
-        put(*product(2 * BG))
+        product, approx = times(0), times(BG)
+        put(product, approx)
         return carry
 
-    lax.fori_loop(0, ITERS - 1, step, 0)
-    (main, tail), = product(BG)
+    lax.fori_loop(0, ITERS - 1, step, 0, unroll=True)
+    main, tail = times(BG)
     out[0], out[1] = split(jnp.concatenate([main, tail], axis=1))
     rows[...] = half_rows(left[c], out)
 
@@ -445,13 +440,14 @@
     )
     g_in = [send(near_x[0], "x", 1), send(near_x[1], "x", 3)]
     y_in = [send(near_y[0], "y", 1), send(near_y[1], "y", 3)]
-    g_in, y_in, far_x, far_y = lax.optimization_barrier((g_in, y_in, far_x, far_y))
+    g_in, far_x = lax.optimization_barrier((g_in, far_x))
+    g_in, y_in, far_y = lax.optimization_barrier((g_in, y_in, far_y))
     g_in = [own_x, *g_in, send(far_x, "x", 2)]
     y_in = [own_y, *y_in, send(far_y, "y", 2)]
-    g_in, y_in = lax.optimization_barrier((g_in, y_in))
-
+
+    a_own, a_other = a_cov(y_in)
+    g_in, a_own, a_other = lax.optimization_barrier((g_in, a_own, a_other))
     g_own, g_other = g_cov(g_in)
-    a_own, a_other = a_cov(y_in)
     cut = local(
         cores_kernel, [tile_shape(4, 14)] * 4 + [tile_shape(2, 9)] * 4,
         g_own, swap_cores(g_other), a_own, swap_cores(a_other),

time: 132 us -> 129 us (0.977)
  waiting for transfers between devices: 49.3 us -> 45.8 us
  starting transfers between devices: 54.4 us -> 56.9 us
    ppermute x27, waiting for transfers between devices: 43 us -> 38.8 us  [send(): return lax.ppermute(value, axis, [(i, (i + s) % 4) for i in range(4)])]
    ppermute x27, starting transfers between devices: 42.2 us -> 44 us  [send(): return lax.ppermute(value, axis, [(i, (i + s) % 4) for i in range(4)])]
where the time goes in v4:
time: 129 us
  starting transfers between devices  56.9 us (44%)
  waiting for transfers between devices  45.8 us (36%)
  Pallas kernels  25.3 us (20%)
    ppermute x27, starting transfers between devices, send(): return lax.ppermute(value, axis, [(i, (i + s) % 4) for i in range(4)])  44 us
    ppermute x27, waiting for transfers between devices, send(): return lax.ppermute(value, axis, [(i, (i + s) % 4) for i in range(4)])  38.8 us
    ppermute x3, starting transfers between devices, swap_cores(): return lax.ppermute(value, 'c', [(0, 1), (1, 0)])  9.83 us
    pallas_call x3, Pallas kernels, pack(): pl.pallas_call(kernel, out_shape=out_shape, in_specs=[pl.BlockSpec(memory...  8.57 us
    pallas_call x1, Pallas kernels, g_side(): pl.pallas_call(functools.partial(g_side_kernel, token_total=token_total),...  6.45 us
    ppermute x2, waiting for transfers between devices, swap_pair(): return lax.ppermute(value, 'zl', [(0, 1), (1, 0)])  4.57 us
    pallas_call x1, Pallas kernels, a_side(): pl.pallas_call(functools.partial(a_side_kernel, token_total=token_total),...  4.04 us
    pallas_call x1, Pallas kernels, g_cov(): pl.pallas_call(g_cov_kernel, grid=(4,), out_shape=[jax.ShapeDtypeStruct((...  3.46 us
  transfers between devices with their start and end apart: 32, of which 16 were waited for; matrix products, arithmetic and copies ran while one was open for 0% of the time, Pallas kernels for 9%

profile of v4, /device:TPU:1, one launch (start us, length us, event | category | flops | bytes accessed | tf_op | source)
XLA Modules:
  0.0 129.3 jit_solution(5333243253536789239)
XLA Ops:
  0.0 2.5 %shard_map.55 = (bf16[4,128,640]{2,1,0:T(8,128)(2,1)}, bf16[4,128,640]{2,1,0:T(8,128)(2,1)}) custom-call(bf16[128,10240]{1,0:T(8,128)(2,1)} %src.2), custom_call_target="tpu_custom_call" | custom-call | tf_op jit(solution)/shard_map/pallas_call | solution.py:87
  2.5 2.1 %collective-permute-start = (bf16[4,128,640]{2,1,0:T(8,128)(2,1)}, bf16[4,128,640]{2,1,0:T(8,128)(2,1)S(1)}, u32[]{:S(2)}, u32[]{:S(2)}) collective-permute-start(bf16[4,128,640]{2,1,0:T(8,128)(2,1)} %get-tuple-element.76), channel_id=1, source_target_pairs={{0,16},{16,32},{32,48},{48,0},{1,17},{17,33},{33,49},{49,1},{2,18}... | collective-permute-start | bytes 1966088 | tf_op jit(solution)/shard_map/ppermute | solution.py:28
  4.7 1.4 %collective-permute-start.1 = (bf16[4,128,640]{2,1,0:T(8,128)(2,1)}, bf16[4,128,640]{2,1,0:T(8,128)(2,1)S(1)}, u32[]{:S(2)}, u32[]{:S(2)}) collective-permute-start(bf16[4,128,640]{2,1,0:T(8,128)(2,1)} %get-tuple-element.77), channel_id=1, source_target_pairs={{0,48},{16,0},{32,16},{48,32},{1,49},{17,1},{33,17},{49,33},{2,50}... | collective-permute-start | bytes 1966088 | tf_op jit(solution)/shard_map/ppermute | solution.py:28
  6.0 2.5 %shard_map.56 = (bf16[128,2304]{1,0:T(8,128)(2,1)}, bf16[128,2304]{1,0:T(8,128)(2,1)}) custom-call(bf16[128,4096]{1,0:T(8,128)(2,1)} %samples.1, bf16[1,1024,640]{2,1,0:T(8,128)(2,1)} %grads.3), custom_call_target="tpu_custom_call" | custom-call | tf_op jit(solution)/shard_map/pallas_call | solution.py:87
  8.5 1.5 %collective-permute-start.2 = (bf16[128,2304]{1,0:T(8,128)(2,1)}, bf16[128,2304]{1,0:T(8,128)(2,1)S(1)}, u32[]{:S(2)}, u32[]{:S(2)}) collective-permute-start(bf16[128,2304]{1,0:T(8,128)(2,1)} %get-tuple-element.81), channel_id=1, source_target_pairs={{0,1},{1,2},{2,3},{3,0},{4,5},{5,6},{6,7},{7,4},{8,9},{9,10},{10,1... | collective-permute-start | bytes 1769480 | tf_op jit(solution)/shard_map/ppermute | solution.py:28
  10.0 1.5 %collective-permute-start.3 = (bf16[128,2304]{1,0:T(8,128)(2,1)}, bf16[128,2304]{1,0:T(8,128)(2,1)S(1)}, u32[]{:S(2)}, u32[]{:S(2)}) collective-permute-start(bf16[128,2304]{1,0:T(8,128)(2,1)} %get-tuple-element.82), channel_id=1, source_target_pairs={{0,3},{1,0},{2,1},{3,2},{4,7},{5,4},{6,5},{7,6},{8,11},{9,8},{10,9... | collective-permute-start | bytes 1769480 | tf_op jit(solution)/shard_map/ppermute | solution.py:28
  11.5 3.6 %shard_map.57 = (bf16[4,128,640]{2,1,0:T(8,128)(2,1)}, bf16[128,2304]{1,0:T(8,128)(2,1)}, bf16[4,128,640]{2,1,0:T(8,128)(2,1)}, bf16[128,2304]{1,0:T(8,128)(2,1)}, f32[256,256]{1,0:T(8,128)}) custom-call(bf16[128,10240]{1,0:T(8,128)(2,1)} %src.2, bf16[128,4096]{1,0:T(8,128)(2,1)} %samples.1, bf16[1,1024,640]{2,1,0:T(8,128)(2,1)} %grads.3, ...), custom_call_target="tpu_custom_call" | custom-call | tf_op jit(solution)/shard_map/pallas_call | solution.py:87
  15.1 3.2 %collective-permute-done.i1 = bf16[4,128,640]{2,1,0:T(8,128)(2,1)S(1)} collective-permute-done((bf16[4,128,640]{2,1,0:T(8,128)(2,1)}, bf16[4,128,640]{2,1,0:T(8,128)(2,1)S(1)}, u32[]{:S(2)}, u32[]{:S(2)}) %collective-permute-start) | collective-permute-done | bytes 655392 | tf_op jit(solution)/shard_map/ppermute | solution.py:28
  18.3 1.5 %collective-permute-done.1.i2 = bf16[4,128,640]{2,1,0:T(8,128)(2,1)S(1)} collective-permute-done((bf16[4,128,640]{2,1,0:T(8,128)(2,1)}, bf16[4,128,640]{2,1,0:T(8,128)(2,1)S(1)}, u32[]{:S(2)}, u32[]{:S(2)}) %collective-permute-start.1) | collective-permute-done | bytes 655392 | tf_op jit(solution)/shard_map/ppermute | solution.py:28
  19.8 2.6 %collective-permute-start.4 = (bf16[4,128,640]{2,1,0:T(8,128)(2,1)}, bf16[4,128,640]{2,1,0:T(8,128)(2,1)S(1)}, u32[]{:S(2)}, u32[]{:S(2)}) collective-permute-start(bf16[4,128,640]{2,1,0:T(8,128)(2,1)} %get-tuple-element.86), channel_id=1, source_target_pairs={{0,32},{16,48},{32,0},{48,16},{1,33},{17,49},{33,1},{49,17},{2,34}... | collective-permute-start | bytes 1966088 | tf_op jit(solution)/shard_map/ppermute | solution.py:28
  22.4 0.8 collective-permute-done.3.i2.g2
  23.2 2.9 %collective-permute-start.5 = (bf16[128,2304]{1,0:T(8,128)(2,1)}, bf16[128,2304]{1,0:T(8,128)(2,1)S(1)}, u32[]{:S(2)}, u32[]{:S(2)}) collective-permute-start(bf16[128,2304]{1,0:T(8,128)(2,1)} %get-tuple-element.90), channel_id=1, source_target_pairs={{0,2},{1,3},{2,0},{3,1},{4,6},{5,7},{6,4},{7,5},{8,10},{9,11},{10,... | collective-permute-start | bytes 1769480 | tf_op jit(solution)/shard_map/ppermute | solution.py:28
  26.1 11.0 %collective-permute-done.5.i3.g3 = bf16[128,2304]{1,0:T(8,128)(2,1)S(1)} collective-permute-done((bf16[128,2304]{1,0:T(8,128)(2,1)}, bf16[128,2304]{1,0:T(8,128)(2,1)S(1)}, u32[]{:S(2)}, u32[]{:S(2)}) %collective-permute-start.5) | collective-permute-done | bytes 589856 | tf_op jit(solution)/shard_map/ppermute | solution.py:28
  37.1 1.1 copy-done.1
  38.2 0.6 shard_map.58
  38.8 3.5 %shard_map.59 = (f32[4,56,8,128]{3,2,1,0:T(8,128)S(1)}, f32[4,56,8,128]{3,2,1,0:T(8,128)S(1)}) custom-call(bf16[4,128,640]{2,1,0:T(8,128)(2,1)S(1)} %copy-done, bf16[4,128,640]{2,1,0:T(8,128)(2,1)S(1)} %collective-permute-done.i1, bf16[4,128,640]{2,1,0:T(8,128)(2,1)S(1)} %collective-permute-done.1.i2, bf16[4,128,640]{2,1,0:T(8,128)(2,1)S(1)} %collective-permute-done.4.i3), custom_call_target="tpu_custom_call" | custom-call | tf_op jit(solution)/shard_map/pallas_call | solution.py:134
  42.3 3.7 %collective-permute-start.6 = (f32[4,56,8,128]{3,2,1,0:T(8,128)S(1)}, f32[4,56,8,128]{3,2,1,0:T(8,128)S(1)}, u32[]{:S(2)}, u32[]{:S(2)}) collective-permute-start(f32[4,56,8,128]{3,2,1,0:T(8,128)S(1)} %get-tuple-element.98), channel_id=1, source_target_pairs={{0,4},{4,0},{1,5},{5,1},{2,6},{6,2},{3,7},{7,3},{8,12},{12,8},{9,1... | collective-permute-start | bytes 2752520 | tf_op jit(solution)/shard_map/ppermute | solution.py:24
  46.0 2.4 %collective-permute-done.7.a_got = f32[2,36,8,128]{3,2,1,0:T(8,128)S(1)} collective-permute-done((f32[2,36,8,128]{3,2,1,0:T(8,128)S(1)}, f32[2,36,8,128]{3,2,1,0:T(8,128)S(1)}, u32[]{:S(2)}, u32[]{:S(2)}) %collective-permute-start.7) | collective-permute-done | bytes 294944 | tf_op jit(solution)/shard_map/ppermute | solution.py:24
  48.6 1.6 %collective-permute-start.8 = (f32[4,14,8,128]{3,2,1,0:T(8,128)S(1)}, f32[4,14,8,128]{3,2,1,0:T(8,128)S(1)}, u32[]{:S(2)}, u32[]{:S(2)}) collective-permute-start(f32[4,14,8,128]{3,2,1,0:T(8,128)S(1)} %get-tuple-element.102), channel_id=1, source_target_pairs={{0,1},{1,2},{2,3},{3,0},{4,5},{5,6},{6,7},{7,4},{8,9},{9,10},{10,1... | collective-permute-start | bytes 688136 | tf_op jit(solution)/shard_map/ppermute | solution.py:28
  50.2 1.8 %collective-permute-start.9 = (f32[4,14,8,128]{3,2,1,0:T(8,128)S(1)}, f32[4,14,8,128]{3,2,1,0:T(8,128)S(1)}, u32[]{:S(2)}, u32[]{:S(2)}) collective-permute-start(f32[4,14,8,128]{3,2,1,0:T(8,128)S(1)} %get-tuple-element.103), channel_id=1, source_target_pairs={{0,2},{1,3},{2,0},{3,1},{4,6},{5,7},{6,4},{7,5},{8,10},{9,11},{10,... | collective-permute-start | bytes 688136 | tf_op jit(solution)/shard_map/ppermute | solution.py:28
  52.0 1.6 %collective-permute-start.10 = (f32[4,14,8,128]{3,2,1,0:T(8,128)S(1)}, f32[4,14,8,128]{3,2,1,0:T(8,128)S(1)}, u32[]{:S(2)}, u32[]{:S(2)}) collective-permute-start(f32[4,14,8,128]{3,2,1,0:T(8,128)S(1)} %get-tuple-element.104), channel_id=1, source_target_pairs={{0,3},{1,0},{2,1},{3,2},{4,7},{5,4},{6,5},{7,6},{8,11},{9,8},{10,9... | collective-permute-start | bytes 688136 | tf_op jit(solution)/shard_map/ppermute | solution.py:28
  53.9 2.2 %collective-permute-start.12 = (f32[2,9,8,128]{3,2,1,0:T(8,128)S(1)}, f32[2,9,8,128]{3,2,1,0:T(8,128)S(1)}, u32[]{:S(2)}, u32[]{:S(2)}) collective-permute-start(f32[2,9,8,128]{3,2,1,0:T(8,128)S(1)} %get-tuple-element.107), channel_id=1, source_target_pairs={{0,32},{16,48},{32,0},{48,16},{1,33},{17,49},{33,1},{49,17},{2,34}... | collective-permute-start | bytes 221192 | tf_op jit(solution)/shard_map/ppermute | solution.py:28
  56.1 3.0 %collective-permute-done.11.a1 = f32[2,9,8,128]{3,2,1,0:T(8,128)S(1)} collective-permute-done((f32[2,9,8,128]{3,2,1,0:T(8,128)S(1)}, f32[2,9,8,128]{3,2,1,0:T(8,128)S(1)}, u32[]{:S(2)}, u32[]{:S(2)}) %collective-permute-start.11) | collective-permute-done | bytes 73760 | tf_op jit(solution)/shard_map/ppermute | solution.py:28
  59.1 3.5 %collective-permute-done.13.a3 = f32[2,9,8,128]{3,2,1,0:T(8,128)S(1)} collective-permute-done((f32[2,9,8,128]{3,2,1,0:T(8,128)S(1)}, f32[2,9,8,128]{3,2,1,0:T(8,128)S(1)}, u32[]{:S(2)}, u32[]{:S(2)}) %collective-permute-start.13) | collective-permute-done | bytes 73760 | tf_op jit(solution)/shard_map/ppermute | solution.py:28
  62.7 2.4 %collective-permute-start.14 = (f32[37,8,128]{2,1,0:T(8,128)S(1)}, f32[37,8,128]{2,1,0:T(8,128)S(1)}, u32[]{:S(2)}, u32[]{:S(2)}) collective-permute-start(f32[37,8,128]{2,1,0:T(8,128)S(1)} %get-tuple-element.118), channel_id=1, source_target_pairs={{0,8},{8,0},{1,9},{9,1},{2,10},{10,2},{3,11},{11,3},{4,12},{12,4},... | collective-permute-start | bytes 454664 | tf_op jit(solution)/shard_map/ppermute | solution.py:32
  65.1 2.6 %collective-permute-done.14.got = f32[37,8,128]{2,1,0:T(8,128)S(1)} collective-permute-done((f32[37,8,128]{2,1,0:T(8,128)S(1)}, f32[37,8,128]{2,1,0:T(8,128)S(1)}, u32[]{:S(2)}, u32[]{:S(2)}) %collective-permute-start.14) | collective-permute-done | bytes 151584 | tf_op jit(solution)/shard_map/ppermute | solution.py:32
  67.7 3.2 %collective-permute-start.15 = (f32[16,8,128]{2,1,0:T(8,128)S(1)}, f32[16,8,128]{2,1,0:T(8,128)S(1)}, u32[]{:S(2)}, u32[]{:S(2)}) collective-permute-start(f32[16,8,128]{2,1,0:T(8,128)S(1)} %get-tuple-element.120), channel_id=1, source_target_pairs={{0,64},{64,128},{128,192},{192,0},{1,65},{65,129},{129,193},{193,1... | collective-permute-start | bytes 196616 | tf_op jit(solution)/shard_map/ppermute | solution.py:28
  70.9 4.9 %collective-permute-start.16 = (f32[16,8,128]{2,1,0:T(8,128)S(1)}, f32[16,8,128]{2,1,0:T(8,128)S(1)}, u32[]{:S(2)}, u32[]{:S(2)}) collective-permute-start(f32[16,8,128]{2,1,0:T(8,128)S(1)} %get-tuple-element.121), channel_id=1, source_target_pairs={{0,128},{64,192},{128,0},{192,64},{1,129},{65,193},{129,1},{193,65... | collective-permute-start | bytes 196616 | tf_op jit(solution)/shard_map/ppermute | solution.py:28
  75.9 2.4 %collective-permute-start.17 = (f32[16,8,128]{2,1,0:T(8,128)S(1)}, f32[16,8,128]{2,1,0:T(8,128)S(1)}, u32[]{:S(2)}, u32[]{:S(2)}) collective-permute-start(f32[16,8,128]{2,1,0:T(8,128)S(1)} %get-tuple-element.122), channel_id=1, source_target_pairs={{0,192},{64,0},{128,64},{192,128},{1,193},{65,1},{129,65},{193,129... | collective-permute-start | bytes 196616 | tf_op jit(solution)/shard_map/ppermute | solution.py:28
  78.5 2.2 %collective-permute-done.17.p3 = f32[16,8,128]{2,1,0:T(8,128)S(1)} collective-permute-done((f32[16,8,128]{2,1,0:T(8,128)S(1)}, f32[16,8,128]{2,1,0:T(8,128)S(1)}, u32[]{:S(2)}, u32[]{:S(2)}) %collective-permute-start.17) | collective-permute-done | bytes 65568 | tf_op jit(solution)/shard_map/ppermute | solution.py:28
  80.7 1.3 %collective-permute-start.24 = (f32[9,8,128]{2,1,0:T(8,128)S(1)}, f32[9,8,128]{2,1,0:T(8,128)S(1)}, u32[]{:S(2)}, u32[]{:S(2)}) collective-permute-start(f32[9,8,128]{2,1,0:T(8,128)S(1)} %get-tuple-element.124.p0), channel_id=1, source_target_pairs={{0,48},{16,0},{32,16},{48,32},{1,49},{17,1},{33,17},{49,33},{2,50}... | collective-permute-start | bytes 110600 | tf_op jit(solution)/shard_map/ppermute | solution.py:28
  82.5 0.6 collective-permute-start.22
  83.1 0.7 collective-permute-start.18
  83.9 2.0 %collective-permute-done.18.got = f32[7,8,128]{2,1,0:T(8,128)S(1)} collective-permute-done((f32[7,8,128]{2,1,0:T(8,128)S(1)}, f32[7,8,128]{2,1,0:T(8,128)S(1)}, u32[]{:S(2)}, u32[]{:S(2)}) %collective-permute-start.18) | collective-permute-done | bytes 28704 | tf_op jit(solution)/shard_map/ppermute | solution.py:32
  85.9 4.6 %collective-permute-start.21 = (f32[14,8,128]{2,1,0:T(8,128)S(1)}, f32[14,8,128]{2,1,0:T(8,128)S(1)}, u32[]{:S(2)}, u32[]{:S(2)}) collective-permute-start(f32[14,8,128]{2,1,0:T(8,128)S(1)} %shard_map.64.p0), channel_id=1, source_target_pairs={{0,3},{1,0},{2,1},{3,2},{4,7},{5,4},{6,5},{7,6},{8,11},{9,8},{10,9... | collective-permute-start | bytes 172040 | tf_op jit(solution)/shard_map/ppermute | solution.py:28
  91.2 4.0 %shard_map.65.left = f32[2,256,320]{2,1,0:T(8,128)S(1)} custom-call(f32[9,8,128]{2,1,0:T(8,128)S(1)} %get-tuple-element.124.p0, f32[9,8,128]{2,1,0:T(8,128)S(1)} %collective-permute-done.22.p1, f32[9,8,128]{2,1,0:T(8,128)S(1)} %collective-permute-done.23.p2, f32[9,8,128]{2,1,0:T(8,128)S(1)} %collective-permute-done.24.p3, f32[256,256]{1,0:T(8,128)S(1)} %copy-done.4, ...), custom_call_target="tpu_custom_call" | custom-call | flops 2500000000 | bytes 2000000 | tf_op jit(solution)/shard_map/pallas_call | solution.py:296
  95.7 6.5 %shard_map.66 = (bf16[2,320,384]{2,1,0:T(8,128)(2,1)S(1)}, bf16[128,640]{1,0:T(8,128)(2,1)S(1)}) custom-call(f32[14,8,128]{2,1,0:T(8,128)S(1)} %shard_map.64.p0, f32[14,8,128]{2,1,0:T(8,128)S(1)} %collective-permute-done.19.p1, f32[14,8,128]{2,1,0:T(8,128)S(1)} %collective-permute-done.20.p2, f32[14,8,128]{2,1,0:T(8,128)S(1)} %collective-permute-done.21.p3, ...), custom_call_target="tpu_custom_call" | custom-call | flops 6000000000 | bytes 3000000 | tf_op jit(solution)/shard_map/pallas_call | solution.py:396
  102.1 6.0 %collective-permute-start.28 = (bf16[2,320,384]{2,1,0:T(8,128)(2,1)S(1)}, bf16[2,320,384]{2,1,0:T(8,128)(2,1)S(1)}, u32[]{:S(2)}, u32[]{:S(2)}) collective-permute-start(bf16[2,320,384]{2,1,0:T(8,128)(2,1)S(1)} %get-tuple-element.132), channel_id=1, source_target_pairs={{0,4},{4,0},{1,5},{5,1},{2,6},{6,2},{3,7},{7,3},{8,12},{12,8},{9,1... | collective-permute-start | bytes 1474568 | tf_op jit(solution)/shard_map/ppermute | solution.py:24
  108.2 1.7 %collective-permute-start.27 = (bf16[128,640]{1,0:T(8,128)(2,1)S(1)}, bf16[128,640]{1,0:T(8,128)(2,1)S(1)}, u32[]{:S(2)}, u32[]{:S(2)}) collective-permute-start(bf16[128,640]{1,0:T(8,128)(2,1)S(1)} %get-tuple-element.131.refs_0_), channel_id=1, source_target_pairs={{0,3},{1,0},{2,1},{3,2},{4,7},{5,4},{6,5},{7,6},{8,11},{9,8},{10,9... | collective-permute-start | bytes 491528 | tf_op jit(solution)/shard_map/ppermute | solution.py:28
  109.9 1.0 collective-permute-start.26
  110.9 0.6 shard_map.67.refs_4_
  111.5 2.7 %collective-permute-start.31 = (bf16[128,640]{1,0:T(8,128)(2,1)S(1)}, bf16[128,640]{1,0:T(8,128)(2,1)S(1)}, u32[]{:S(2)}, u32[]{:S(2)}) collective-permute-start(bf16[128,640]{1,0:T(8,128)(2,1)S(1)} %shard_map.67.refs_4_), channel_id=1, source_target_pairs={{0,3},{1,0},{2,1},{3,2},{4,7},{5,4},{6,5},{7,6},{8,11},{9,8},{10,9... | collective-permute-start | bytes 491528 | tf_op jit(solution)/shard_map/ppermute | solution.py:28
  114.2 0.8 collective-permute-start.30
  115.0 1.9 %collective-permute-done.26.refs_2_ = bf16[128,640]{1,0:T(8,128)(2,1)S(1)} collective-permute-done((bf16[128,640]{1,0:T(8,128)(2,1)S(1)}, bf16[128,640]{1,0:T(8,128)(2,1)S(1)}, u32[]{:S(2)}, u32[]{:S(2)}) %collective-permute-start.26) | collective-permute-done | bytes 163872 | tf_op jit(solution)/shard_map/ppermute | solution.py:28
  116.9 4.8 %collective-permute-done.25.refs_1_ = bf16[128,640]{1,0:T(8,128)(2,1)S(1)} collective-permute-done((bf16[128,640]{1,0:T(8,128)(2,1)S(1)}, bf16[128,640]{1,0:T(8,128)(2,1)S(1)}, u32[]{:S(2)}, u32[]{:S(2)}) %collective-permute-start.25) | collective-permute-done | bytes 163872 | tf_op jit(solution)/shard_map/ppermute | solution.py:28
  121.7 2.3 %collective-permute-done.30.refs_6_ = bf16[128,640]{1,0:T(8,128)(2,1)S(1)} collective-permute-done((bf16[128,640]{1,0:T(8,128)(2,1)S(1)}, bf16[128,640]{1,0:T(8,128)(2,1)S(1)}, u32[]{:S(2)}, u32[]{:S(2)}) %collective-permute-start.30) | collective-permute-done | bytes 163872 | tf_op jit(solution)/shard_map/ppermute | solution.py:28
  123.9 4.0 %collective-permute-done.29.refs_5_ = bf16[128,640]{1,0:T(8,128)(2,1)S(1)} collective-permute-done((bf16[128,640]{1,0:T(8,128)(2,1)S(1)}, bf16[128,640]{1,0:T(8,128)(2,1)S(1)}, u32[]{:S(2)}, u32[]{:S(2)}) %collective-permute-start.29) | collective-permute-done | bytes 163872 | tf_op jit(solution)/shard_map/ppermute | solution.py:28
  127.9 1.3 %shard_map.68 = bf16[1024,640]{1,0:T(8,128)(2,1)} custom-call(bf16[128,640]{1,0:T(8,128)(2,1)S(1)} %get-tuple-element.131.refs_0_, bf16[128,640]{1,0:T(8,128)(2,1)S(1)} %collective-permute-done.25.refs_1_, bf16[128,640]{1,0:T(8,128)(2,1)S(1)} %collective-permute-done.26.refs_2_, bf16[128,640]{1,0:T(8,128)(2,1)S(1)} %collective-permute-done.27.refs_3_, ...), custom_call_target="tpu_custom_call" | custom-call | tf_op jit(solution)/shard_map/pallas_call | solution.py:181
  (40 shorter events, 2.4 us)
Async XLA Ops:
  2.5 15.8 %collective-permute-start = (bf16[4,128,640]{2,1,0:T(8,128)(2,1)}, bf16[4,128,640]{2,1,0:T(8,128)(2,1)S(1)}, u32[]{:S(2)}, u32[]{:S(2)}) collective-permute-start(bf16[4,128,640]{2,1,0:T(8,128)(2,1)} %get-tuple-element.76), channel_id=1, source_target_pairs={{0,16},{16,32},{32,48},{48,0},{1,17},{17,33},{33,49},{49,1},{2,18}... | collective-permute-start | bytes 1966088 | tf_op jit(solution)/shard_map/ppermute | solution.py:28
  4.7 15.1 %collective-permute-start.1 = (bf16[4,128,640]{2,1,0:T(8,128)(2,1)}, bf16[4,128,640]{2,1,0:T(8,128)(2,1)S(1)}, u32[]{:S(2)}, u32[]{:S(2)}) collective-permute-start(bf16[4,128,640]{2,1,0:T(8,128)(2,1)} %get-tuple-element.77), channel_id=1, source_target_pairs={{0,48},{16,0},{32,16},{48,32},{1,49},{17,1},{33,17},{49,33},{2,50}... | collective-permute-start | bytes 1966088 | tf_op jit(solution)/shard_map/ppermute | solution.py:28
  8.5 13.9 %collective-permute-start.2 = (bf16[128,2304]{1,0:T(8,128)(2,1)}, bf16[128,2304]{1,0:T(8,128)(2,1)S(1)}, u32[]{:S(2)}, u32[]{:S(2)}) collective-permute-start(bf16[128,2304]{1,0:T(8,128)(2,1)} %get-tuple-element.81), channel_id=1, source_target_pairs={{0,1},{1,2},{2,3},{3,0},{4,5},{5,6},{6,7},{7,4},{8,9},{9,10},{10,1... | collective-permute-start | bytes 1769480 | tf_op jit(solution)/shard_map/ppermute | solution.py:28
  10.0 13.3 %collective-permute-start.3 = (bf16[128,2304]{1,0:T(8,128)(2,1)}, bf16[128,2304]{1,0:T(8,128)(2,1)S(1)}, u32[]{:S(2)}, u32[]{:S(2)}) collective-permute-start(bf16[128,2304]{1,0:T(8,128)(2,1)} %get-tuple-element.82), channel_id=1, source_target_pairs={{0,3},{1,0},{2,1},{3,2},{4,7},{5,4},{6,5},{7,6},{8,11},{9,8},{10,9... | collective-permute-start | bytes 1769480 | tf_op jit(solution)/shard_map/ppermute | solution.py:28
  15.1 23.7 %copy-start = (bf16[4,128,640]{2,1,0:T(8,128)(2,1)S(1)}, bf16[4,128,640]{2,1,0:T(8,128)(2,1)}, u32[]{:S(2)}) copy-start(bf16[4,128,640]{2,1,0:T(8,128)(2,1)} %get-tuple-element.93.i0) | copy-start | bytes 1966084
  19.8 19.0 %collective-permute-start.4 = (bf16[4,128,640]{2,1,0:T(8,128)(2,1)}, bf16[4,128,640]{2,1,0:T(8,128)(2,1)S(1)}, u32[]{:S(2)}, u32[]{:S(2)}) collective-permute-start(bf16[4,128,640]{2,1,0:T(8,128)(2,1)} %get-tuple-element.86), channel_id=1, source_target_pairs={{0,32},{16,48},{32,0},{48,16},{1,33},{17,49},{33,1},{49,17},{2,34}... | collective-permute-start | bytes 1966088 | tf_op jit(solution)/shard_map/ppermute | solution.py:28
  23.2 13.8 %collective-permute-start.5 = (bf16[128,2304]{1,0:T(8,128)(2,1)}, bf16[128,2304]{1,0:T(8,128)(2,1)S(1)}, u32[]{:S(2)}, u32[]{:S(2)}) collective-permute-start(bf16[128,2304]{1,0:T(8,128)(2,1)} %get-tuple-element.90), channel_id=1, source_target_pairs={{0,2},{1,3},{2,0},{3,1},{4,6},{5,7},{6,4},{7,5},{8,10},{9,11},{10,... | collective-permute-start | bytes 1769480 | tf_op jit(solution)/shard_map/ppermute | solution.py:28
  37.1 1.1 copy-start.1
  42.2 49.0 %copy-start.2 = (bf16[128,2304]{1,0:T(8,128)(2,1)S(1)}, bf16[128,2304]{1,0:T(8,128)(2,1)}, u32[]{:S(2)}) copy-start(bf16[128,2304]{1,0:T(8,128)(2,1)} %get-tuple-element.87.i0.g0) | copy-start | bytes 1769476
  42.3 49.0 %copy-start.4 = (f32[256,256]{1,0:T(8,128)S(1)}, f32[256,256]{1,0:T(8,128)}, u32[]{:S(2)}) copy-start(f32[256,256]{1,0:T(8,128)} %get-tuple-element.125.running) | copy-start | bytes 786436
  42.3 6.2 %collective-permute-start.6 = (f32[4,56,8,128]{3,2,1,0:T(8,128)S(1)}, f32[4,56,8,128]{3,2,1,0:T(8,128)S(1)}, u32[]{:S(2)}, u32[]{:S(2)}) collective-permute-start(f32[4,56,8,128]{3,2,1,0:T(8,128)S(1)} %get-tuple-element.98), channel_id=1, source_target_pairs={{0,4},{4,0},{1,5},{5,1},{2,6},{6,2},{3,7},{7,3},{8,12},{12,8},{9,1... | collective-permute-start | bytes 2752520 | tf_op jit(solution)/shard_map/ppermute | solution.py:24
  45.9 2.5 %collective-permute-start.7 = (f32[2,36,8,128]{3,2,1,0:T(8,128)S(1)}, f32[2,36,8,128]{3,2,1,0:T(8,128)S(1)}, u32[]{:S(2)}, u32[]{:S(2)}) collective-permute-start(f32[2,36,8,128]{3,2,1,0:T(8,128)S(1)} %get-tuple-element.100), channel_id=1, source_target_pairs={{0,4},{4,0},{1,5},{5,1},{2,6},{6,2},{3,7},{7,3},{8,12},{12,8},{9,1... | collective-permute-start | bytes 884744 | tf_op jit(solution)/shard_map/ppermute | solution.py:24
  48.6 14.0 %collective-permute-start.8 = (f32[4,14,8,128]{3,2,1,0:T(8,128)S(1)}, f32[4,14,8,128]{3,2,1,0:T(8,128)S(1)}, u32[]{:S(2)}, u32[]{:S(2)}) collective-permute-start(f32[4,14,8,128]{3,2,1,0:T(8,128)S(1)} %get-tuple-element.102), channel_id=1, source_target_pairs={{0,1},{1,2},{2,3},{3,0},{4,5},{5,6},{6,7},{7,4},{8,9},{9,10},{10,1... | collective-permute-start | bytes 688136 | tf_op jit(solution)/shard_map/ppermute | solution.py:28
  50.2 12.4 %collective-permute-start.9 = (f32[4,14,8,128]{3,2,1,0:T(8,128)S(1)}, f32[4,14,8,128]{3,2,1,0:T(8,128)S(1)}, u32[]{:S(2)}, u32[]{:S(2)}) collective-permute-start(f32[4,14,8,128]{3,2,1,0:T(8,128)S(1)} %get-tuple-element.103), channel_id=1, source_target_pairs={{0,2},{1,3},{2,0},{3,1},{4,6},{5,7},{6,4},{7,5},{8,10},{9,11},{10,... | collective-permute-start | bytes 688136 | tf_op jit(solution)/shard_map/ppermute | solution.py:28
  52.0 10.6 %collective-permute-start.10 = (f32[4,14,8,128]{3,2,1,0:T(8,128)S(1)}, f32[4,14,8,128]{3,2,1,0:T(8,128)S(1)}, u32[]{:S(2)}, u32[]{:S(2)}) collective-permute-start(f32[4,14,8,128]{3,2,1,0:T(8,128)S(1)} %get-tuple-element.104), channel_id=1, source_target_pairs={{0,3},{1,0},{2,1},{3,2},{4,7},{5,4},{6,5},{7,6},{8,11},{9,8},{10,9... | collective-permute-start | bytes 688136 | tf_op jit(solution)/shard_map/ppermute | solution.py:28
  53.6 5.5 %collective-permute-start.11 = (f32[2,9,8,128]{3,2,1,0:T(8,128)S(1)}, f32[2,9,8,128]{3,2,1,0:T(8,128)S(1)}, u32[]{:S(2)}, u32[]{:S(2)}) collective-permute-start(f32[2,9,8,128]{3,2,1,0:T(8,128)S(1)} %get-tuple-element.106), channel_id=1, source_target_pairs={{0,16},{16,32},{32,48},{48,0},{1,17},{17,33},{33,49},{49,1},{2,18}... | collective-permute-start | bytes 221192 | tf_op jit(solution)/shard_map/ppermute | solution.py:28
  53.9 5.3 %collective-permute-start.12 = (f32[2,9,8,128]{3,2,1,0:T(8,128)S(1)}, f32[2,9,8,128]{3,2,1,0:T(8,128)S(1)}, u32[]{:S(2)}, u32[]{:S(2)}) collective-permute-start(f32[2,9,8,128]{3,2,1,0:T(8,128)S(1)} %get-tuple-element.107), channel_id=1, source_target_pairs={{0,32},{16,48},{32,0},{48,16},{1,33},{17,49},{33,1},{49,17},{2,34}... | collective-permute-start | bytes 221192 | tf_op jit(solution)/shard_map/ppermute | solution.py:28
  59.1 3.5 %collective-permute-start.13 = (f32[2,9,8,128]{3,2,1,0:T(8,128)S(1)}, f32[2,9,8,128]{3,2,1,0:T(8,128)S(1)}, u32[]{:S(2)}, u32[]{:S(2)}) collective-permute-start(f32[2,9,8,128]{3,2,1,0:T(8,128)S(1)} %get-tuple-element.108), channel_id=1, source_target_pairs={{0,48},{16,0},{32,16},{48,32},{1,49},{17,1},{33,17},{49,33},{2,50}... | collective-permute-start | bytes 221192 | tf_op jit(solution)/shard_map/ppermute | solution.py:28
  62.7 4.9 %collective-permute-start.14 = (f32[37,8,128]{2,1,0:T(8,128)S(1)}, f32[37,8,128]{2,1,0:T(8,128)S(1)}, u32[]{:S(2)}, u32[]{:S(2)}) collective-permute-start(f32[37,8,128]{2,1,0:T(8,128)S(1)} %get-tuple-element.118), channel_id=1, source_target_pairs={{0,8},{8,0},{1,9},{9,1},{2,10},{10,2},{3,11},{11,3},{4,12},{12,4},... | collective-permute-start | bytes 454664 | tf_op jit(solution)/shard_map/ppermute | solution.py:32
  67.7 10.6 %collective-permute-start.15 = (f32[16,8,128]{2,1,0:T(8,128)S(1)}, f32[16,8,128]{2,1,0:T(8,128)S(1)}, u32[]{:S(2)}, u32[]{:S(2)}) collective-permute-start(f32[16,8,128]{2,1,0:T(8,128)S(1)} %get-tuple-element.120), channel_id=1, source_target_pairs={{0,64},{64,128},{128,192},{192,0},{1,65},{65,129},{129,193},{193,1... | collective-permute-start | bytes 196616 | tf_op jit(solution)/shard_map/ppermute | solution.py:28
  70.9 7.6 %collective-permute-start.16 = (f32[16,8,128]{2,1,0:T(8,128)S(1)}, f32[16,8,128]{2,1,0:T(8,128)S(1)}, u32[]{:S(2)}, u32[]{:S(2)}) collective-permute-start(f32[16,8,128]{2,1,0:T(8,128)S(1)} %get-tuple-element.121), channel_id=1, source_target_pairs={{0,128},{64,192},{128,0},{192,64},{1,129},{65,193},{129,1},{193,65... | collective-permute-start | bytes 196616 | tf_op jit(solution)/shard_map/ppermute | solution.py:28
  75.9 4.8 %collective-permute-start.17 = (f32[16,8,128]{2,1,0:T(8,128)S(1)}, f32[16,8,128]{2,1,0:T(8,128)S(1)}, u32[]{:S(2)}, u32[]{:S(2)}) collective-permute-start(f32[16,8,128]{2,1,0:T(8,128)S(1)} %get-tuple-element.122), channel_id=1, source_target_pairs={{0,192},{64,0},{128,64},{192,128},{1,193},{65,1},{129,65},{193,129... | collective-permute-start | bytes 196616 | tf_op jit(solution)/shard_map/ppermute | solution.py:28
  80.7 10.2 %collective-permute-start.24 = (f32[9,8,128]{2,1,0:T(8,128)S(1)}, f32[9,8,128]{2,1,0:T(8,128)S(1)}, u32[]{:S(2)}, u32[]{:S(2)}) collective-permute-start(f32[9,8,128]{2,1,0:T(8,128)S(1)} %get-tuple-element.124.p0), channel_id=1, source_target_pairs={{0,48},{16,0},{32,16},{48,32},{1,49},{17,1},{33,17},{49,33},{2,50}... | collective-permute-start | bytes 110600 | tf_op jit(solution)/shard_map/ppermute | solution.py:28
  82.0 9.2 %collective-permute-start.23 = (f32[9,8,128]{2,1,0:T(8,128)S(1)}, f32[9,8,128]{2,1,0:T(8,128)S(1)}, u32[]{:S(2)}, u32[]{:S(2)}) collective-permute-start(f32[9,8,128]{2,1,0:T(8,128)S(1)} %get-tuple-element.124.p0), channel_id=1, source_target_pairs={{0,32},{16,48},{32,0},{48,16},{1,33},{17,49},{33,1},{49,17},{2,34}... | collective-permute-start | bytes 110600 | tf_op jit(solution)/shard_map/ppermute | solution.py:28
  82.5 8.7 %collective-permute-start.22 = (f32[9,8,128]{2,1,0:T(8,128)S(1)}, f32[9,8,128]{2,1,0:T(8,128)S(1)}, u32[]{:S(2)}, u32[]{:S(2)}) collective-permute-start(f32[9,8,128]{2,1,0:T(8,128)S(1)} %get-tuple-element.124.p0), channel_id=1, source_target_pairs={{0,16},{16,32},{32,48},{48,0},{1,17},{17,33},{33,49},{49,1},{2,18}... | collective-permute-start | bytes 110600 | tf_op jit(solution)/shard_map/ppermute | solution.py:28
  83.1 2.7 %collective-permute-start.18 = (f32[7,8,128]{2,1,0:T(8,128)S(1)}, f32[7,8,128]{2,1,0:T(8,128)S(1)}, u32[]{:S(2)}, u32[]{:S(2)}) collective-permute-start(f32[7,8,128]{2,1,0:T(8,128)S(1)} %get-tuple-element.123.own), channel_id=1, source_target_pairs={{0,8},{8,0},{1,9},{9,1},{2,10},{10,2},{3,11},{11,3},{4,12},{12,4},... | collective-permute-start | bytes 86024 | tf_op jit(solution)/shard_map/ppermute | solution.py:32
  85.9 9.4 %collective-permute-start.21 = (f32[14,8,128]{2,1,0:T(8,128)S(1)}, f32[14,8,128]{2,1,0:T(8,128)S(1)}, u32[]{:S(2)}, u32[]{:S(2)}) collective-permute-start(f32[14,8,128]{2,1,0:T(8,128)S(1)} %shard_map.64.p0), channel_id=1, source_target_pairs={{0,3},{1,0},{2,1},{3,2},{4,7},{5,4},{6,5},{7,6},{8,11},{9,8},{10,9... | collective-permute-start | bytes 172040 | tf_op jit(solution)/shard_map/ppermute | solution.py:28
  90.5 4.8 %collective-permute-start.20 = (f32[14,8,128]{2,1,0:T(8,128)S(1)}, f32[14,8,128]{2,1,0:T(8,128)S(1)}, u32[]{:S(2)}, u32[]{:S(2)}) collective-permute-start(f32[14,8,128]{2,1,0:T(8,128)S(1)} %shard_map.64.p0), channel_id=1, source_target_pairs={{0,2},{1,3},{2,0},{3,1},{4,6},{5,7},{6,4},{7,5},{8,10},{9,11},{10,... | collective-permute-start | bytes 172040 | tf_op jit(solution)/shard_map/ppermute | solution.py:28
  90.9 4.8 %collective-permute-start.19 = (f32[14,8,128]{2,1,0:T(8,128)S(1)}, f32[14,8,128]{2,1,0:T(8,128)S(1)}, u32[]{:S(2)}, u32[]{:S(2)}) collective-permute-start(f32[14,8,128]{2,1,0:T(8,128)S(1)} %shard_map.64.p0), channel_id=1, source_target_pairs={{0,1},{1,2},{2,3},{3,0},{4,5},{5,6},{6,7},{7,4},{8,9},{9,10},{10,1... | collective-permute-start | bytes 172040 | tf_op jit(solution)/shard_map/ppermute | solution.py:28
  91.2 4.4 %copy-start.3 = (f32[2,320,320]{2,1,0:T(8,128)S(1)}, f32[2,320,320]{2,1,0:T(8,128)}, u32[]{:S(2)}) copy-start(f32[2,320,320]{2,1,0:T(8,128)} %running.3) | copy-start | bytes 2457604
  102.1 8.8 %collective-permute-start.28 = (bf16[2,320,384]{2,1,0:T(8,128)(2,1)S(1)}, bf16[2,320,384]{2,1,0:T(8,128)(2,1)S(1)}, u32[]{:S(2)}, u32[]{:S(2)}) collective-permute-start(bf16[2,320,384]{2,1,0:T(8,128)(2,1)S(1)} %get-tuple-element.132), channel_id=1, source_target_pairs={{0,4},{4,0},{1,5},{5,1},{2,6},{6,2},{3,7},{7,3},{8,12},{12,8},{9,1... | collective-permute-start | bytes 1474568 | tf_op jit(solution)/shard_map/ppermute | solution.py:24
  108.2 6.8 %collective-permute-start.27 = (bf16[128,640]{1,0:T(8,128)(2,1)S(1)}, bf16[128,640]{1,0:T(8,128)(2,1)S(1)}, u32[]{:S(2)}, u32[]{:S(2)}) collective-permute-start(bf16[128,640]{1,0:T(8,128)(2,1)S(1)} %get-tuple-element.131.refs_0_), channel_id=1, source_target_pairs={{0,3},{1,0},{2,1},{3,2},{4,7},{5,4},{6,5},{7,6},{8,11},{9,8},{10,9... | collective-permute-start | bytes 491528 | tf_op jit(solution)/shard_map/ppermute | solution.py:28
  109.9 7.0 %collective-permute-start.26 = (bf16[128,640]{1,0:T(8,128)(2,1)S(1)}, bf16[128,640]{1,0:T(8,128)(2,1)S(1)}, u32[]{:S(2)}, u32[]{:S(2)}) collective-permute-start(bf16[128,640]{1,0:T(8,128)(2,1)S(1)} %get-tuple-element.131.refs_0_), channel_id=1, source_target_pairs={{0,2},{1,3},{2,0},{3,1},{4,6},{5,7},{6,4},{7,5},{8,10},{9,11},{10,... | collective-permute-start | bytes 491528 | tf_op jit(solution)/shard_map/ppermute | solution.py:28
  110.9 10.8 %collective-permute-start.25 = (bf16[128,640]{1,0:T(8,128)(2,1)S(1)}, bf16[128,640]{1,0:T(8,128)(2,1)S(1)}, u32[]{:S(2)}, u32[]{:S(2)}) collective-permute-start(bf16[128,640]{1,0:T(8,128)(2,1)S(1)} %get-tuple-element.131.refs_0_), channel_id=1, source_target_pairs={{0,1},{1,2},{2,3},{3,0},{4,5},{5,6},{6,7},{7,4},{8,9},{9,10},{10,1... | collective-permute-start | bytes 491528 | tf_op jit(solution)/shard_map/ppermute | solution.py:28
  111.5 10.2 %collective-permute-start.31 = (bf16[128,640]{1,0:T(8,128)(2,1)S(1)}, bf16[128,640]{1,0:T(8,128)(2,1)S(1)}, u32[]{:S(2)}, u32[]{:S(2)}) collective-permute-start(bf16[128,640]{1,0:T(8,128)(2,1)S(1)} %shard_map.67.refs_4_), channel_id=1, source_target_pairs={{0,3},{1,0},{2,1},{3,2},{4,7},{5,4},{6,5},{7,6},{8,11},{9,8},{10,9... | collective-permute-start | bytes 491528 | tf_op jit(solution)/shard_map/ppermute | solution.py:28
  114.2 9.7 %collective-permute-start.30 = (bf16[128,640]{1,0:T(8,128)(2,1)S(1)}, bf16[128,640]{1,0:T(8,128)(2,1)S(1)}, u32[]{:S(2)}, u32[]{:S(2)}) collective-permute-start(bf16[128,640]{1,0:T(8,128)(2,1)S(1)} %shard_map.67.refs_4_), channel_id=1, source_target_pairs={{0,2},{1,3},{2,0},{3,1},{4,6},{5,7},{6,4},{7,5},{8,10},{9,11},{10,... | collective-permute-start | bytes 491528 | tf_op jit(solution)/shard_map/ppermute | solution.py:28
  115.0 12.9 %collective-permute-start.29 = (bf16[128,640]{1,0:T(8,128)(2,1)S(1)}, bf16[128,640]{1,0:T(8,128)(2,1)S(1)}, u32[]{:S(2)}, u32[]{:S(2)}) collective-permute-start(bf16[128,640]{1,0:T(8,128)(2,1)S(1)} %shard_map.67.refs_4_), channel_id=1, source_target_pairs={{0,1},{1,2},{2,3},{3,0},{4,5},{5,6},{6,7},{7,4},{8,9},{9,10},{10,1... | collective-permute-start | bytes 491528 | tf_op jit(solution)/shard_map/ppermute | solution.py:28

commit v5 on v4

--- a/solution.py
+++ b/solution.py
@@ -118,37 +118,33 @@
     tiles[n, 48:56] = jnp.concatenate([cov[256:BG, 256:BG], beside], axis=1).reshape(8, 8, 128)
 
 
-def g_cov_kernel(i0, i1, i2, i3, own, other, rows, tiles):
+def g_cov_kernel(i0, own_before, other_before, own, other, rows, tiles):
     c = lax.axis_index("c")
-    for s, ref in enumerate((i0, i1, i2, i3)):
-        rows[s * 128:(s + 1) * 128, :] = ref[0]
-    fold_block(gram(rows[:, 0:BGP]), tiles, 0)
-    fold_block(gram(rows[:, 2 * BG - BGP:2 * BG])[BGP - BG:, BGP - BG:], tiles, 1)
-    own[0] = tiles[c]
-    other[0] = tiles[1 - c]
-
-
-def g_cov(chunks):
-    spec = pl.BlockSpec((1, 128, 2 * BG), lambda q: (q, 0, 0))
-    out = pl.BlockSpec((1, 56, 8, 128), lambda q: (q, 0, 0, 0))
-    return pl.pallas_call(
-        g_cov_kernel,
-        grid=(4,),
-        out_shape=[jax.ShapeDtypeStruct((4, 56, 8, 128), jnp.float32)] * 2,
-        in_specs=[spec] * 4,
-        out_specs=[out] * 2,
-        scratch_shapes=[pltpu.VMEM((512, 2 * BG), jnp.bfloat16), pltpu.VMEM((2, G_TILES, 8, 128), jnp.float32)],
-        compiler_params=pltpu.CompilerParams(vmem_limit_bytes=16 << 20),
-    )(*chunks)
-
-
-def a_cov_kernel(i0, i1, i2, i3, own, other, rows, tiles):
+    for q in range(4):
+        rows[q] = i0[q]
+        fold_block(gram(rows[q, :, 0:BGP]), tiles.at[q], 0)
+        fold_block(gram(rows[q, :, 2 * BG - BGP:2 * BG])[BGP - BG:, BGP - BG:], tiles.at[q], 1)
+        own[q] = tiles[q, c] + own_before[q]
+        other[q] = tiles[q, 1 - c] + other_before[q]
+
+
+def g_cov_first_kernel(i0, i1, i2, own, other, rows, tiles):
     c = lax.axis_index("c")
+    for q in range(4):
+        for s, ref in enumerate((i0, i1, i2)):
+            rows[q, s * 128:(s + 1) * 128, :] = ref[q]
+        fold_block(gram(rows[q, :, 0:BGP]), tiles.at[q], 0)
+        fold_block(gram(rows[q, :, 2 * BG - BGP:2 * BG])[BGP - BG:, BGP - BG:], tiles.at[q], 1)
+        own[q] = tiles[q, c]
+        other[q] = tiles[q, 1 - c]
+
+
+def a_cov_blocks(chunks, rows, tiles):
     r, k = grid_of(128)
     for zl in range(2):
         for core in range(2):
             q = zl * 2 + core
-            for s, ref in enumerate((i0, i1, i2, i3)):
+            for s, ref in enumerate(chunks):
                 rows[s * 128:(s + 1) * 128, :] = ref[:, q * BA:(q + 1) * BA]
             cov = gram(rows[...])
             corner = cov[128:, 128:]
@@ -158,19 +154,49 @@
             tiles[core, 16:32] = fold.reshape(16, 8, 128)
             tiles[core, 32] = jnp.broadcast_to(diag, (8, 128))
             tiles[core, 33:] = jnp.zeros((A_TILES - 33, 8, 128), jnp.float32)
+        yield zl
+
+
+def a_cov_first_kernel(i0, i1, i2, own, other, rows, tiles):
+    c = lax.axis_index("c")
+    for zl in a_cov_blocks((i0, i1, i2), rows, tiles):
         own[zl] = tiles[c]
         other[zl] = tiles[1 - c]
 
 
-def a_cov(chunks):
+def a_cov_kernel(i0, own_before, other_before, own, other, rows, tiles):
+    c = lax.axis_index("c")
+    for zl in a_cov_blocks((i0,), rows, tiles):
+        own[zl] = tiles[c] + own_before[zl]
+        other[zl] = tiles[1 - c] + other_before[zl]
+
+
+def cov(kernel, out_dims, rows, tiles, *args):
     return pl.pallas_call(
-        a_cov_kernel,
-        out_shape=[jax.ShapeDtypeStruct((2, A_TILES, 8, 128), jnp.float32)] * 2,
-        in_specs=[VMEM] * 4,
+        kernel,
+        out_shape=[jax.ShapeDtypeStruct((*out_dims, 8, 128), jnp.float32)] * 2,
+        in_specs=[VMEM] * len(args),
         out_specs=[VMEM] * 2,
-        scratch_shapes=[pltpu.VMEM((512, BA), jnp.bfloat16), pltpu.VMEM((2, A_TILES, 8, 128), jnp.float32)],
+        scratch_shapes=[pltpu.VMEM(rows, jnp.bfloat16), pltpu.VMEM((*tiles, 8, 128), jnp.float32)],
         compiler_params=pltpu.CompilerParams(vmem_limit_bytes=16 << 20),
-    )(*chunks)
+        cost_estimate=pl.CostEstimate(flops=1_500_000_000, bytes_accessed=4_000_000, transcendentals=0),
+    )(*args)
+
+
+def g_cov_first(chunks):
+    return cov(g_cov_first_kernel, (4, 56), (4, 384, 2 * BG), (4, 2, G_TILES), *chunks)
+
+
+def g_cov(chunk, before):
+    return cov(g_cov_kernel, (4, 56), (4, 128, 2 * BG), (4, 2, G_TILES), chunk, *before)
+
+
+def a_cov_first(chunks):
+    return cov(a_cov_first_kernel, (2, A_TILES), (384, BA), (2, A_TILES), *chunks)
+
+
+def a_cov(chunk, before):
+    return cov(a_cov_kernel, (2, A_TILES), (128, BA), (2, A_TILES), chunk, *before)
 
 
 def tile_shape(*dims):
@@ -442,12 +468,13 @@
     y_in = [send(near_y[0], "y", 1), send(near_y[1], "y", 3)]
     g_in, far_x = lax.optimization_barrier((g_in, far_x))
     g_in, y_in, far_y = lax.optimization_barrier((g_in, y_in, far_y))
-    g_in = [own_x, *g_in, send(far_x, "x", 2)]
-    y_in = [own_y, *y_in, send(far_y, "y", 2)]
-
-    a_own, a_other = a_cov(y_in)
-    g_in, a_own, a_other = lax.optimization_barrier((g_in, a_own, a_other))
-    g_own, g_other = g_cov(g_in)
+    far_x, far_y = send(far_x, "x", 2), send(far_y, "y", 2)
+
+    g_before = g_cov_first([own_x, *g_in])
+    a_before = a_cov_first([own_y, *y_in])
+    a_own, a_other = a_cov(far_y, a_before)
+    far_x, a_own, a_other = lax.optimization_barrier((far_x, a_own, a_other))
+    g_own, g_other = g_cov(far_x, g_before)
     cut = local(
         cores_kernel, [tile_shape(4, 14)] * 4 + [tile_shape(2, 9)] * 4,
         g_own, swap_cores(g_other), a_own, swap_cores(a_other),
@@ -460,7 +487,7 @@
     a_pieces = send_round("x", [a_piece] * 4)
     g_pair = local(join_kernel, tile_shape(14), g_piece, swap_pair(g_piece))
     g_pieces = send_round("y", [g_pair] * 4)
-    left = a_side(a_pieces, a_previous, y_in, token_total)
+    left = a_side(a_pieces, a_previous, [own_y, *y_in, far_y], token_total)
     g_pieces, left = lax.optimization_barrier((g_pieces, left))
     inverse, first = g_side(g_pieces, g_running, left, token_total)
     second = local(apply_kernel, HALF, left, swap_cores(inverse))

time: 129 us -> 127 us (0.984)
  starting transfers between devices: 56.9 us -> 51.4 us
  waiting for transfers between devices: 45.8 us -> 47.9 us
    ppermute x27, starting transfers between devices: 44 us -> 38.5 us  [send(): return lax.ppermute(value, axis, [(i, (i + s) % 4) for i in range(4)])]
    ppermute x27, waiting for transfers between devices: 38.8 us -> 40.4 us  [send(): return lax.ppermute(value, axis, [(i, (i + s) % 4) for i in range(4)])]
    ppermute x3, starting transfers between devices: 9.83 us -> 11.1 us  [swap_cores(): return lax.ppermute(value, 'c', [(0, 1), (1, 0)])]
    ppermute x2, starting transfers between devices: 3.09 us -> 1.78 us  [swap_pair(): return lax.ppermute(value, 'zl', [(0, 1), (1, 0)])]
    pallas_call x2 -> x4, Pallas kernels: 4.06 us -> 4.79 us  [cov(): pl.pallas_call(kernel, out_shape=[jax.ShapeDtypeStruct((*out_dims, 8, 128...]
  transfers between devices with their start and end apart: 32 -> 32, of which waited for: 16 -> 19; matrix products, arithmetic and copies ran while one was open for 0% -> 0% of each run, Pallas kernels for 9% -> 11%
where the time goes in v5:
time: 127 us
  starting transfers between devices  51.4 us (40%)
  waiting for transfers between devices  47.9 us (38%)
  Pallas kernels  26 us (20%)
    ppermute x27, waiting for transfers between devices, send(): return lax.ppermute(value, axis, [(i, (i + s) % 4) for i in range(4)])  40.4 us
    ppermute x27, starting transfers between devices, send(): return lax.ppermute(value, axis, [(i, (i + s) % 4) for i in range(4)])  38.5 us
    ppermute x3, starting transfers between devices, swap_cores(): return lax.ppermute(value, 'c', [(0, 1), (1, 0)])  11.1 us
    pallas_call x3, Pallas kernels, pack(): pl.pallas_call(kernel, out_shape=out_shape, in_specs=[pl.BlockSpec(memory...  8.57 us
    pallas_call x1, Pallas kernels, g_side(): pl.pallas_call(functools.partial(g_side_kernel, token_total=token_total),...  6.46 us
    ppermute x2, waiting for transfers between devices, swap_pair(): return lax.ppermute(value, 'zl', [(0, 1), (1, 0)])  5.06 us
    pallas_call x4, Pallas kernels, cov(): pl.pallas_call(kernel, out_shape=[jax.ShapeDtypeStruct((*out_dims, 8, 128...  4.79 us
    pallas_call x1, Pallas kernels, a_side(): pl.pallas_call(functools.partial(a_side_kernel, token_total=token_total),...  4.04 us
  transfers between devices with their start and end apart: 32, of which 19 were waited for; matrix products, arithmetic and copies ran while one was open for 0% of the time, Pallas kernels for 11%

profile of v5, /device:TPU:1, one launch (start us, length us, event | category | flops | bytes accessed | tf_op | source)
XLA Modules:
  0.0 126.6 jit_solution(11298060680633979989)
XLA Ops:
  0.0 2.5 %shard_map.55 = (bf16[4,128,640]{2,1,0:T(8,128)(2,1)}, bf16[4,128,640]{2,1,0:T(8,128)(2,1)}) custom-call(bf16[128,10240]{1,0:T(8,128)(2,1)} %src.2), custom_call_target="tpu_custom_call" | custom-call | tf_op jit(solution)/shard_map/pallas_call | solution.py:87
  2.5 2.1 %collective-permute-start = (bf16[4,128,640]{2,1,0:T(8,128)(2,1)}, bf16[4,128,640]{2,1,0:T(8,128)(2,1)S(1)}, u32[]{:S(2)}, u32[]{:S(2)}) collective-permute-start(bf16[4,128,640]{2,1,0:T(8,128)(2,1)} %get-tuple-element.72), channel_id=1, source_target_pairs={{0,16},{16,32},{32,48},{48,0},{1,17},{17,33},{33,49},{49,1},{2,18}... | collective-permute-start | bytes 1966088 | tf_op jit(solution)/shard_map/ppermute | solution.py:28
  4.7 1.4 %collective-permute-start.1 = (bf16[4,128,640]{2,1,0:T(8,128)(2,1)}, bf16[4,128,640]{2,1,0:T(8,128)(2,1)S(1)}, u32[]{:S(2)}, u32[]{:S(2)}) collective-permute-start(bf16[4,128,640]{2,1,0:T(8,128)(2,1)} %get-tuple-element.73), channel_id=1, source_target_pairs={{0,48},{16,0},{32,16},{48,32},{1,49},{17,1},{33,17},{49,33},{2,50}... | collective-permute-start | bytes 1966088 | tf_op jit(solution)/shard_map/ppermute | solution.py:28
  6.0 2.5 %shard_map.56 = (bf16[128,2304]{1,0:T(8,128)(2,1)}, bf16[128,2304]{1,0:T(8,128)(2,1)}) custom-call(bf16[128,4096]{1,0:T(8,128)(2,1)} %samples.1, bf16[1,1024,640]{2,1,0:T(8,128)(2,1)} %grads.3), custom_call_target="tpu_custom_call" | custom-call | tf_op jit(solution)/shard_map/pallas_call | solution.py:87
  8.5 1.5 %collective-permute-start.3 = (bf16[128,2304]{1,0:T(8,128)(2,1)}, bf16[128,2304]{1,0:T(8,128)(2,1)S(1)}, u32[]{:S(2)}, u32[]{:S(2)}) collective-permute-start(bf16[128,2304]{1,0:T(8,128)(2,1)} %get-tuple-element.82), channel_id=1, source_target_pairs={{0,1},{1,2},{2,3},{3,0},{4,5},{5,6},{6,7},{7,4},{8,9},{9,10},{10,1... | collective-permute-start | bytes 1769480 | tf_op jit(solution)/shard_map/ppermute | solution.py:28
  10.0 1.5 %collective-permute-start.4 = (bf16[128,2304]{1,0:T(8,128)(2,1)}, bf16[128,2304]{1,0:T(8,128)(2,1)S(1)}, u32[]{:S(2)}, u32[]{:S(2)}) collective-permute-start(bf16[128,2304]{1,0:T(8,128)(2,1)} %get-tuple-element.83), channel_id=1, source_target_pairs={{0,3},{1,0},{2,1},{3,2},{4,7},{5,4},{6,5},{7,6},{8,11},{9,8},{10,9... | collective-permute-start | bytes 1769480 | tf_op jit(solution)/shard_map/ppermute | solution.py:28
  11.5 3.5 %shard_map.57 = (bf16[4,128,640]{2,1,0:T(8,128)(2,1)}, bf16[128,2304]{1,0:T(8,128)(2,1)}, bf16[4,128,640]{2,1,0:T(8,128)(2,1)}, bf16[128,2304]{1,0:T(8,128)(2,1)}, f32[256,256]{1,0:T(8,128)}) custom-call(bf16[128,10240]{1,0:T(8,128)(2,1)} %src.2, bf16[128,4096]{1,0:T(8,128)(2,1)} %samples.1, bf16[1,1024,640]{2,1,0:T(8,128)(2,1)} %grads.3, ...), custom_call_target="tpu_custom_call" | custom-call | tf_op jit(solution)/shard_map/pallas_call | solution.py:87
  15.1 3.2 %collective-permute-done.i1 = bf16[4,128,640]{2,1,0:T(8,128)(2,1)S(1)} collective-permute-done((bf16[4,128,640]{2,1,0:T(8,128)(2,1)}, bf16[4,128,640]{2,1,0:T(8,128)(2,1)S(1)}, u32[]{:S(2)}, u32[]{:S(2)}) %collective-permute-start) | collective-permute-done | bytes 655392 | tf_op jit(solution)/shard_map/ppermute | solution.py:28
  18.3 1.5 %collective-permute-done.1.i2 = bf16[4,128,640]{2,1,0:T(8,128)(2,1)S(1)} collective-permute-done((bf16[4,128,640]{2,1,0:T(8,128)(2,1)}, bf16[4,128,640]{2,1,0:T(8,128)(2,1)S(1)}, u32[]{:S(2)}, u32[]{:S(2)}) %collective-permute-start.1) | collective-permute-done | bytes 655392 | tf_op jit(solution)/shard_map/ppermute | solution.py:28
  19.8 2.3 %collective-permute-done.3.i1.g1 = bf16[128,2304]{1,0:T(8,128)(2,1)S(1)} collective-permute-done((bf16[128,2304]{1,0:T(8,128)(2,1)}, bf16[128,2304]{1,0:T(8,128)(2,1)S(1)}, u32[]{:S(2)}, u32[]{:S(2)}) %collective-permute-start.3) | collective-permute-done | bytes 589856 | tf_op jit(solution)/shard_map/ppermute | solution.py:28
  22.1 1.2 collective-permute-done.4.i2.g2
  23.3 2.9 %collective-permute-start.5 = (bf16[128,2304]{1,0:T(8,128)(2,1)}, bf16[128,2304]{1,0:T(8,128)(2,1)S(1)}, u32[]{:S(2)}, u32[]{:S(2)}) collective-permute-start(bf16[128,2304]{1,0:T(8,128)(2,1)} %get-tuple-element.85), channel_id=1, source_target_pairs={{0,2},{1,3},{2,0},{3,1},{4,6},{5,7},{6,4},{7,5},{8,10},{9,11},{10,... | collective-permute-start | bytes 1769480 | tf_op jit(solution)/shard_map/ppermute | solution.py:28
  26.1 1.5 %collective-permute-start.2 = (bf16[4,128,640]{2,1,0:T(8,128)(2,1)}, bf16[4,128,640]{2,1,0:T(8,128)(2,1)S(1)}, u32[]{:S(2)}, u32[]{:S(2)}) collective-permute-start(bf16[4,128,640]{2,1,0:T(8,128)(2,1)} %get-tuple-element.79), channel_id=1, source_target_pairs={{0,32},{16,48},{32,0},{48,16},{1,33},{17,49},{33,1},{49,17},{2,34}... | collective-permute-start | bytes 1966088 | tf_op jit(solution)/shard_map/ppermute | solution.py:28
  27.7 1.1 copy-done.1
  28.8 2.2 %shard_map.60 = (f32[4,56,8,128]{3,2,1,0:T(8,128)S(1)}, f32[4,56,8,128]{3,2,1,0:T(8,128)S(1)}) custom-call(bf16[4,128,640]{2,1,0:T(8,128)(2,1)S(1)} %copy-done.1, bf16[4,128,640]{2,1,0:T(8,128)(2,1)S(1)} %collective-permute-done.i1, bf16[4,128,640]{2,1,0:T(8,128)(2,1)S(1)} %collective-permute-done.1.i2), custom_call_target="tpu_custom_call" | custom-call | flops 1500000000 | bytes 4000000 | tf_op jit(solution)/shard_map/pallas_call | solution.py:175
  31.6 5.5 %collective-permute-done.5.i0.g3 = bf16[128,2304]{1,0:T(8,128)(2,1)S(1)} collective-permute-done((bf16[128,2304]{1,0:T(8,128)(2,1)}, bf16[128,2304]{1,0:T(8,128)(2,1)S(1)}, u32[]{:S(2)}, u32[]{:S(2)}) %collective-permute-start.5) | collective-permute-done | bytes 589856 | tf_op jit(solution)/shard_map/ppermute | solution.py:28
  37.5 3.8 %collective-permute-done.2.i0 = bf16[4,128,640]{2,1,0:T(8,128)(2,1)S(1)} collective-permute-done((bf16[4,128,640]{2,1,0:T(8,128)(2,1)}, bf16[4,128,640]{2,1,0:T(8,128)(2,1)S(1)}, u32[]{:S(2)}, u32[]{:S(2)}) %collective-permute-start.2) | collective-permute-done | bytes 655392 | tf_op jit(solution)/shard_map/ppermute | solution.py:28
  41.3 1.5 %shard_map.61 = (f32[4,56,8,128]{3,2,1,0:T(8,128)S(1)}, f32[4,56,8,128]{3,2,1,0:T(8,128)S(1)}) custom-call(bf16[4,128,640]{2,1,0:T(8,128)(2,1)S(1)} %collective-permute-done.2.i0, f32[4,56,8,128]{3,2,1,0:T(8,128)S(1)} %get-tuple-element.97.own_before, f32[4,56,8,128]{3,2,1,0:T(8,128)S(1)} %get-tuple-element.98.other_before), custom_call_target="tpu_custom_call" | custom-call | flops 1500000000 | bytes 4000000 | tf_op jit(solution)/shard_map/pallas_call | solution.py:175
  42.9 3.7 %collective-permute-start.6 = (f32[4,56,8,128]{3,2,1,0:T(8,128)S(1)}, f32[4,56,8,128]{3,2,1,0:T(8,128)S(1)}, u32[]{:S(2)}, u32[]{:S(2)}) collective-permute-start(f32[4,56,8,128]{3,2,1,0:T(8,128)S(1)} %get-tuple-element.100), channel_id=1, source_target_pairs={{0,4},{4,0},{1,5},{5,1},{2,6},{6,2},{3,7},{7,3},{8,12},{12,8},{9,1... | collective-permute-start | bytes 2752520 | tf_op jit(solution)/shard_map/ppermute | solution.py:24
  46.7 2.4 %collective-permute-done.7.a_got = f32[2,36,8,128]{3,2,1,0:T(8,128)S(1)} collective-permute-done((f32[2,36,8,128]{3,2,1,0:T(8,128)S(1)}, f32[2,36,8,128]{3,2,1,0:T(8,128)S(1)}, u32[]{:S(2)}, u32[]{:S(2)}) %collective-permute-start.7) | collective-permute-done | bytes 294944 | tf_op jit(solution)/shard_map/ppermute | solution.py:24
  49.2 1.1 collective-permute-start.10
  50.8 0.9 collective-permute-start.9
  51.7 2.5 %collective-permute-start.12 = (f32[2,9,8,128]{3,2,1,0:T(8,128)S(1)}, f32[2,9,8,128]{3,2,1,0:T(8,128)S(1)}, u32[]{:S(2)}, u32[]{:S(2)}) collective-permute-start(f32[2,9,8,128]{3,2,1,0:T(8,128)S(1)} %get-tuple-element.109), channel_id=1, source_target_pairs={{0,32},{16,48},{32,0},{48,16},{1,33},{17,49},{33,1},{49,17},{2,34}... | collective-permute-start | bytes 221192 | tf_op jit(solution)/shard_map/ppermute | solution.py:28
  54.2 2.9 %collective-permute-done.11.a1 = f32[2,9,8,128]{3,2,1,0:T(8,128)S(1)} collective-permute-done((f32[2,9,8,128]{3,2,1,0:T(8,128)S(1)}, f32[2,9,8,128]{3,2,1,0:T(8,128)S(1)}, u32[]{:S(2)}, u32[]{:S(2)}) %collective-permute-start.11) | collective-permute-done | bytes 73760 | tf_op jit(solution)/shard_map/ppermute | solution.py:28
  57.2 3.5 %collective-permute-done.13.a3 = f32[2,9,8,128]{3,2,1,0:T(8,128)S(1)} collective-permute-done((f32[2,9,8,128]{3,2,1,0:T(8,128)S(1)}, f32[2,9,8,128]{3,2,1,0:T(8,128)S(1)}, u32[]{:S(2)}, u32[]{:S(2)}) %collective-permute-start.13) | collective-permute-done | bytes 73760 | tf_op jit(solution)/shard_map/ppermute | solution.py:28
  60.7 2.3 %collective-permute-done.8.g1 = f32[4,14,8,128]{3,2,1,0:T(8,128)S(1)} collective-permute-done((f32[4,14,8,128]{3,2,1,0:T(8,128)S(1)}, f32[4,14,8,128]{3,2,1,0:T(8,128)S(1)}, u32[]{:S(2)}, u32[]{:S(2)}) %collective-permute-start.8) | collective-permute-done | bytes 229408 | tf_op jit(solution)/shard_map/ppermute | solution.py:28
  63.1 1.0 collective-permute-start.14
  64.1 3.1 %collective-permute-done.14.got = f32[37,8,128]{2,1,0:T(8,128)S(1)} collective-permute-done((f32[37,8,128]{2,1,0:T(8,128)S(1)}, f32[37,8,128]{2,1,0:T(8,128)S(1)}, u32[]{:S(2)}, u32[]{:S(2)}) %collective-permute-start.14) | collective-permute-done | bytes 151584 | tf_op jit(solution)/shard_map/ppermute | solution.py:32
  67.3 2.5 %collective-permute-start.15 = (f32[16,8,128]{2,1,0:T(8,128)S(1)}, f32[16,8,128]{2,1,0:T(8,128)S(1)}, u32[]{:S(2)}, u32[]{:S(2)}) collective-permute-start(f32[16,8,128]{2,1,0:T(8,128)S(1)} %get-tuple-element.122), channel_id=1, source_target_pairs={{0,64},{64,128},{128,192},{192,0},{1,65},{65,129},{129,193},{193,1... | collective-permute-start | bytes 196616 | tf_op jit(solution)/shard_map/ppermute | solution.py:28
  69.8 4.9 %collective-permute-start.16 = (f32[16,8,128]{2,1,0:T(8,128)S(1)}, f32[16,8,128]{2,1,0:T(8,128)S(1)}, u32[]{:S(2)}, u32[]{:S(2)}) collective-permute-start(f32[16,8,128]{2,1,0:T(8,128)S(1)} %get-tuple-element.123), channel_id=1, source_target_pairs={{0,128},{64,192},{128,0},{192,64},{1,129},{65,193},{129,1},{193,65... | collective-permute-start | bytes 196616 | tf_op jit(solution)/shard_map/ppermute | solution.py:28
  74.7 2.4 %collective-permute-start.17 = (f32[16,8,128]{2,1,0:T(8,128)S(1)}, f32[16,8,128]{2,1,0:T(8,128)S(1)}, u32[]{:S(2)}, u32[]{:S(2)}) collective-permute-start(f32[16,8,128]{2,1,0:T(8,128)S(1)} %get-tuple-element.124), channel_id=1, source_target_pairs={{0,192},{64,0},{128,64},{192,128},{1,193},{65,1},{129,65},{193,129... | collective-permute-start | bytes 196616 | tf_op jit(solution)/shard_map/ppermute | solution.py:28
  77.1 2.3 %collective-permute-done.17.p3 = f32[16,8,128]{2,1,0:T(8,128)S(1)} collective-permute-done((f32[16,8,128]{2,1,0:T(8,128)S(1)}, f32[16,8,128]{2,1,0:T(8,128)S(1)}, u32[]{:S(2)}, u32[]{:S(2)}) %collective-permute-start.17) | collective-permute-done | bytes 65568 | tf_op jit(solution)/shard_map/ppermute | solution.py:28
  79.6 2.4 %collective-permute-start.23 = (f32[9,8,128]{2,1,0:T(8,128)S(1)}, f32[9,8,128]{2,1,0:T(8,128)S(1)}, u32[]{:S(2)}, u32[]{:S(2)}) collective-permute-start(f32[9,8,128]{2,1,0:T(8,128)S(1)} %get-tuple-element.126.p0), channel_id=1, source_target_pairs={{0,32},{16,48},{32,0},{48,16},{1,33},{17,49},{33,1},{49,17},{2,34}... | collective-permute-start | bytes 110600 | tf_op jit(solution)/shard_map/ppermute | solution.py:28
  82.0 1.2 collective-permute-start.24
  83.2 0.8 collective-permute-start.18
  84.0 1.9 %collective-permute-done.18.got = f32[7,8,128]{2,1,0:T(8,128)S(1)} collective-permute-done((f32[7,8,128]{2,1,0:T(8,128)S(1)}, f32[7,8,128]{2,1,0:T(8,128)S(1)}, u32[]{:S(2)}, u32[]{:S(2)}) %collective-permute-start.18) | collective-permute-done | bytes 28704 | tf_op jit(solution)/shard_map/ppermute | solution.py:32
  86.0 2.3 %collective-permute-start.20 = (f32[14,8,128]{2,1,0:T(8,128)S(1)}, f32[14,8,128]{2,1,0:T(8,128)S(1)}, u32[]{:S(2)}, u32[]{:S(2)}) collective-permute-start(f32[14,8,128]{2,1,0:T(8,128)S(1)} %shard_map.66.p0), channel_id=1, source_target_pairs={{0,2},{1,3},{2,0},{3,1},{4,6},{5,7},{6,4},{7,5},{8,10},{9,11},{10,... | collective-permute-start | bytes 172040 | tf_op jit(solution)/shard_map/ppermute | solution.py:28
  88.3 1.2 collective-permute-start.21
  89.5 4.0 %shard_map.67.left = f32[2,256,320]{2,1,0:T(8,128)S(1)} custom-call(f32[9,8,128]{2,1,0:T(8,128)S(1)} %get-tuple-element.126.p0, f32[9,8,128]{2,1,0:T(8,128)S(1)} %collective-permute-done.22.p1, f32[9,8,128]{2,1,0:T(8,128)S(1)} %collective-permute-done.23.p2, f32[9,8,128]{2,1,0:T(8,128)S(1)} %collective-permute-done.24.p3, f32[256,256]{1,0:T(8,128)S(1)} %copy-done.3, ...), custom_call_target="tpu_custom_call" | custom-call | flops 2500000000 | bytes 2000000 | tf_op jit(solution)/shard_map/pallas_call | solution.py:322
  93.6 6.5 %shard_map.68 = (bf16[2,320,384]{2,1,0:T(8,128)(2,1)S(1)}, bf16[128,640]{1,0:T(8,128)(2,1)S(1)}) custom-call(f32[14,8,128]{2,1,0:T(8,128)S(1)} %shard_map.66.p0, f32[14,8,128]{2,1,0:T(8,128)S(1)} %collective-permute-done.19.p1, f32[14,8,128]{2,1,0:T(8,128)S(1)} %collective-permute-done.20.p2, f32[14,8,128]{2,1,0:T(8,128)S(1)} %collective-permute-done.21.p3, ...), custom_call_target="tpu_custom_call" | custom-call | flops 6000000000 | bytes 3000000 | tf_op jit(solution)/shard_map/pallas_call | solution.py:422
  100.1 7.3 %collective-permute-start.28 = (bf16[2,320,384]{2,1,0:T(8,128)(2,1)S(1)}, bf16[2,320,384]{2,1,0:T(8,128)(2,1)S(1)}, u32[]{:S(2)}, u32[]{:S(2)}) collective-permute-start(bf16[2,320,384]{2,1,0:T(8,128)(2,1)S(1)} %get-tuple-element.134), channel_id=1, source_target_pairs={{0,4},{4,0},{1,5},{5,1},{2,6},{6,2},{3,7},{7,3},{8,12},{12,8},{9,1... | collective-permute-start | bytes 1474568 | tf_op jit(solution)/shard_map/ppermute | solution.py:24
  107.4 2.2 %collective-permute-start.26 = (bf16[128,640]{1,0:T(8,128)(2,1)S(1)}, bf16[128,640]{1,0:T(8,128)(2,1)S(1)}, u32[]{:S(2)}, u32[]{:S(2)}) collective-permute-start(bf16[128,640]{1,0:T(8,128)(2,1)S(1)} %get-tuple-element.133.refs_0_), channel_id=1, source_target_pairs={{0,2},{1,3},{2,0},{3,1},{4,6},{5,7},{6,4},{7,5},{8,10},{9,11},{10,... | collective-permute-start | bytes 491528 | tf_op jit(solution)/shard_map/ppermute | solution.py:28
  109.6 1.4 %collective-permute-start.27 = (bf16[128,640]{1,0:T(8,128)(2,1)S(1)}, bf16[128,640]{1,0:T(8,128)(2,1)S(1)}, u32[]{:S(2)}, u32[]{:S(2)}) collective-permute-start(bf16[128,640]{1,0:T(8,128)(2,1)S(1)} %get-tuple-element.133.refs_0_), channel_id=1, source_target_pairs={{0,3},{1,0},{2,1},{3,2},{4,7},{5,4},{6,5},{7,6},{8,11},{9,8},{10,9... | collective-permute-start | bytes 491528 | tf_op jit(solution)/shard_map/ppermute | solution.py:28
  111.7 1.5 %collective-permute-start.30 = (bf16[128,640]{1,0:T(8,128)(2,1)S(1)}, bf16[128,640]{1,0:T(8,128)(2,1)S(1)}, u32[]{:S(2)}, u32[]{:S(2)}) collective-permute-start(bf16[128,640]{1,0:T(8,128)(2,1)S(1)} %shard_map.69.refs_4_), channel_id=1, source_target_pairs={{0,2},{1,3},{2,0},{3,1},{4,6},{5,7},{6,4},{7,5},{8,10},{9,11},{10,... | collective-permute-start | bytes 491528 | tf_op jit(solution)/shard_map/ppermute | solution.py:28
  113.2 1.6 %collective-permute-done.25.refs_1_ = bf16[128,640]{1,0:T(8,128)(2,1)S(1)} collective-permute-done((bf16[128,640]{1,0:T(8,128)(2,1)S(1)}, bf16[128,640]{1,0:T(8,128)(2,1)S(1)}, u32[]{:S(2)}, u32[]{:S(2)}) %collective-permute-start.25) | collective-permute-done | bytes 163872 | tf_op jit(solution)/shard_map/ppermute | solution.py:28
  115.2 2.2 %collective-permute-done.26.refs_2_ = bf16[128,640]{1,0:T(8,128)(2,1)S(1)} collective-permute-done((bf16[128,640]{1,0:T(8,128)(2,1)S(1)}, bf16[128,640]{1,0:T(8,128)(2,1)S(1)}, u32[]{:S(2)}, u32[]{:S(2)}) %collective-permute-start.26) | collective-permute-done | bytes 163872 | tf_op jit(solution)/shard_map/ppermute | solution.py:28
  118.2 6.9 %collective-permute-done.29.refs_5_ = bf16[128,640]{1,0:T(8,128)(2,1)S(1)} collective-permute-done((bf16[128,640]{1,0:T(8,128)(2,1)S(1)}, bf16[128,640]{1,0:T(8,128)(2,1)S(1)}, u32[]{:S(2)}, u32[]{:S(2)}) %collective-permute-start.29) | collective-permute-done | bytes 163872 | tf_op jit(solution)/shard_map/ppermute | solution.py:28
  125.3 1.3 %shard_map.70 = bf16[1024,640]{1,0:T(8,128)(2,1)} custom-call(bf16[128,640]{1,0:T(8,128)(2,1)S(1)} %get-tuple-element.133.refs_0_, bf16[128,640]{1,0:T(8,128)(2,1)S(1)} %collective-permute-done.25.refs_1_, bf16[128,640]{1,0:T(8,128)(2,1)S(1)} %collective-permute-done.26.refs_2_, bf16[128,640]{1,0:T(8,128)(2,1)S(1)} %collective-permute-done.27.refs_3_, ...), custom_call_target="tpu_custom_call" | custom-call | tf_op jit(solution)/shard_map/pallas_call | solution.py:207
  (40 shorter events, 4.1 us)
Async XLA Ops:
  2.5 15.8 %collective-permute-start = (bf16[4,128,640]{2,1,0:T(8,128)(2,1)}, bf16[4,128,640]{2,1,0:T(8,128)(2,1)S(1)}, u32[]{:S(2)}, u32[]{:S(2)}) collective-permute-start(bf16[4,128,640]{2,1,0:T(8,128)(2,1)} %get-tuple-element.72), channel_id=1, source_target_pairs={{0,16},{16,32},{32,48},{48,0},{1,17},{17,33},{33,49},{49,1},{2,18}... | collective-permute-start | bytes 1966088 | tf_op jit(solution)/shard_map/ppermute | solution.py:28
  4.7 15.1 %collective-permute-start.1 = (bf16[4,128,640]{2,1,0:T(8,128)(2,1)}, bf16[4,128,640]{2,1,0:T(8,128)(2,1)S(1)}, u32[]{:S(2)}, u32[]{:S(2)}) collective-permute-start(bf16[4,128,640]{2,1,0:T(8,128)(2,1)} %get-tuple-element.73), channel_id=1, source_target_pairs={{0,48},{16,0},{32,16},{48,32},{1,49},{17,1},{33,17},{49,33},{2,50}... | collective-permute-start | bytes 1966088 | tf_op jit(solution)/shard_map/ppermute | solution.py:28
  8.5 13.6 %collective-permute-start.3 = (bf16[128,2304]{1,0:T(8,128)(2,1)}, bf16[128,2304]{1,0:T(8,128)(2,1)S(1)}, u32[]{:S(2)}, u32[]{:S(2)}) collective-permute-start(bf16[128,2304]{1,0:T(8,128)(2,1)} %get-tuple-element.82), channel_id=1, source_target_pairs={{0,1},{1,2},{2,3},{3,0},{4,5},{5,6},{6,7},{7,4},{8,9},{9,10},{10,1... | collective-permute-start | bytes 1769480 | tf_op jit(solution)/shard_map/ppermute | solution.py:28
  10.0 13.3 %collective-permute-start.4 = (bf16[128,2304]{1,0:T(8,128)(2,1)}, bf16[128,2304]{1,0:T(8,128)(2,1)S(1)}, u32[]{:S(2)}, u32[]{:S(2)}) collective-permute-start(bf16[128,2304]{1,0:T(8,128)(2,1)} %get-tuple-element.83), channel_id=1, source_target_pairs={{0,3},{1,0},{2,1},{3,2},{4,7},{5,4},{6,5},{7,6},{8,11},{9,8},{10,9... | collective-permute-start | bytes 1769480 | tf_op jit(solution)/shard_map/ppermute | solution.py:28
  23.3 13.8 %collective-permute-start.5 = (bf16[128,2304]{1,0:T(8,128)(2,1)}, bf16[128,2304]{1,0:T(8,128)(2,1)S(1)}, u32[]{:S(2)}, u32[]{:S(2)}) collective-permute-start(bf16[128,2304]{1,0:T(8,128)(2,1)} %get-tuple-element.85), channel_id=1, source_target_pairs={{0,2},{1,3},{2,0},{3,1},{4,6},{5,7},{6,4},{7,5},{8,10},{9,11},{10,... | collective-permute-start | bytes 1769480 | tf_op jit(solution)/shard_map/ppermute | solution.py:28
  26.1 15.2 %collective-permute-start.2 = (bf16[4,128,640]{2,1,0:T(8,128)(2,1)}, bf16[4,128,640]{2,1,0:T(8,128)(2,1)S(1)}, u32[]{:S(2)}, u32[]{:S(2)}) collective-permute-start(bf16[4,128,640]{2,1,0:T(8,128)(2,1)} %get-tuple-element.79), channel_id=1, source_target_pairs={{0,32},{16,48},{32,0},{48,16},{1,33},{17,49},{33,1},{49,17},{2,34}... | collective-permute-start | bytes 1966088 | tf_op jit(solution)/shard_map/ppermute | solution.py:28
  27.7 1.1 copy-start.1
  28.7 2.2 %copy-start.2 = (bf16[128,2304]{1,0:T(8,128)(2,1)S(1)}, bf16[128,2304]{1,0:T(8,128)(2,1)}, u32[]{:S(2)}) copy-start(bf16[128,2304]{1,0:T(8,128)(2,1)} %get-tuple-element.86.i0.g0) | copy-start | bytes 1769476
  42.9 46.7 %copy-start.3 = (f32[256,256]{1,0:T(8,128)S(1)}, f32[256,256]{1,0:T(8,128)}, u32[]{:S(2)}) copy-start(f32[256,256]{1,0:T(8,128)} %get-tuple-element.127.running) | copy-start | bytes 786436
  42.9 6.2 %collective-permute-start.6 = (f32[4,56,8,128]{3,2,1,0:T(8,128)S(1)}, f32[4,56,8,128]{3,2,1,0:T(8,128)S(1)}, u32[]{:S(2)}, u32[]{:S(2)}) collective-permute-start(f32[4,56,8,128]{3,2,1,0:T(8,128)S(1)} %get-tuple-element.100), channel_id=1, source_target_pairs={{0,4},{4,0},{1,5},{5,1},{2,6},{6,2},{3,7},{7,3},{8,12},{12,8},{9,1... | collective-permute-start | bytes 2752520 | tf_op jit(solution)/shard_map/ppermute | solution.py:24
  46.6 2.5 %collective-permute-start.7 = (f32[2,36,8,128]{3,2,1,0:T(8,128)S(1)}, f32[2,36,8,128]{3,2,1,0:T(8,128)S(1)}, u32[]{:S(2)}, u32[]{:S(2)}) collective-permute-start(f32[2,36,8,128]{3,2,1,0:T(8,128)S(1)} %get-tuple-element.102), channel_id=1, source_target_pairs={{0,4},{4,0},{1,5},{5,1},{2,6},{6,2},{3,7},{7,3},{8,12},{12,8},{9,1... | collective-permute-start | bytes 884744 | tf_op jit(solution)/shard_map/ppermute | solution.py:24
  49.2 11.4 %collective-permute-start.10 = (f32[4,14,8,128]{3,2,1,0:T(8,128)S(1)}, f32[4,14,8,128]{3,2,1,0:T(8,128)S(1)}, u32[]{:S(2)}, u32[]{:S(2)}) collective-permute-start(f32[4,14,8,128]{3,2,1,0:T(8,128)S(1)} %get-tuple-element.106), channel_id=1, source_target_pairs={{0,3},{1,0},{2,1},{3,2},{4,7},{5,4},{6,5},{7,6},{8,11},{9,8},{10,9... | collective-permute-start | bytes 688136 | tf_op jit(solution)/shard_map/ppermute | solution.py:28
  50.4 12.6 %collective-permute-start.8 = (f32[4,14,8,128]{3,2,1,0:T(8,128)S(1)}, f32[4,14,8,128]{3,2,1,0:T(8,128)S(1)}, u32[]{:S(2)}, u32[]{:S(2)}) collective-permute-start(f32[4,14,8,128]{3,2,1,0:T(8,128)S(1)} %get-tuple-element.104), channel_id=1, source_target_pairs={{0,1},{1,2},{2,3},{3,0},{4,5},{5,6},{6,7},{7,4},{8,9},{9,10},{10,1... | collective-permute-start | bytes 688136 | tf_op jit(solution)/shard_map/ppermute | solution.py:28
  50.8 12.2 %collective-permute-start.9 = (f32[4,14,8,128]{3,2,1,0:T(8,128)S(1)}, f32[4,14,8,128]{3,2,1,0:T(8,128)S(1)}, u32[]{:S(2)}, u32[]{:S(2)}) collective-permute-start(f32[4,14,8,128]{3,2,1,0:T(8,128)S(1)} %get-tuple-element.105), channel_id=1, source_target_pairs={{0,2},{1,3},{2,0},{3,1},{4,6},{5,7},{6,4},{7,5},{8,10},{9,11},{10,... | collective-permute-start | bytes 688136 | tf_op jit(solution)/shard_map/ppermute | solution.py:28
  51.7 5.5 %collective-permute-start.11 = (f32[2,9,8,128]{3,2,1,0:T(8,128)S(1)}, f32[2,9,8,128]{3,2,1,0:T(8,128)S(1)}, u32[]{:S(2)}, u32[]{:S(2)}) collective-permute-start(f32[2,9,8,128]{3,2,1,0:T(8,128)S(1)} %get-tuple-element.108), channel_id=1, source_target_pairs={{0,16},{16,32},{32,48},{48,0},{1,17},{17,33},{33,49},{49,1},{2,18}... | collective-permute-start | bytes 221192 | tf_op jit(solution)/shard_map/ppermute | solution.py:28
  51.7 5.5 %collective-permute-start.12 = (f32[2,9,8,128]{3,2,1,0:T(8,128)S(1)}, f32[2,9,8,128]{3,2,1,0:T(8,128)S(1)}, u32[]{:S(2)}, u32[]{:S(2)}) collective-permute-start(f32[2,9,8,128]{3,2,1,0:T(8,128)S(1)} %get-tuple-element.109), channel_id=1, source_target_pairs={{0,32},{16,48},{32,0},{48,16},{1,33},{17,49},{33,1},{49,17},{2,34}... | collective-permute-start | bytes 221192 | tf_op jit(solution)/shard_map/ppermute | solution.py:28
  57.2 3.5 %collective-permute-start.13 = (f32[2,9,8,128]{3,2,1,0:T(8,128)S(1)}, f32[2,9,8,128]{3,2,1,0:T(8,128)S(1)}, u32[]{:S(2)}, u32[]{:S(2)}) collective-permute-start(f32[2,9,8,128]{3,2,1,0:T(8,128)S(1)} %get-tuple-element.110), channel_id=1, source_target_pairs={{0,48},{16,0},{32,16},{48,32},{1,49},{17,1},{33,17},{49,33},{2,50}... | collective-permute-start | bytes 221192 | tf_op jit(solution)/shard_map/ppermute | solution.py:28
  63.1 4.1 %collective-permute-start.14 = (f32[37,8,128]{2,1,0:T(8,128)S(1)}, f32[37,8,128]{2,1,0:T(8,128)S(1)}, u32[]{:S(2)}, u32[]{:S(2)}) collective-permute-start(f32[37,8,128]{2,1,0:T(8,128)S(1)} %get-tuple-element.120), channel_id=1, source_target_pairs={{0,8},{8,0},{1,9},{9,1},{2,10},{10,2},{3,11},{11,3},{4,12},{12,4},... | collective-permute-start | bytes 454664 | tf_op jit(solution)/shard_map/ppermute | solution.py:32
  67.3 9.8 %collective-permute-start.15 = (f32[16,8,128]{2,1,0:T(8,128)S(1)}, f32[16,8,128]{2,1,0:T(8,128)S(1)}, u32[]{:S(2)}, u32[]{:S(2)}) collective-permute-start(f32[16,8,128]{2,1,0:T(8,128)S(1)} %get-tuple-element.122), channel_id=1, source_target_pairs={{0,64},{64,128},{128,192},{192,0},{1,65},{65,129},{129,193},{193,1... | collective-permute-start | bytes 196616 | tf_op jit(solution)/shard_map/ppermute | solution.py:28
  69.8 7.4 %collective-permute-start.16 = (f32[16,8,128]{2,1,0:T(8,128)S(1)}, f32[16,8,128]{2,1,0:T(8,128)S(1)}, u32[]{:S(2)}, u32[]{:S(2)}) collective-permute-start(f32[16,8,128]{2,1,0:T(8,128)S(1)} %get-tuple-element.123), channel_id=1, source_target_pairs={{0,128},{64,192},{128,0},{192,64},{1,129},{65,193},{129,1},{193,65... | collective-permute-start | bytes 196616 | tf_op jit(solution)/shard_map/ppermute | solution.py:28
  74.7 4.8 %collective-permute-start.17 = (f32[16,8,128]{2,1,0:T(8,128)S(1)}, f32[16,8,128]{2,1,0:T(8,128)S(1)}, u32[]{:S(2)}, u32[]{:S(2)}) collective-permute-start(f32[16,8,128]{2,1,0:T(8,128)S(1)} %get-tuple-element.124), channel_id=1, source_target_pairs={{0,192},{64,0},{128,64},{192,128},{1,193},{65,1},{129,65},{193,129... | collective-permute-start | bytes 196616 | tf_op jit(solution)/shard_map/ppermute | solution.py:28
  79.5 8.8 %collective-permute-start.22 = (f32[9,8,128]{2,1,0:T(8,128)S(1)}, f32[9,8,128]{2,1,0:T(8,128)S(1)}, u32[]{:S(2)}, u32[]{:S(2)}) collective-permute-start(f32[9,8,128]{2,1,0:T(8,128)S(1)} %get-tuple-element.126.p0), channel_id=1, source_target_pairs={{0,16},{16,32},{32,48},{48,0},{1,17},{17,33},{33,49},{49,1},{2,18}... | collective-permute-start | bytes 110600 | tf_op jit(solution)/shard_map/ppermute | solution.py:28
  79.6 9.9 %collective-permute-start.23 = (f32[9,8,128]{2,1,0:T(8,128)S(1)}, f32[9,8,128]{2,1,0:T(8,128)S(1)}, u32[]{:S(2)}, u32[]{:S(2)}) collective-permute-start(f32[9,8,128]{2,1,0:T(8,128)S(1)} %get-tuple-element.126.p0), channel_id=1, source_target_pairs={{0,32},{16,48},{32,0},{48,16},{1,33},{17,49},{33,1},{49,17},{2,34}... | collective-permute-start | bytes 110600 | tf_op jit(solution)/shard_map/ppermute | solution.py:28
  82.0 7.5 %collective-permute-start.24 = (f32[9,8,128]{2,1,0:T(8,128)S(1)}, f32[9,8,128]{2,1,0:T(8,128)S(1)}, u32[]{:S(2)}, u32[]{:S(2)}) collective-permute-start(f32[9,8,128]{2,1,0:T(8,128)S(1)} %get-tuple-element.126.p0), channel_id=1, source_target_pairs={{0,48},{16,0},{32,16},{48,32},{1,49},{17,1},{33,17},{49,33},{2,50}... | collective-permute-start | bytes 110600 | tf_op jit(solution)/shard_map/ppermute | solution.py:28
  83.2 2.7 %collective-permute-start.18 = (f32[7,8,128]{2,1,0:T(8,128)S(1)}, f32[7,8,128]{2,1,0:T(8,128)S(1)}, u32[]{:S(2)}, u32[]{:S(2)}) collective-permute-start(f32[7,8,128]{2,1,0:T(8,128)S(1)} %get-tuple-element.125.own), channel_id=1, source_target_pairs={{0,8},{8,0},{1,9},{9,1},{2,10},{10,2},{3,11},{11,3},{4,12},{12,4},... | collective-permute-start | bytes 86024 | tf_op jit(solution)/shard_map/ppermute | solution.py:32
  85.9 7.7 %collective-permute-start.19 = (f32[14,8,128]{2,1,0:T(8,128)S(1)}, f32[14,8,128]{2,1,0:T(8,128)S(1)}, u32[]{:S(2)}, u32[]{:S(2)}) collective-permute-start(f32[14,8,128]{2,1,0:T(8,128)S(1)} %shard_map.66.p0), channel_id=1, source_target_pairs={{0,1},{1,2},{2,3},{3,0},{4,5},{5,6},{6,7},{7,4},{8,9},{9,10},{10,1... | collective-permute-start | bytes 172040 | tf_op jit(solution)/shard_map/ppermute | solution.py:28
  86.0 7.6 %collective-permute-start.20 = (f32[14,8,128]{2,1,0:T(8,128)S(1)}, f32[14,8,128]{2,1,0:T(8,128)S(1)}, u32[]{:S(2)}, u32[]{:S(2)}) collective-permute-start(f32[14,8,128]{2,1,0:T(8,128)S(1)} %shard_map.66.p0), channel_id=1, source_target_pairs={{0,2},{1,3},{2,0},{3,1},{4,6},{5,7},{6,4},{7,5},{8,10},{9,11},{10,... | collective-permute-start | bytes 172040 | tf_op jit(solution)/shard_map/ppermute | solution.py:28
  88.3 5.3 %collective-permute-start.21 = (f32[14,8,128]{2,1,0:T(8,128)S(1)}, f32[14,8,128]{2,1,0:T(8,128)S(1)}, u32[]{:S(2)}, u32[]{:S(2)}) collective-permute-start(f32[14,8,128]{2,1,0:T(8,128)S(1)} %shard_map.66.p0), channel_id=1, source_target_pairs={{0,3},{1,0},{2,1},{3,2},{4,7},{5,4},{6,5},{7,6},{8,11},{9,8},{10,9... | collective-permute-start | bytes 172040 | tf_op jit(solution)/shard_map/ppermute | solution.py:28
  89.5 4.1 %copy-start = (f32[2,320,320]{2,1,0:T(8,128)S(1)}, f32[2,320,320]{2,1,0:T(8,128)}, u32[]{:S(2)}) copy-start(f32[2,320,320]{2,1,0:T(8,128)} %running.3) | copy-start | bytes 2457604
  100.1 10.9 %collective-permute-start.28 = (bf16[2,320,384]{2,1,0:T(8,128)(2,1)S(1)}, bf16[2,320,384]{2,1,0:T(8,128)(2,1)S(1)}, u32[]{:S(2)}, u32[]{:S(2)}) collective-permute-start(bf16[2,320,384]{2,1,0:T(8,128)(2,1)S(1)} %get-tuple-element.134), channel_id=1, source_target_pairs={{0,4},{4,0},{1,5},{5,1},{2,6},{6,2},{3,7},{7,3},{8,12},{12,8},{9,1... | collective-permute-start | bytes 1474568 | tf_op jit(solution)/shard_map/ppermute | solution.py:24
  107.4 7.5 %collective-permute-start.25 = (bf16[128,640]{1,0:T(8,128)(2,1)S(1)}, bf16[128,640]{1,0:T(8,128)(2,1)S(1)}, u32[]{:S(2)}, u32[]{:S(2)}) collective-permute-start(bf16[128,640]{1,0:T(8,128)(2,1)S(1)} %get-tuple-element.133.refs_0_), channel_id=1, source_target_pairs={{0,1},{1,2},{2,3},{3,0},{4,5},{5,6},{6,7},{7,4},{8,9},{9,10},{10,1... | collective-permute-start | bytes 491528 | tf_op jit(solution)/shard_map/ppermute | solution.py:28
  107.4 10.0 %collective-permute-start.26 = (bf16[128,640]{1,0:T(8,128)(2,1)S(1)}, bf16[128,640]{1,0:T(8,128)(2,1)S(1)}, u32[]{:S(2)}, u32[]{:S(2)}) collective-permute-start(bf16[128,640]{1,0:T(8,128)(2,1)S(1)} %get-tuple-element.133.refs_0_), channel_id=1, source_target_pairs={{0,2},{1,3},{2,0},{3,1},{4,6},{5,7},{6,4},{7,5},{8,10},{9,11},{10,... | collective-permute-start | bytes 491528 | tf_op jit(solution)/shard_map/ppermute | solution.py:28
  109.6 8.6 %collective-permute-start.27 = (bf16[128,640]{1,0:T(8,128)(2,1)S(1)}, bf16[128,640]{1,0:T(8,128)(2,1)S(1)}, u32[]{:S(2)}, u32[]{:S(2)}) collective-permute-start(bf16[128,640]{1,0:T(8,128)(2,1)S(1)} %get-tuple-element.133.refs_0_), channel_id=1, source_target_pairs={{0,3},{1,0},{2,1},{3,2},{4,7},{5,4},{6,5},{7,6},{8,11},{9,8},{10,9... | collective-permute-start | bytes 491528 | tf_op jit(solution)/shard_map/ppermute | solution.py:28
  111.6 13.5 %collective-permute-start.29 = (bf16[128,640]{1,0:T(8,128)(2,1)S(1)}, bf16[128,640]{1,0:T(8,128)(2,1)S(1)}, u32[]{:S(2)}, u32[]{:S(2)}) collective-permute-start(bf16[128,640]{1,0:T(8,128)(2,1)S(1)} %shard_map.69.refs_4_), channel_id=1, source_target_pairs={{0,1},{1,2},{2,3},{3,0},{4,5},{5,6},{6,7},{7,4},{8,9},{9,10},{10,1... | collective-permute-start | bytes 491528 | tf_op jit(solution)/shard_map/ppermute | solution.py:28
  111.7 13.3 %collective-permute-start.30 = (bf16[128,640]{1,0:T(8,128)(2,1)S(1)}, bf16[128,640]{1,0:T(8,128)(2,1)S(1)}, u32[]{:S(2)}, u32[]{:S(2)}) collective-permute-start(bf16[128,640]{1,0:T(8,128)(2,1)S(1)} %shard_map.69.refs_4_), channel_id=1, source_target_pairs={{0,2},{1,3},{2,0},{3,1},{4,6},{5,7},{6,4},{7,5},{8,10},{9,11},{10,... | collective-permute-start | bytes 491528 | tf_op jit(solution)/shard_map/ppermute | solution.py:28
  114.9 10.4 %collective-permute-start.31 = (bf16[128,640]{1,0:T(8,128)(2,1)S(1)}, bf16[128,640]{1,0:T(8,128)(2,1)S(1)}, u32[]{:S(2)}, u32[]{:S(2)}) collective-permute-start(bf16[128,640]{1,0:T(8,128)(2,1)S(1)} %shard_map.69.refs_4_), channel_id=1, source_target_pairs={{0,3},{1,0},{2,1},{3,2},{4,7},{5,4},{6,5},{7,6},{8,11},{9,8},{10,9... | collective-permute-start | bytes 491528 | tf_op jit(solution)/shard_map/ppermute | solution.py:28

commit v6 on v5

--- a/solution.py
+++ b/solution.py
@@ -278,14 +278,17 @@
             lhs[n:2 * n, i * n:(i + 1) * n] = part
 
     trace = jnp.sum(matrix * identity)
-    put(identity / trace, matrix / trace)
+    scaled = matrix / trace
+    approx = (2.0 * identity - scaled) / trace
+    put(approx, scaled)
+    put(approx, jnp.dot(lhs[0:n], rhs[...], preferred_element_type=jnp.float32))
 
     def step(_, carry):
         both = jnp.dot(lhs[...], rhs[...], preferred_element_type=jnp.float32)
         put(both[n:], both[:n])
         return carry
 
-    lax.fori_loop(0, ITERS - 1, step, 0)
+    lax.fori_loop(0, ITERS - 2, step, 0)
     return jnp.dot(lhs[n:2 * n], rhs[...], preferred_element_type=jnp.float32)
 
 
@@ -400,19 +403,23 @@
     rhs_main[...] = jnp.zeros(rhs_main.shape, jnp.bfloat16)
     rhs_tail[...] = jnp.zeros(rhs_tail.shape, jnp.bfloat16)
     put = functools.partial(g_put, lhs, rhs_main, rhs_tail, ident)
-    put([part / trace for part in matrix], [same / trace for same in ident])
+    scaled = [part / trace for part in matrix]
+    approx = [(2.0 * same - part) / trace for same, part in zip(ident, scaled)]
+    put(scaled, approx)
 
     def times(row):
         main = jnp.dot(lhs[row:row + BG], rhs_main[...], preferred_element_type=jnp.float32)
         corner = jnp.dot(lhs[row + 256:row + BG], rhs_tail[...], preferred_element_type=jnp.float32)
         return main, jnp.concatenate([turned_tail(main), corner], axis=0)
 
+    put(times(0), approx)
+
     def step(_, carry):
         product, approx = times(0), times(BG)
         put(product, approx)
         return carry
 
-    lax.fori_loop(0, ITERS - 1, step, 0, unroll=True)
+    lax.fori_loop(0, ITERS - 2, step, 0, unroll=True)
     main, tail = times(BG)
     out[0], out[1] = split(jnp.concatenate([main, tail], axis=1))
     rows[...] = half_rows(left[c], out)
@@ -472,6 +479,7 @@
 
     g_before = g_cov_first([own_x, *g_in])
     a_before = a_cov_first([own_y, *y_in])
+    far_x, far_y = lax.optimization_barrier((far_x, far_y))
     a_own, a_other = a_cov(far_y, a_before)
     far_x, a_own, a_other = lax.optimization_barrier((far_x, a_own, a_other))
     g_own, g_other = g_cov(far_x, g_before)

time: 127 us -> 124 us (0.976)
  waiting for transfers between devices: 47.9 us -> 39.7 us
  starting transfers between devices: 51.4 us -> 57.4 us
    ppermute x27, waiting for transfers between devices: 40.4 us -> 32.7 us  [send(): return lax.ppermute(value, axis, [(i, (i + s) % 4) for i in range(4)])]
    ppermute x27, starting transfers between devices: 38.5 us -> 42.7 us  [send(): return lax.ppermute(value, axis, [(i, (i + s) % 4) for i in range(4)])]
    ppermute x2, starting transfers between devices: 1.78 us -> 3.89 us  [swap_pair(): return lax.ppermute(value, 'zl', [(0, 1), (1, 0)])]
  transfers between devices with their start and end apart: 32 -> 32, of which waited for: 19 -> 18; matrix products, arithmetic and copies ran while one was open for 0% -> 0% of each run, Pallas kernels for 11% -> 11%
where the time goes in v6:
time: 124 us
  starting transfers between devices  57.4 us (46%)
  waiting for transfers between devices  39.7 us (32%)
  Pallas kernels  25.7 us (21%)
    ppermute x27, starting transfers between devices, send(): return lax.ppermute(value, axis, [(i, (i + s) % 4) for i in range(4)])  42.7 us
    ppermute x27, waiting for transfers between devices, send(): return lax.ppermute(value, axis, [(i, (i + s) % 4) for i in range(4)])  32.7 us
    ppermute x3, starting transfers between devices, swap_cores(): return lax.ppermute(value, 'c', [(0, 1), (1, 0)])  10.8 us
    pallas_call x3, Pallas kernels, pack(): pl.pallas_call(kernel, out_shape=out_shape, in_specs=[pl.BlockSpec(memory...  8.57 us
    pallas_call x1, Pallas kernels, g_side(): pl.pallas_call(functools.partial(g_side_kernel, token_total=token_total),...  6.2 us
    pallas_call x4, Pallas kernels, cov(): pl.pallas_call(kernel, out_shape=[jax.ShapeDtypeStruct((*out_dims, 8, 128...  4.8 us
    ppermute x2, waiting for transfers between devices, swap_pair(): return lax.ppermute(value, 'zl', [(0, 1), (1, 0)])  4.57 us
    pallas_call x1, Pallas kernels, a_side(): pl.pallas_call(functools.partial(a_side_kernel, token_total=token_total),...  3.97 us
  transfers between devices with their start and end apart: 32, of which 18 were waited for; matrix products, arithmetic and copies ran while one was open for 0% of the time, Pallas kernels for 11%

profile of v6, /device:TPU:1, one launch (start us, length us, event | category | flops | bytes accessed | tf_op | source)
XLA Modules:
  0.0 124.1 jit_solution(3237503472231621289)
XLA Ops:
  0.0 2.5 %shard_map.55 = (bf16[4,128,640]{2,1,0:T(8,128)(2,1)}, bf16[4,128,640]{2,1,0:T(8,128)(2,1)}) custom-call(bf16[128,10240]{1,0:T(8,128)(2,1)} %src.2), custom_call_target="tpu_custom_call" | custom-call | tf_op jit(solution)/shard_map/pallas_call | solution.py:87
  2.5 2.1 %collective-permute-start = (bf16[4,128,640]{2,1,0:T(8,128)(2,1)}, bf16[4,128,640]{2,1,0:T(8,128)(2,1)S(1)}, u32[]{:S(2)}, u32[]{:S(2)}) collective-permute-start(bf16[4,128,640]{2,1,0:T(8,128)(2,1)} %get-tuple-element.74), channel_id=1, source_target_pairs={{0,16},{16,32},{32,48},{48,0},{1,17},{17,33},{33,49},{49,1},{2,18}... | collective-permute-start | bytes 1966088 | tf_op jit(solution)/shard_map/ppermute | solution.py:28
  4.7 1.4 %collective-permute-start.1 = (bf16[4,128,640]{2,1,0:T(8,128)(2,1)}, bf16[4,128,640]{2,1,0:T(8,128)(2,1)S(1)}, u32[]{:S(2)}, u32[]{:S(2)}) collective-permute-start(bf16[4,128,640]{2,1,0:T(8,128)(2,1)} %get-tuple-element.75), channel_id=1, source_target_pairs={{0,48},{16,0},{32,16},{48,32},{1,49},{17,1},{33,17},{49,33},{2,50}... | collective-permute-start | bytes 1966088 | tf_op jit(solution)/shard_map/ppermute | solution.py:28
  6.0 2.5 %shard_map.56 = (bf16[128,2304]{1,0:T(8,128)(2,1)}, bf16[128,2304]{1,0:T(8,128)(2,1)}) custom-call(bf16[128,4096]{1,0:T(8,128)(2,1)} %samples.1, bf16[1,1024,640]{2,1,0:T(8,128)(2,1)} %grads.3), custom_call_target="tpu_custom_call" | custom-call | tf_op jit(solution)/shard_map/pallas_call | solution.py:87
  8.5 1.5 %collective-permute-start.3 = (bf16[128,2304]{1,0:T(8,128)(2,1)}, bf16[128,2304]{1,0:T(8,128)(2,1)S(1)}, u32[]{:S(2)}, u32[]{:S(2)}) collective-permute-start(bf16[128,2304]{1,0:T(8,128)(2,1)} %get-tuple-element.84), channel_id=1, source_target_pairs={{0,1},{1,2},{2,3},{3,0},{4,5},{5,6},{6,7},{7,4},{8,9},{9,10},{10,1... | collective-permute-start | bytes 1769480 | tf_op jit(solution)/shard_map/ppermute | solution.py:28
  10.0 1.5 %collective-permute-start.4 = (bf16[128,2304]{1,0:T(8,128)(2,1)}, bf16[128,2304]{1,0:T(8,128)(2,1)S(1)}, u32[]{:S(2)}, u32[]{:S(2)}) collective-permute-start(bf16[128,2304]{1,0:T(8,128)(2,1)} %get-tuple-element.85), channel_id=1, source_target_pairs={{0,3},{1,0},{2,1},{3,2},{4,7},{5,4},{6,5},{7,6},{8,11},{9,8},{10,9... | collective-permute-start | bytes 1769480 | tf_op jit(solution)/shard_map/ppermute | solution.py:28
  11.5 3.5 %shard_map.57 = (bf16[4,128,640]{2,1,0:T(8,128)(2,1)}, bf16[128,2304]{1,0:T(8,128)(2,1)}, bf16[4,128,640]{2,1,0:T(8,128)(2,1)}, bf16[128,2304]{1,0:T(8,128)(2,1)}, f32[256,256]{1,0:T(8,128)}) custom-call(bf16[128,10240]{1,0:T(8,128)(2,1)} %src.2, bf16[128,4096]{1,0:T(8,128)(2,1)} %samples.1, bf16[1,1024,640]{2,1,0:T(8,128)(2,1)} %grads.3, ...), custom_call_target="tpu_custom_call" | custom-call | tf_op jit(solution)/shard_map/pallas_call | solution.py:87
  15.1 3.2 %collective-permute-done.i1 = bf16[4,128,640]{2,1,0:T(8,128)(2,1)S(1)} collective-permute-done((bf16[4,128,640]{2,1,0:T(8,128)(2,1)}, bf16[4,128,640]{2,1,0:T(8,128)(2,1)S(1)}, u32[]{:S(2)}, u32[]{:S(2)}) %collective-permute-start) | collective-permute-done | bytes 655392 | tf_op jit(solution)/shard_map/ppermute | solution.py:28
  18.3 1.5 %collective-permute-done.1.i2 = bf16[4,128,640]{2,1,0:T(8,128)(2,1)S(1)} collective-permute-done((bf16[4,128,640]{2,1,0:T(8,128)(2,1)}, bf16[4,128,640]{2,1,0:T(8,128)(2,1)S(1)}, u32[]{:S(2)}, u32[]{:S(2)}) %collective-permute-start.1) | collective-permute-done | bytes 655392 | tf_op jit(solution)/shard_map/ppermute | solution.py:28
  19.8 2.6 %collective-permute-start.2 = (bf16[4,128,640]{2,1,0:T(8,128)(2,1)}, bf16[4,128,640]{2,1,0:T(8,128)(2,1)S(1)}, u32[]{:S(2)}, u32[]{:S(2)}) collective-permute-start(bf16[4,128,640]{2,1,0:T(8,128)(2,1)} %get-tuple-element.81), channel_id=1, source_target_pairs={{0,32},{16,48},{32,0},{48,16},{1,33},{17,49},{33,1},{49,17},{2,34}... | collective-permute-start | bytes 1966088 | tf_op jit(solution)/shard_map/ppermute | solution.py:28
  22.4 0.9 collective-permute-done.4.i2.g2
  23.3 2.9 %collective-permute-start.5 = (bf16[128,2304]{1,0:T(8,128)(2,1)}, bf16[128,2304]{1,0:T(8,128)(2,1)S(1)}, u32[]{:S(2)}, u32[]{:S(2)}) collective-permute-start(bf16[128,2304]{1,0:T(8,128)(2,1)} %get-tuple-element.87), channel_id=1, source_target_pairs={{0,2},{1,3},{2,0},{3,1},{4,6},{5,7},{6,4},{7,5},{8,10},{9,11},{10,... | collective-permute-start | bytes 1769480 | tf_op jit(solution)/shard_map/ppermute | solution.py:28
  26.1 1.1 copy-done.1
  27.2 2.2 %shard_map.60 = (f32[4,56,8,128]{3,2,1,0:T(8,128)S(1)}, f32[4,56,8,128]{3,2,1,0:T(8,128)S(1)}) custom-call(bf16[4,128,640]{2,1,0:T(8,128)(2,1)S(1)} %copy-done.1, bf16[4,128,640]{2,1,0:T(8,128)(2,1)S(1)} %collective-permute-done.i1, bf16[4,128,640]{2,1,0:T(8,128)(2,1)S(1)} %collective-permute-done.1.i2), custom_call_target="tpu_custom_call" | custom-call | flops 1500000000 | bytes 4000000 | tf_op jit(solution)/shard_map/pallas_call | solution.py:175
  30.1 7.0 %collective-permute-done.5.i0.g3 = bf16[128,2304]{1,0:T(8,128)(2,1)S(1)} collective-permute-done((bf16[128,2304]{1,0:T(8,128)(2,1)}, bf16[128,2304]{1,0:T(8,128)(2,1)S(1)}, u32[]{:S(2)}, u32[]{:S(2)}) %collective-permute-start.5) | collective-permute-done | bytes 589856 | tf_op jit(solution)/shard_map/ppermute | solution.py:28
  37.5 1.5 %shard_map.61 = (f32[4,56,8,128]{3,2,1,0:T(8,128)S(1)}, f32[4,56,8,128]{3,2,1,0:T(8,128)S(1)}) custom-call(bf16[4,128,640]{2,1,0:T(8,128)(2,1)S(1)} %collective-permute-done.2.i0, f32[4,56,8,128]{3,2,1,0:T(8,128)S(1)} %get-tuple-element.101.own_before, f32[4,56,8,128]{3,2,1,0:T(8,128)S(1)} %get-tuple-element.102.other_before), custom_call_target="tpu_custom_call" | custom-call | flops 1500000000 | bytes 4000000 | tf_op jit(solution)/shard_map/pallas_call | solution.py:175
  39.1 3.7 %collective-permute-start.6 = (f32[4,56,8,128]{3,2,1,0:T(8,128)S(1)}, f32[4,56,8,128]{3,2,1,0:T(8,128)S(1)}, u32[]{:S(2)}, u32[]{:S(2)}) collective-permute-start(f32[4,56,8,128]{3,2,1,0:T(8,128)S(1)} %get-tuple-element.104), channel_id=1, source_target_pairs={{0,4},{4,0},{1,5},{5,1},{2,6},{6,2},{3,7},{7,3},{8,12},{12,8},{9,1... | collective-permute-start | bytes 2752520 | tf_op jit(solution)/shard_map/ppermute | solution.py:24
  42.9 2.4 %collective-permute-done.7.a_got = f32[2,36,8,128]{3,2,1,0:T(8,128)S(1)} collective-permute-done((f32[2,36,8,128]{3,2,1,0:T(8,128)S(1)}, f32[2,36,8,128]{3,2,1,0:T(8,128)S(1)}, u32[]{:S(2)}, u32[]{:S(2)}) %collective-permute-start.7) | collective-permute-done | bytes 294944 | tf_op jit(solution)/shard_map/ppermute | solution.py:24
  45.4 2.2 %collective-permute-start.10 = (f32[4,14,8,128]{3,2,1,0:T(8,128)S(1)}, f32[4,14,8,128]{3,2,1,0:T(8,128)S(1)}, u32[]{:S(2)}, u32[]{:S(2)}) collective-permute-start(f32[4,14,8,128]{3,2,1,0:T(8,128)S(1)} %get-tuple-element.110), channel_id=1, source_target_pairs={{0,3},{1,0},{2,1},{3,2},{4,7},{5,4},{6,5},{7,6},{8,11},{9,8},{10,9... | collective-permute-start | bytes 688136 | tf_op jit(solution)/shard_map/ppermute | solution.py:28
  47.6 2.2 %collective-permute-start.9 = (f32[4,14,8,128]{3,2,1,0:T(8,128)S(1)}, f32[4,14,8,128]{3,2,1,0:T(8,128)S(1)}, u32[]{:S(2)}, u32[]{:S(2)}) collective-permute-start(f32[4,14,8,128]{3,2,1,0:T(8,128)S(1)} %get-tuple-element.109), channel_id=1, source_target_pairs={{0,2},{1,3},{2,0},{3,1},{4,6},{5,7},{6,4},{7,5},{8,10},{9,11},{10,... | collective-permute-start | bytes 688136 | tf_op jit(solution)/shard_map/ppermute | solution.py:28
  50.0 2.3 %collective-permute-start.12 = (f32[2,9,8,128]{3,2,1,0:T(8,128)S(1)}, f32[2,9,8,128]{3,2,1,0:T(8,128)S(1)}, u32[]{:S(2)}, u32[]{:S(2)}) collective-permute-start(f32[2,9,8,128]{3,2,1,0:T(8,128)S(1)} %get-tuple-element.113), channel_id=1, source_target_pairs={{0,32},{16,48},{32,0},{48,16},{1,33},{17,49},{33,1},{49,17},{2,34}... | collective-permute-start | bytes 221192 | tf_op jit(solution)/shard_map/ppermute | solution.py:28
  52.3 3.0 %collective-permute-done.11.a1 = f32[2,9,8,128]{3,2,1,0:T(8,128)S(1)} collective-permute-done((f32[2,9,8,128]{3,2,1,0:T(8,128)S(1)}, f32[2,9,8,128]{3,2,1,0:T(8,128)S(1)}, u32[]{:S(2)}, u32[]{:S(2)}) %collective-permute-start.11) | collective-permute-done | bytes 73760 | tf_op jit(solution)/shard_map/ppermute | solution.py:28
  55.3 3.5 %collective-permute-done.13.a3 = f32[2,9,8,128]{3,2,1,0:T(8,128)S(1)} collective-permute-done((f32[2,9,8,128]{3,2,1,0:T(8,128)S(1)}, f32[2,9,8,128]{3,2,1,0:T(8,128)S(1)}, u32[]{:S(2)}, u32[]{:S(2)}) %collective-permute-start.13) | collective-permute-done | bytes 73760 | tf_op jit(solution)/shard_map/ppermute | solution.py:28
  58.8 1.0 collective-permute-done.9.g2
  59.9 3.2 %collective-permute-start.14 = (f32[37,8,128]{2,1,0:T(8,128)S(1)}, f32[37,8,128]{2,1,0:T(8,128)S(1)}, u32[]{:S(2)}, u32[]{:S(2)}) collective-permute-start(f32[37,8,128]{2,1,0:T(8,128)S(1)} %get-tuple-element.124), channel_id=1, source_target_pairs={{0,8},{8,0},{1,9},{9,1},{2,10},{10,2},{3,11},{11,3},{4,12},{12,4},... | collective-permute-start | bytes 454664 | tf_op jit(solution)/shard_map/ppermute | solution.py:32
  63.1 2.6 %collective-permute-done.14.got = f32[37,8,128]{2,1,0:T(8,128)S(1)} collective-permute-done((f32[37,8,128]{2,1,0:T(8,128)S(1)}, f32[37,8,128]{2,1,0:T(8,128)S(1)}, u32[]{:S(2)}, u32[]{:S(2)}) %collective-permute-start.14) | collective-permute-done | bytes 151584 | tf_op jit(solution)/shard_map/ppermute | solution.py:32
  65.7 3.1 %collective-permute-start.15 = (f32[16,8,128]{2,1,0:T(8,128)S(1)}, f32[16,8,128]{2,1,0:T(8,128)S(1)}, u32[]{:S(2)}, u32[]{:S(2)}) collective-permute-start(f32[16,8,128]{2,1,0:T(8,128)S(1)} %get-tuple-element.126), channel_id=1, source_target_pairs={{0,64},{64,128},{128,192},{192,0},{1,65},{65,129},{129,193},{193,1... | collective-permute-start | bytes 196616 | tf_op jit(solution)/shard_map/ppermute | solution.py:28
  68.7 4.9 %collective-permute-start.16 = (f32[16,8,128]{2,1,0:T(8,128)S(1)}, f32[16,8,128]{2,1,0:T(8,128)S(1)}, u32[]{:S(2)}, u32[]{:S(2)}) collective-permute-start(f32[16,8,128]{2,1,0:T(8,128)S(1)} %get-tuple-element.127), channel_id=1, source_target_pairs={{0,128},{64,192},{128,0},{192,64},{1,129},{65,193},{129,1},{193,65... | collective-permute-start | bytes 196616 | tf_op jit(solution)/shard_map/ppermute | solution.py:28
  73.7 2.4 %collective-permute-start.17 = (f32[16,8,128]{2,1,0:T(8,128)S(1)}, f32[16,8,128]{2,1,0:T(8,128)S(1)}, u32[]{:S(2)}, u32[]{:S(2)}) collective-permute-start(f32[16,8,128]{2,1,0:T(8,128)S(1)} %get-tuple-element.128), channel_id=1, source_target_pairs={{0,192},{64,0},{128,64},{192,128},{1,193},{65,1},{129,65},{193,129... | collective-permute-start | bytes 196616 | tf_op jit(solution)/shard_map/ppermute | solution.py:28
  76.3 2.1 %collective-permute-done.17.p3 = f32[16,8,128]{2,1,0:T(8,128)S(1)} collective-permute-done((f32[16,8,128]{2,1,0:T(8,128)S(1)}, f32[16,8,128]{2,1,0:T(8,128)S(1)}, u32[]{:S(2)}, u32[]{:S(2)}) %collective-permute-start.17) | collective-permute-done | bytes 65568 | tf_op jit(solution)/shard_map/ppermute | solution.py:28
  78.6 2.4 %collective-permute-start.23 = (f32[9,8,128]{2,1,0:T(8,128)S(1)}, f32[9,8,128]{2,1,0:T(8,128)S(1)}, u32[]{:S(2)}, u32[]{:S(2)}) collective-permute-start(f32[9,8,128]{2,1,0:T(8,128)S(1)} %get-tuple-element.130.p0), channel_id=1, source_target_pairs={{0,32},{16,48},{32,0},{48,16},{1,33},{17,49},{33,1},{49,17},{2,34}... | collective-permute-start | bytes 110600 | tf_op jit(solution)/shard_map/ppermute | solution.py:28
  81.0 1.2 collective-permute-start.24
  82.2 0.7 collective-permute-start.18
  82.9 2.0 %collective-permute-done.18.got = f32[7,8,128]{2,1,0:T(8,128)S(1)} collective-permute-done((f32[7,8,128]{2,1,0:T(8,128)S(1)}, f32[7,8,128]{2,1,0:T(8,128)S(1)}, u32[]{:S(2)}, u32[]{:S(2)}) %collective-permute-start.18) | collective-permute-done | bytes 28704 | tf_op jit(solution)/shard_map/ppermute | solution.py:32
  85.0 1.5 %collective-permute-start.20 = (f32[14,8,128]{2,1,0:T(8,128)S(1)}, f32[14,8,128]{2,1,0:T(8,128)S(1)}, u32[]{:S(2)}, u32[]{:S(2)}) collective-permute-start(f32[14,8,128]{2,1,0:T(8,128)S(1)} %shard_map.66.p0), channel_id=1, source_target_pairs={{0,2},{1,3},{2,0},{3,1},{4,6},{5,7},{6,4},{7,5},{8,10},{9,11},{10,... | collective-permute-start | bytes 172040 | tf_op jit(solution)/shard_map/ppermute | solution.py:28
  86.5 1.2 collective-permute-start.21
  87.7 4.0 %shard_map.67.left = f32[2,256,320]{2,1,0:T(8,128)S(1)} custom-call(f32[9,8,128]{2,1,0:T(8,128)S(1)} %get-tuple-element.130.p0, f32[9,8,128]{2,1,0:T(8,128)S(1)} %collective-permute-done.22.p1, f32[9,8,128]{2,1,0:T(8,128)S(1)} %collective-permute-done.23.p2, f32[9,8,128]{2,1,0:T(8,128)S(1)} %collective-permute-done.24.p3, f32[256,256]{1,0:T(8,128)S(1)} %copy-done.3, ...), custom_call_target="tpu_custom_call" | custom-call | flops 2500000000 | bytes 2000000 | tf_op jit(solution)/shard_map/pallas_call | solution.py:325
  91.7 6.2 %shard_map.68 = (bf16[2,320,384]{2,1,0:T(8,128)(2,1)S(1)}, bf16[128,640]{1,0:T(8,128)(2,1)S(1)}) custom-call(f32[14,8,128]{2,1,0:T(8,128)S(1)} %shard_map.66.p0, f32[14,8,128]{2,1,0:T(8,128)S(1)} %collective-permute-done.19.p1, f32[14,8,128]{2,1,0:T(8,128)S(1)} %collective-permute-done.20.p2, f32[14,8,128]{2,1,0:T(8,128)S(1)} %collective-permute-done.21.p3, ...), custom_call_target="tpu_custom_call" | custom-call | flops 6000000000 | bytes 3000000 | tf_op jit(solution)/shard_map/pallas_call | solution.py:429
  97.9 7.1 %collective-permute-start.28 = (bf16[2,320,384]{2,1,0:T(8,128)(2,1)S(1)}, bf16[2,320,384]{2,1,0:T(8,128)(2,1)S(1)}, u32[]{:S(2)}, u32[]{:S(2)}) collective-permute-start(bf16[2,320,384]{2,1,0:T(8,128)(2,1)S(1)} %get-tuple-element.138), channel_id=1, source_target_pairs={{0,4},{4,0},{1,5},{5,1},{2,6},{6,2},{3,7},{7,3},{8,12},{12,8},{9,1... | collective-permute-start | bytes 1474568 | tf_op jit(solution)/shard_map/ppermute | solution.py:24
  105.0 0.7 collective-permute-start.25
  105.7 2.2 %collective-permute-start.26 = (bf16[128,640]{1,0:T(8,128)(2,1)S(1)}, bf16[128,640]{1,0:T(8,128)(2,1)S(1)}, u32[]{:S(2)}, u32[]{:S(2)}) collective-permute-start(bf16[128,640]{1,0:T(8,128)(2,1)S(1)} %get-tuple-element.137.refs_0_), channel_id=1, source_target_pairs={{0,2},{1,3},{2,0},{3,1},{4,6},{5,7},{6,4},{7,5},{8,10},{9,11},{10,... | collective-permute-start | bytes 491528 | tf_op jit(solution)/shard_map/ppermute | solution.py:28
  107.8 1.8 %collective-permute-start.27 = (bf16[128,640]{1,0:T(8,128)(2,1)S(1)}, bf16[128,640]{1,0:T(8,128)(2,1)S(1)}, u32[]{:S(2)}, u32[]{:S(2)}) collective-permute-start(bf16[128,640]{1,0:T(8,128)(2,1)S(1)} %get-tuple-element.137.refs_0_), channel_id=1, source_target_pairs={{0,3},{1,0},{2,1},{3,2},{4,7},{5,4},{6,5},{7,6},{8,11},{9,8},{10,9... | collective-permute-start | bytes 491528 | tf_op jit(solution)/shard_map/ppermute | solution.py:28
  110.3 1.2 collective-permute-start.30
  111.9 1.1 collective-permute-start.31
  113.0 2.6 %collective-permute-done.26.refs_2_ = bf16[128,640]{1,0:T(8,128)(2,1)S(1)} collective-permute-done((bf16[128,640]{1,0:T(8,128)(2,1)S(1)}, bf16[128,640]{1,0:T(8,128)(2,1)S(1)}, u32[]{:S(2)}, u32[]{:S(2)}) %collective-permute-start.26) | collective-permute-done | bytes 163872 | tf_op jit(solution)/shard_map/ppermute | solution.py:28
  115.7 4.2 %collective-permute-done.29.refs_5_ = bf16[128,640]{1,0:T(8,128)(2,1)S(1)} collective-permute-done((bf16[128,640]{1,0:T(8,128)(2,1)S(1)}, bf16[128,640]{1,0:T(8,128)(2,1)S(1)}, u32[]{:S(2)}, u32[]{:S(2)}) %collective-permute-start.29) | collective-permute-done | bytes 163872 | tf_op jit(solution)/shard_map/ppermute | solution.py:28
  119.9 2.8 %collective-permute-done.30.refs_6_ = bf16[128,640]{1,0:T(8,128)(2,1)S(1)} collective-permute-done((bf16[128,640]{1,0:T(8,128)(2,1)S(1)}, bf16[128,640]{1,0:T(8,128)(2,1)S(1)}, u32[]{:S(2)}, u32[]{:S(2)}) %collective-permute-start.30) | collective-permute-done | bytes 163872 | tf_op jit(solution)/shard_map/ppermute | solution.py:28
  122.8 1.3 %shard_map.70 = bf16[1024,640]{1,0:T(8,128)(2,1)} custom-call(bf16[128,640]{1,0:T(8,128)(2,1)S(1)} %get-tuple-element.137.refs_0_, bf16[128,640]{1,0:T(8,128)(2,1)S(1)} %collective-permute-done.25.refs_1_, bf16[128,640]{1,0:T(8,128)(2,1)S(1)} %collective-permute-done.26.refs_2_, bf16[128,640]{1,0:T(8,128)(2,1)S(1)} %collective-permute-done.27.refs_3_, ...), custom_call_target="tpu_custom_call" | custom-call | tf_op jit(solution)/shard_map/pallas_call | solution.py:207
  (40 shorter events, 3.4 us)
Async XLA Ops:
  2.5 15.8 %collective-permute-start = (bf16[4,128,640]{2,1,0:T(8,128)(2,1)}, bf16[4,128,640]{2,1,0:T(8,128)(2,1)S(1)}, u32[]{:S(2)}, u32[]{:S(2)}) collective-permute-start(bf16[4,128,640]{2,1,0:T(8,128)(2,1)} %get-tuple-element.74), channel_id=1, source_target_pairs={{0,16},{16,32},{32,48},{48,0},{1,17},{17,33},{33,49},{49,1},{2,18}... | collective-permute-start | bytes 1966088 | tf_op jit(solution)/shard_map/ppermute | solution.py:28
  4.7 15.1 %collective-permute-start.1 = (bf16[4,128,640]{2,1,0:T(8,128)(2,1)}, bf16[4,128,640]{2,1,0:T(8,128)(2,1)S(1)}, u32[]{:S(2)}, u32[]{:S(2)}) collective-permute-start(bf16[4,128,640]{2,1,0:T(8,128)(2,1)} %get-tuple-element.75), channel_id=1, source_target_pairs={{0,48},{16,0},{32,16},{48,32},{1,49},{17,1},{33,17},{49,33},{2,50}... | collective-permute-start | bytes 1966088 | tf_op jit(solution)/shard_map/ppermute | solution.py:28
  8.5 13.9 %collective-permute-start.3 = (bf16[128,2304]{1,0:T(8,128)(2,1)}, bf16[128,2304]{1,0:T(8,128)(2,1)S(1)}, u32[]{:S(2)}, u32[]{:S(2)}) collective-permute-start(bf16[128,2304]{1,0:T(8,128)(2,1)} %get-tuple-element.84), channel_id=1, source_target_pairs={{0,1},{1,2},{2,3},{3,0},{4,5},{5,6},{6,7},{7,4},{8,9},{9,10},{10,1... | collective-permute-start | bytes 1769480 | tf_op jit(solution)/shard_map/ppermute | solution.py:28
  10.0 13.3 %collective-permute-start.4 = (bf16[128,2304]{1,0:T(8,128)(2,1)}, bf16[128,2304]{1,0:T(8,128)(2,1)S(1)}, u32[]{:S(2)}, u32[]{:S(2)}) collective-permute-start(bf16[128,2304]{1,0:T(8,128)(2,1)} %get-tuple-element.85), channel_id=1, source_target_pairs={{0,3},{1,0},{2,1},{3,2},{4,7},{5,4},{6,5},{7,6},{8,11},{9,8},{10,9... | collective-permute-start | bytes 1769480 | tf_op jit(solution)/shard_map/ppermute | solution.py:28
  19.8 17.3 %collective-permute-start.2 = (bf16[4,128,640]{2,1,0:T(8,128)(2,1)}, bf16[4,128,640]{2,1,0:T(8,128)(2,1)S(1)}, u32[]{:S(2)}, u32[]{:S(2)}) collective-permute-start(bf16[4,128,640]{2,1,0:T(8,128)(2,1)} %get-tuple-element.81), channel_id=1, source_target_pairs={{0,32},{16,48},{32,0},{48,16},{1,33},{17,49},{33,1},{49,17},{2,34}... | collective-permute-start | bytes 1966088 | tf_op jit(solution)/shard_map/ppermute | solution.py:28
  23.3 13.8 %collective-permute-start.5 = (bf16[128,2304]{1,0:T(8,128)(2,1)}, bf16[128,2304]{1,0:T(8,128)(2,1)S(1)}, u32[]{:S(2)}, u32[]{:S(2)}) collective-permute-start(bf16[128,2304]{1,0:T(8,128)(2,1)} %get-tuple-element.87), channel_id=1, source_target_pairs={{0,2},{1,3},{2,0},{3,1},{4,6},{5,7},{6,4},{7,5},{8,10},{9,11},{10,... | collective-permute-start | bytes 1769480 | tf_op jit(solution)/shard_map/ppermute | solution.py:28
  26.1 1.1 copy-start.1
  27.2 2.2 %copy-start.2 = (bf16[128,2304]{1,0:T(8,128)(2,1)S(1)}, bf16[128,2304]{1,0:T(8,128)(2,1)}, u32[]{:S(2)}) copy-start(bf16[128,2304]{1,0:T(8,128)(2,1)} %get-tuple-element.90.i0.g0) | copy-start | bytes 1769476
  39.1 48.6 %copy-start.3 = (f32[256,256]{1,0:T(8,128)S(1)}, f32[256,256]{1,0:T(8,128)}, u32[]{:S(2)}) copy-start(f32[256,256]{1,0:T(8,128)} %get-tuple-element.131.running) | copy-start | bytes 786436
  39.1 6.2 %collective-permute-start.6 = (f32[4,56,8,128]{3,2,1,0:T(8,128)S(1)}, f32[4,56,8,128]{3,2,1,0:T(8,128)S(1)}, u32[]{:S(2)}, u32[]{:S(2)}) collective-permute-start(f32[4,56,8,128]{3,2,1,0:T(8,128)S(1)} %get-tuple-element.104), channel_id=1, source_target_pairs={{0,4},{4,0},{1,5},{5,1},{2,6},{6,2},{3,7},{7,3},{8,12},{12,8},{9,1... | collective-permute-start | bytes 2752520 | tf_op jit(solution)/shard_map/ppermute | solution.py:24
  42.8 2.5 %collective-permute-start.7 = (f32[2,36,8,128]{3,2,1,0:T(8,128)S(1)}, f32[2,36,8,128]{3,2,1,0:T(8,128)S(1)}, u32[]{:S(2)}, u32[]{:S(2)}) collective-permute-start(f32[2,36,8,128]{3,2,1,0:T(8,128)S(1)} %get-tuple-element.106), channel_id=1, source_target_pairs={{0,4},{4,0},{1,5},{5,1},{2,6},{6,2},{3,7},{7,3},{8,12},{12,8},{9,1... | collective-permute-start | bytes 884744 | tf_op jit(solution)/shard_map/ppermute | solution.py:24
  45.4 13.4 %collective-permute-start.10 = (f32[4,14,8,128]{3,2,1,0:T(8,128)S(1)}, f32[4,14,8,128]{3,2,1,0:T(8,128)S(1)}, u32[]{:S(2)}, u32[]{:S(2)}) collective-permute-start(f32[4,14,8,128]{3,2,1,0:T(8,128)S(1)} %get-tuple-element.110), channel_id=1, source_target_pairs={{0,3},{1,0},{2,1},{3,2},{4,7},{5,4},{6,5},{7,6},{8,11},{9,8},{10,9... | collective-permute-start | bytes 688136 | tf_op jit(solution)/shard_map/ppermute | solution.py:28
  47.6 11.3 %collective-permute-start.8 = (f32[4,14,8,128]{3,2,1,0:T(8,128)S(1)}, f32[4,14,8,128]{3,2,1,0:T(8,128)S(1)}, u32[]{:S(2)}, u32[]{:S(2)}) collective-permute-start(f32[4,14,8,128]{3,2,1,0:T(8,128)S(1)} %get-tuple-element.108), channel_id=1, source_target_pairs={{0,1},{1,2},{2,3},{3,0},{4,5},{5,6},{6,7},{7,4},{8,9},{9,10},{10,1... | collective-permute-start | bytes 688136 | tf_op jit(solution)/shard_map/ppermute | solution.py:28
  47.6 12.2 %collective-permute-start.9 = (f32[4,14,8,128]{3,2,1,0:T(8,128)S(1)}, f32[4,14,8,128]{3,2,1,0:T(8,128)S(1)}, u32[]{:S(2)}, u32[]{:S(2)}) collective-permute-start(f32[4,14,8,128]{3,2,1,0:T(8,128)S(1)} %get-tuple-element.109), channel_id=1, source_target_pairs={{0,2},{1,3},{2,0},{3,1},{4,6},{5,7},{6,4},{7,5},{8,10},{9,11},{10,... | collective-permute-start | bytes 688136 | tf_op jit(solution)/shard_map/ppermute | solution.py:28
  49.8 5.5 %collective-permute-start.11 = (f32[2,9,8,128]{3,2,1,0:T(8,128)S(1)}, f32[2,9,8,128]{3,2,1,0:T(8,128)S(1)}, u32[]{:S(2)}, u32[]{:S(2)}) collective-permute-start(f32[2,9,8,128]{3,2,1,0:T(8,128)S(1)} %get-tuple-element.112), channel_id=1, source_target_pairs={{0,16},{16,32},{32,48},{48,0},{1,17},{17,33},{33,49},{49,1},{2,18}... | collective-permute-start | bytes 221192 | tf_op jit(solution)/shard_map/ppermute | solution.py:28
  50.0 5.3 %collective-permute-start.12 = (f32[2,9,8,128]{3,2,1,0:T(8,128)S(1)}, f32[2,9,8,128]{3,2,1,0:T(8,128)S(1)}, u32[]{:S(2)}, u32[]{:S(2)}) collective-permute-start(f32[2,9,8,128]{3,2,1,0:T(8,128)S(1)} %get-tuple-element.113), channel_id=1, source_target_pairs={{0,32},{16,48},{32,0},{48,16},{1,33},{17,49},{33,1},{49,17},{2,34}... | collective-permute-start | bytes 221192 | tf_op jit(solution)/shard_map/ppermute | solution.py:28
  55.3 3.5 %collective-permute-start.13 = (f32[2,9,8,128]{3,2,1,0:T(8,128)S(1)}, f32[2,9,8,128]{3,2,1,0:T(8,128)S(1)}, u32[]{:S(2)}, u32[]{:S(2)}) collective-permute-start(f32[2,9,8,128]{3,2,1,0:T(8,128)S(1)} %get-tuple-element.114), channel_id=1, source_target_pairs={{0,48},{16,0},{32,16},{48,32},{1,49},{17,1},{33,17},{49,33},{2,50}... | collective-permute-start | bytes 221192 | tf_op jit(solution)/shard_map/ppermute | solution.py:28
  59.9 5.7 %collective-permute-start.14 = (f32[37,8,128]{2,1,0:T(8,128)S(1)}, f32[37,8,128]{2,1,0:T(8,128)S(1)}, u32[]{:S(2)}, u32[]{:S(2)}) collective-permute-start(f32[37,8,128]{2,1,0:T(8,128)S(1)} %get-tuple-element.124), channel_id=1, source_target_pairs={{0,8},{8,0},{1,9},{9,1},{2,10},{10,2},{3,11},{11,3},{4,12},{12,4},... | collective-permute-start | bytes 454664 | tf_op jit(solution)/shard_map/ppermute | solution.py:32
  65.7 10.4 %collective-permute-start.15 = (f32[16,8,128]{2,1,0:T(8,128)S(1)}, f32[16,8,128]{2,1,0:T(8,128)S(1)}, u32[]{:S(2)}, u32[]{:S(2)}) collective-permute-start(f32[16,8,128]{2,1,0:T(8,128)S(1)} %get-tuple-element.126), channel_id=1, source_target_pairs={{0,64},{64,128},{128,192},{192,0},{1,65},{65,129},{129,193},{193,1... | collective-permute-start | bytes 196616 | tf_op jit(solution)/shard_map/ppermute | solution.py:28
  68.7 7.6 %collective-permute-start.16 = (f32[16,8,128]{2,1,0:T(8,128)S(1)}, f32[16,8,128]{2,1,0:T(8,128)S(1)}, u32[]{:S(2)}, u32[]{:S(2)}) collective-permute-start(f32[16,8,128]{2,1,0:T(8,128)S(1)} %get-tuple-element.127), channel_id=1, source_target_pairs={{0,128},{64,192},{128,0},{192,64},{1,129},{65,193},{129,1},{193,65... | collective-permute-start | bytes 196616 | tf_op jit(solution)/shard_map/ppermute | solution.py:28
  73.7 4.8 %collective-permute-start.17 = (f32[16,8,128]{2,1,0:T(8,128)S(1)}, f32[16,8,128]{2,1,0:T(8,128)S(1)}, u32[]{:S(2)}, u32[]{:S(2)}) collective-permute-start(f32[16,8,128]{2,1,0:T(8,128)S(1)} %get-tuple-element.128), channel_id=1, source_target_pairs={{0,192},{64,0},{128,64},{192,128},{1,193},{65,1},{129,65},{193,129... | collective-permute-start | bytes 196616 | tf_op jit(solution)/shard_map/ppermute | solution.py:28
  78.5 8.0 %collective-permute-start.22 = (f32[9,8,128]{2,1,0:T(8,128)S(1)}, f32[9,8,128]{2,1,0:T(8,128)S(1)}, u32[]{:S(2)}, u32[]{:S(2)}) collective-permute-start(f32[9,8,128]{2,1,0:T(8,128)S(1)} %get-tuple-element.130.p0), channel_id=1, source_target_pairs={{0,16},{16,32},{32,48},{48,0},{1,17},{17,33},{33,49},{49,1},{2,18}... | collective-permute-start | bytes 110600 | tf_op jit(solution)/shard_map/ppermute | solution.py:28
  78.6 9.1 %collective-permute-start.23 = (f32[9,8,128]{2,1,0:T(8,128)S(1)}, f32[9,8,128]{2,1,0:T(8,128)S(1)}, u32[]{:S(2)}, u32[]{:S(2)}) collective-permute-start(f32[9,8,128]{2,1,0:T(8,128)S(1)} %get-tuple-element.130.p0), channel_id=1, source_target_pairs={{0,32},{16,48},{32,0},{48,16},{1,33},{17,49},{33,1},{49,17},{2,34}... | collective-permute-start | bytes 110600 | tf_op jit(solution)/shard_map/ppermute | solution.py:28
  81.0 6.7 %collective-permute-start.24 = (f32[9,8,128]{2,1,0:T(8,128)S(1)}, f32[9,8,128]{2,1,0:T(8,128)S(1)}, u32[]{:S(2)}, u32[]{:S(2)}) collective-permute-start(f32[9,8,128]{2,1,0:T(8,128)S(1)} %get-tuple-element.130.p0), channel_id=1, source_target_pairs={{0,48},{16,0},{32,16},{48,32},{1,49},{17,1},{33,17},{49,33},{2,50}... | collective-permute-start | bytes 110600 | tf_op jit(solution)/shard_map/ppermute | solution.py:28
  82.2 2.7 %collective-permute-start.18 = (f32[7,8,128]{2,1,0:T(8,128)S(1)}, f32[7,8,128]{2,1,0:T(8,128)S(1)}, u32[]{:S(2)}, u32[]{:S(2)}) collective-permute-start(f32[7,8,128]{2,1,0:T(8,128)S(1)} %get-tuple-element.129.own), channel_id=1, source_target_pairs={{0,8},{8,0},{1,9},{9,1},{2,10},{10,2},{3,11},{11,3},{4,12},{12,4},... | collective-permute-start | bytes 86024 | tf_op jit(solution)/shard_map/ppermute | solution.py:32
  84.9 6.8 %collective-permute-start.19 = (f32[14,8,128]{2,1,0:T(8,128)S(1)}, f32[14,8,128]{2,1,0:T(8,128)S(1)}, u32[]{:S(2)}, u32[]{:S(2)}) collective-permute-start(f32[14,8,128]{2,1,0:T(8,128)S(1)} %shard_map.66.p0), channel_id=1, source_target_pairs={{0,1},{1,2},{2,3},{3,0},{4,5},{5,6},{6,7},{7,4},{8,9},{9,10},{10,1... | collective-permute-start | bytes 172040 | tf_op jit(solution)/shard_map/ppermute | solution.py:28
  85.0 6.7 %collective-permute-start.20 = (f32[14,8,128]{2,1,0:T(8,128)S(1)}, f32[14,8,128]{2,1,0:T(8,128)S(1)}, u32[]{:S(2)}, u32[]{:S(2)}) collective-permute-start(f32[14,8,128]{2,1,0:T(8,128)S(1)} %shard_map.66.p0), channel_id=1, source_target_pairs={{0,2},{1,3},{2,0},{3,1},{4,6},{5,7},{6,4},{7,5},{8,10},{9,11},{10,... | collective-permute-start | bytes 172040 | tf_op jit(solution)/shard_map/ppermute | solution.py:28
  86.5 5.2 %collective-permute-start.21 = (f32[14,8,128]{2,1,0:T(8,128)S(1)}, f32[14,8,128]{2,1,0:T(8,128)S(1)}, u32[]{:S(2)}, u32[]{:S(2)}) collective-permute-start(f32[14,8,128]{2,1,0:T(8,128)S(1)} %shard_map.66.p0), channel_id=1, source_target_pairs={{0,3},{1,0},{2,1},{3,2},{4,7},{5,4},{6,5},{7,6},{8,11},{9,8},{10,9... | collective-permute-start | bytes 172040 | tf_op jit(solution)/shard_map/ppermute | solution.py:28
  87.7 4.0 %copy-start = (f32[2,320,320]{2,1,0:T(8,128)S(1)}, f32[2,320,320]{2,1,0:T(8,128)}, u32[]{:S(2)}) copy-start(f32[2,320,320]{2,1,0:T(8,128)} %running.3) | copy-start | bytes 2457604
  97.9 11.8 %collective-permute-start.28 = (bf16[2,320,384]{2,1,0:T(8,128)(2,1)S(1)}, bf16[2,320,384]{2,1,0:T(8,128)(2,1)S(1)}, u32[]{:S(2)}, u32[]{:S(2)}) collective-permute-start(bf16[2,320,384]{2,1,0:T(8,128)(2,1)S(1)} %get-tuple-element.138), channel_id=1, source_target_pairs={{0,4},{4,0},{1,5},{5,1},{2,6},{6,2},{3,7},{7,3},{8,12},{12,8},{9,1... | collective-permute-start | bytes 1474568 | tf_op jit(solution)/shard_map/ppermute | solution.py:24
  105.0 7.0 %collective-permute-start.25 = (bf16[128,640]{1,0:T(8,128)(2,1)S(1)}, bf16[128,640]{1,0:T(8,128)(2,1)S(1)}, u32[]{:S(2)}, u32[]{:S(2)}) collective-permute-start(bf16[128,640]{1,0:T(8,128)(2,1)S(1)} %get-tuple-element.137.refs_0_), channel_id=1, source_target_pairs={{0,1},{1,2},{2,3},{3,0},{4,5},{5,6},{6,7},{7,4},{8,9},{9,10},{10,1... | collective-permute-start | bytes 491528 | tf_op jit(solution)/shard_map/ppermute | solution.py:28
  105.7 10.0 %collective-permute-start.26 = (bf16[128,640]{1,0:T(8,128)(2,1)S(1)}, bf16[128,640]{1,0:T(8,128)(2,1)S(1)}, u32[]{:S(2)}, u32[]{:S(2)}) collective-permute-start(bf16[128,640]{1,0:T(8,128)(2,1)S(1)} %get-tuple-element.137.refs_0_), channel_id=1, source_target_pairs={{0,2},{1,3},{2,0},{3,1},{4,6},{5,7},{6,4},{7,5},{8,10},{9,11},{10,... | collective-permute-start | bytes 491528 | tf_op jit(solution)/shard_map/ppermute | solution.py:28
  107.8 7.9 %collective-permute-start.27 = (bf16[128,640]{1,0:T(8,128)(2,1)S(1)}, bf16[128,640]{1,0:T(8,128)(2,1)S(1)}, u32[]{:S(2)}, u32[]{:S(2)}) collective-permute-start(bf16[128,640]{1,0:T(8,128)(2,1)S(1)} %get-tuple-element.137.refs_0_), channel_id=1, source_target_pairs={{0,3},{1,0},{2,1},{3,2},{4,7},{5,4},{6,5},{7,6},{8,11},{9,8},{10,9... | collective-permute-start | bytes 491528 | tf_op jit(solution)/shard_map/ppermute | solution.py:28
  110.3 9.6 %collective-permute-start.29 = (bf16[128,640]{1,0:T(8,128)(2,1)S(1)}, bf16[128,640]{1,0:T(8,128)(2,1)S(1)}, u32[]{:S(2)}, u32[]{:S(2)}) collective-permute-start(bf16[128,640]{1,0:T(8,128)(2,1)S(1)} %shard_map.69.refs_4_), channel_id=1, source_target_pairs={{0,1},{1,2},{2,3},{3,0},{4,5},{5,6},{6,7},{7,4},{8,9},{9,10},{10,1... | collective-permute-start | bytes 491528 | tf_op jit(solution)/shard_map/ppermute | solution.py:28
  110.3 12.3 %collective-permute-start.30 = (bf16[128,640]{1,0:T(8,128)(2,1)S(1)}, bf16[128,640]{1,0:T(8,128)(2,1)S(1)}, u32[]{:S(2)}, u32[]{:S(2)}) collective-permute-start(bf16[128,640]{1,0:T(8,128)(2,1)S(1)} %shard_map.69.refs_4_), channel_id=1, source_target_pairs={{0,2},{1,3},{2,0},{3,1},{4,6},{5,7},{6,4},{7,5},{8,10},{9,11},{10,... | collective-permute-start | bytes 491528 | tf_op jit(solution)/shard_map/ppermute | solution.py:28
  111.9 10.8 %collective-permute-start.31 = (bf16[128,640]{1,0:T(8,128)(2,1)S(1)}, bf16[128,640]{1,0:T(8,128)(2,1)S(1)}, u32[]{:S(2)}, u32[]{:S(2)}) collective-permute-start(bf16[128,640]{1,0:T(8,128)(2,1)S(1)} %shard_map.69.refs_4_), channel_id=1, source_target_pairs={{0,3},{1,0},{2,1},{3,2},{4,7},{5,4},{6,5},{7,6},{8,11},{9,8},{10,9... | collective-permute-start | bytes 491528 | tf_op jit(solution)/shard_map/ppermute | solution.py:28

commit v7 on v6

--- a/solution.py
+++ b/solution.py
@@ -61,12 +61,11 @@
         yield grads.at[0, pl.ds(start, 128), :], out.at[:, pl.ds(4 * BA + h * 2 * BG, 2 * BG)]
 
 
-def near_x_kernel(src, out1, out3, sem):
-    run_copies([pair for s, out in ((1, out1), (3, out3)) for pair in x_chunk(src, s, out)], sem)
-
-
-def near_y_kernel(samples, grads, out1, out3, sem):
-    run_copies([pair for s, out in ((1, out1), (3, out3)) for pair in y_chunk(samples, grads, s, out)], sem)
+def near_kernel(src, samples, grads, x1, x3, y1, y3, sem):
+    run_copies([
+        *x_chunk(src, 1, x1), *x_chunk(src, 3, x3),
+        *y_chunk(samples, grads, 1, y1), *y_chunk(samples, grads, 3, y3),
+    ], sem)
 
 
 def rest_kernel(src, samples, grads, running, far_x, far_y, own_x, own_y, previous, sem):
@@ -463,10 +462,9 @@
     token_total = float(activations.shape[0] * 256)
     y = lax.axis_index("y")
 
-    near_x = pack(near_x_kernel, 8, [X_CHUNK] * 2, out_grads)
-    near_x, activations = lax.optimization_barrier((near_x, activations))
-    near_y = pack(near_y_kernel, 12, [Y_CHUNK] * 2, activations, grad_partial)
-    near_y, out_grads = lax.optimization_barrier((near_y, out_grads))
+    near = pack(near_kernel, 20, [X_CHUNK] * 2 + [Y_CHUNK] * 2, out_grads, activations, grad_partial)
+    near, out_grads = lax.optimization_barrier((near, out_grads))
+    near_x, near_y = near[:2], near[2:]
     far_x, far_y, own_x, own_y, a_previous = pack(
         rest_kernel, 21, [X_CHUNK, Y_CHUNK, X_CHUNK, Y_CHUNK, PREVIOUS],
         out_grads, activations, grad_partial, a_running,

time: 124 us -> 124 us (level)
  waiting for transfers between devices: 39.7 us -> 41.6 us
  Pallas kernels: 25.7 us -> 24.2 us
    ppermute x27, waiting for transfers between devices: 32.7 us -> 34.7 us  [send(): return lax.ppermute(value, axis, [(i, (i + s) % 4) for i in range(4)])]
    pallas_call x3 -> x2, Pallas kernels: 8.57 us -> 7.04 us  [pack(): pl.pallas_call(kernel, out_shape=out_shape, in_specs=[pl.BlockSpec(memory...]
    ppermute x2, starting transfers between devices: 3.89 us -> 2.53 us  [swap_pair(): return lax.ppermute(value, 'zl', [(0, 1), (1, 0)])]
  transfers between devices with their start and end apart: 32 -> 32, of which waited for: 18 -> 18; matrix products, arithmetic and copies ran while one was open for 0% -> 0% of each run, Pallas kernels for 11% -> 9%
where the time goes in v7:
time: 124 us
  starting transfers between devices  56.7 us (46%)
  waiting for transfers between devices  41.6 us (34%)
  Pallas kernels  24.2 us (20%)
    ppermute x27, starting transfers between devices, send(): return lax.ppermute(value, axis, [(i, (i + s) % 4) for i in range(4)])  43.9 us
    ppermute x27, waiting for transfers between devices, send(): return lax.ppermute(value, axis, [(i, (i + s) % 4) for i in range(4)])  34.7 us
    ppermute x3, starting transfers between devices, swap_cores(): return lax.ppermute(value, 'c', [(0, 1), (1, 0)])  10.3 us
    pallas_call x2, Pallas kernels, pack(): pl.pallas_call(kernel, out_shape=out_shape, in_specs=[pl.BlockSpec(memory...  7.04 us
    pallas_call x1, Pallas kernels, g_side(): pl.pallas_call(functools.partial(g_side_kernel, token_total=token_total),...  6.2 us
    pallas_call x4, Pallas kernels, cov(): pl.pallas_call(kernel, out_shape=[jax.ShapeDtypeStruct((*out_dims, 8, 128...  4.8 us
    ppermute x2, waiting for transfers between devices, swap_pair(): return lax.ppermute(value, 'zl', [(0, 1), (1, 0)])  4.49 us
    pallas_call x1, Pallas kernels, a_side(): pl.pallas_call(functools.partial(a_side_kernel, token_total=token_total),...  3.97 us
  transfers between devices with their start and end apart: 32, of which 18 were waited for; matrix products, arithmetic and copies ran while one was open for 0% of the time, Pallas kernels for 9%

profile of v7, /device:TPU:1, one launch (start us, length us, event | category | flops | bytes accessed | tf_op | source)
XLA Modules:
  0.0 123.8 jit_solution(13488767750388789569)
XLA Ops:
  0.0 3.5 %shard_map.55 = (bf16[4,128,640]{2,1,0:T(8,128)(2,1)}, bf16[4,128,640]{2,1,0:T(8,128)(2,1)}, bf16[128,2304]{1,0:T(8,128)(2,1)}, bf16[128,2304]{1,0:T(8,128)(2,1)}) custom-call(bf16[128,10240]{1,0:T(8,128)(2,1)} %src.2, bf16[128,4096]{1,0:T(8,128)(2,1)} %samples.3, bf16[1,1024,640]{2,1,0:T(8,128)(2,1)} %grads.3), custom_call_target="tpu_custom_call" | custom-call | tf_op jit(solution)/shard_map/pallas_call | solution.py:86
  3.5 2.1 %collective-permute-start = (bf16[4,128,640]{2,1,0:T(8,128)(2,1)}, bf16[4,128,640]{2,1,0:T(8,128)(2,1)S(1)}, u32[]{:S(2)}, u32[]{:S(2)}) collective-permute-start(bf16[4,128,640]{2,1,0:T(8,128)(2,1)} %get-tuple-element.75), channel_id=1, source_target_pairs={{0,16},{16,32},{32,48},{48,0},{1,17},{17,33},{33,49},{49,1},{2,18}... | collective-permute-start | bytes 1966088 | tf_op jit(solution)/shard_map/ppermute | solution.py:28
  5.6 1.4 %collective-permute-start.1 = (bf16[4,128,640]{2,1,0:T(8,128)(2,1)}, bf16[4,128,640]{2,1,0:T(8,128)(2,1)S(1)}, u32[]{:S(2)}, u32[]{:S(2)}) collective-permute-start(bf16[4,128,640]{2,1,0:T(8,128)(2,1)} %get-tuple-element.76), channel_id=1, source_target_pairs={{0,48},{16,0},{32,16},{48,32},{1,49},{17,1},{33,17},{49,33},{2,50}... | collective-permute-start | bytes 1966088 | tf_op jit(solution)/shard_map/ppermute | solution.py:28
  7.0 1.4 %collective-permute-start.3 = (bf16[128,2304]{1,0:T(8,128)(2,1)}, bf16[128,2304]{1,0:T(8,128)(2,1)S(1)}, u32[]{:S(2)}, u32[]{:S(2)}) collective-permute-start(bf16[128,2304]{1,0:T(8,128)(2,1)} %get-tuple-element.82), channel_id=1, source_target_pairs={{0,1},{1,2},{2,3},{3,0},{4,5},{5,6},{6,7},{7,4},{8,9},{9,10},{10,1... | collective-permute-start | bytes 1769480 | tf_op jit(solution)/shard_map/ppermute | solution.py:28
  8.4 1.4 %collective-permute-start.4 = (bf16[128,2304]{1,0:T(8,128)(2,1)}, bf16[128,2304]{1,0:T(8,128)(2,1)S(1)}, u32[]{:S(2)}, u32[]{:S(2)}) collective-permute-start(bf16[128,2304]{1,0:T(8,128)(2,1)} %get-tuple-element.83), channel_id=1, source_target_pairs={{0,3},{1,0},{2,1},{3,2},{4,7},{5,4},{6,5},{7,6},{8,11},{9,8},{10,9... | collective-permute-start | bytes 1769480 | tf_op jit(solution)/shard_map/ppermute | solution.py:28
  9.8 3.6 %shard_map.56 = (bf16[4,128,640]{2,1,0:T(8,128)(2,1)}, bf16[128,2304]{1,0:T(8,128)(2,1)}, bf16[4,128,640]{2,1,0:T(8,128)(2,1)}, bf16[128,2304]{1,0:T(8,128)(2,1)}, f32[256,256]{1,0:T(8,128)}) custom-call(bf16[128,10240]{1,0:T(8,128)(2,1)} %src.2, bf16[128,4096]{1,0:T(8,128)(2,1)} %samples.3, bf16[1,1024,640]{2,1,0:T(8,128)(2,1)} %grads.3, ...), custom_call_target="tpu_custom_call" | custom-call | tf_op jit(solution)/shard_map/pallas_call | solution.py:86
  13.4 5.9 %collective-permute-done.i1 = bf16[4,128,640]{2,1,0:T(8,128)(2,1)S(1)} collective-permute-done((bf16[4,128,640]{2,1,0:T(8,128)(2,1)}, bf16[4,128,640]{2,1,0:T(8,128)(2,1)S(1)}, u32[]{:S(2)}, u32[]{:S(2)}) %collective-permute-start) | collective-permute-done | bytes 655392 | tf_op jit(solution)/shard_map/ppermute | solution.py:28
  19.2 1.5 %collective-permute-done.1.i2 = bf16[4,128,640]{2,1,0:T(8,128)(2,1)S(1)} collective-permute-done((bf16[4,128,640]{2,1,0:T(8,128)(2,1)}, bf16[4,128,640]{2,1,0:T(8,128)(2,1)S(1)}, u32[]{:S(2)}, u32[]{:S(2)}) %collective-permute-start.1) | collective-permute-done | bytes 655392 | tf_op jit(solution)/shard_map/ppermute | solution.py:28
  20.8 2.6 %collective-permute-start.2 = (bf16[4,128,640]{2,1,0:T(8,128)(2,1)}, bf16[4,128,640]{2,1,0:T(8,128)(2,1)S(1)}, u32[]{:S(2)}, u32[]{:S(2)}) collective-permute-start(bf16[4,128,640]{2,1,0:T(8,128)(2,1)} %get-tuple-element.79), channel_id=1, source_target_pairs={{0,32},{16,48},{32,0},{48,16},{1,33},{17,49},{33,1},{49,17},{2,34}... | collective-permute-start | bytes 1966088 | tf_op jit(solution)/shard_map/ppermute | solution.py:28
  23.4 3.1 %collective-permute-start.5 = (bf16[128,2304]{1,0:T(8,128)(2,1)}, bf16[128,2304]{1,0:T(8,128)(2,1)S(1)}, u32[]{:S(2)}, u32[]{:S(2)}) collective-permute-start(bf16[128,2304]{1,0:T(8,128)(2,1)} %get-tuple-element.85), channel_id=1, source_target_pairs={{0,2},{1,3},{2,0},{3,1},{4,6},{5,7},{6,4},{7,5},{8,10},{9,11},{10,... | collective-permute-start | bytes 1769480 | tf_op jit(solution)/shard_map/ppermute | solution.py:28
  26.5 1.1 copy-done.1
  27.6 2.2 %shard_map.59 = (f32[4,56,8,128]{3,2,1,0:T(8,128)S(1)}, f32[4,56,8,128]{3,2,1,0:T(8,128)S(1)}) custom-call(bf16[4,128,640]{2,1,0:T(8,128)(2,1)S(1)} %copy-done.1, bf16[4,128,640]{2,1,0:T(8,128)(2,1)S(1)} %collective-permute-done.i1, bf16[4,128,640]{2,1,0:T(8,128)(2,1)S(1)} %collective-permute-done.1.i2), custom_call_target="tpu_custom_call" | custom-call | flops 1500000000 | bytes 4000000 | tf_op jit(solution)/shard_map/pallas_call | solution.py:174
  30.4 7.4 %collective-permute-done.5.i0.g3 = bf16[128,2304]{1,0:T(8,128)(2,1)S(1)} collective-permute-done((bf16[128,2304]{1,0:T(8,128)(2,1)}, bf16[128,2304]{1,0:T(8,128)(2,1)S(1)}, u32[]{:S(2)}, u32[]{:S(2)}) %collective-permute-start.5) | collective-permute-done | bytes 589856 | tf_op jit(solution)/shard_map/ppermute | solution.py:28
  38.3 1.5 %shard_map.60 = (f32[4,56,8,128]{3,2,1,0:T(8,128)S(1)}, f32[4,56,8,128]{3,2,1,0:T(8,128)S(1)}) custom-call(bf16[4,128,640]{2,1,0:T(8,128)(2,1)S(1)} %collective-permute-done.2.i0, f32[4,56,8,128]{3,2,1,0:T(8,128)S(1)} %get-tuple-element.99.own_before, f32[4,56,8,128]{3,2,1,0:T(8,128)S(1)} %get-tuple-element.100.other_before), custom_call_target="tpu_custom_call" | custom-call | flops 1500000000 | bytes 4000000 | tf_op jit(solution)/shard_map/pallas_call | solution.py:174
  39.8 3.2 %collective-permute-start.6 = (f32[4,56,8,128]{3,2,1,0:T(8,128)S(1)}, f32[4,56,8,128]{3,2,1,0:T(8,128)S(1)}, u32[]{:S(2)}, u32[]{:S(2)}) collective-permute-start(f32[4,56,8,128]{3,2,1,0:T(8,128)S(1)} %get-tuple-element.102), channel_id=1, source_target_pairs={{0,4},{4,0},{1,5},{5,1},{2,6},{6,2},{3,7},{7,3},{8,12},{12,8},{9,1... | collective-permute-start | bytes 2752520 | tf_op jit(solution)/shard_map/ppermute | solution.py:24
  43.1 2.4 %collective-permute-done.7.a_got = f32[2,36,8,128]{3,2,1,0:T(8,128)S(1)} collective-permute-done((f32[2,36,8,128]{3,2,1,0:T(8,128)S(1)}, f32[2,36,8,128]{3,2,1,0:T(8,128)S(1)}, u32[]{:S(2)}, u32[]{:S(2)}) %collective-permute-start.7) | collective-permute-done | bytes 294944 | tf_op jit(solution)/shard_map/ppermute | solution.py:24
  45.7 2.9 %collective-permute-start.10 = (f32[4,14,8,128]{3,2,1,0:T(8,128)S(1)}, f32[4,14,8,128]{3,2,1,0:T(8,128)S(1)}, u32[]{:S(2)}, u32[]{:S(2)}) collective-permute-start(f32[4,14,8,128]{3,2,1,0:T(8,128)S(1)} %get-tuple-element.108), channel_id=1, source_target_pairs={{0,3},{1,0},{2,1},{3,2},{4,7},{5,4},{6,5},{7,6},{8,11},{9,8},{10,9... | collective-permute-start | bytes 688136 | tf_op jit(solution)/shard_map/ppermute | solution.py:28
  48.5 1.6 %collective-permute-start.9 = (f32[4,14,8,128]{3,2,1,0:T(8,128)S(1)}, f32[4,14,8,128]{3,2,1,0:T(8,128)S(1)}, u32[]{:S(2)}, u32[]{:S(2)}) collective-permute-start(f32[4,14,8,128]{3,2,1,0:T(8,128)S(1)} %get-tuple-element.107), channel_id=1, source_target_pairs={{0,2},{1,3},{2,0},{3,1},{4,6},{5,7},{6,4},{7,5},{8,10},{9,11},{10,... | collective-permute-start | bytes 688136 | tf_op jit(solution)/shard_map/ppermute | solution.py:28
  50.2 0.8 collective-permute-start.11
  51.0 2.0 %collective-permute-start.12 = (f32[2,9,8,128]{3,2,1,0:T(8,128)S(1)}, f32[2,9,8,128]{3,2,1,0:T(8,128)S(1)}, u32[]{:S(2)}, u32[]{:S(2)}) collective-permute-start(f32[2,9,8,128]{3,2,1,0:T(8,128)S(1)} %get-tuple-element.111), channel_id=1, source_target_pairs={{0,32},{16,48},{32,0},{48,16},{1,33},{17,49},{33,1},{49,17},{2,34}... | collective-permute-start | bytes 221192 | tf_op jit(solution)/shard_map/ppermute | solution.py:28
  53.0 1.9 %collective-permute-done.11.a1 = f32[2,9,8,128]{3,2,1,0:T(8,128)S(1)} collective-permute-done((f32[2,9,8,128]{3,2,1,0:T(8,128)S(1)}, f32[2,9,8,128]{3,2,1,0:T(8,128)S(1)}, u32[]{:S(2)}, u32[]{:S(2)}) %collective-permute-start.11) | collective-permute-done | bytes 73760 | tf_op jit(solution)/shard_map/ppermute | solution.py:28
  55.8 2.6 %collective-permute-done.13.a3 = f32[2,9,8,128]{3,2,1,0:T(8,128)S(1)} collective-permute-done((f32[2,9,8,128]{3,2,1,0:T(8,128)S(1)}, f32[2,9,8,128]{3,2,1,0:T(8,128)S(1)}, u32[]{:S(2)}, u32[]{:S(2)}) %collective-permute-start.13) | collective-permute-done | bytes 73760 | tf_op jit(solution)/shard_map/ppermute | solution.py:28
  58.4 1.8 %collective-permute-done.9.g2 = f32[4,14,8,128]{3,2,1,0:T(8,128)S(1)} collective-permute-done((f32[4,14,8,128]{3,2,1,0:T(8,128)S(1)}, f32[4,14,8,128]{3,2,1,0:T(8,128)S(1)}, u32[]{:S(2)}, u32[]{:S(2)}) %collective-permute-start.9) | collective-permute-done | bytes 229408 | tf_op jit(solution)/shard_map/ppermute | solution.py:28
  60.2 1.7 %collective-permute-start.14 = (f32[37,8,128]{2,1,0:T(8,128)S(1)}, f32[37,8,128]{2,1,0:T(8,128)S(1)}, u32[]{:S(2)}, u32[]{:S(2)}) collective-permute-start(f32[37,8,128]{2,1,0:T(8,128)S(1)} %get-tuple-element.122), channel_id=1, source_target_pairs={{0,8},{8,0},{1,9},{9,1},{2,10},{10,2},{3,11},{11,3},{4,12},{12,4},... | collective-permute-start | bytes 454664 | tf_op jit(solution)/shard_map/ppermute | solution.py:32
  62.0 2.6 %collective-permute-done.14.got = f32[37,8,128]{2,1,0:T(8,128)S(1)} collective-permute-done((f32[37,8,128]{2,1,0:T(8,128)S(1)}, f32[37,8,128]{2,1,0:T(8,128)S(1)}, u32[]{:S(2)}, u32[]{:S(2)}) %collective-permute-start.14) | collective-permute-done | bytes 151584 | tf_op jit(solution)/shard_map/ppermute | solution.py:32
  64.6 3.1 %collective-permute-start.15 = (f32[16,8,128]{2,1,0:T(8,128)S(1)}, f32[16,8,128]{2,1,0:T(8,128)S(1)}, u32[]{:S(2)}, u32[]{:S(2)}) collective-permute-start(f32[16,8,128]{2,1,0:T(8,128)S(1)} %get-tuple-element.124), channel_id=1, source_target_pairs={{0,64},{64,128},{128,192},{192,0},{1,65},{65,129},{129,193},{193,1... | collective-permute-start | bytes 196616 | tf_op jit(solution)/shard_map/ppermute | solution.py:28
  67.6 4.9 %collective-permute-start.16 = (f32[16,8,128]{2,1,0:T(8,128)S(1)}, f32[16,8,128]{2,1,0:T(8,128)S(1)}, u32[]{:S(2)}, u32[]{:S(2)}) collective-permute-start(f32[16,8,128]{2,1,0:T(8,128)S(1)} %get-tuple-element.125), channel_id=1, source_target_pairs={{0,128},{64,192},{128,0},{192,64},{1,129},{65,193},{129,1},{193,65... | collective-permute-start | bytes 196616 | tf_op jit(solution)/shard_map/ppermute | solution.py:28
  72.6 2.4 %collective-permute-start.17 = (f32[16,8,128]{2,1,0:T(8,128)S(1)}, f32[16,8,128]{2,1,0:T(8,128)S(1)}, u32[]{:S(2)}, u32[]{:S(2)}) collective-permute-start(f32[16,8,128]{2,1,0:T(8,128)S(1)} %get-tuple-element.126), channel_id=1, source_target_pairs={{0,192},{64,0},{128,64},{192,128},{1,193},{65,1},{129,65},{193,129... | collective-permute-start | bytes 196616 | tf_op jit(solution)/shard_map/ppermute | solution.py:28
  75.0 2.3 %collective-permute-done.17.p3 = f32[16,8,128]{2,1,0:T(8,128)S(1)} collective-permute-done((f32[16,8,128]{2,1,0:T(8,128)S(1)}, f32[16,8,128]{2,1,0:T(8,128)S(1)}, u32[]{:S(2)}, u32[]{:S(2)}) %collective-permute-start.17) | collective-permute-done | bytes 65568 | tf_op jit(solution)/shard_map/ppermute | solution.py:28
  77.4 0.9 collective-permute-start.22
  78.3 2.0 %collective-permute-start.23 = (f32[9,8,128]{2,1,0:T(8,128)S(1)}, f32[9,8,128]{2,1,0:T(8,128)S(1)}, u32[]{:S(2)}, u32[]{:S(2)}) collective-permute-start(f32[9,8,128]{2,1,0:T(8,128)S(1)} %get-tuple-element.128.p0), channel_id=1, source_target_pairs={{0,32},{16,48},{32,0},{48,16},{1,33},{17,49},{33,1},{49,17},{2,34}... | collective-permute-start | bytes 110600 | tf_op jit(solution)/shard_map/ppermute | solution.py:28
  80.3 0.7 collective-permute-start.24
  80.9 0.8 collective-permute-start.18
  81.7 1.9 %collective-permute-done.18.got = f32[7,8,128]{2,1,0:T(8,128)S(1)} collective-permute-done((f32[7,8,128]{2,1,0:T(8,128)S(1)}, f32[7,8,128]{2,1,0:T(8,128)S(1)}, u32[]{:S(2)}, u32[]{:S(2)}) %collective-permute-start.18) | collective-permute-done | bytes 28704 | tf_op jit(solution)/shard_map/ppermute | solution.py:32
  83.8 2.5 %collective-permute-start.20 = (f32[14,8,128]{2,1,0:T(8,128)S(1)}, f32[14,8,128]{2,1,0:T(8,128)S(1)}, u32[]{:S(2)}, u32[]{:S(2)}) collective-permute-start(f32[14,8,128]{2,1,0:T(8,128)S(1)} %shard_map.65.p0), channel_id=1, source_target_pairs={{0,2},{1,3},{2,0},{3,1},{4,6},{5,7},{6,4},{7,5},{8,10},{9,11},{10,... | collective-permute-start | bytes 172040 | tf_op jit(solution)/shard_map/ppermute | solution.py:28
  86.2 1.2 collective-permute-start.21
  87.4 4.0 %shard_map.66.left = f32[2,256,320]{2,1,0:T(8,128)S(1)} custom-call(f32[9,8,128]{2,1,0:T(8,128)S(1)} %get-tuple-element.128.p0, f32[9,8,128]{2,1,0:T(8,128)S(1)} %collective-permute-done.22.p1, f32[9,8,128]{2,1,0:T(8,128)S(1)} %collective-permute-done.23.p2, f32[9,8,128]{2,1,0:T(8,128)S(1)} %collective-permute-done.24.p3, f32[256,256]{1,0:T(8,128)S(1)} %copy-done.3, ...), custom_call_target="tpu_custom_call" | custom-call | flops 2500000000 | bytes 2000000 | tf_op jit(solution)/shard_map/pallas_call | solution.py:324
  91.4 6.2 %shard_map.67 = (bf16[2,320,384]{2,1,0:T(8,128)(2,1)S(1)}, bf16[128,640]{1,0:T(8,128)(2,1)S(1)}) custom-call(f32[14,8,128]{2,1,0:T(8,128)S(1)} %shard_map.65.p0, f32[14,8,128]{2,1,0:T(8,128)S(1)} %collective-permute-done.19.p1, f32[14,8,128]{2,1,0:T(8,128)S(1)} %collective-permute-done.20.p2, f32[14,8,128]{2,1,0:T(8,128)S(1)} %collective-permute-done.21.p3, ...), custom_call_target="tpu_custom_call" | custom-call | flops 6000000000 | bytes 3000000 | tf_op jit(solution)/shard_map/pallas_call | solution.py:428
  97.7 7.0 %collective-permute-start.28 = (bf16[2,320,384]{2,1,0:T(8,128)(2,1)S(1)}, bf16[2,320,384]{2,1,0:T(8,128)(2,1)S(1)}, u32[]{:S(2)}, u32[]{:S(2)}) collective-permute-start(bf16[2,320,384]{2,1,0:T(8,128)(2,1)S(1)} %get-tuple-element.136), channel_id=1, source_target_pairs={{0,4},{4,0},{1,5},{5,1},{2,6},{6,2},{3,7},{7,3},{8,12},{12,8},{9,1... | collective-permute-start | bytes 1474568 | tf_op jit(solution)/shard_map/ppermute | solution.py:24
  105.0 2.4 %collective-permute-start.26 = (bf16[128,640]{1,0:T(8,128)(2,1)S(1)}, bf16[128,640]{1,0:T(8,128)(2,1)S(1)}, u32[]{:S(2)}, u32[]{:S(2)}) collective-permute-start(bf16[128,640]{1,0:T(8,128)(2,1)S(1)} %get-tuple-element.135.refs_0_), channel_id=1, source_target_pairs={{0,2},{1,3},{2,0},{3,1},{4,6},{5,7},{6,4},{7,5},{8,10},{9,11},{10,... | collective-permute-start | bytes 491528 | tf_op jit(solution)/shard_map/ppermute | solution.py:28
  107.5 1.6 %collective-permute-start.27 = (bf16[128,640]{1,0:T(8,128)(2,1)S(1)}, bf16[128,640]{1,0:T(8,128)(2,1)S(1)}, u32[]{:S(2)}, u32[]{:S(2)}) collective-permute-start(bf16[128,640]{1,0:T(8,128)(2,1)S(1)} %get-tuple-element.135.refs_0_), channel_id=1, source_target_pairs={{0,3},{1,0},{2,1},{3,2},{4,7},{5,4},{6,5},{7,6},{8,11},{9,8},{10,9... | collective-permute-start | bytes 491528 | tf_op jit(solution)/shard_map/ppermute | solution.py:28
  109.7 1.2 collective-permute-start.30
  110.9 0.7 collective-permute-done.25.refs_1_
  111.6 0.8 collective-permute-start.31
  112.4 2.9 %collective-permute-done.26.refs_2_ = bf16[128,640]{1,0:T(8,128)(2,1)S(1)} collective-permute-done((bf16[128,640]{1,0:T(8,128)(2,1)S(1)}, bf16[128,640]{1,0:T(8,128)(2,1)S(1)}, u32[]{:S(2)}, u32[]{:S(2)}) %collective-permute-start.26) | collective-permute-done | bytes 163872 | tf_op jit(solution)/shard_map/ppermute | solution.py:28
  115.4 4.1 %collective-permute-done.29.refs_5_ = bf16[128,640]{1,0:T(8,128)(2,1)S(1)} collective-permute-done((bf16[128,640]{1,0:T(8,128)(2,1)S(1)}, bf16[128,640]{1,0:T(8,128)(2,1)S(1)}, u32[]{:S(2)}, u32[]{:S(2)}) %collective-permute-start.29) | collective-permute-done | bytes 163872 | tf_op jit(solution)/shard_map/ppermute | solution.py:28
  119.5 2.8 %collective-permute-done.30.refs_6_ = bf16[128,640]{1,0:T(8,128)(2,1)S(1)} collective-permute-done((bf16[128,640]{1,0:T(8,128)(2,1)S(1)}, bf16[128,640]{1,0:T(8,128)(2,1)S(1)}, u32[]{:S(2)}, u32[]{:S(2)}) %collective-permute-start.30) | collective-permute-done | bytes 163872 | tf_op jit(solution)/shard_map/ppermute | solution.py:28
  122.4 1.3 %shard_map.69 = bf16[1024,640]{1,0:T(8,128)(2,1)} custom-call(bf16[128,640]{1,0:T(8,128)(2,1)S(1)} %get-tuple-element.135.refs_0_, bf16[128,640]{1,0:T(8,128)(2,1)S(1)} %collective-permute-done.25.refs_1_, bf16[128,640]{1,0:T(8,128)(2,1)S(1)} %collective-permute-done.26.refs_2_, bf16[128,640]{1,0:T(8,128)(2,1)S(1)} %collective-permute-done.27.refs_3_, ...), custom_call_target="tpu_custom_call" | custom-call | tf_op jit(solution)/shard_map/pallas_call | solution.py:206
  (39 shorter events, 3.8 us)
Async XLA Ops:
  3.5 15.8 %collective-permute-start = (bf16[4,128,640]{2,1,0:T(8,128)(2,1)}, bf16[4,128,640]{2,1,0:T(8,128)(2,1)S(1)}, u32[]{:S(2)}, u32[]{:S(2)}) collective-permute-start(bf16[4,128,640]{2,1,0:T(8,128)(2,1)} %get-tuple-element.75), channel_id=1, source_target_pairs={{0,16},{16,32},{32,48},{48,0},{1,17},{17,33},{33,49},{49,1},{2,18}... | collective-permute-start | bytes 1966088 | tf_op jit(solution)/shard_map/ppermute | solution.py:28
  5.6 15.1 %collective-permute-start.1 = (bf16[4,128,640]{2,1,0:T(8,128)(2,1)}, bf16[4,128,640]{2,1,0:T(8,128)(2,1)S(1)}, u32[]{:S(2)}, u32[]{:S(2)}) collective-permute-start(bf16[4,128,640]{2,1,0:T(8,128)(2,1)} %get-tuple-element.76), channel_id=1, source_target_pairs={{0,48},{16,0},{32,16},{48,32},{1,49},{17,1},{33,17},{49,33},{2,50}... | collective-permute-start | bytes 1966088 | tf_op jit(solution)/shard_map/ppermute | solution.py:28
  7.0 16.4 %collective-permute-start.3 = (bf16[128,2304]{1,0:T(8,128)(2,1)}, bf16[128,2304]{1,0:T(8,128)(2,1)S(1)}, u32[]{:S(2)}, u32[]{:S(2)}) collective-permute-start(bf16[128,2304]{1,0:T(8,128)(2,1)} %get-tuple-element.82), channel_id=1, source_target_pairs={{0,1},{1,2},{2,3},{3,0},{4,5},{5,6},{6,7},{7,4},{8,9},{9,10},{10,1... | collective-permute-start | bytes 1769480 | tf_op jit(solution)/shard_map/ppermute | solution.py:28
  8.4 15.0 %collective-permute-start.4 = (bf16[128,2304]{1,0:T(8,128)(2,1)}, bf16[128,2304]{1,0:T(8,128)(2,1)S(1)}, u32[]{:S(2)}, u32[]{:S(2)}) collective-permute-start(bf16[128,2304]{1,0:T(8,128)(2,1)} %get-tuple-element.83), channel_id=1, source_target_pairs={{0,3},{1,0},{2,1},{3,2},{4,7},{5,4},{6,5},{7,6},{8,11},{9,8},{10,9... | collective-permute-start | bytes 1769480 | tf_op jit(solution)/shard_map/ppermute | solution.py:28
  20.8 17.1 %collective-permute-start.2 = (bf16[4,128,640]{2,1,0:T(8,128)(2,1)}, bf16[4,128,640]{2,1,0:T(8,128)(2,1)S(1)}, u32[]{:S(2)}, u32[]{:S(2)}) collective-permute-start(bf16[4,128,640]{2,1,0:T(8,128)(2,1)} %get-tuple-element.79), channel_id=1, source_target_pairs={{0,32},{16,48},{32,0},{48,16},{1,33},{17,49},{33,1},{49,17},{2,34}... | collective-permute-start | bytes 1966088 | tf_op jit(solution)/shard_map/ppermute | solution.py:28
  23.4 14.5 %collective-permute-start.5 = (bf16[128,2304]{1,0:T(8,128)(2,1)}, bf16[128,2304]{1,0:T(8,128)(2,1)S(1)}, u32[]{:S(2)}, u32[]{:S(2)}) collective-permute-start(bf16[128,2304]{1,0:T(8,128)(2,1)} %get-tuple-element.85), channel_id=1, source_target_pairs={{0,2},{1,3},{2,0},{3,1},{4,6},{5,7},{6,4},{7,5},{8,10},{9,11},{10,... | collective-permute-start | bytes 1769480 | tf_op jit(solution)/shard_map/ppermute | solution.py:28
  26.5 1.1 copy-start.1
  27.6 2.2 %copy-start.2 = (bf16[128,2304]{1,0:T(8,128)(2,1)S(1)}, bf16[128,2304]{1,0:T(8,128)(2,1)}, u32[]{:S(2)}) copy-start(bf16[128,2304]{1,0:T(8,128)(2,1)} %get-tuple-element.88.i0.g0) | copy-start | bytes 1769476
  39.8 47.6 %copy-start.3 = (f32[256,256]{1,0:T(8,128)S(1)}, f32[256,256]{1,0:T(8,128)}, u32[]{:S(2)}) copy-start(f32[256,256]{1,0:T(8,128)} %get-tuple-element.129.running) | copy-start | bytes 786436
  39.8 5.7 %collective-permute-start.6 = (f32[4,56,8,128]{3,2,1,0:T(8,128)S(1)}, f32[4,56,8,128]{3,2,1,0:T(8,128)S(1)}, u32[]{:S(2)}, u32[]{:S(2)}) collective-permute-start(f32[4,56,8,128]{3,2,1,0:T(8,128)S(1)} %get-tuple-element.102), channel_id=1, source_target_pairs={{0,4},{4,0},{1,5},{5,1},{2,6},{6,2},{3,7},{7,3},{8,12},{12,8},{9,1... | collective-permute-start | bytes 2752520 | tf_op jit(solution)/shard_map/ppermute | solution.py:24
  43.0 2.5 %collective-permute-start.7 = (f32[2,36,8,128]{3,2,1,0:T(8,128)S(1)}, f32[2,36,8,128]{3,2,1,0:T(8,128)S(1)}, u32[]{:S(2)}, u32[]{:S(2)}) collective-permute-start(f32[2,36,8,128]{3,2,1,0:T(8,128)S(1)} %get-tuple-element.104), channel_id=1, source_target_pairs={{0,4},{4,0},{1,5},{5,1},{2,6},{6,2},{3,7},{7,3},{8,12},{12,8},{9,1... | collective-permute-start | bytes 884744 | tf_op jit(solution)/shard_map/ppermute | solution.py:24
  45.7 12.7 %collective-permute-start.10 = (f32[4,14,8,128]{3,2,1,0:T(8,128)S(1)}, f32[4,14,8,128]{3,2,1,0:T(8,128)S(1)}, u32[]{:S(2)}, u32[]{:S(2)}) collective-permute-start(f32[4,14,8,128]{3,2,1,0:T(8,128)S(1)} %get-tuple-element.108), channel_id=1, source_target_pairs={{0,3},{1,0},{2,1},{3,2},{4,7},{5,4},{6,5},{7,6},{8,11},{9,8},{10,9... | collective-permute-start | bytes 688136 | tf_op jit(solution)/shard_map/ppermute | solution.py:28
  48.5 9.9 %collective-permute-start.8 = (f32[4,14,8,128]{3,2,1,0:T(8,128)S(1)}, f32[4,14,8,128]{3,2,1,0:T(8,128)S(1)}, u32[]{:S(2)}, u32[]{:S(2)}) collective-permute-start(f32[4,14,8,128]{3,2,1,0:T(8,128)S(1)} %get-tuple-element.106), channel_id=1, source_target_pairs={{0,1},{1,2},{2,3},{3,0},{4,5},{5,6},{6,7},{7,4},{8,9},{9,10},{10,1... | collective-permute-start | bytes 688136 | tf_op jit(solution)/shard_map/ppermute | solution.py:28
  48.5 11.6 %collective-permute-start.9 = (f32[4,14,8,128]{3,2,1,0:T(8,128)S(1)}, f32[4,14,8,128]{3,2,1,0:T(8,128)S(1)}, u32[]{:S(2)}, u32[]{:S(2)}) collective-permute-start(f32[4,14,8,128]{3,2,1,0:T(8,128)S(1)} %get-tuple-element.107), channel_id=1, source_target_pairs={{0,2},{1,3},{2,0},{3,1},{4,6},{5,7},{6,4},{7,5},{8,10},{9,11},{10,... | collective-permute-start | bytes 688136 | tf_op jit(solution)/shard_map/ppermute | solution.py:28
  50.2 4.7 %collective-permute-start.11 = (f32[2,9,8,128]{3,2,1,0:T(8,128)S(1)}, f32[2,9,8,128]{3,2,1,0:T(8,128)S(1)}, u32[]{:S(2)}, u32[]{:S(2)}) collective-permute-start(f32[2,9,8,128]{3,2,1,0:T(8,128)S(1)} %get-tuple-element.110), channel_id=1, source_target_pairs={{0,16},{16,32},{32,48},{48,0},{1,17},{17,33},{33,49},{49,1},{2,18}... | collective-permute-start | bytes 221192 | tf_op jit(solution)/shard_map/ppermute | solution.py:28
  51.0 4.8 %collective-permute-start.12 = (f32[2,9,8,128]{3,2,1,0:T(8,128)S(1)}, f32[2,9,8,128]{3,2,1,0:T(8,128)S(1)}, u32[]{:S(2)}, u32[]{:S(2)}) collective-permute-start(f32[2,9,8,128]{3,2,1,0:T(8,128)S(1)} %get-tuple-element.111), channel_id=1, source_target_pairs={{0,32},{16,48},{32,0},{48,16},{1,33},{17,49},{33,1},{49,17},{2,34}... | collective-permute-start | bytes 221192 | tf_op jit(solution)/shard_map/ppermute | solution.py:28
  54.9 3.5 %collective-permute-start.13 = (f32[2,9,8,128]{3,2,1,0:T(8,128)S(1)}, f32[2,9,8,128]{3,2,1,0:T(8,128)S(1)}, u32[]{:S(2)}, u32[]{:S(2)}) collective-permute-start(f32[2,9,8,128]{3,2,1,0:T(8,128)S(1)} %get-tuple-element.112), channel_id=1, source_target_pairs={{0,48},{16,0},{32,16},{48,32},{1,49},{17,1},{33,17},{49,33},{2,50}... | collective-permute-start | bytes 221192 | tf_op jit(solution)/shard_map/ppermute | solution.py:28
  60.2 4.3 %collective-permute-start.14 = (f32[37,8,128]{2,1,0:T(8,128)S(1)}, f32[37,8,128]{2,1,0:T(8,128)S(1)}, u32[]{:S(2)}, u32[]{:S(2)}) collective-permute-start(f32[37,8,128]{2,1,0:T(8,128)S(1)} %get-tuple-element.122), channel_id=1, source_target_pairs={{0,8},{8,0},{1,9},{9,1},{2,10},{10,2},{3,11},{11,3},{4,12},{12,4},... | collective-permute-start | bytes 454664 | tf_op jit(solution)/shard_map/ppermute | solution.py:32
  64.6 10.4 %collective-permute-start.15 = (f32[16,8,128]{2,1,0:T(8,128)S(1)}, f32[16,8,128]{2,1,0:T(8,128)S(1)}, u32[]{:S(2)}, u32[]{:S(2)}) collective-permute-start(f32[16,8,128]{2,1,0:T(8,128)S(1)} %get-tuple-element.124), channel_id=1, source_target_pairs={{0,64},{64,128},{128,192},{192,0},{1,65},{65,129},{129,193},{193,1... | collective-permute-start | bytes 196616 | tf_op jit(solution)/shard_map/ppermute | solution.py:28
  67.6 7.4 %collective-permute-start.16 = (f32[16,8,128]{2,1,0:T(8,128)S(1)}, f32[16,8,128]{2,1,0:T(8,128)S(1)}, u32[]{:S(2)}, u32[]{:S(2)}) collective-permute-start(f32[16,8,128]{2,1,0:T(8,128)S(1)} %get-tuple-element.125), channel_id=1, source_target_pairs={{0,128},{64,192},{128,0},{192,64},{1,129},{65,193},{129,1},{193,65... | collective-permute-start | bytes 196616 | tf_op jit(solution)/shard_map/ppermute | solution.py:28
  72.6 4.8 %collective-permute-start.17 = (f32[16,8,128]{2,1,0:T(8,128)S(1)}, f32[16,8,128]{2,1,0:T(8,128)S(1)}, u32[]{:S(2)}, u32[]{:S(2)}) collective-permute-start(f32[16,8,128]{2,1,0:T(8,128)S(1)} %get-tuple-element.126), channel_id=1, source_target_pairs={{0,192},{64,0},{128,64},{192,128},{1,193},{65,1},{129,65},{193,129... | collective-permute-start | bytes 196616 | tf_op jit(solution)/shard_map/ppermute | solution.py:28
  77.4 8.8 %collective-permute-start.22 = (f32[9,8,128]{2,1,0:T(8,128)S(1)}, f32[9,8,128]{2,1,0:T(8,128)S(1)}, u32[]{:S(2)}, u32[]{:S(2)}) collective-permute-start(f32[9,8,128]{2,1,0:T(8,128)S(1)} %get-tuple-element.128.p0), channel_id=1, source_target_pairs={{0,16},{16,32},{32,48},{48,0},{1,17},{17,33},{33,49},{49,1},{2,18}... | collective-permute-start | bytes 110600 | tf_op jit(solution)/shard_map/ppermute | solution.py:28
  78.3 9.1 %collective-permute-start.23 = (f32[9,8,128]{2,1,0:T(8,128)S(1)}, f32[9,8,128]{2,1,0:T(8,128)S(1)}, u32[]{:S(2)}, u32[]{:S(2)}) collective-permute-start(f32[9,8,128]{2,1,0:T(8,128)S(1)} %get-tuple-element.128.p0), channel_id=1, source_target_pairs={{0,32},{16,48},{32,0},{48,16},{1,33},{17,49},{33,1},{49,17},{2,34}... | collective-permute-start | bytes 110600 | tf_op jit(solution)/shard_map/ppermute | solution.py:28
  80.3 7.1 %collective-permute-start.24 = (f32[9,8,128]{2,1,0:T(8,128)S(1)}, f32[9,8,128]{2,1,0:T(8,128)S(1)}, u32[]{:S(2)}, u32[]{:S(2)}) collective-permute-start(f32[9,8,128]{2,1,0:T(8,128)S(1)} %get-tuple-element.128.p0), channel_id=1, source_target_pairs={{0,48},{16,0},{32,16},{48,32},{1,49},{17,1},{33,17},{49,33},{2,50}... | collective-permute-start | bytes 110600 | tf_op jit(solution)/shard_map/ppermute | solution.py:28
  80.9 2.7 %collective-permute-start.18 = (f32[7,8,128]{2,1,0:T(8,128)S(1)}, f32[7,8,128]{2,1,0:T(8,128)S(1)}, u32[]{:S(2)}, u32[]{:S(2)}) collective-permute-start(f32[7,8,128]{2,1,0:T(8,128)S(1)} %get-tuple-element.127.own), channel_id=1, source_target_pairs={{0,8},{8,0},{1,9},{9,1},{2,10},{10,2},{3,11},{11,3},{4,12},{12,4},... | collective-permute-start | bytes 86024 | tf_op jit(solution)/shard_map/ppermute | solution.py:32
  83.7 7.7 %collective-permute-start.19 = (f32[14,8,128]{2,1,0:T(8,128)S(1)}, f32[14,8,128]{2,1,0:T(8,128)S(1)}, u32[]{:S(2)}, u32[]{:S(2)}) collective-permute-start(f32[14,8,128]{2,1,0:T(8,128)S(1)} %shard_map.65.p0), channel_id=1, source_target_pairs={{0,1},{1,2},{2,3},{3,0},{4,5},{5,6},{6,7},{7,4},{8,9},{9,10},{10,1... | collective-permute-start | bytes 172040 | tf_op jit(solution)/shard_map/ppermute | solution.py:28
  83.8 7.7 %collective-permute-start.20 = (f32[14,8,128]{2,1,0:T(8,128)S(1)}, f32[14,8,128]{2,1,0:T(8,128)S(1)}, u32[]{:S(2)}, u32[]{:S(2)}) collective-permute-start(f32[14,8,128]{2,1,0:T(8,128)S(1)} %shard_map.65.p0), channel_id=1, source_target_pairs={{0,2},{1,3},{2,0},{3,1},{4,6},{5,7},{6,4},{7,5},{8,10},{9,11},{10,... | collective-permute-start | bytes 172040 | tf_op jit(solution)/shard_map/ppermute | solution.py:28
  86.2 5.2 %collective-permute-start.21 = (f32[14,8,128]{2,1,0:T(8,128)S(1)}, f32[14,8,128]{2,1,0:T(8,128)S(1)}, u32[]{:S(2)}, u32[]{:S(2)}) collective-permute-start(f32[14,8,128]{2,1,0:T(8,128)S(1)} %shard_map.65.p0), channel_id=1, source_target_pairs={{0,3},{1,0},{2,1},{3,2},{4,7},{5,4},{6,5},{7,6},{8,11},{9,8},{10,9... | collective-permute-start | bytes 172040 | tf_op jit(solution)/shard_map/ppermute | solution.py:28
  87.4 4.0 %copy-start = (f32[2,320,320]{2,1,0:T(8,128)S(1)}, f32[2,320,320]{2,1,0:T(8,128)}, u32[]{:S(2)}) copy-start(f32[2,320,320]{2,1,0:T(8,128)} %running.3) | copy-start | bytes 2457604
  97.7 11.4 %collective-permute-start.28 = (bf16[2,320,384]{2,1,0:T(8,128)(2,1)S(1)}, bf16[2,320,384]{2,1,0:T(8,128)(2,1)S(1)}, u32[]{:S(2)}, u32[]{:S(2)}) collective-permute-start(bf16[2,320,384]{2,1,0:T(8,128)(2,1)S(1)} %get-tuple-element.136), channel_id=1, source_target_pairs={{0,4},{4,0},{1,5},{5,1},{2,6},{6,2},{3,7},{7,3},{8,12},{12,8},{9,1... | collective-permute-start | bytes 1474568 | tf_op jit(solution)/shard_map/ppermute | solution.py:24
  104.6 7.0 %collective-permute-start.25 = (bf16[128,640]{1,0:T(8,128)(2,1)S(1)}, bf16[128,640]{1,0:T(8,128)(2,1)S(1)}, u32[]{:S(2)}, u32[]{:S(2)}) collective-permute-start(bf16[128,640]{1,0:T(8,128)(2,1)S(1)} %get-tuple-element.135.refs_0_), channel_id=1, source_target_pairs={{0,1},{1,2},{2,3},{3,0},{4,5},{5,6},{6,7},{7,4},{8,9},{9,10},{10,1... | collective-permute-start | bytes 491528 | tf_op jit(solution)/shard_map/ppermute | solution.py:28
  105.0 10.2 %collective-permute-start.26 = (bf16[128,640]{1,0:T(8,128)(2,1)S(1)}, bf16[128,640]{1,0:T(8,128)(2,1)S(1)}, u32[]{:S(2)}, u32[]{:S(2)}) collective-permute-start(bf16[128,640]{1,0:T(8,128)(2,1)S(1)} %get-tuple-element.135.refs_0_), channel_id=1, source_target_pairs={{0,2},{1,3},{2,0},{3,1},{4,6},{5,7},{6,4},{7,5},{8,10},{9,11},{10,... | collective-permute-start | bytes 491528 | tf_op jit(solution)/shard_map/ppermute | solution.py:28
  107.5 7.9 %collective-permute-start.27 = (bf16[128,640]{1,0:T(8,128)(2,1)S(1)}, bf16[128,640]{1,0:T(8,128)(2,1)S(1)}, u32[]{:S(2)}, u32[]{:S(2)}) collective-permute-start(bf16[128,640]{1,0:T(8,128)(2,1)S(1)} %get-tuple-element.135.refs_0_), channel_id=1, source_target_pairs={{0,3},{1,0},{2,1},{3,2},{4,7},{5,4},{6,5},{7,6},{8,11},{9,8},{10,9... | collective-permute-start | bytes 491528 | tf_op jit(solution)/shard_map/ppermute | solution.py:28
  109.6 9.9 %collective-permute-start.29 = (bf16[128,640]{1,0:T(8,128)(2,1)S(1)}, bf16[128,640]{1,0:T(8,128)(2,1)S(1)}, u32[]{:S(2)}, u32[]{:S(2)}) collective-permute-start(bf16[128,640]{1,0:T(8,128)(2,1)S(1)} %shard_map.68.refs_4_), channel_id=1, source_target_pairs={{0,1},{1,2},{2,3},{3,0},{4,5},{5,6},{6,7},{7,4},{8,9},{9,10},{10,1... | collective-permute-start | bytes 491528 | tf_op jit(solution)/shard_map/ppermute | solution.py:28
  109.7 12.6 %collective-permute-start.30 = (bf16[128,640]{1,0:T(8,128)(2,1)S(1)}, bf16[128,640]{1,0:T(8,128)(2,1)S(1)}, u32[]{:S(2)}, u32[]{:S(2)}) collective-permute-start(bf16[128,640]{1,0:T(8,128)(2,1)S(1)} %shard_map.68.refs_4_), channel_id=1, source_target_pairs={{0,2},{1,3},{2,0},{3,1},{4,6},{5,7},{6,4},{7,5},{8,10},{9,11},{10,... | collective-permute-start | bytes 491528 | tf_op jit(solution)/shard_map/ppermute | solution.py:28
  111.6 10.8 %collective-permute-start.31 = (bf16[128,640]{1,0:T(8,128)(2,1)S(1)}, bf16[128,640]{1,0:T(8,128)(2,1)S(1)}, u32[]{:S(2)}, u32[]{:S(2)}) collective-permute-start(bf16[128,640]{1,0:T(8,128)(2,1)S(1)} %shard_map.68.refs_4_), channel_id=1, source_target_pairs={{0,3},{1,0},{2,1},{3,2},{4,7},{5,4},{6,5},{7,6},{8,11},{9,8},{10,9... | collective-permute-start | bytes 491528 | tf_op jit(solution)/shard_map/ppermute | solution.py:28
